TPU v7x, 32 devices: a whole 2x2x4 slice. The times are simulated.
32 devices in a mesh: dp: 2 (over x), ctx: 4 (over z), tensor: 4 (over y, core).
Axes of the slice: x: 2, y: 2, z: 4, core: 2. Of those that a mesh axis runs over, the one named last changes fastest.
Arguments:
- tokens: bfloat16 [6144, 2048], P(('dp', 'ctx')), may hold values from -6 to 6
- attn_gain: float32 [2048], replicated, may hold values from 0.5 to 1.5
- w_query: bfloat16 [2048, 2048], P(None, 'tensor'), may hold values from -0.125 to 0.125
- w_key: bfloat16 [2048, 2048], P(None, 'tensor'), may hold values from -0.125 to 0.125
- w_value: bfloat16 [2048, 2048], P(None, 'tensor'), may hold values from -0.125 to 0.125
- w_out: bfloat16 [2048, 2048], P('tensor'), may hold values from -0.75 to 0.75
- mlp_gain: float32 [2048], replicated, may hold values from 0.5 to 1.5
- w_gate: bfloat16 [2048, 8192], P(None, 'tensor'), may hold values from -0.125 to 0.125
- w_up: bfloat16 [2048, 8192], P(None, 'tensor'), may hold values from -0.125 to 0.125
- w_down: bfloat16 [8192, 2048], P('tensor'), may hold values from -0.0625 to 0.0625
- cotangent: bfloat16 [6144, 2048], P(('dp', 'ctx')), may hold values from -6 to 6
Outputs:
- output: bfloat16 [6144, 2048], P(('dp', 'ctx'))
- input_grad: bfloat16 [6144, 2048], P(('dp', 'ctx'))
- attn_gain_grad: float32 [2048], P(('dp', 'ctx'))
- query_grad: float32 [2048, 2048], P(('dp', 'ctx'), 'tensor')
- key_grad: float32 [2048, 2048], P(('dp', 'ctx'), 'tensor')
- value_grad: float32 [2048, 2048], P(('dp', 'ctx'), 'tensor')
- out_grad: float32 [2048, 2048], P('tensor', ('dp', 'ctx'))
- mlp_gain_grad: float32 [2048], P(('dp', 'ctx'))
- gate_grad: float32 [2048, 8192], P(('dp', 'ctx'), 'tensor')
- up_grad: float32 [2048, 8192], P(('dp', 'ctx'), 'tensor')
- down_grad: float32 [8192, 2048], P('tensor', ('dp', 'ctx'))
All inputs are finite; a program needn't handle non-finite values.
Results may differ from a plain program's by a relative error of at most 0.022.
Values may be sent and summed in bfloat16 or wider, within the bound.
No kernel may reach another device: no remote copies, remote signals or barrier semaphores. Data moves between devices by JAX's collectives and lax.ppermute only.
A program may use at most 256 MiB of HBM per device.

v0:
```python
import jax
import jax.numpy as jnp
from jax import lax
from jax.sharding import PartitionSpec as P

HEAD_DIM = 64


EPS = 1e-05
THETA = 130000.0


def rope_tables(positions):
    half = HEAD_DIM // 2
    freq = jnp.power(THETA, -jnp.arange(half, dtype=jnp.float32) * (2.0 / HEAD_DIM))
    angle = positions.astype(jnp.float32)[:, None] * freq[None, :]
    return (jnp.cos(angle), jnp.sin(angle))


def rotate(vector, cosine, sine):
    half = vector.shape[-1] // 2
    first = vector[..., :half]
    second = vector[..., half:]
    cos_h = cosine[:, None, :]
    sin_h = sine[:, None, :]
    return jnp.concatenate(
        [first * cos_h - second * sin_h, second * cos_h + first * sin_h], axis=-1
    )


def unrotate(vector, cosine, sine):
    half = vector.shape[-1] // 2
    first = vector[..., :half]
    second = vector[..., half:]
    cos_h = cosine[:, None, :]
    sin_h = sine[:, None, :]
    return jnp.concatenate(
        [first * cos_h + second * sin_h, second * cos_h - first * sin_h], axis=-1
    )


def normalize(vector):
    inverse = lax.rsqrt(jnp.mean(vector * vector, axis=-1, keepdims=True) + EPS)
    return (vector * inverse, inverse)


def norm_back(grad_rows, normed, inverse, gain):
    scaled = grad_rows * gain
    gain_grad = jnp.sum(grad_rows * normed, axis=0)
    row_back = inverse * (scaled - normed * jnp.mean(scaled * normed, axis=-1, keepdims=True))
    return (row_back, gain_grad)


def across(left, right):
    return lax.dot_general(
        left, right, (((0,), (0,)), ((), ())), preferred_element_type=jnp.float32
    )


def against(left, right):
    return lax.dot_general(
        left, right, (((1,), (1,)), ((), ())), preferred_element_type=jnp.float32
    )


def head_scores(queries, key_rows, positions):
    scores = against(queries, key_rows) * HEAD_DIM ** (-0.5)
    places = jnp.arange(key_rows.shape[0], dtype=jnp.int32)
    return jnp.where(positions[:, None] >= places[None, :], scores, -1e30)


def head_forward(queries, key_rows, value_rows, positions):
    scores = head_scores(queries, key_rows, positions)
    peak = jnp.max(scores, axis=-1, keepdims=True)
    weights = jnp.exp(scores - peak)
    mass_sum = jnp.sum(weights, axis=-1, keepdims=True)
    chance = (weights / mass_sum).astype(jnp.bfloat16)
    return (jnp.dot(chance, value_rows, preferred_element_type=jnp.float32), peak, mass_sum)


def head_backward(queries, key_rows, value_rows, upstream, peak, mass_sum, positions):
    scores = head_scores(queries, key_rows, positions)
    chance = jnp.exp(scores - peak) / mass_sum
    value_back = across(chance.astype(jnp.bfloat16), upstream)
    chance_back = against(upstream, value_rows)
    score_back = (
        chance * (chance_back - jnp.sum(chance * chance_back, axis=-1, keepdims=True))
    ).astype(jnp.bfloat16)
    query_back = jnp.dot(score_back, key_rows, preferred_element_type=jnp.float32) * HEAD_DIM ** (
        -0.5
    )
    key_back = across(score_back, queries) * HEAD_DIM ** (-0.5)
    return (query_back, key_back, value_back)


def per_device(
    tokens, attn_gain, w_query, w_key, w_value, w_out, mlp_gain, w_gate, w_up, w_down, cotangent
):
    rows_here = tokens.shape[0]
    local_width = w_query.shape[1]
    head_count = local_width // HEAD_DIM
    positions = lax.axis_index("ctx") * rows_here + jnp.arange(rows_here, dtype=jnp.int32)
    cosine, sine = rope_tables(positions)
    inputs = tokens.astype(jnp.float32)
    normed_one, inverse_one = normalize(inputs)
    first_in = (normed_one * attn_gain).astype(jnp.bfloat16)

    def heads_of(flat):
        return flat.reshape(rows_here, head_count, HEAD_DIM)

    def project(weight):
        return jnp.dot(first_in, weight, preferred_element_type=jnp.float32)

    query_rot = rotate(heads_of(project(w_query)), cosine, sine).astype(jnp.bfloat16)
    key_rot = rotate(heads_of(project(w_key)), cosine, sine).astype(jnp.bfloat16)
    value_low = project(w_value).astype(jnp.bfloat16)
    key_all, value_all = (
        lax.all_gather(key_rot.reshape(rows_here, local_width), "ctx", axis=0, tiled=True),
        lax.all_gather(value_low, "ctx", axis=0, tiled=True),
    )
    key_count = key_all.shape[0]

    def per_head(flat, length):
        return flat.reshape(length, head_count, HEAD_DIM).transpose(1, 0, 2)

    queries_h = query_rot.transpose(1, 0, 2)
    keys_h = per_head(key_all, key_count)
    values_h = per_head(value_all, key_count)

    def forward_one(group):
        return head_forward(group[0], group[1], group[2], positions)

    mixed, peak, mass_sum = lax.map(forward_one, (queries_h, keys_h, values_h))
    attended = mixed.transpose(1, 0, 2).reshape(rows_here, local_width).astype(jnp.bfloat16)
    branch_one = lax.psum(
        jnp.dot(attended, w_out, preferred_element_type=jnp.float32).astype(jnp.bfloat16), "tensor"
    ).astype(jnp.float32)
    middle = inputs + branch_one
    normed_two, inverse_two = normalize(middle)
    second_in = (normed_two * mlp_gain).astype(jnp.bfloat16)
    gate_val = jnp.dot(second_in, w_gate, preferred_element_type=jnp.float32)
    up_val = jnp.dot(second_in, w_up, preferred_element_type=jnp.float32)
    sigmoid_gate = jax.nn.sigmoid(gate_val)
    swish = gate_val * sigmoid_gate
    hidden = (swish * up_val).astype(jnp.bfloat16)
    branch_two = lax.psum(
        jnp.dot(hidden, w_down, preferred_element_type=jnp.float32).astype(jnp.bfloat16), "tensor"
    ).astype(jnp.float32)
    output = (middle + branch_two).astype(jnp.bfloat16)
    upstream = cotangent.astype(jnp.float32)
    down_wgrad = across(hidden, cotangent)
    hidden_back = against(cotangent, w_down)
    gate_back = (
        hidden_back * up_val * sigmoid_gate * (1.0 + gate_val * (1.0 - sigmoid_gate))
    ).astype(jnp.bfloat16)
    up_back = (hidden_back * swish).astype(jnp.bfloat16)
    gate_wgrad = across(second_in, gate_back)
    up_wgrad = across(second_in, up_back)
    second_part = against(gate_back, w_gate) + against(up_back, w_up)
    second_sum = lax.psum(second_part.astype(jnp.bfloat16), "tensor").astype(jnp.float32)
    middle_back, mlp_gain_grad = norm_back(second_sum, normed_two, inverse_two, mlp_gain)
    middle_grad = upstream + middle_back
    branch_low = middle_grad.astype(jnp.bfloat16)
    out_wgrad = across(attended, branch_low)
    attended_back = against(branch_low, w_out).astype(jnp.bfloat16)
    upstream_h = heads_of(attended_back).transpose(1, 0, 2)

    def backward_one(group):
        return head_backward(group[0], group[1], group[2], group[3], group[4], group[5], positions)

    query_back, key_back, value_back = lax.map(
        backward_one, (queries_h, keys_h, values_h, upstream_h, peak, mass_sum)
    )
    key_flat = key_back.transpose(1, 0, 2).reshape(key_count, local_width)
    value_flat = value_back.transpose(1, 0, 2).reshape(key_count, local_width)
    key_mine, value_mine = (
        lax.psum_scatter(
            key_flat.astype(jnp.bfloat16), "ctx", scatter_dimension=0, tiled=True
        ).astype(jnp.float32),
        lax.psum_scatter(
            value_flat.astype(jnp.bfloat16), "ctx", scatter_dimension=0, tiled=True
        ).astype(jnp.float32),
    )
    query_low = (
        unrotate(query_back.transpose(1, 0, 2), cosine, sine)
        .reshape(rows_here, local_width)
        .astype(jnp.bfloat16)
    )
    key_low = (
        unrotate(heads_of(key_mine), cosine, sine)
        .reshape(rows_here, local_width)
        .astype(jnp.bfloat16)
    )
    value_low_back = value_mine.astype(jnp.bfloat16)
    query_wgrad = across(first_in, query_low)
    key_wgrad = across(first_in, key_low)
    value_wgrad = across(first_in, value_low_back)
    first_part = (
        against(query_low, w_query) + against(key_low, w_key) + against(value_low_back, w_value)
    )
    first_sum = lax.psum(first_part.astype(jnp.bfloat16), "tensor").astype(jnp.float32)
    input_back, attn_gain_grad = norm_back(first_sum, normed_one, inverse_one, attn_gain)
    input_grad = (middle_grad + input_back).astype(jnp.bfloat16)
    shares = (
        lax.psum_scatter(
            attn_gain_grad.astype(jnp.bfloat16), ("dp", "ctx"), scatter_dimension=0, tiled=True
        ).astype(jnp.float32),
        lax.psum_scatter(
            query_wgrad.astype(jnp.bfloat16), ("dp", "ctx"), scatter_dimension=0, tiled=True
        ).astype(jnp.float32),
        lax.psum_scatter(
            key_wgrad.astype(jnp.bfloat16), ("dp", "ctx"), scatter_dimension=0, tiled=True
        ).astype(jnp.float32),
        lax.psum_scatter(
            value_wgrad.astype(jnp.bfloat16), ("dp", "ctx"), scatter_dimension=0, tiled=True
        ).astype(jnp.float32),
        lax.psum_scatter(
            out_wgrad.astype(jnp.bfloat16), ("dp", "ctx"), scatter_dimension=1, tiled=True
        ).astype(jnp.float32),
        lax.psum_scatter(
            mlp_gain_grad.astype(jnp.bfloat16), ("dp", "ctx"), scatter_dimension=0, tiled=True
        ).astype(jnp.float32),
        lax.psum_scatter(
            gate_wgrad.astype(jnp.bfloat16), ("dp", "ctx"), scatter_dimension=0, tiled=True
        ).astype(jnp.float32),
        lax.psum_scatter(
            up_wgrad.astype(jnp.bfloat16), ("dp", "ctx"), scatter_dimension=0, tiled=True
        ).astype(jnp.float32),
        lax.psum_scatter(
            down_wgrad.astype(jnp.bfloat16), ("dp", "ctx"), scatter_dimension=1, tiled=True
        ).astype(jnp.float32),
    )
    return (
        output,
        input_grad,
        shares[0],
        shares[1],
        shares[2],
        shares[3],
        shares[4],
        shares[5],
        shares[6],
        shares[7],
        shares[8],
    )


def solution(mesh):
    in_specs = (
        P(("dp", "ctx"), None),
        P(),
        P(None, "tensor"),
        P(None, "tensor"),
        P(None, "tensor"),
        P("tensor", None),
        P(),
        P(None, "tensor"),
        P(None, "tensor"),
        P("tensor", None),
        P(("dp", "ctx"), None),
    )
    out_specs = (
        P(("dp", "ctx"), None),
        P(("dp", "ctx"), None),
        P(("dp", "ctx")),
        P(("dp", "ctx"), "tensor"),
        P(("dp", "ctx"), "tensor"),
        P(("dp", "ctx"), "tensor"),
        P("tensor", ("dp", "ctx")),
        P(("dp", "ctx")),
        P(("dp", "ctx"), "tensor"),
        P(("dp", "ctx"), "tensor"),
        P("tensor", ("dp", "ctx")),
    )
    return jax.shard_map(
        per_device, mesh=mesh, in_specs=in_specs, out_specs=out_specs, check_vma=False
    )
```

profile of v0, /device:TPU:0, one launch (start us, length us, event | category | flops | bytes accessed | tf_op | source)
XLA Modules:
  0.0 1741.4 jit_solution(11654948339593056651)
XLA Ops:
  10.0 5.9 fusion.84
  23.6 5.3 convolution_convert_fusion.9
  32.1 57.8 %all-gather.3.cloned.1.call-done = bf16[3072,512]{0,1:T(8,128)(2,1)} async-done(((bf16[768,512]{0,1:T(8,128)(2,1)}), bf16[3072,512]{0,1:T(8,128)(2,1)}) %all-gather.3.cloned.1.call-update) | async-done | bytes 3145744 | tf_op jit(solution)/shard_map/all_gather | solution.py:118
  89.9 6.6 copy.36
  96.5 57.8 %all-gather.5.cloned.1.call-done = bf16[3072,512]{1,0:T(8,128)(2,1)} async-done(((bf16[768,512]{1,0:T(8,128)(2,1)}), bf16[3072,512]{1,0:T(8,128)(2,1)}) %all-gather.5.cloned.1.call-update) | async-done | bytes 3145744 | tf_op jit(solution)/shard_map/all_gather | solution.py:119
  154.3 4.6 copy.34
  158.9 6.6 copy.37
  165.5 82.6 %while.32 = (s32[]{:T(128)}, bf16[8,768,64]{1,2,0:T(8,128)(2,1)S(1)}, f32[8,768,1]{1,2,0:T(1,128)S(1)}, f32[8,768,1]{1,2,0:T(1,128)S(1)}, bf16[8,768,64]{2,1,0:T...) while((s32[]{:T(128)}, ...), condition=%wide.region_4.5_spmd.clone.clone, body=%wide.region_1.4_spmd.clone.sunk.clone | while | flops 639368448 | bytes 30324828 | solution.py:133
  251.6 67.2 %all-reduce.8.cloned.1.call-done = bf16[768,2048]{1,0:T(8,128)(2,1)} async-done(((bf16[768,2048]{1,0:T(8,128)(2,1)}), bf16[768,2048]{1,0:T(8,128)(2,1)}) %all-reduce.8.cloned.1.call-update) | async-done | bytes 3145744 | tf_op jit(solution)/shard_map/psum | solution.py:135
  326.5 8.8 fusion.86
  335.2 10.8 fusion.87
  346.1 15.9 multiply_convert_fusion.1
  362.0 11.2 fusion.88
  373.2 10.5 add_convert_fusion.1
  383.8 68.6 %all-reduce.10.cloned.1.call-done = bf16[768,2048]{1,0:T(8,128)(2,1)} async-done(((bf16[768,2048]{1,0:T(8,128)(2,1)}), bf16[768,2048]{1,0:T(8,128)(2,1)}) %all-reduce.10.cloned.1.call-update) | async-done | bytes 3145744 | tf_op jit(solution)/shard_map/psum | solution.py:160
  452.5 6.9 fusion.65
  459.4 5.1 fusion.64
  468.0 278.6 %while.33 = (s32[]{:T(128)}, f32[8,768,64]{1,2,0:T(8,128)}, bf16[8,3072,64]{1,2,0:T(8,128)(2,1)}, bf16[8,3072,64]{1,2,0:T(8,128)(2,1)}, bf16[8,768,64]{2,1,0:T(8...) while((s32[]{:T(128)}, f32[8,768,64]{1,2,0:T(8,128)}, ...), condition=%wide.region_12.13_spmd.clone.clone, body=%wide.region_10.12_spmd.clone.sunk.clone | while | flops 1536147456 | bytes 132353192 | solution.py:171
  471.0 8.0 multiply_reduce_fusion.4
  479.0 11.2 multiply_convert_fusion.7
  497.8 5.4 fusion.174
  505.8 8.0 multiply_reduce_fusion.4
  513.8 11.2 multiply_convert_fusion.7
  532.6 5.4 fusion.174
  540.5 8.0 multiply_reduce_fusion.4
  548.5 11.2 multiply_convert_fusion.7
  567.3 5.4 fusion.174
  575.3 8.0 multiply_reduce_fusion.4
  583.3 11.2 multiply_convert_fusion.7
  602.0 5.4 fusion.174
  610.0 8.0 multiply_reduce_fusion.4
  618.0 11.2 multiply_convert_fusion.7
  636.8 5.4 fusion.174
  644.8 8.0 multiply_reduce_fusion.4
  652.8 11.2 multiply_convert_fusion.7
  671.6 5.4 fusion.174
  679.6 8.0 multiply_reduce_fusion.4
  687.6 11.2 multiply_convert_fusion.7
  706.3 5.4 fusion.174
  714.3 8.0 multiply_reduce_fusion.4
  722.3 11.2 multiply_convert_fusion.7
  741.1 5.4 fusion.174
  747.7 6.0 convolution_convert_fusion.5
  753.8 12.0 convolution_convert_fusion.3
  765.8 41.3 %reduce-scatter.10.cloned.1.call-done = bf16[768,512]{0,1:T(8,128)(2,1)} async-done(((bf16[3072,512]{0,1:T(8,128)(2,1)}), bf16[768,512]{0,1:T(8,128)(2,1)}) %reduce-scatter.10.cloned.1.call-update) | async-done | bytes 786448 | tf_op jit(solution)/shard_map/reduce_scatter | solution.py:177
  810.5 4.5 fusion.89
  819.4 50.2 %reduce-scatter.12.cloned.1.call-done = bf16[768,512]{0,1:T(8,128)(2,1)} async-done(((bf16[3072,512]{0,1:T(8,128)(2,1)}), bf16[768,512]{0,1:T(8,128)(2,1)}) %reduce-scatter.12.cloned.1.call-update) | async-done | bytes 786448 | tf_op jit(solution)/shard_map/reduce_scatter | solution.py:180
  869.6 9.0 add_convert_fusion
  879.2 5.5 convolution_convert_fusion.8
  885.0 5.3 convolution_convert_fusion.7
  890.4 5.3 convolution_convert_fusion.6
  895.8 11.4 convolution_convert_fusion.2
  907.3 11.4 convolution_convert_fusion.1
  919.1 11.4 convolution_convert_fusion
  932.4 8.8 reduce-scatter.20.cloned.1.call-done
  942.9 119.5 %all-reduce.12.cloned.1.call-done = (bf16[768,2048]{1,0:T(8,128)(2,1)}, bf16[768,2048]{1,0:T(8,128)(2,1)}) async-done(((bf16[768,2048]{1,0:T(8,128)(2,1)}, bf16[768,2048]{1,0:T(8,128)(2,1)}), (bf16[768,2048]{1,0:T(8,128)(2,1)}, bf16[768,2048]{1,0:T(8,128)(2,1)})) %all-reduce.12.cloned.1.call-update) | async-done | bytes 6291472 | tf_op jit(solution)/shard_map/psum | solution.py:146
  1066.6 22.2 %all-reduce.2 = (bf16[2048]{0:T(1024)(128)(2,1)S(1)}, bf16[2048]{0:T(1024)(128)(2,1)S(1)}) all-reduce(bf16[2048]{0:T(1024)(128)(2,1)S(1)} %get-tuple-element.223, bf16[2048]{0:T(1024)(128)(2,1)S(1)} %copy-done.28), channel_id=4, replica_groups=mesh['dp'=2,'ctx'=4,'tensor'=4] {'dp','ctx'}, use_global_device_ids=true, to_apply=%region_18.19.clone | all-reduce | flops 4096 | bytes 16384
  1090.1 10.5 fusion.61
  1100.6 34.3 %reduce-scatter.14.cloned.1.call-done = bf16[256,512]{1,0:T(8,128)(2,1)} async-done(((bf16[2048,512]{1,0:T(8,128)(2,1)}), bf16[256,512]{1,0:T(8,128)(2,1)}) %reduce-scatter.14.cloned.1.call-update) | async-done | bytes 262160 | tf_op jit(solution)/shard_map/reduce_scatter | solution.py:208
  1136.7 68.8 %reduce-scatter.16.cloned.1.call-done = bf16[256,512]{1,0:T(8,128)(2,1)} async-done(((bf16[2048,512]{1,0:T(8,128)(2,1)}), bf16[256,512]{1,0:T(8,128)(2,1)}) %reduce-scatter.16.cloned.1.call-update) | async-done | bytes 262160 | tf_op jit(solution)/shard_map/reduce_scatter | solution.py:211
  1207.3 68.9 %reduce-scatter.18.cloned.1.call-done = bf16[256,512]{1,0:T(8,128)(2,1)} async-done(((bf16[2048,512]{1,0:T(8,128)(2,1)}), bf16[256,512]{1,0:T(8,128)(2,1)}) %reduce-scatter.18.cloned.1.call-update) | async-done | bytes 262160 | tf_op jit(solution)/shard_map/reduce_scatter | solution.py:214
  1278.0 149.7 %reduce-scatter.22.cloned.1.call-done = bf16[256,2048]{1,0:T(8,128)(2,1)} async-done(((bf16[2048,2048]{1,0:T(8,128)(2,1)}), bf16[256,2048]{1,0:T(8,128)(2,1)}) %reduce-scatter.22.cloned.1.call-update) | async-done | bytes 1048592 | tf_op jit(solution)/shard_map/reduce_scatter | solution.py:223
  1430.5 149.3 %reduce-scatter.24.cloned.1.call-done = bf16[256,2048]{1,0:T(8,128)(2,1)} async-done(((bf16[2048,2048]{1,0:T(8,128)(2,1)}), bf16[256,2048]{1,0:T(8,128)(2,1)}) %reduce-scatter.24.cloned.1.call-update) | async-done | bytes 1048592 | tf_op jit(solution)/shard_map/reduce_scatter | solution.py:226
  1582.5 149.1 %reduce-scatter.26.cloned.1.call-done = bf16[2048,256]{1,0:T(8,128)(2,1)} async-done(((bf16[2048,2048]{1,0:T(8,128)(2,1)}), bf16[2048,256]{1,0:T(8,128)(2,1)}) %reduce-scatter.26.cloned.1.call-update) | async-done | bytes 1048592 | tf_op jit(solution)/shard_map/reduce_scatter | solution.py:229
  (239 shorter events, 224.4 us)
Async XLA Ops:
  7.2 240.9 %copy-start = (bf16[512,2048]{1,0:T(8,128)(2,1)S(1)}, bf16[512,2048]{1,0:T(8,128)(2,1)}, u32[]{:S(2)}) copy-start(bf16[512,2048]{1,0:T(8,128)(2,1)} %param.20) | copy-start | bytes 6291460
  7.2 82.7 %all-gather.3.cloned.1.call-start = ((), (), s32[]{:S(2)}) async-start(), calls=%async_computation.9 | async-start | bytes 3932160 | tf_op jit(solution)/shard_map/all_gather | solution.py:118
  10.0 13.6 copy-start.24
  10.0 5.9 copy-start.4
  10.0 5.9 copy-start.14
  10.0 5.9 copy-start.26
  19.5 4.1 copy-start.16
  19.5 4.0 copy-start.18
  23.6 130.7 %all-gather.5.cloned.1.call-start = ((), (), s32[]{:S(2)}) async-start(), calls=%async_computation.10 | async-start | bytes 3932160 | tf_op jit(solution)/shard_map/all_gather | solution.py:119
  28.9 289.9 %all-reduce.8.cloned.1.call-start = ((), (), s32[]{:S(2)}) async-start(), calls=%async_computation.11 | async-start | bytes 6291456 | tf_op jit(solution)/shard_map/psum | solution.py:135
  248.1 74.9 %copy-start.21 = (bf16[8,768,64]{1,2,0:T(8,128)(2,1)}, bf16[8,768,64]{1,2,0:T(8,128)(2,1)S(1)}, u32[]{:S(2)}) copy-start(bf16[8,768,64]{1,2,0:T(8,128)(2,1)S(1)} %get-tuple-element.114) | copy-start | bytes 2359300
  251.6 71.4 %copy-start.23 = (f32[2048]{0:T(1024)S(1)}, f32[2048]{0:T(1024)}, u32[]{:S(2)}) copy-start(f32[2048]{0:T(1024)} %param.21) | copy-start | bytes 24580
  251.6 200.9 %all-reduce.10.cloned.1.call-start = ((), (), s32[]{:S(2)}) async-start(), calls=%async_computation.12 | async-start | bytes 6291456 | tf_op jit(solution)/shard_map/psum | solution.py:160
  318.8 4.1 copy-start.5
  318.8 4.7 copy-start.7
  322.9 3.5 copy-start.29
  326.5 8.8 copy-start.11
  335.2 10.8 copy-start.12
  362.0 11.2 copy-start.31
  383.8 423.3 %reduce-scatter.10.cloned.1.call-start = ((), (), s32[]{:S(2)}) async-start(), calls=%async_computation.13 | async-start | bytes 3932160 | tf_op jit(solution)/shard_map/reduce_scatter | solution.py:177
  452.5 6.9 copy-start.6
  452.5 6.9 copy-start.8
  452.5 6.9 copy-start.10
  464.5 2.6 copy-start.9
  470.9 8.1 copy-start.3
  490.2 4.2 copy-start.2
  505.7 8.0 copy-start.3
  524.9 4.2 copy-start.2
  540.5 8.1 copy-start.3
  559.7 4.2 copy-start.2
  575.2 8.0 copy-start.3
  594.4 4.2 copy-start.2
  610.0 8.1 copy-start.3
  629.2 4.2 copy-start.2
  644.7 8.1 copy-start.3
  664.0 4.2 copy-start.2
  679.5 8.1 copy-start.3
  698.7 4.2 copy-start.2
  714.3 8.0 copy-start.3
  733.5 4.2 copy-start.2
  746.6 1.1 copy-start.22
  746.6 123.0 %reduce-scatter.12.cloned.1.call-start = ((), (), s32[]{:S(2)}) async-start(), calls=%async_computation.14 | async-start | bytes 3932160 | tf_op jit(solution)/shard_map/reduce_scatter | solution.py:180
  747.2 194.0 %reduce-scatter.20.cloned.1.call-start = ((), (), s32[]{:S(2)}) async-start(), calls=%async_computation.18 | async-start | bytes 2359296 | tf_op jit(solution)/shard_map/reduce_scatter | solution.py:217
  753.7 308.7 %all-reduce.12.cloned.1.call-start = ((), (), s32[]{:S(2)}) async-start(), calls=%async_computation.22 | async-start | bytes 12582912 | tf_op jit(solution)/shard_map/psum | solution.py:146
  753.8 54.7 %copy-start.17 = (f32[768,32]{0,1:T(8,128)S(1)}, f32[768,32]{0,1:T(8,128)}, u32[]{:S(2)}) copy-start(f32[768,32]{0,1:T(8,128)} %copy-done.16) | copy-start | bytes 294916
  753.8 54.7 %copy-start.19 = (f32[768,32]{0,1:T(8,128)S(1)}, f32[768,32]{0,1:T(8,128)}, u32[]{:S(2)}) copy-start(f32[768,32]{0,1:T(8,128)} %copy-done.18) | copy-start | bytes 294916
  807.1 3.4 copy-start.13
  810.4 4.6 copy-start.15
  878.5 0.7 copy-start.25
  878.5 0.7 copy-start.27
  878.6 256.3 %reduce-scatter.14.cloned.1.call-start = ((), (), s32[]{:S(2)}) async-start(), calls=%async_computation.15 | async-start | bytes 2359296 | tf_op jit(solution)/shard_map/reduce_scatter | solution.py:208
  884.7 5.7 copy-start.20
  884.7 320.7 %reduce-scatter.16.cloned.1.call-start = ((), (), s32[]{:S(2)}) async-start(), calls=%async_computation.16 | async-start | bytes 2359296 | tf_op jit(solution)/shard_map/reduce_scatter | solution.py:211
  890.3 385.9 %reduce-scatter.18.cloned.1.call-start = ((), (), s32[]{:S(2)}) async-start(), calls=%async_computation.17 | async-start | bytes 2359296 | tf_op jit(solution)/shard_map/reduce_scatter | solution.py:214
  895.7 532.0 %reduce-scatter.22.cloned.1.call-start = ((), (), s32[]{:S(2)}) async-start(), calls=%async_computation.19 | async-start | bytes 9437184 | tf_op jit(solution)/shard_map/reduce_scatter | solution.py:223
  907.2 672.5 %reduce-scatter.24.cloned.1.call-start = ((), (), s32[]{:S(2)}) async-start(), calls=%async_computation.20 | async-start | bytes 9437184 | tf_op jit(solution)/shard_map/reduce_scatter | solution.py:226
  918.8 812.9 %reduce-scatter.26.cloned.1.call-start = ((), (), s32[]{:S(2)}) async-start(), calls=%async_computation.21 | async-start | bytes 9437184 | tf_op jit(solution)/shard_map/reduce_scatter | solution.py:229
  930.5 0.7 copy-start.30
  930.5 136.1 %copy-start.28 = (bf16[2048]{0:T(1024)(128)(2,1)S(1)}, bf16[2048]{0:T(1024)(128)(2,1)}, u32[]{:S(2)}) copy-start(bf16[2048]{0:T(1024)(128)(2,1)} %get-tuple-element.221) | copy-start | bytes 12292
  1090.1 644.3 %copy-start.1 = (bf16[512,2048]{1,0:T(8,128)(2,1)S(1)}, bf16[512,2048]{1,0:T(8,128)(2,1)}, u32[]{:S(2)}) copy-start(bf16[512,2048]{1,0:T(8,128)(2,1)} %param.20) | copy-start | bytes 6291460
Sparse Core Ops, SparseCore 0:
  23.7 66.1 all-gather.2
  92.0 62.1 all-gather.4
  251.7 67.0 all-reduce.7
  383.9 68.5 all-reduce.9
  746.7 60.3 reduce-scatter.9
  809.3 60.2 reduce-scatter.11
  873.1 68.0 reduce-scatter.19
  943.6 118.8 all-reduce.11
  1066.6 68.2 reduce-scatter.13
  1138.9 66.5 reduce-scatter.15
  1209.6 66.5 reduce-scatter.17
  1279.7 147.9 reduce-scatter.21
  1431.8 147.9 reduce-scatter.23
  1583.3 148.3 reduce-scatter.25
where the time goes:
time: 1750 us; the launch traced here: 1740 us
  waiting for transfers between devices  1090 us (62%)
  matrix products  410 us (23%)
  other arithmetic  174 us (10%)
  local copies, waits for them, and re-layouts  25.3 us (1%)
  blocking collectives  22.2 us (1%)
    dot_general x31, matrix products, against(): lax.dot_general(left, right, (((1,), (1,)), ((), ())), preferred_element_...  166 us
    reduce_scatter x1, waiting for transfers between devices, per_device(): lax.psum_scatter(gate_wgrad.astype(jnp.bfloat16), ('dp', 'ctx'), scatter_...  150 us
    reduce_scatter x1, waiting for transfers between devices, per_device(): lax.psum_scatter(up_wgrad.astype(jnp.bfloat16), ('dp', 'ctx'), scatter_di...  149 us
    reduce_scatter x1, waiting for transfers between devices, per_device(): lax.psum_scatter(down_wgrad.astype(jnp.bfloat16), ('dp', 'ctx'), scatter_...  149 us
    dot_general x23, matrix products, across(): lax.dot_general(left, right, (((0,), (0,)), ((), ())), preferred_element_...  134 us
    psum x1, waiting for transfers between devices, per_device(): lax.psum(jnp.dot(hidden, w_down, preferred_element_type=jnp.float32).asty...  120 us
    convert_element_type x8, other arithmetic, head_backward(): score_back = (chance * (chance_back - jnp.sum(chance * chance_back, axis=...  89.4 us
    reduce_scatter x1, waiting for transfers between devices, per_device(): lax.psum_scatter(value_wgrad.astype(jnp.bfloat16), ('dp', 'ctx'), scatter...  68.9 us
  transfers between devices with their start and end apart: 14, of which 14 were waited for; matrix products, arithmetic and copies ran while one was open for 8% of the time, Pallas kernels for 0%

commit v1 on v0

v1 whole, which is shorter than its diff:
```python
import functools

import jax
import jax.numpy as jnp
from jax import lax
from jax.experimental import pallas as pl
from jax.experimental.pallas import tpu as pltpu
from jax.sharding import PartitionSpec as P

HEAD_DIM = 64
EPS = 1e-05
THETA = 130000.0
BLOCK = 384
MIB = 1 << 20
LOW = jnp.bfloat16
F32 = jnp.float32
ANY = pl.BlockSpec(memory_space=pl.ANY)


def swap(value, axis, size, distance):
    return lax.ppermute(value, axis, [(i, i ^ distance) for i in range(size)])


def dot(left, right):
    return jnp.dot(left, right, preferred_element_type=F32)


def against(left, right):
    return lax.dot_general(left, right, (((1,), (1,)), ((), ())), preferred_element_type=F32)


def across(left, right):
    return lax.dot_general(left, right, (((0,), (0,)), ((), ())), preferred_element_type=F32)


def params(mib):
    return pltpu.CompilerParams(
        vmem_limit_bytes=mib * MIB, dimension_semantics=("arbitrary",)
    )


def cost(flops, moved, exps=0):
    return pl.CostEstimate(flops=int(flops), bytes_accessed=int(moved), transcendentals=int(exps))


def half_turn(rows, width):
    lane = lax.broadcasted_iota(jnp.int32, (1, width), 1)
    first = (lane % HEAD_DIM) < HEAD_DIM // 2
    return jnp.where(first, pltpu.roll(rows, width - 32, 1), pltpu.roll(rows, 32, 1))


def rope_tables(count):
    half = HEAD_DIM // 2
    freq = jnp.power(THETA, -jnp.arange(half, dtype=F32) * (2.0 / HEAD_DIM))
    angle = jnp.arange(count, dtype=jnp.int32).astype(F32)[:, None] * freq[None, :]
    cosine, sine = jnp.cos(angle), jnp.sin(angle)
    return (
        jnp.concatenate([cosine] * 4, axis=1),
        jnp.concatenate([-sine, sine, -sine, sine], axis=1),
    )


def project_kernel(me_ref, tok_ref, gain_ref, cos_ref, sin_ref, wq_ref, wk_ref, wv_ref, first_ref, out_ref):
    me = me_ref[0]
    rows = tok_ref[...].astype(F32)
    inverse = lax.rsqrt(jnp.mean(rows * rows, axis=-1, keepdims=True) + EPS)
    first = (rows * inverse * gain_ref[...]).astype(LOW)
    first_ref[...] = first
    cosine, sine = cos_ref[...], sin_ref[...]
    for place, weight in enumerate((wq_ref, wk_ref, wv_ref)):
        flat = dot(first, weight[...])
        for group in range(4):
            part = flat[:, group * 128 : (group + 1) * 128]
            if place < 2:
                part = part * cosine + half_turn(part, 128) * sine
            if place == 0:
                part = part * HEAD_DIM**-0.5
            out_ref[group ^ me, :, place * 128 : (place + 1) * 128] = part.astype(LOW)


def project(me, tokens, gain, cosine, sine, wq, wk, wv):
    rows, width = tokens.shape
    local = wq.shape[1]
    step = 256
    whole = lambda i, m: (0, 0)
    return pl.pallas_call(
        project_kernel,
        grid_spec=pltpu.PrefetchScalarGridSpec(
            num_scalar_prefetch=1,
            grid=(rows // step,),
            in_specs=[
                pl.BlockSpec((step, width), lambda i, m: (i, 0)),
                pl.BlockSpec((1, width), whole),
                pl.BlockSpec((step, 128), lambda i, m: (m[0] * (rows // step) + i, 0)),
                pl.BlockSpec((step, 128), lambda i, m: (m[0] * (rows // step) + i, 0)),
                pl.BlockSpec((width, local), whole),
                pl.BlockSpec((width, local), whole),
                pl.BlockSpec((width, local), whole),
            ],
            out_specs=[
                pl.BlockSpec((step, width), lambda i, m: (i, 0)),
                pl.BlockSpec((4, step, 384), lambda i, m: (0, i, 0)),
            ],
        ),
        out_shape=[
            jax.ShapeDtypeStruct((rows, width), LOW),
            jax.ShapeDtypeStruct((4, rows, 384), LOW),
        ],
        compiler_params=params(48),
        cost_estimate=cost(2 * rows * width * local * 3, 16 * MIB),
        name="project",
    )(me, tokens, gain.reshape(1, -1), cosine, sine, wq, wk, wv)


def own_lanes(rows, head):
    lane = lax.broadcasted_iota(jnp.int32, (1, 128), 1)
    inside = (lane < HEAD_DIM) if head == 0 else (lane >= HEAD_DIM)
    return jnp.where(inside, rows, jnp.zeros_like(rows))


def attend_kernel(me_ref, r0, r1, r2, r3, out_ref, raw_ref, lse_ref, held, sems):
    me = me_ref[0]
    here = pl.program_id(0)
    stretch = r0.shape[0]

    @pl.when(here == 0)
    def _():
        copies = [
            pltpu.make_async_copy(ref, held.at[pl.ds((me ^ k) * stretch, stretch)], sems.at[k])
            for k, ref in enumerate((r0, r1, r2, r3))
        ]
        for copy in copies:
            copy.start()
        for copy in copies:
            copy.wait()

    query = held[pl.ds(here * BLOCK, BLOCK), 0:128]
    queries = [own_lanes(query, head) for head in range(2)]

    def step(at, carry, diagonal):
        rows = pl.ds(at * BLOCK, BLOCK)
        keys, values = held[rows, 128:256], held[rows, 256:384]
        out = []
        for head in range(2):
            peak, mass, total = carry[3 * head : 3 * head + 3]
            scores = against(queries[head], keys)
            if diagonal:
                down = lax.broadcasted_iota(jnp.int32, (BLOCK, BLOCK), 0)
                along = lax.broadcasted_iota(jnp.int32, (BLOCK, BLOCK), 1)
                scores = jnp.where(down >= along, scores, -1e30)
            top = jnp.maximum(peak, jnp.max(scores, axis=-1, keepdims=True))
            weights = jnp.exp(scores - top)
            fade = jnp.exp(peak - top)
            mass = mass * fade + jnp.sum(weights, axis=-1, keepdims=True)
            total = total * fade + dot(weights.astype(LOW), values)
            out += [top, mass, total]
        return tuple(out)

    start = (
        jnp.full((BLOCK, 1), -1e30, F32),
        jnp.zeros((BLOCK, 1), F32),
        jnp.zeros((BLOCK, 128), F32),
    ) * 2
    carry = lax.fori_loop(0, here, lambda at, c: step(at, c, False), start)
    peak0, mass0, total0, peak1, mass1, total1 = step(here, carry, True)
    lane = lax.broadcasted_iota(jnp.int32, (1, 128), 1)
    mixed = jnp.where(lane < HEAD_DIM, total0 / mass0, total1 / mass1)
    raw_ref[...] = mixed
    out_ref[0] = mixed.astype(LOW)
    turned = jnp.where(lane < HEAD_DIM, peak0 + jnp.log(mass0), peak1 + jnp.log(mass1)).T
    lse_ref[0:8] = turned[0:8]
    lse_ref[8:16] = turned[64:72]


def attend(me, pieces):
    stretch = pieces[0].shape[0]
    length = 4 * stretch
    per = stretch // BLOCK
    pairs = length * length
    return pl.pallas_call(
        attend_kernel,
        grid_spec=pltpu.PrefetchScalarGridSpec(
            num_scalar_prefetch=1,
            grid=(length // BLOCK,),
            in_specs=[ANY] * 4,
            out_specs=[
                pl.BlockSpec((1, BLOCK, 128), lambda i, m: ((i // per) ^ m[0], i % per, 0)),
                pl.BlockSpec((BLOCK, 128), lambda i, m: (i, 0)),
                pl.BlockSpec((16, BLOCK), lambda i, m: (0, i)),
            ],
            scratch_shapes=[pltpu.VMEM((length, 384), LOW), pltpu.SemaphoreType.DMA((4,))],
        ),
        out_shape=[
            jax.ShapeDtypeStruct((4, stretch, 128), LOW),
            jax.ShapeDtypeStruct((length, 128), F32),
            jax.ShapeDtypeStruct((16, length), F32),
        ],
        compiler_params=params(32),
        cost_estimate=cost(2 * pairs * 128 * 2 * 2, 6 * MIB, pairs),
        name="attend",
    )(me, *pieces)


def attend_back_kernel(
    me_ref, r0, r1, r2, r3, u0, u1, u2, u3, raw_ref, lse_ref, cos_ref, sin_ref, out_ref,
    held, up, query_at, up_at, delta, query_sum, key_sum, value_sum, sems,
):
    me = me_ref[0]
    here = pl.program_id(0)
    count = pl.num_programs(0)
    stretch = r0.shape[0]
    per = stretch // BLOCK

    @pl.when(here == 0)
    def _():
        copies = []
        for k, (ref, other) in enumerate(zip((r0, r1, r2, r3), (u0, u1, u2, u3))):
            rows = pl.ds((me ^ k) * stretch, stretch)
            copies.append(pltpu.make_async_copy(ref, held.at[rows], sems.at[k]))
            copies.append(pltpu.make_async_copy(other, up.at[rows], sems.at[4 + k]))
        for copy in copies:
            copy.start()
        for copy in copies:
            copy.wait()
        query_sum[...] = jnp.zeros_like(query_sum)

        def prepare(at, _):
            rows = pl.ds(at * BLOCK, BLOCK)
            query, upstream = held[rows, 0:128], up[rows, :]
            turned = (upstream.astype(F32) * raw_ref[rows, :]).T
            for head in range(2):
                query_at[head, rows, :] = own_lanes(query, head)
                up_at[head, rows, :] = own_lanes(upstream, head)
                total = jnp.sum(turned[head * 64 : head * 64 + 64], axis=0, keepdims=True)
                delta[at, head * 8 : head * 8 + 8, :] = jnp.broadcast_to(total, (8, BLOCK))
            return 0

        lax.fori_loop(0, count, prepare, 0)

    here_rows = pl.ds(here * BLOCK, BLOCK)
    key, value = held[here_rows, 128:256], held[here_rows, 256:384]
    keys = [own_lanes(key, head) for head in range(2)]
    values = [own_lanes(value, head) for head in range(2)]

    def step(at, diagonal):
        rows = pl.ds(at * BLOCK, BLOCK)
        query, upstream = held[rows, 0:128], up[rows, :]
        key_total = value_total = query_total = None
        for head in range(2):
            scores = against(keys[head], query)
            lse = lse_ref[at, head * 8 : head * 8 + 1, :]
            chance = jnp.exp(scores - lse)
            if diagonal:
                down = lax.broadcasted_iota(jnp.int32, (BLOCK, BLOCK), 0)
                along = lax.broadcasted_iota(jnp.int32, (BLOCK, BLOCK), 1)
                chance = jnp.where(along >= down, chance, 0.0)
            chance_back = against(values[head], upstream)
            shift = delta[at, head * 8 : head * 8 + 1, :]
            score_back = (chance * (chance_back - shift)).astype(LOW)
            value_part = dot(chance.astype(LOW), up_at[head, rows, :])
            key_part = dot(score_back, query_at[head, rows, :])
            query_part = across(score_back, keys[head])
            if head == 0:
                value_total, key_total, query_total = value_part, key_part, query_part
            else:
                value_total += value_part
                key_total += key_part
                query_total += query_part
        query_sum[rows, :] += query_total
        return key_total, value_total

    key_sum[...], value_sum[...] = step(here, True)

    def later(at, _):
        key_total, value_total = step(at, False)
        key_sum[...] += key_total
        value_sum[...] += value_total
        return 0

    lax.fori_loop(here + 1, count, later, 0)

    def back_rope(rows, at):
        places = pl.ds(at * BLOCK, BLOCK)
        return rows * cos_ref[places, :] - half_turn(rows, 128) * sin_ref[places, :]

    slot = (here // per) ^ me
    inner = pl.ds((here % per) * BLOCK, BLOCK)
    out_ref[slot, inner, 128:256] = back_rope(key_sum[...], here).astype(LOW)
    out_ref[slot, inner, 256:384] = value_sum[...].astype(LOW)

    @pl.when(here == count - 1)
    def _():
        def finish(at, _):
            rows = query_sum[pl.ds(at * BLOCK, BLOCK), :] * HEAD_DIM**-0.5
            place = pl.ds((at % per) * BLOCK, BLOCK)
            out_ref[(at // per) ^ me, place, 0:128] = back_rope(rows, at).astype(LOW)
            return 0

        lax.fori_loop(0, count, finish, 0)


def attend_back(me, pieces, upstreams, raw, lse, cosine, sine):
    stretch = pieces[0].shape[0]
    length = 4 * stretch
    count = length // BLOCK
    pairs = length * length
    lse = lse.reshape(16, count, BLOCK).transpose(1, 0, 2)
    whole = lambda i, m: (0, 0)
    return pl.pallas_call(
        attend_back_kernel,
        grid_spec=pltpu.PrefetchScalarGridSpec(
            num_scalar_prefetch=1,
            grid=(count,),
            in_specs=[ANY] * 8
            + [
                pl.BlockSpec((length, 128), whole),
                pl.BlockSpec((count, 16, BLOCK), lambda i, m: (0, 0, 0)),
                pl.BlockSpec((length, 128), whole),
                pl.BlockSpec((length, 128), whole),
            ],
            out_specs=pl.BlockSpec((4, stretch, 384), lambda i, m: (0, 0, 0)),
            scratch_shapes=[
                pltpu.VMEM((length, 384), LOW),
                pltpu.VMEM((length, 128), LOW),
                pltpu.VMEM((2, length, 128), LOW),
                pltpu.VMEM((2, length, 128), LOW),
                pltpu.VMEM((count, 16, BLOCK), F32),
                pltpu.VMEM((length, 128), F32),
                pltpu.VMEM((BLOCK, 128), F32),
                pltpu.VMEM((BLOCK, 128), F32),
                pltpu.SemaphoreType.DMA((8,)),
            ],
        ),
        out_shape=jax.ShapeDtypeStruct((4, stretch, 384), LOW),
        compiler_params=params(48),
        cost_estimate=cost(2 * pairs * 128 * 5 * 2, 12 * MIB, pairs),
        name="attend_back",
    )(me, *pieces, *upstreams, raw, lse, cosine, sine)


def place_of(quarter):
    return (quarter & 1) * 2 + (quarter >> 1)


def quarters_kernel(t_ref, *refs, count, turned):
    t = t_ref[0]
    out_ref = refs[-1]
    rows = out_ref.shape[1]
    total = None
    for left, right in zip(refs[:count], refs[count : 2 * count]):
        part = (against if turned else dot)(left[...], right[...])
        total = part if total is None else total + part
    for quarter in range(4):
        out_ref[place_of(quarter ^ t)] = total[quarter * rows : (quarter + 1) * rows].astype(LOW)


def quarters(t, lefts, rights, turned, step, name):
    rows, depth = lefts[0].shape
    width = rights[0].shape[0] if turned else rights[0].shape[1]
    if turned:
        spec = pl.BlockSpec((step, depth), lambda i, m: (i, 0))
    else:
        spec = pl.BlockSpec((depth, step), lambda i, m: (0, i))
    count = len(lefts)
    return pl.pallas_call(
        functools.partial(quarters_kernel, count=count, turned=turned),
        grid_spec=pltpu.PrefetchScalarGridSpec(
            num_scalar_prefetch=1,
            grid=(width // step,),
            in_specs=[pl.BlockSpec((rows, depth), lambda i, m: (0, 0))] * count + [spec] * count,
            out_specs=pl.BlockSpec((4, rows // 4, step), lambda i, m: (0, 0, i)),
        ),
        out_shape=jax.ShapeDtypeStruct((4, rows // 4, width), LOW),
        compiler_params=params(48),
        cost_estimate=cost(2 * rows * depth * width * count, count * (rows + width) * depth * 2 + rows * width * 2),
        name=name,
    )(t, *lefts, *rights)


def sum_quarters(slots):
    other = swap(slots[2:], "tensor", 4, 1)
    pair = slots[:2].astype(F32) + other.astype(F32)
    across_y = swap(pair[1].astype(LOW), "tensor", 4, 2)
    return pair[0] + across_y.astype(F32)


def spread(quarter):
    two = swap(quarter, "tensor", 4, 2)
    one = swap(quarter, "tensor", 4, 1)
    three = swap(two, "tensor", 4, 1)
    return (quarter, one, two, three)


def join_kernel(t_ref, q0, q1, q2, q3, out_ref, sems):
    t = t_ref[0]
    rows = q0.shape[0]
    copies = [
        pltpu.make_async_copy(ref, out_ref.at[pl.ds((t ^ k) * rows, rows)], sems.at[k])
        for k, ref in enumerate((q0, q1, q2, q3))
    ]
    for copy in copies:
        copy.start()
    for copy in copies:
        copy.wait()


def join(t, pieces):
    rows, width = pieces[0].shape
    return pl.pallas_call(
        join_kernel,
        grid_spec=pltpu.PrefetchScalarGridSpec(
            num_scalar_prefetch=1,
            grid=(1,),
            in_specs=[ANY] * 4,
            out_specs=ANY,
            scratch_shapes=[pltpu.SemaphoreType.DMA((4,))],
        ),
        out_shape=jax.ShapeDtypeStruct((4 * rows, width), pieces[0].dtype),
        compiler_params=params(16),
        cost_estimate=cost(0, 16 * rows * width),
        name="join",
    )(t, *pieces)


def feed_kernel(t_ref, q0, q1, q2, q3, wg_ref, wu_ref, hb_ref, rows_ref, hid_ref, gb_ref, ub_ref, held, sems):
    t = t_ref[0]
    rows = q0.shape[0]
    here = pl.program_id(0)

    @pl.when(here == 0)
    def _():
        copies = [
            pltpu.make_async_copy(ref, held.at[pl.ds((t ^ k) * rows, rows)], sems.at[k])
            for k, ref in enumerate((q0, q1, q2, q3))
        ]
        for copy in copies:
            copy.start()
        for copy in copies:
            copy.wait()
        pltpu.make_async_copy(held, rows_ref, sems.at[4]).start()

    for part in range(3):
        at = slice(part * 256, (part + 1) * 256)
        second = held[at, :]
        gate = dot(second, wg_ref[...])
        up = dot(second, wu_ref[...])
        back = hb_ref[at, :].astype(F32)
        sig = 1.0 / (1.0 + jnp.exp(-gate))
        swish = gate * sig
        hid_ref[at, :] = (swish * up).astype(LOW)
        gb_ref[at, :] = (back * up * sig * (1.0 + gate * (1.0 - sig))).astype(LOW)
        ub_ref[at, :] = (back * swish).astype(LOW)

    @pl.when(here == pl.num_programs(0) - 1)
    def _():
        pltpu.make_async_copy(held, rows_ref, sems.at[4]).wait()


def feed(t, pieces, w_gate, w_up, hidden_back):
    rows, width = pieces[0].shape
    rows = 4 * rows
    units = w_gate.shape[1]
    step = 256
    col = lambda i, m: (0, i)
    block = pl.BlockSpec((rows, step), col)
    low = jax.ShapeDtypeStruct((rows, units), LOW)
    return pl.pallas_call(
        feed_kernel,
        grid_spec=pltpu.PrefetchScalarGridSpec(
            num_scalar_prefetch=1,
            grid=(units // step,),
            in_specs=[ANY] * 4 + [pl.BlockSpec((width, step), col)] * 2 + [block],
            out_specs=[ANY, block, block, block],
            scratch_shapes=[pltpu.VMEM((rows, width), LOW), pltpu.SemaphoreType.DMA((5,))],
        ),
        out_shape=[jax.ShapeDtypeStruct((rows, width), LOW), low, low, low],
        compiler_params=params(48),
        cost_estimate=cost(4 * rows * width * units, 38 * MIB, rows * units),
        name="feed",
    )(t, *pieces, w_gate, w_up, hidden_back)


def branch_back_kernel(t_ref, q0, q1, q2, q3, w_ref, rows_ref, out_ref, held, sems):
    t = t_ref[0]
    rows = q0.shape[0]
    copies = [
        pltpu.make_async_copy(ref, held.at[pl.ds((t ^ k) * rows, rows)], sems.at[k])
        for k, ref in enumerate((q0, q1, q2, q3))
    ]
    for copy in copies:
        copy.start()
    for copy in copies:
        copy.wait()
    keep = pltpu.make_async_copy(held, rows_ref, sems.at[4])
    keep.start()
    for part in range(3):
        at = slice(part * 256, (part + 1) * 256)
        flat = against(held[at, :], w_ref[...]).astype(LOW)
        for slot in range(4):
            out_ref[slot, at, :] = flat[:, slot * 128 : (slot + 1) * 128]
    keep.wait()


def branch_back(t, pieces, weight):
    rows, width = pieces[0].shape
    rows = 4 * rows
    local = weight.shape[0]
    return pl.pallas_call(
        branch_back_kernel,
        grid_spec=pltpu.PrefetchScalarGridSpec(
            num_scalar_prefetch=1,
            grid=(1,),
            in_specs=[ANY] * 4 + [pl.BlockSpec((local, width), lambda i, m: (0, 0))],
            out_specs=[ANY, pl.BlockSpec((4, rows, 128), lambda i, m: (0, 0, 0))],
            scratch_shapes=[pltpu.VMEM((rows, width), LOW), pltpu.SemaphoreType.DMA((5,))],
        ),
        out_shape=[
            jax.ShapeDtypeStruct((rows, width), LOW),
            jax.ShapeDtypeStruct((4, rows, 128), LOW),
        ],
        compiler_params=params(32),
        cost_estimate=cost(2 * rows * width * local, 8 * MIB),
        name="branch_back",
    )(t, *pieces, weight)


def normalize(vector):
    inverse = lax.rsqrt(jnp.mean(vector * vector, axis=-1, keepdims=True) + EPS)
    return (vector * inverse, inverse)


def norm_back(grad_rows, normed, inverse, gain):
    scaled = grad_rows * gain
    gain_grad = jnp.sum(grad_rows * normed, axis=0)
    row_back = inverse * (scaled - normed * jnp.mean(scaled * normed, axis=-1, keepdims=True))
    return (row_back, gain_grad)


def per_device(
    dp_size, tokens, attn_gain, w_query, w_key, w_value, w_out, mlp_gain, w_gate, w_up, w_down, cotangent
):
    rows_here, width = tokens.shape
    local_width = w_query.shape[1]
    units = w_gate.shape[1]
    quarter_rows = rows_here // 4
    me, t, d = lax.axis_index("ctx"), lax.axis_index("tensor"), lax.axis_index("dp")
    me_at, t_at = me.astype(jnp.int32).reshape(1), t.astype(jnp.int32).reshape(1)
    order = me ^ jnp.arange(4)
    half = width // 2

    def quarter_of(rows):
        return lax.dynamic_slice_in_dim(rows, t * quarter_rows, quarter_rows, 0)

    def dp_half(value, which, axis):
        size = value.shape[axis] // 2
        return lax.dynamic_slice_in_dim(value, which * size, size, axis)

    def over_ctx(slots):
        return [slots[0]] + [swap(slots[k], "ctx", 4, k) for k in range(1, 4)]

    cosine, sine = rope_tables(4 * rows_here)
    first_in, slots = project(me_at, tokens, attn_gain, cosine, sine, w_query, w_key, w_value)
    pieces = over_ctx(slots)

    hidden_back = against(cotangent, w_down)
    w_out_slots = w_out.reshape(4, 128, width)[order].reshape(local_width, width)
    w_slots = jnp.concatenate(
        [w.reshape(width, 4, 1, 128) for w in (w_query, w_key, w_value)], axis=2
    )[:, order].reshape(width, 4 * 384)
    tokens_mine = quarter_of(tokens).astype(F32)
    cot_mine = quarter_of(cotangent).astype(F32)

    mixed, raw, lse = attend(me_at, pieces)
    attended = jnp.concatenate(over_ctx(mixed), axis=1)
    slots = quarters(t_at, [attended], [w_out_slots], False, 512, "join_heads")
    middle = tokens_mine + sum_quarters(slots)
    normed_two, inverse_two = normalize(middle)
    second_mine = (normed_two * mlp_gain).astype(LOW)

    second_in, hidden, gate_back, up_back = feed(t_at, spread(second_mine), w_gate, w_up, hidden_back)
    slots = quarters(t_at, [gate_back, up_back], [w_gate, w_up], True, 256, "feed_back")
    second_sum = sum_quarters(slots)
    slots = quarters(t_at, [hidden], [w_down], False, 256, "feed_down")
    output = join(t_at, spread((middle + sum_quarters(slots)).astype(LOW)))
    middle_back, mlp_gain_part = norm_back(second_sum, normed_two, inverse_two, mlp_gain)
    middle_grad = cot_mine + middle_back
    branch_low, slots = branch_back(t_at, spread(middle_grad.astype(LOW)), w_out_slots)
    upstreams = over_ctx(slots)

    slots = attend_back(me_at, pieces, upstreams, raw, lse, cosine, sine)
    back = jnp.concatenate(over_ctx(slots), axis=1)
    back_slots = quarters(t_at, [back], [w_slots], True, 256, "project_back")
    first_sum = sum_quarters(back_slots)
    normed_one, inverse_one = normalize(tokens_mine)
    input_back, attn_gain_part = norm_back(first_sum, normed_one, inverse_one, attn_gain)
    input_grad = join(t_at, spread((middle_grad + input_back).astype(LOW)))

    first_mine = quarter_of(first_in)
    far = jnp.stack([swap(first_mine, "ctx", 4, k) for k in range(1, 4)])
    far_two = swap(far, "tensor", 4, 2)
    far_one = swap(far, "tensor", 4, 1)
    far_three = swap(far_two, "tensor", 4, 1)
    far_all = jnp.stack([far, far_one, far_two, far_three], axis=1)[:, t ^ jnp.arange(4)]
    first_all = jnp.concatenate(
        [first_in, far_all.reshape(3 * rows_here, width)], axis=0
    )
    qkv_part = across(first_all, slots.reshape(4 * rows_here, 384))
    out_part = across(attended, branch_low).reshape(4, 128, width)[order].reshape(local_width, width)

    def rows_over_dp(part):
        if dp_size == 2:
            other = swap(dp_half(part, 1 - d, 0).astype(LOW), "dp", 2, 1)
            return dp_half(part, d, 0) + other.astype(F32)
        return lax.psum_scatter(part.astype(LOW), "dp", scatter_dimension=0, tiled=True).astype(F32)

    def columns_over_dp(part):
        if dp_size == 2:
            other = swap(dp_half(part, 1 - d, 1).astype(LOW), "dp", 2, 1)
            return dp_half(part, d, 1) + other.astype(F32)
        return lax.psum_scatter(part.astype(LOW), "dp", scatter_dimension=1, tiled=True).astype(F32)

    def over_stretches(part, axis):
        return lax.psum_scatter(
            part.astype(LOW), "ctx", scatter_dimension=axis, tiled=True
        ).astype(F32)

    if dp_size == 2:
        hidden_two = jnp.concatenate([hidden, swap(hidden, "dp", 2, 1)], axis=0)
        gate_two = jnp.concatenate([gate_back, swap(gate_back, "dp", 2, 1)], axis=0)
        up_two = jnp.concatenate([up_back, swap(up_back, "dp", 2, 1)], axis=0)

        def two_halves(rows):
            other = swap(dp_half(rows, 1 - d, 1), "dp", 2, 1)
            return jnp.concatenate([dp_half(rows, d, 1), other], axis=0)

        cot_two, second_two = two_halves(cotangent), two_halves(second_in)
        down_part = across(hidden_two, cot_two)
        gate_part = across(second_two, gate_two)
        up_part = across(second_two, up_two)
    else:
        down_part = columns_over_dp(across(hidden, cotangent))
        gate_part = rows_over_dp(across(second_in, gate_back))
        up_part = rows_over_dp(across(second_in, up_back))
    down_grad = over_stretches(down_part, 1)
    gate_grad = over_stretches(gate_part, 0)
    up_grad = over_stretches(up_part, 0)
    out_grad = over_stretches(columns_over_dp(out_part), 1)
    share = out_grad.shape[1]

    qkv_part = rows_over_dp(qkv_part).astype(LOW).reshape(4, share, 384)[order]
    parts = jnp.stack(over_ctx(qkv_part))[order]
    qkv = parts.reshape(4, share, 3, 128).transpose(2, 1, 0, 3).reshape(3, share, local_width)
    qkv = qkv.astype(F32)

    gains = jnp.stack([attn_gain_part, mlp_gain_part])
    gains = gains + swap(gains, "tensor", 4, 1)
    gains = gains + swap(gains, "tensor", 4, 2)
    if dp_size == 2:
        gains = dp_half(gains, d, 1) + swap(dp_half(gains, 1 - d, 1), "dp", 2, 1)
    else:
        gains = lax.psum_scatter(gains, "dp", scatter_dimension=1, tiled=True)
    gains = gains.reshape(2, 4, share).transpose(1, 0, 2)[order]
    gains = sum(over_ctx(gains))

    return (
        output,
        input_grad,
        gains[0],
        qkv[0],
        qkv[1],
        qkv[2],
        out_grad,
        gains[1],
        gate_grad,
        up_grad,
        down_grad,
    )


def solution(mesh):
    rows, tensor = ("dp", "ctx"), "tensor"
    in_specs = (
        P(rows, None),
        P(),
        P(None, tensor),
        P(None, tensor),
        P(None, tensor),
        P(tensor, None),
        P(),
        P(None, tensor),
        P(None, tensor),
        P(tensor, None),
        P(rows, None),
    )
    out_specs = (
        P(rows, None),
        P(rows, None),
        P(rows),
        P(rows, tensor),
        P(rows, tensor),
        P(rows, tensor),
        P(tensor, rows),
        P(rows),
        P(rows, tensor),
        P(rows, tensor),
        P(tensor, rows),
    )
    return jax.shard_map(
        functools.partial(per_device, mesh.shape["dp"]),
        mesh=mesh,
        in_specs=in_specs,
        out_specs=out_specs,
        check_vma=False,
    )
```

time: 1750 us -> 1080 us (0.62)
  waiting for transfers between devices: 1090 us -> 524 us
  matrix products: 410 us -> 56.3 us
  Pallas kernels: 0 us -> 163 us
  starting transfers between devices: 1.51 us -> 148 us
  other arithmetic: 174 us -> 65.9 us
  local copies, waits for them, and re-layouts: 25.3 us -> 102 us
  blocking collectives: 22.2 us -> 0 us
    reduce_scatter x9 -> x4, waiting for transfers between devices: 720 us -> 0.03 us  [over_stretches(): lax.psum_scatter(part.astype(LOW), 'ctx', scatter_dimension=axis, tiled=T...]
    ppermute x0 -> x54, waiting for transfers between devices: none -> 524 us  [swap(): return lax.ppermute(value, axis, [(i, i ^ distance) for i in range(size)])]
    psum x3 -> x0, waiting for transfers between devices: 255 us -> none  [the longest x1 120 us: per_device(): lax.psum(jnp.dot(hidden, w_down, preferred_element_type=jnp.float32).asty...]
    pallas_call x0 -> x11, Pallas kernels: none -> 163 us  [the longest x1 44.7 us: attend_back(): pl.pallas_call(attend_back_kernel, grid_spec=pltpu.PrefetchScalarGridSpec...]
    dot_general x31 -> x1, matrix products: 166 us -> 10.9 us  [against(): lax.dot_general(left, right, (((1,), (1,)), ((), ())), preferred_element_...]
    ppermute x0 -> x54, starting transfers between devices: none -> 148 us  [swap(): return lax.ppermute(value, axis, [(i, i ^ distance) for i in range(size)])]
    all_gather x2 -> x0, waiting for transfers between devices: 116 us -> none  [the longest x1 57.8 us: per_device(): lax.all_gather(key_rot.reshape(rows_here, local_width), 'ctx', axis=0, ti...]
    dot_general x23 -> x0, matrix products: 110 us -> none  [the longest x8 33.8 us: head_forward(): jnp.dot(chance, value_rows, preferred_element_type=jnp.float32)]
  transfers between devices with their start and end apart: 14 -> 58, of which waited for: 14 -> 25; matrix products, arithmetic and copies ran while one was open for 8% -> 18% of each run, Pallas kernels for 0% -> 7%
where the time goes in v1:
time: 1080 us; the launch traced here: 1070 us
  waiting for transfers between devices  524 us (49%)
  Pallas kernels  163 us (15%)
  starting transfers between devices  148 us (14%)
  local copies, waits for them, and re-layouts  102 us (9%)
  other arithmetic  65.9 us (6%)
  matrix products  56.3 us (5%)
  between operations  15 us (1%)
    ppermute x54, waiting for transfers between devices, swap(): return lax.ppermute(value, axis, [(i, i ^ distance) for i in range(size)])  524 us
    ppermute x54, starting transfers between devices, swap(): return lax.ppermute(value, axis, [(i, i ^ distance) for i in range(size)])  148 us
    dot_general x5, matrix products, across(): lax.dot_general(left, right, (((0,), (0,)), ((), ())), preferred_element_...  45.3 us
    pallas_call x1, Pallas kernels, attend_back(): pl.pallas_call(attend_back_kernel, grid_spec=pltpu.PrefetchScalarGridSpec...  44.7 us
    pallas_call x4, Pallas kernels, quarters(): pl.pallas_call(functools.partial(quarters_kernel, count=count, turned=tur...  42 us
    pallas_call x1, Pallas kernels, attend(): pl.pallas_call(attend_kernel, grid_spec=pltpu.PrefetchScalarGridSpec(num_...  36.9 us
    unnamed x85, local copies, waits for them, and re-layouts  34.4 us
  transfers between devices with their start and end apart: 58, of which 25 were waited for; matrix products, arithmetic and copies ran while one was open for 18% of the time, Pallas kernels for 7%

profile of v1, /device:TPU:0, one launch (start us, length us, event | category | flops | bytes accessed | tf_op | source)
XLA Modules:
  0.0 1074.2 jit_solution(1116073680957493922)
XLA Ops:
  7.3 5.8 fusion.48
  15.6 11.4 %project.1 = (bf16[768,2048]{1,0:T(8,128)(2,1)}, bf16[4,768,384]{2,1,0:T(8,128)(2,1)}) custom-call(s32[1]{0:T(128)} %bitcast.1.me_ref, bf16[768,2048]{1,0:T(8,128)(2,1)} %tok_ref.1, f32[1,2048]{1,0:T(1,128)S(1)} %bitcast.158, f32[3072,128]{1,0:T(8,128)S(1)} %get-tuple-element.115.cos_ref, f32[3072,128]{1,0:T(8,128)S(1)} %get-tuple-element.116.sin_ref, ...), custom_call_target="tpu_custom_call" | custom-call | flops 4831838208 | bytes 16777216 | tf_op jit(solution)/shard_map/project/pallas_call | solution.py:86
  27.1 2.9 slice_bitcast_fusion.8
  29.9 3.0 collective-permute-start
  35.5 22.8 %collective-permute-done.r1 = bf16[768,384]{1,0:T(8,128)(2,1)S(1)} collective-permute-done((bf16[768,384]{1,0:T(8,128)(2,1)}, bf16[768,384]{1,0:T(8,128)(2,1)S(1)}, u32[]{:S(2)}, u32[]{:S(2)}) %collective-permute-start) | collective-permute-done | bytes 589856 | tf_op jit(solution)/shard_map/ppermute | solution.py:21
  58.4 17.4 %collective-permute-done.1.r2 = bf16[768,384]{1,0:T(8,128)(2,1)} collective-permute-done((bf16[768,384]{1,0:T(8,128)(2,1)}, bf16[768,384]{1,0:T(8,128)(2,1)}, u32[]{:S(2)}, u32[]{:S(2)}) %collective-permute-start.1) | collective-permute-done | bytes 589856 | tf_op jit(solution)/shard_map/ppermute | solution.py:21
  75.7 36.9 %attend.1 = (bf16[4,768,128]{2,1,0:T(8,128)(2,1)S(1)}, f32[3072,128]{1,0:T(8,128)S(1)}, f32[16,3072]{1,0:T(8,128)S(1)}) custom-call(s32[1]{0:T(128)} %bitcast.1.me_ref, bf16[768,384]{1,0:T(8,128)(2,1)S(1)} %get-tuple-element.90.r0, bf16[768,384]{1,0:T(8,128)(2,1)S(1)} %collective-permute-done.r1, bf16[768,384]{1,0:T(8,128)(2,1)} %collective-permute-done.1.r2, ...), custom_call_target="tpu_custom_call" | custom-call | flops 9663676416 | bytes 6291456 | tf_op jit(solution)/shard_map/attend/pallas_call | solution.py:180
  114.6 11.8 %collective-permute-start.3 = (bf16[768,128]{1,0:T(8,128)(2,1)}, bf16[768,128]{1,0:T(8,128)(2,1)S(1)}, u32[]{:S(2)}, u32[]{:S(2)}) collective-permute-start(bf16[768,128]{1,0:T(8,128)(2,1)} %get-tuple-element.106), channel_id=1, source_target_pairs={{0,4},{4,0},{8,12},{12,8},{1,5},{5,1},{9,13},{13,9},{2,6},{6,2},{1... | collective-permute-start | bytes 589832 | tf_op jit(solution)/shard_map/ppermute | solution.py:21
  132.9 10.4 collective-permute-done.4
  145.0 3.2 join_heads.1
  148.5 3.4 collective-permute-done.6
  155.9 18.1 %collective-permute-done.7 = bf16[192,2048]{1,0:T(8,128)(2,1)S(1)} collective-permute-done((bf16[192,2048]{1,0:T(8,128)(2,1)S(1)}, bf16[192,2048]{1,0:T(8,128)(2,1)S(1)}, u32[]{:S(2)}, u32[]{:S(2)}) %collective-permute-start.7) | collective-permute-done | bytes 786464 | tf_op jit(solution)/shard_map/ppermute | solution.py:21
  178.4 17.2 %collective-permute-done.9.q2 = bf16[192,2048]{1,0:T(8,128)(2,1)S(1)} collective-permute-done((bf16[192,2048]{1,0:T(8,128)(2,1)S(1)}, bf16[192,2048]{1,0:T(8,128)(2,1)S(1)}, u32[]{:S(2)}, u32[]{:S(2)}) %collective-permute-start.9) | collective-permute-done | bytes 786464 | tf_op jit(solution)/shard_map/ppermute | solution.py:21
  195.7 10.9 %fusion.66.hb_ref = f32[768,2048]{1,0:T(8,128)} fusion(bf16[768,2048]{1,0:T(8,128)(2,1)S(1)} %copy-done.24, bf16[2048,2048]{1,0:T(8,128)(2,1)} %refs_1_.1), kind=kOutput, calls=%fused_computation.146 | convolution fusion | flops 6442450944 | bytes 17825792 | tf_op jit(solution)/shard_map/dot_general | solution.py:29
  206.6 20.2 %feed.1 = (bf16[768,2048]{1,0:T(8,128)(2,1)}, bf16[768,2048]{1,0:T(8,128)(2,1)}, bf16[768,2048]{1,0:T(8,128)(2,1)}, bf16[768,2048]{1,0:T(8,128)(2,1)}) custom-call(s32[1]{0:T(128)} %bitcast.t_ref, bf16[192,2048]{1,0:T(8,128)(2,1)S(1)} %multiply_convert_fusion.q0, bf16[192,2048]{1,0:T(8,128)(2,1)S(1)} %collective-permute-done.8.q1, ...), custom_call_target="tpu_custom_call" | custom-call | flops 12884901888 | bytes 39845888 | tf_op jit(solution)/shard_map/feed/pallas_call | solution.py:467
  226.8 18.6 %feed_back.1 = bf16[4,192,2048]{2,1,0:T(8,128)(2,1)S(1)} custom-call(s32[1]{0:T(128)} %bitcast.t_ref, bf16[768,2048]{1,0:T(8,128)(2,1)} %get-tuple-element.25.refs_0_, bf16[768,2048]{1,0:T(8,128)(2,1)} %get-tuple-element.26.refs_1_, bf16[2048,2048]{1,0:T(8,128)(2,1)} %refs_2_.1, bf16[2048,2048]{1,0:T(8,128)(2,1)} %refs_3_.1), custom_call_target="tpu_custom_call" | custom-call | flops 12884901888 | bytes 26214400 | tf_op jit(solution)/shard_map/feed_back/pallas_call | solution.py:365
  246.1 11.2 %feed_down.1 = bf16[4,192,2048]{2,1,0:T(8,128)(2,1)S(1)} custom-call(s32[1]{0:T(128)} %bitcast.t_ref, bf16[768,2048]{1,0:T(8,128)(2,1)} %get-tuple-element.24.refs_0_, bf16[2048,2048]{1,0:T(8,128)(2,1)} %refs_1_.1), custom_call_target="tpu_custom_call" | custom-call | flops 6442450944 | bytes 14680064 | tf_op jit(solution)/shard_map/feed_down/pallas_call | solution.py:365
  263.2 16.9 %collective-permute-done.17 = bf16[192,2048]{1,0:T(8,128)(2,1)S(1)} collective-permute-done((bf16[192,2048]{1,0:T(8,128)(2,1)S(1)}, bf16[192,2048]{1,0:T(8,128)(2,1)S(1)}, u32[]{:S(2)}, u32[]{:S(2)}) %collective-permute-start.17) | collective-permute-done | bytes 786464 | tf_op jit(solution)/shard_map/ppermute | solution.py:21
  281.2 15.3 %collective-permute-done.12 = bf16[192,2048]{1,0:T(8,128)(2,1)S(1)} collective-permute-done((bf16[192,2048]{1,0:T(8,128)(2,1)S(1)}, bf16[192,2048]{1,0:T(8,128)(2,1)S(1)}, u32[]{:S(2)}, u32[]{:S(2)}) %collective-permute-start.12) | collective-permute-done | bytes 786464 | tf_op jit(solution)/shard_map/ppermute | solution.py:21
  296.5 3.5 fusion.61
  301.6 17.9 %collective-permute-done.19.q2 = bf16[192,2048]{1,0:T(8,128)(2,1)} collective-permute-done((bf16[192,2048]{1,0:T(8,128)(2,1)}, bf16[192,2048]{1,0:T(8,128)(2,1)}, u32[]{:S(2)}, u32[]{:S(2)}) %collective-permute-start.19) | collective-permute-done | bytes 786464 | tf_op jit(solution)/shard_map/ppermute | solution.py:21
  322.2 4.1 branch_back.1
  326.3 3.9 fusion.59
  330.2 5.0 gather_fusion.5
  335.2 2.7 dynamic-slice_convert_fusion
  339.4 3.5 constant_dynamic-slice_fusion.3
  343.5 69.8 %collective-permute-done.48 = bf16[512,1024]{1,0:T(8,128)(2,1)} collective-permute-done((bf16[512,1024]{1,0:T(8,128)(2,1)}, bf16[512,1024]{1,0:T(8,128)(2,1)}, u32[]{:S(2)}, u32[]{:S(2)}) %collective-permute-start.48) | collective-permute-done | bytes 1048608 | tf_op jit(solution)/shard_map/ppermute | solution.py:21
  415.9 30.7 %collective-permute-done.49 = bf16[768,1024]{1,0:T(8,128)(2,1)} collective-permute-done((bf16[768,1024]{1,0:T(8,128)(2,1)}, bf16[768,1024]{1,0:T(8,128)(2,1)}, u32[]{:S(2)}, u32[]{:S(2)}) %collective-permute-start.49) | collective-permute-done | bytes 1572896 | tf_op jit(solution)/shard_map/ppermute | solution.py:21
  446.5 10.8 %fusion.16 = bf16[1024,2048]{1,0:T(8,128)(2,1)} fusion(bf16[768,2048]{1,0:T(8,128)(2,1)} %collective-permute-done.51, bf16[768,2048]{1,0:T(8,128)(2,1)} %get-tuple-element.26.refs_1_, bf16[768,1024]{1,0:T(8,128)(2,1)} %collective-permute-done.49, bf16[768,1024]{1,0:T(8,128)(2,1)S(1)} %get-tuple-element.78), kind=kOutput, calls=%fused_computation.27 | convolution fusion | flops 6463422464 | bytes 13631488 | tf_op jit(solution)/shard_map/dot_general | solution.py:33
  459.0 68.4 %collective-permute-done.50 = bf16[768,2048]{1,0:T(8,128)(2,1)S(1)} collective-permute-done((bf16[768,2048]{1,0:T(8,128)(2,1)}, bf16[768,2048]{1,0:T(8,128)(2,1)S(1)}, u32[]{:S(2)}, u32[]{:S(2)}) %collective-permute-start.50) | collective-permute-done | bytes 3145760 | tf_op jit(solution)/shard_map/ppermute | solution.py:21
  527.4 10.2 fusion.19
  538.9 2.7 collective-permute-start.38
  544.1 62.2 %collective-permute-done.38 = bf16[192,2048]{1,0:T(8,128)(2,1)S(1)} collective-permute-done((bf16[192,2048]{1,0:T(8,128)(2,1)S(1)}, bf16[192,2048]{1,0:T(8,128)(2,1)S(1)}, u32[]{:S(2)}, u32[]{:S(2)}) %collective-permute-start.38) | collective-permute-done | bytes 786464 | tf_op jit(solution)/shard_map/ppermute | solution.py:21
  606.3 17.0 %collective-permute-done.39 = bf16[192,2048]{1,0:T(8,128)(2,1)S(1)} collective-permute-done((bf16[192,2048]{1,0:T(8,128)(2,1)S(1)}, bf16[192,2048]{1,0:T(8,128)(2,1)S(1)}, u32[]{:S(2)}, u32[]{:S(2)}) %collective-permute-start.39) | collective-permute-done | bytes 786464 | tf_op jit(solution)/shard_map/ppermute | solution.py:21
  623.3 18.0 %collective-permute-done.40 = bf16[192,2048]{1,0:T(8,128)(2,1)S(1)} collective-permute-done((bf16[192,2048]{1,0:T(8,128)(2,1)S(1)}, bf16[192,2048]{1,0:T(8,128)(2,1)S(1)}, u32[]{:S(2)}, u32[]{:S(2)}) %collective-permute-start.40) | collective-permute-done | bytes 786464 | tf_op jit(solution)/shard_map/ppermute | solution.py:21
  645.6 45.7 %collective-permute-done.42 = bf16[3,192,2048]{2,1,0:T(8,128)(2,1)} collective-permute-done((bf16[3,192,2048]{2,1,0:T(8,128)(2,1)}, bf16[3,192,2048]{2,1,0:T(8,128)(2,1)}, u32[]{:S(2)}, u32[]{:S(2)}) %collective-permute-start.42) | collective-permute-done | bytes 2359328 | tf_op jit(solution)/shard_map/ppermute | solution.py:21
  697.9 3.9 copy.48
  701.8 4.1 copy.49
  705.9 5.5 pad_maximum_fusion.2
  711.4 6.4 gather_fusion.1
  717.8 8.7 copy.50.refs_1_
  726.6 9.4 pad_maximum_fusion
  738.3 35.4 %collective-permute-start.21 = (bf16[768,128]{1,0:T(8,128)(2,1)}, bf16[768,128]{1,0:T(8,128)(2,1)S(1)}, u32[]{:S(2)}, u32[]{:S(2)}) collective-permute-start(bf16[768,128]{1,0:T(8,128)(2,1)} %get-tuple-element.101), channel_id=1, source_target_pairs={{0,4},{4,0},{8,12},{12,8},{1,5},{5,1},{9,13},{13,9},{2,6},{6,2},{1... | collective-permute-start | bytes 589832 | tf_op jit(solution)/shard_map/ppermute | solution.py:21
  775.8 20.0 %collective-permute-done.53 = bf16[768,1024]{1,0:T(8,128)(2,1)} collective-permute-done((bf16[768,1024]{1,0:T(8,128)(2,1)}, bf16[768,1024]{1,0:T(8,128)(2,1)}, u32[]{:S(2)}, u32[]{:S(2)}) %collective-permute-start.53) | collective-permute-done | bytes 1572896 | tf_op jit(solution)/shard_map/ppermute | solution.py:21
  798.3 10.7 fusion.22
  811.4 44.7 %attend_back.1 = bf16[4,768,384]{2,1,0:T(8,128)(2,1)} custom-call(s32[1]{0:T(128)} %bitcast.1.me_ref, bf16[768,384]{1,0:T(8,128)(2,1)S(1)} %get-tuple-element.90.r0, bf16[768,384]{1,0:T(8,128)(2,1)S(1)} %copy-done.15, bf16[768,384]{1,0:T(8,128)(2,1)} %collective-permute-done.1.r2, bf16[768,384]{1,0:T(8,128)(2,1)} %collective-permute-done.2.r3, ...), custom_call_target="tpu_custom_call" | custom-call | flops 24159191040 | bytes 12582912 | tf_op jit(solution)/shard_map/attend_back/pallas_call | solution.py:309
  856.1 2.9 slice_bitcast_fusion.7
  859.0 36.0 %collective-permute-start.24 = (bf16[768,384]{1,0:T(8,128)(2,1)}, bf16[768,384]{1,0:T(8,128)(2,1)}, u32[]{:S(2)}, u32[]{:S(2)}) collective-permute-start(bf16[768,384]{1,0:T(8,128)(2,1)} %get-tuple-element.86), channel_id=1, source_target_pairs={{0,4},{4,0},{8,12},{12,8},{1,5},{5,1},{9,13},{13,9},{2,6},{6,2},{1... | collective-permute-start | bytes 1769480 | tf_op jit(solution)/shard_map/ppermute | solution.py:21
  897.3 9.2 fusion.62
  906.5 5.4 gather_fusion.6
  911.9 5.3 gather_fusion.7
  917.2 9.4 pad_maximum_fusion.1
  926.6 9.2 copy.51
  936.4 6.9 collective-permute-done.24
  943.3 14.9 %collective-permute-done.26 = bf16[768,384]{1,0:T(8,128)(2,1)} collective-permute-done((bf16[768,384]{1,0:T(8,128)(2,1)}, bf16[768,384]{1,0:T(8,128)(2,1)}, u32[]{:S(2)}, u32[]{:S(2)}) %collective-permute-start.26) | collective-permute-done | bytes 589856 | tf_op jit(solution)/shard_map/ppermute | solution.py:21
  959.8 9.0 project_back.1
  970.5 9.8 fusion
  986.9 12.7 %collective-permute-done.44 = bf16[1024,384]{1,0:T(8,128)(2,1)S(1)} collective-permute-done((bf16[1024,384]{1,0:T(8,128)(2,1)S(1)}, bf16[1024,384]{1,0:T(8,128)(2,1)S(1)}, u32[]{:S(2)}, u32[]{:S(2)}) %collective-permute-start.44) | collective-permute-done | bytes 786464 | tf_op jit(solution)/shard_map/ppermute | solution.py:21
  1000.6 11.8 %collective-permute-start.45 = (bf16[256,384]{1,0:T(8,128)(2,1)S(1)}, bf16[256,384]{1,0:T(8,128)(2,1)S(1)}, u32[]{:S(2)}, u32[]{:S(2)}) collective-permute-start(bf16[256,384]{1,0:T(8,128)(2,1)S(1)} %get-tuple-element.97), channel_id=1, source_target_pairs={{0,4},{4,0},{8,12},{12,8},{1,5},{5,1},{9,13},{13,9},{2,6},{6,2},{1... | collective-permute-start | bytes 589832 | tf_op jit(solution)/shard_map/ppermute | solution.py:21
  1024.4 4.4 collective-permute-done.46
  1031.6 10.0 collective-permute-done.30.q2
  1058.8 2.9 convert_element_type.176
  1061.7 2.8 convert_element_type.174
  1064.5 2.7 convert_element_type.178
  (232 shorter events, 111.8 us)
Async XLA Ops:
  7.2 121.7 %copy-start = (bf16[512,2048]{1,0:T(8,128)(2,1)S(1)}, bf16[512,2048]{1,0:T(8,128)(2,1)}, u32[]{:S(2)}) copy-start(bf16[512,2048]{1,0:T(8,128)(2,1)} %param.16) | copy-start | bytes 6291460
  7.2 1047.5 %reduce-scatter.5.cloned.1.call-start = ((), (), s32[]{:S(2)}) async-start(), calls=%async_computation.4 | async-start | bytes 1310720 | tf_op jit(solution)/shard_map/reduce_scatter | solution.py:623
  29.9 28.4 %collective-permute-start = (bf16[768,384]{1,0:T(8,128)(2,1)}, bf16[768,384]{1,0:T(8,128)(2,1)S(1)}, u32[]{:S(2)}, u32[]{:S(2)}) collective-permute-start(bf16[768,384]{1,0:T(8,128)(2,1)} %get-tuple-element.89), channel_id=1, source_target_pairs={{0,4},{4,0},{8,12},{12,8},{1,5},{5,1},{9,13},{13,9},{2,6},{6,2},{1... | collective-permute-start | bytes 1769480 | tf_op jit(solution)/shard_map/ppermute | solution.py:21
  33.0 42.8 %collective-permute-start.1 = (bf16[768,384]{1,0:T(8,128)(2,1)}, bf16[768,384]{1,0:T(8,128)(2,1)}, u32[]{:S(2)}, u32[]{:S(2)}) collective-permute-start(bf16[768,384]{1,0:T(8,128)(2,1)} %get-tuple-element.88), channel_id=1, source_target_pairs={{0,8},{4,12},{8,0},{12,4},{1,9},{5,13},{9,1},{13,5},{2,10},{6,14},... | collective-permute-start | bytes 1769480 | tf_op jit(solution)/shard_map/ppermute | solution.py:21
  35.5 40.2 %collective-permute-start.2 = (bf16[768,384]{1,0:T(8,128)(2,1)}, bf16[768,384]{1,0:T(8,128)(2,1)}, u32[]{:S(2)}, u32[]{:S(2)}) collective-permute-start(bf16[768,384]{1,0:T(8,128)(2,1)} %get-tuple-element.87), channel_id=1, source_target_pairs={{0,12},{4,8},{8,4},{12,0},{1,13},{5,9},{9,5},{13,1},{2,14},{6,10},... | collective-permute-start | bytes 1769480 | tf_op jit(solution)/shard_map/ppermute | solution.py:21
  58.3 54.3 %copy-start.14 = (bf16[768,384]{1,0:T(8,128)(2,1)}, bf16[768,384]{1,0:T(8,128)(2,1)S(1)}, u32[]{:S(2)}) copy-start(bf16[768,384]{1,0:T(8,128)(2,1)S(1)} %collective-permute-done.r1) | copy-start | bytes 1769476
  114.6 18.3 %collective-permute-start.3 = (bf16[768,128]{1,0:T(8,128)(2,1)}, bf16[768,128]{1,0:T(8,128)(2,1)S(1)}, u32[]{:S(2)}, u32[]{:S(2)}) collective-permute-start(bf16[768,128]{1,0:T(8,128)(2,1)} %get-tuple-element.106), channel_id=1, source_target_pairs={{0,4},{4,0},{8,12},{12,8},{1,5},{5,1},{9,13},{13,9},{2,6},{6,2},{1... | collective-permute-start | bytes 589832 | tf_op jit(solution)/shard_map/ppermute | solution.py:21
  126.4 16.9 %collective-permute-start.4 = (bf16[768,128]{1,0:T(8,128)(2,1)}, bf16[768,128]{1,0:T(8,128)(2,1)S(1)}, u32[]{:S(2)}, u32[]{:S(2)}) collective-permute-start(bf16[768,128]{1,0:T(8,128)(2,1)} %get-tuple-element.105), channel_id=1, source_target_pairs={{0,8},{4,12},{8,0},{12,4},{1,9},{5,13},{9,1},{13,5},{2,10},{6,14},... | collective-permute-start | bytes 589832 | tf_op jit(solution)/shard_map/ppermute | solution.py:21
  127.5 15.8 %collective-permute-start.5 = (bf16[768,128]{1,0:T(8,128)(2,1)}, bf16[768,128]{1,0:T(8,128)(2,1)S(1)}, u32[]{:S(2)}, u32[]{:S(2)}) collective-permute-start(bf16[768,128]{1,0:T(8,128)(2,1)} %get-tuple-element.104), channel_id=1, source_target_pairs={{0,12},{4,8},{8,4},{12,0},{1,13},{5,9},{9,5},{13,1},{2,14},{6,10},... | collective-permute-start | bytes 589832 | tf_op jit(solution)/shard_map/ppermute | solution.py:21
  148.5 3.5 collective-permute-start.6
  154.3 19.6 %collective-permute-start.7 = (bf16[192,2048]{1,0:T(8,128)(2,1)S(1)}, bf16[192,2048]{1,0:T(8,128)(2,1)S(1)}, u32[]{:S(2)}, u32[]{:S(2)}) collective-permute-start(bf16[192,2048]{1,0:T(8,128)(2,1)S(1)} %fusion.44), channel_id=1, source_target_pairs={{0,2},{1,3},{2,0},{3,1},{4,6},{5,7},{6,4},{7,5},{8,10},{9,11},{10,... | collective-permute-start | bytes 2359304 | tf_op jit(solution)/shard_map/ppermute | solution.py:21
  176.8 18.8 %collective-permute-start.9 = (bf16[192,2048]{1,0:T(8,128)(2,1)S(1)}, bf16[192,2048]{1,0:T(8,128)(2,1)S(1)}, u32[]{:S(2)}, u32[]{:S(2)}) collective-permute-start(bf16[192,2048]{1,0:T(8,128)(2,1)S(1)} %multiply_convert_fusion.q0), channel_id=1, source_target_pairs={{0,2},{1,3},{2,0},{3,1},{4,6},{5,7},{6,4},{7,5},{8,10},{9,11},{10,... | collective-permute-start | bytes 2359304 | tf_op jit(solution)/shard_map/ppermute | solution.py:21
  178.4 28.2 %collective-permute-start.8 = (bf16[192,2048]{1,0:T(8,128)(2,1)S(1)}, bf16[192,2048]{1,0:T(8,128)(2,1)S(1)}, u32[]{:S(2)}, u32[]{:S(2)}) collective-permute-start(bf16[192,2048]{1,0:T(8,128)(2,1)S(1)} %multiply_convert_fusion.q0), channel_id=1, source_target_pairs={{0,1},{1,0},{2,3},{3,2},{4,5},{5,4},{6,7},{7,6},{8,9},{9,8},{10,11... | collective-permute-start | bytes 2359304 | tf_op jit(solution)/shard_map/ppermute | solution.py:21
  195.7 10.9 %collective-permute-start.10 = (bf16[192,2048]{1,0:T(8,128)(2,1)S(1)}, bf16[192,2048]{1,0:T(8,128)(2,1)S(1)}, u32[]{:S(2)}, u32[]{:S(2)}) collective-permute-start(bf16[192,2048]{1,0:T(8,128)(2,1)S(1)} %collective-permute-done.9.q2), channel_id=1, source_target_pairs={{0,1},{1,0},{2,3},{3,2},{4,5},{5,4},{6,7},{7,6},{8,9},{9,8},{10,11... | collective-permute-start | bytes 2359304 | tf_op jit(solution)/shard_map/ppermute | solution.py:21
  245.5 12.1 %collective-permute-start.16 = (bf16[2,192,2048]{2,1,0:T(8,128)(2,1)S(1)}, bf16[2,192,2048]{2,1,0:T(8,128)(2,1)}, u32[]{:S(2)}, u32[]{:S(2)}) collective-permute-start(bf16[2,192,2048]{2,1,0:T(8,128)(2,1)S(1)} %slice.212), channel_id=1, source_target_pairs={{0,1},{1,0},{2,3},{3,2},{4,5},{5,4},{6,7},{7,6},{8,9},{9,8},{10,11... | collective-permute-start | bytes 4718600 | tf_op jit(solution)/shard_map/ppermute | solution.py:21
  257.5 3.8 collective-permute-start.11
  259.7 20.4 %collective-permute-start.17 = (bf16[192,2048]{1,0:T(8,128)(2,1)S(1)}, bf16[192,2048]{1,0:T(8,128)(2,1)S(1)}, u32[]{:S(2)}, u32[]{:S(2)}) collective-permute-start(bf16[192,2048]{1,0:T(8,128)(2,1)S(1)} %fusion.46), channel_id=1, source_target_pairs={{0,2},{1,3},{2,0},{3,1},{4,6},{5,7},{6,4},{7,5},{8,10},{9,11},{10,... | collective-permute-start | bytes 2359304 | tf_op jit(solution)/shard_map/ppermute | solution.py:21
  261.9 34.6 %collective-permute-start.12 = (bf16[192,2048]{1,0:T(8,128)(2,1)S(1)}, bf16[192,2048]{1,0:T(8,128)(2,1)S(1)}, u32[]{:S(2)}, u32[]{:S(2)}) collective-permute-start(bf16[192,2048]{1,0:T(8,128)(2,1)S(1)} %fusion.45), channel_id=1, source_target_pairs={{0,2},{1,3},{2,0},{3,1},{4,6},{5,7},{6,4},{7,5},{8,10},{9,11},{10,... | collective-permute-start | bytes 2359304 | tf_op jit(solution)/shard_map/ppermute | solution.py:21
  300.1 19.4 %collective-permute-start.19 = (bf16[192,2048]{1,0:T(8,128)(2,1)}, bf16[192,2048]{1,0:T(8,128)(2,1)}, u32[]{:S(2)}, u32[]{:S(2)}) collective-permute-start(bf16[192,2048]{1,0:T(8,128)(2,1)} %get-tuple-element.70.q0), channel_id=1, source_target_pairs={{0,2},{1,3},{2,0},{3,1},{4,6},{5,7},{6,4},{7,5},{8,10},{9,11},{10,... | collective-permute-start | bytes 2359304 | tf_op jit(solution)/shard_map/ppermute | solution.py:21
  301.6 19.5 %collective-permute-start.18 = (bf16[192,2048]{1,0:T(8,128)(2,1)}, bf16[192,2048]{1,0:T(8,128)(2,1)}, u32[]{:S(2)}, u32[]{:S(2)}) collective-permute-start(bf16[192,2048]{1,0:T(8,128)(2,1)} %get-tuple-element.70.q0), channel_id=1, source_target_pairs={{0,1},{1,0},{2,3},{3,2},{4,5},{5,4},{6,7},{7,6},{8,9},{9,8},{10,11... | collective-permute-start | bytes 2359304 | tf_op jit(solution)/shard_map/ppermute | solution.py:21
  319.5 2.6 collective-permute-start.20
  319.5 127.0 %collective-permute-start.51 = (bf16[768,2048]{1,0:T(8,128)(2,1)}, bf16[768,2048]{1,0:T(8,128)(2,1)}, u32[]{:S(2)}, u32[]{:S(2)}) collective-permute-start(bf16[768,2048]{1,0:T(8,128)(2,1)} %get-tuple-element.26.refs_1_), channel_id=1, source_target_pairs={{0,16},{16,0},{1,17},{17,1},{2,18},{18,2},{3,19},{19,3},{4,20},{20... | collective-permute-start | bytes 9437192 | tf_op jit(solution)/shard_map/ppermute | solution.py:21
  337.9 75.3 %collective-permute-start.48 = (bf16[512,1024]{1,0:T(8,128)(2,1)}, bf16[512,1024]{1,0:T(8,128)(2,1)}, u32[]{:S(2)}, u32[]{:S(2)}) collective-permute-start(bf16[512,1024]{1,0:T(8,128)(2,1)} %dynamic-slice_convert_fusion), channel_id=1, source_target_pairs={{0,16},{16,0},{1,17},{17,1},{2,18},{18,2},{3,19},{19,3},{4,20},{20... | collective-permute-start | bytes 3145736 | tf_op jit(solution)/shard_map/ppermute | solution.py:21
  339.4 73.8 %copy-start.20 = (f32[4,128,2048]{2,1,0:T(8,128)S(1)}, f32[4,128,2048]{2,1,0:T(8,128)}, u32[]{:S(2)}) copy-start(f32[4,128,2048]{2,1,0:T(8,128)} %gather_fusion.5) | copy-start | bytes 12582916
  342.9 103.6 %collective-permute-start.49 = (bf16[768,1024]{1,0:T(8,128)(2,1)}, bf16[768,1024]{1,0:T(8,128)(2,1)}, u32[]{:S(2)}, u32[]{:S(2)}) collective-permute-start(bf16[768,1024]{1,0:T(8,128)(2,1)} %get-tuple-element.79), channel_id=1, source_target_pairs={{0,16},{16,0},{1,17},{17,1},{2,18},{18,2},{3,19},{19,3},{4,20},{20... | collective-permute-start | bytes 4718600 | tf_op jit(solution)/shard_map/ppermute | solution.py:21
  415.8 642.9 %reduce-scatter.9.cloned.1.call-start = ((), (), s32[]{:S(2)}) async-start(), calls=%async_computation.6 | async-start | bytes 5242880 | tf_op jit(solution)/shard_map/reduce_scatter | solution.py:623
  457.3 604.4 %reduce-scatter.7.cloned.1.call-start = ((), (), s32[]{:S(2)}) async-start(), calls=%async_computation.5 | async-start | bytes 5242880 | tf_op jit(solution)/shard_map/reduce_scatter | solution.py:623
  457.4 70.0 %collective-permute-start.50 = (bf16[768,2048]{1,0:T(8,128)(2,1)}, bf16[768,2048]{1,0:T(8,128)(2,1)S(1)}, u32[]{:S(2)}, u32[]{:S(2)}) collective-permute-start(bf16[768,2048]{1,0:T(8,128)(2,1)} %get-tuple-element.25.refs_0_), channel_id=1, source_target_pairs={{0,16},{16,0},{1,17},{17,1},{2,18},{18,2},{3,19},{19,3},{4,20},{20... | collective-permute-start | bytes 9437192 | tf_op jit(solution)/shard_map/ppermute | solution.py:21
  537.6 526.9 %reduce-scatter.11.cloned.1.call-start = ((), (), s32[]{:S(2)}) async-start(), calls=%async_computation.7 | async-start | bytes 5242880 | tf_op jit(solution)/shard_map/reduce_scatter | solution.py:623
  538.9 67.4 %collective-permute-start.38 = (bf16[192,2048]{1,0:T(8,128)(2,1)S(1)}, bf16[192,2048]{1,0:T(8,128)(2,1)S(1)}, u32[]{:S(2)}, u32[]{:S(2)}) collective-permute-start(bf16[192,2048]{1,0:T(8,128)(2,1)S(1)} %constant_dynamic-slice_fusion.4), channel_id=1, source_target_pairs={{0,4},{4,0},{8,12},{12,8},{1,5},{5,1},{9,13},{13,9},{2,6},{6,2},{1... | collective-permute-start | bytes 2359304 | tf_op jit(solution)/shard_map/ppermute | solution.py:21
  541.6 81.7 %collective-permute-start.39 = (bf16[192,2048]{1,0:T(8,128)(2,1)S(1)}, bf16[192,2048]{1,0:T(8,128)(2,1)S(1)}, u32[]{:S(2)}, u32[]{:S(2)}) collective-permute-start(bf16[192,2048]{1,0:T(8,128)(2,1)S(1)} %constant_dynamic-slice_fusion.4), channel_id=1, source_target_pairs={{0,8},{4,12},{8,0},{12,4},{1,9},{5,13},{9,1},{13,5},{2,10},{6,14},... | collective-permute-start | bytes 2359304 | tf_op jit(solution)/shard_map/ppermute | solution.py:21
  542.6 98.7 %collective-permute-start.40 = (bf16[192,2048]{1,0:T(8,128)(2,1)S(1)}, bf16[192,2048]{1,0:T(8,128)(2,1)S(1)}, u32[]{:S(2)}, u32[]{:S(2)}) collective-permute-start(bf16[192,2048]{1,0:T(8,128)(2,1)S(1)} %constant_dynamic-slice_fusion.4), channel_id=1, source_target_pairs={{0,12},{4,8},{8,4},{12,0},{1,13},{5,9},{9,5},{13,1},{2,14},{6,10},... | collective-permute-start | bytes 2359304 | tf_op jit(solution)/shard_map/ppermute | solution.py:21
  641.3 51.3 %copy-start.25 = (bf16[768,2048]{1,0:T(8,128)(2,1)S(1)}, bf16[768,2048]{1,0:T(8,128)(2,1)}, u32[]{:S(2)}) copy-start(bf16[768,2048]{1,0:T(8,128)(2,1)} %param.21) | copy-start | bytes 9437188
  644.0 51.3 %copy-start.5 = (bf16[2048,512]{1,0:T(8,128)(2,1)S(1)}, bf16[2048,512]{1,0:T(8,128)(2,1)}, u32[]{:S(2)}) copy-start(bf16[2048,512]{1,0:T(8,128)(2,1)} %wq_ref.1) | copy-start | bytes 6291460
  644.0 47.2 %collective-permute-start.42 = (bf16[3,192,2048]{2,1,0:T(8,128)(2,1)}, bf16[3,192,2048]{2,1,0:T(8,128)(2,1)}, u32[]{:S(2)}, u32[]{:S(2)}) collective-permute-start(bf16[3,192,2048]{2,1,0:T(8,128)(2,1)} %get-tuple-element.82), channel_id=1, source_target_pairs={{0,2},{1,3},{2,0},{3,1},{4,6},{5,7},{6,4},{7,5},{8,10},{9,11},{10,... | collective-permute-start | bytes 7077896 | tf_op jit(solution)/shard_map/ppermute | solution.py:21
  645.6 81.0 %collective-permute-start.41 = (bf16[3,192,2048]{2,1,0:T(8,128)(2,1)}, bf16[3,192,2048]{2,1,0:T(8,128)(2,1)}, u32[]{:S(2)}, u32[]{:S(2)}) collective-permute-start(bf16[3,192,2048]{2,1,0:T(8,128)(2,1)} %get-tuple-element.82), channel_id=1, source_target_pairs={{0,1},{1,0},{2,3},{3,2},{4,5},{5,4},{6,7},{7,6},{8,9},{9,8},{10,11... | collective-permute-start | bytes 7077896 | tf_op jit(solution)/shard_map/ppermute | solution.py:21
  691.2 35.3 %collective-permute-start.43 = (bf16[3,192,2048]{2,1,0:T(8,128)(2,1)}, bf16[3,192,2048]{2,1,0:T(8,128)(2,1)}, u32[]{:S(2)}, u32[]{:S(2)}) collective-permute-start(bf16[3,192,2048]{2,1,0:T(8,128)(2,1)} %collective-permute-done.42), channel_id=1, source_target_pairs={{0,1},{1,0},{2,3},{3,2},{4,5},{5,4},{6,7},{7,6},{8,9},{9,8},{10,11... | collective-permute-start | bytes 7077896 | tf_op jit(solution)/shard_map/ppermute | solution.py:21
  691.2 107.1 %collective-permute-start.52 = (bf16[768,2048]{1,0:T(8,128)(2,1)}, bf16[768,2048]{1,0:T(8,128)(2,1)}, u32[]{:S(2)}, u32[]{:S(2)}) collective-permute-start(bf16[768,2048]{1,0:T(8,128)(2,1)} %get-tuple-element.24.refs_0_), channel_id=1, source_target_pairs={{0,16},{16,0},{1,17},{17,1},{2,18},{18,2},{3,19},{19,3},{4,20},{20... | collective-permute-start | bytes 9437192 | tf_op jit(solution)/shard_map/ppermute | solution.py:21
  694.8 101.0 %collective-permute-start.53 = (bf16[768,1024]{1,0:T(8,128)(2,1)}, bf16[768,1024]{1,0:T(8,128)(2,1)}, u32[]{:S(2)}, u32[]{:S(2)}) collective-permute-start(bf16[768,1024]{1,0:T(8,128)(2,1)} %get-tuple-element.77), channel_id=1, source_target_pairs={{0,16},{16,0},{1,17},{17,1},{2,18},{18,2},{3,19},{19,3},{4,20},{20... | collective-permute-start | bytes 4718600 | tf_op jit(solution)/shard_map/ppermute | solution.py:21
  726.5 71.7 %copy-start.27 = (bf16[768,1024]{1,0:T(8,128)(2,1)S(1)}, bf16[768,1024]{1,0:T(8,128)(2,1)}, u32[]{:S(2)}) copy-start(bf16[768,1024]{1,0:T(8,128)(2,1)} %get-tuple-element.76) | copy-start | bytes 4718596
  735.9 200.0 %collective-permute-start.14 = (bf16[192,2048]{1,0:T(8,128)(2,1)S(1)}, bf16[192,2048]{1,0:T(8,128)(2,1)S(1)}, u32[]{:S(2)}, u32[]{:S(2)}) collective-permute-start(bf16[192,2048]{1,0:T(8,128)(2,1)S(1)} %get-tuple-element.94.q0), channel_id=1, source_target_pairs={{0,2},{1,3},{2,0},{3,1},{4,6},{5,7},{6,4},{7,5},{8,10},{9,11},{10,... | collective-permute-start | bytes 2359304 | tf_op jit(solution)/shard_map/ppermute | solution.py:21
  738.3 70.7 %collective-permute-start.21 = (bf16[768,128]{1,0:T(8,128)(2,1)}, bf16[768,128]{1,0:T(8,128)(2,1)S(1)}, u32[]{:S(2)}, u32[]{:S(2)}) collective-permute-start(bf16[768,128]{1,0:T(8,128)(2,1)} %get-tuple-element.101), channel_id=1, source_target_pairs={{0,4},{4,0},{8,12},{12,8},{1,5},{5,1},{9,13},{13,9},{2,6},{6,2},{1... | collective-permute-start | bytes 589832 | tf_op jit(solution)/shard_map/ppermute | solution.py:21
  773.7 35.3 %collective-permute-start.22 = (bf16[768,128]{1,0:T(8,128)(2,1)}, bf16[768,128]{1,0:T(8,128)(2,1)}, u32[]{:S(2)}, u32[]{:S(2)}) collective-permute-start(bf16[768,128]{1,0:T(8,128)(2,1)} %get-tuple-element.100), channel_id=1, source_target_pairs={{0,8},{4,12},{8,0},{12,4},{1,9},{5,13},{9,1},{13,5},{2,10},{6,14},... | collective-permute-start | bytes 589832 | tf_op jit(solution)/shard_map/ppermute | solution.py:21
  795.8 13.3 %collective-permute-start.23 = (bf16[768,128]{1,0:T(8,128)(2,1)}, bf16[768,128]{1,0:T(8,128)(2,1)}, u32[]{:S(2)}, u32[]{:S(2)}) collective-permute-start(bf16[768,128]{1,0:T(8,128)(2,1)} %get-tuple-element.99), channel_id=1, source_target_pairs={{0,12},{4,8},{8,4},{12,0},{1,13},{5,9},{9,5},{13,1},{2,14},{6,10},... | collective-permute-start | bytes 589832 | tf_op jit(solution)/shard_map/ppermute | solution.py:21
  859.0 84.3 %collective-permute-start.24 = (bf16[768,384]{1,0:T(8,128)(2,1)}, bf16[768,384]{1,0:T(8,128)(2,1)}, u32[]{:S(2)}, u32[]{:S(2)}) collective-permute-start(bf16[768,384]{1,0:T(8,128)(2,1)} %get-tuple-element.86), channel_id=1, source_target_pairs={{0,4},{4,0},{8,12},{12,8},{1,5},{5,1},{9,13},{13,9},{2,6},{6,2},{1... | collective-permute-start | bytes 1769480 | tf_op jit(solution)/shard_map/ppermute | solution.py:21
  895.0 48.3 %collective-permute-start.25 = (bf16[768,384]{1,0:T(8,128)(2,1)}, bf16[768,384]{1,0:T(8,128)(2,1)}, u32[]{:S(2)}, u32[]{:S(2)}) collective-permute-start(bf16[768,384]{1,0:T(8,128)(2,1)} %get-tuple-element.85), channel_id=1, source_target_pairs={{0,8},{4,12},{8,0},{12,4},{1,9},{5,13},{9,1},{13,5},{2,10},{6,14},... | collective-permute-start | bytes 1769480 | tf_op jit(solution)/shard_map/ppermute | solution.py:21
  895.0 63.2 %collective-permute-start.26 = (bf16[768,384]{1,0:T(8,128)(2,1)}, bf16[768,384]{1,0:T(8,128)(2,1)}, u32[]{:S(2)}, u32[]{:S(2)}) collective-permute-start(bf16[768,384]{1,0:T(8,128)(2,1)} %get-tuple-element.84), channel_id=1, source_target_pairs={{0,12},{4,8},{8,4},{12,0},{1,13},{5,9},{9,5},{13,1},{2,14},{6,10},... | collective-permute-start | bytes 1769480 | tf_op jit(solution)/shard_map/ppermute | solution.py:21
  935.9 49.3 %collective-permute-start.13 = (bf16[192,2048]{1,0:T(8,128)(2,1)S(1)}, bf16[192,2048]{1,0:T(8,128)(2,1)S(1)}, u32[]{:S(2)}, u32[]{:S(2)}) collective-permute-start(bf16[192,2048]{1,0:T(8,128)(2,1)S(1)} %get-tuple-element.94.q0), channel_id=1, source_target_pairs={{0,1},{1,0},{2,3},{3,2},{4,5},{5,4},{6,7},{7,6},{8,9},{9,8},{10,11... | collective-permute-start | bytes 2359304 | tf_op jit(solution)/shard_map/ppermute | solution.py:21
  935.9 49.3 %collective-permute-start.15 = (bf16[192,2048]{1,0:T(8,128)(2,1)S(1)}, bf16[192,2048]{1,0:T(8,128)(2,1)S(1)}, u32[]{:S(2)}, u32[]{:S(2)}) collective-permute-start(bf16[192,2048]{1,0:T(8,128)(2,1)S(1)} %collective-permute-done.14.q2), channel_id=1, source_target_pairs={{0,1},{1,0},{2,3},{3,2},{4,5},{5,4},{6,7},{7,6},{8,9},{9,8},{10,11... | collective-permute-start | bytes 2359304 | tf_op jit(solution)/shard_map/ppermute | solution.py:21
  969.0 13.0 %collective-permute-start.27 = (bf16[2,192,2048]{2,1,0:T(8,128)(2,1)S(1)}, bf16[2,192,2048]{2,1,0:T(8,128)(2,1)S(1)}, u32[]{:S(2)}, u32[]{:S(2)}) collective-permute-start(bf16[2,192,2048]{2,1,0:T(8,128)(2,1)S(1)} %slice.220), channel_id=1, source_target_pairs={{0,1},{1,0},{2,3},{3,2},{4,5},{5,4},{6,7},{7,6},{8,9},{9,8},{10,11... | collective-permute-start | bytes 4718600 | tf_op jit(solution)/shard_map/ppermute | solution.py:21
  980.4 19.2 %collective-permute-start.44 = (bf16[1024,384]{1,0:T(8,128)(2,1)S(1)}, bf16[1024,384]{1,0:T(8,128)(2,1)S(1)}, u32[]{:S(2)}, u32[]{:S(2)}) collective-permute-start(bf16[1024,384]{1,0:T(8,128)(2,1)S(1)} %dynamic-slice_convert_fusion.1), channel_id=1, source_target_pairs={{0,16},{16,0},{1,17},{17,1},{2,18},{18,2},{3,19},{19,3},{4,20},{20... | collective-permute-start | bytes 2359304 | tf_op jit(solution)/shard_map/ppermute | solution.py:21
  983.7 31.2 %collective-permute-start.28 = (bf16[192,2048]{1,0:T(8,128)(2,1)}, bf16[192,2048]{1,0:T(8,128)(2,1)}, u32[]{:S(2)}, u32[]{:S(2)}) collective-permute-start(bf16[192,2048]{1,0:T(8,128)(2,1)} %fusion.47), channel_id=1, source_target_pairs={{0,2},{1,3},{2,0},{3,1},{4,6},{5,7},{6,4},{7,5},{8,10},{9,11},{10,... | collective-permute-start | bytes 2359304 | tf_op jit(solution)/shard_map/ppermute | solution.py:21
  1000.6 23.7 %collective-permute-start.45 = (bf16[256,384]{1,0:T(8,128)(2,1)S(1)}, bf16[256,384]{1,0:T(8,128)(2,1)S(1)}, u32[]{:S(2)}, u32[]{:S(2)}) collective-permute-start(bf16[256,384]{1,0:T(8,128)(2,1)S(1)} %get-tuple-element.97), channel_id=1, source_target_pairs={{0,4},{4,0},{8,12},{12,8},{1,5},{5,1},{9,13},{13,9},{2,6},{6,2},{1... | collective-permute-start | bytes 589832 | tf_op jit(solution)/shard_map/ppermute | solution.py:21
  1012.4 16.3 %collective-permute-start.46 = (bf16[256,384]{1,0:T(8,128)(2,1)S(1)}, bf16[256,384]{1,0:T(8,128)(2,1)S(1)}, u32[]{:S(2)}, u32[]{:S(2)}) collective-permute-start(bf16[256,384]{1,0:T(8,128)(2,1)S(1)} %get-tuple-element.96), channel_id=1, source_target_pairs={{0,8},{4,12},{8,0},{12,4},{1,9},{5,13},{9,1},{13,5},{2,10},{6,14},... | collective-permute-start | bytes 589832 | tf_op jit(solution)/shard_map/ppermute | solution.py:21
  1012.5 16.2 %collective-permute-start.47 = (bf16[256,384]{1,0:T(8,128)(2,1)S(1)}, bf16[256,384]{1,0:T(8,128)(2,1)S(1)}, u32[]{:S(2)}, u32[]{:S(2)}) collective-permute-start(bf16[256,384]{1,0:T(8,128)(2,1)S(1)} %get-tuple-element.98), channel_id=1, source_target_pairs={{0,12},{4,8},{8,4},{12,0},{1,13},{5,9},{9,5},{13,1},{2,14},{6,10},... | collective-permute-start | bytes 589832 | tf_op jit(solution)/shard_map/ppermute | solution.py:21
  1017.4 1.2 collective-permute-start.32
  1018.7 4.1 collective-permute-start.33
  1022.2 19.4 %collective-permute-start.30 = (bf16[192,2048]{1,0:T(8,128)(2,1)S(1)}, bf16[192,2048]{1,0:T(8,128)(2,1)S(1)}, u32[]{:S(2)}, u32[]{:S(2)}) collective-permute-start(bf16[192,2048]{1,0:T(8,128)(2,1)S(1)} %fusion.35.q0), channel_id=1, source_target_pairs={{0,2},{1,3},{2,0},{3,1},{4,6},{5,7},{6,4},{7,5},{8,10},{9,11},{10,... | collective-permute-start | bytes 2359304 | tf_op jit(solution)/shard_map/ppermute | solution.py:21
  1022.8 8.2 collective-permute-start.34
  1031.0 26.0 %collective-permute-start.29 = (bf16[192,2048]{1,0:T(8,128)(2,1)S(1)}, bf16[192,2048]{1,0:T(8,128)(2,1)S(1)}, u32[]{:S(2)}, u32[]{:S(2)}) collective-permute-start(bf16[192,2048]{1,0:T(8,128)(2,1)S(1)} %fusion.35.q0), channel_id=1, source_target_pairs={{0,1},{1,0},{2,3},{3,2},{4,5},{5,4},{6,7},{7,6},{8,9},{9,8},{10,11... | collective-permute-start | bytes 2359304 | tf_op jit(solution)/shard_map/ppermute | solution.py:21
  1041.6 15.4 %collective-permute-start.31 = (bf16[192,2048]{1,0:T(8,128)(2,1)S(1)}, bf16[192,2048]{1,0:T(8,128)(2,1)S(1)}, u32[]{:S(2)}, u32[]{:S(2)}) collective-permute-start(bf16[192,2048]{1,0:T(8,128)(2,1)S(1)} %collective-permute-done.30.q2), channel_id=1, source_target_pairs={{0,1},{1,0},{2,3},{3,2},{4,5},{5,4},{6,7},{7,6},{8,9},{9,8},{10,11... | collective-permute-start | bytes 2359304 | tf_op jit(solution)/shard_map/ppermute | solution.py:21
  1041.6 14.8 %collective-permute-start.35 = (f32[2,256]{1,0:T(2,128)S(1)}, f32[2,256]{1,0:T(2,128)S(1)}, u32[]{:S(2)}, u32[]{:S(2)}) collective-permute-start(f32[2,256]{1,0:T(2,128)S(1)} %get-tuple-element.110), channel_id=1, source_target_pairs={{0,4},{4,0},{8,12},{12,8},{1,5},{5,1},{9,13},{13,9},{2,6},{6,2},{1... | collective-permute-start | bytes 6152 | tf_op jit(solution)/shard_map/ppermute | solution.py:21
  1042.7 13.8 %collective-permute-start.36 = (f32[2,256]{1,0:T(2,128)S(1)}, f32[2,256]{1,0:T(2,128)S(1)}, u32[]{:S(2)}, u32[]{:S(2)}) collective-permute-start(f32[2,256]{1,0:T(2,128)S(1)} %get-tuple-element.111), channel_id=1, source_target_pairs={{0,8},{4,12},{8,0},{12,4},{1,9},{5,13},{9,1},{13,5},{2,10},{6,14},... | collective-permute-start | bytes 6152 | tf_op jit(solution)/shard_map/ppermute | solution.py:21
  1043.6 12.8 %collective-permute-start.37 = (f32[2,256]{1,0:T(2,128)S(1)}, f32[2,256]{1,0:T(2,128)S(1)}, u32[]{:S(2)}, u32[]{:S(2)}) collective-permute-start(f32[2,256]{1,0:T(2,128)S(1)} %get-tuple-element.112), channel_id=1, source_target_pairs={{0,12},{4,8},{8,4},{12,0},{1,13},{5,9},{9,5},{13,1},{2,14},{6,10},... | collective-permute-start | bytes 6152 | tf_op jit(solution)/shard_map/ppermute | solution.py:21
  (33 other events, 351.6 us)
Sparse Core Ops, SparseCore 0:
  416.0 28.4 reduce-scatter.4
  457.5 78.0 reduce-scatter.8
  537.8 128.6 reduce-scatter.6
  809.1 133.6 reduce-scatter.10

commit v2 on v0

v2 whole, which is shorter than its diff:
```python
import functools

import jax
import jax.numpy as jnp
from jax import lax
from jax.experimental import pallas as pl
from jax.experimental.pallas import tpu as pltpu
from jax.sharding import PartitionSpec as P

HEAD_DIM = 64
EPS = 1e-05
THETA = 130000.0
BLOCK = 384
MIB = 1 << 20
MOST = 62
COSTS = {
    "attend": 20, "attend_back": 22, "feed": 6, "feed_back": 6, "feed_down": 5, "hidden_back": 4, "wgrad": 4,
    "wgrads": 10, "out_wgrad": 4, "project_back": 5, "rope_tables": 3,
}
LOW = jnp.bfloat16
F32 = jnp.float32
ANY = pl.BlockSpec(memory_space=pl.ANY)


CTX, TENSOR = ("hi", "lo"), ("y", "core")


def swap(value, axis, distance):
    size = 2 if axis == "dp" else 4
    return lax.ppermute(value, axis, [(i, i ^ distance) for i in range(size)])


def dot(left, right):
    return jnp.dot(left, right, preferred_element_type=F32)


def against(left, right):
    return lax.dot_general(left, right, (((1,), (1,)), ((), ())), preferred_element_type=F32)


def across(left, right):
    return lax.dot_general(left, right, (((0,), (0,)), ((), ())), preferred_element_type=F32)


def shaped(shape, dtype=LOW):
    return jax.ShapeDtypeStruct(shape, dtype)


def call(kernel, name, index, grid, inputs, in_specs, outs, out_specs, scratch=(), mib=MOST, after=()):
    count = len(inputs)

    def body(index_ref, *refs):
        kernel(index_ref, *refs[:count], *refs[count + len(after) :])

    return pl.pallas_call(
        body,
        grid_spec=pltpu.PrefetchScalarGridSpec(
            num_scalar_prefetch=1,
            grid=grid,
            in_specs=list(in_specs) + [ANY] * len(after),
            out_specs=out_specs,
            scratch_shapes=list(scratch),
        ),
        out_shape=outs,
        compiler_params=pltpu.CompilerParams(
            vmem_limit_bytes=mib * MIB, dimension_semantics=("arbitrary",) * len(grid)
        ),
        cost_estimate=pl.CostEstimate(flops=0, bytes_accessed=int(COSTS.get(name, 0) * 3.5 * MIB), transcendentals=0),
        name=name,
    )(index, *inputs, *after)


ME, T = 0, 1


def copy_all(pairs, sems):
    copies = [pltpu.make_async_copy(a, b, sems.at[k]) for k, (a, b) in enumerate(pairs)]
    for copy in copies:
        copy.start()
    for copy in copies:
        copy.wait()


def half_turn(rows):
    lane = lax.broadcasted_iota(jnp.int32, (1, 128), 1)
    first = (lane % HEAD_DIM) < HEAD_DIM // 2
    return jnp.where(first, pltpu.roll(rows, 96, 1), pltpu.roll(rows, 32, 1))


def rope_freq():
    half = HEAD_DIM // 2
    freq = jnp.power(THETA, -jnp.arange(half, dtype=F32) * (2.0 / HEAD_DIM))
    return jnp.concatenate([freq] * 4)


def rope_tables(positions):
    sign = jnp.where((jnp.arange(128) % HEAD_DIM) < HEAD_DIM // 2, -1.0, 1.0)
    angle = positions.astype(F32)[:, None] * rope_freq()[None, :]
    return jnp.cos(angle), jnp.sin(angle) * sign


def project_kernel(ix, tok_ref, gain_ref, cos_ref, sin_ref, wq_ref, wk_ref, wv_ref, first_ref, o0, o1, o2, o3, held):
    me = ix[ME]
    rows = tok_ref[...].astype(F32)
    inverse = lax.rsqrt(jnp.mean(rows * rows, axis=-1, keepdims=True) + EPS)
    first = (rows * inverse * gain_ref[...]).astype(LOW)
    first_ref[...] = first
    cosine, sine = cos_ref[...], sin_ref[...]
    for place, weight in enumerate((wq_ref, wk_ref, wv_ref)):
        flat = dot(first, weight[...])
        for group in range(4):
            part = flat[:, group * 128 : (group + 1) * 128]
            if place < 2:
                part = part * cosine + half_turn(part) * sine
            if place == 0:
                part = part * HEAD_DIM**-0.5
            held[group, :, place * 128 : (place + 1) * 128] = part.astype(LOW)
    for slot, out in enumerate((o0, o1, o2, o3)):
        out[...] = held[slot ^ me]


def project(ix, tokens, gain, tables, weights):
    rows, width = tokens.shape
    local = weights[0].shape[1]
    step = 256
    whole = lambda i, m: (0, 0)
    along = lambda i, m: (i, 0)
    return call(
        project_kernel, "project", ix, (rows // step,),
        [tokens, gain.reshape(1, -1), *tables, *weights],
        [pl.BlockSpec((step, width), along), pl.BlockSpec((1, width), whole)]
        + [pl.BlockSpec((step, 128), along)] * 2 + [pl.BlockSpec((width, local), whole)] * 3,
        [shaped((rows, width))] + [shaped((rows, 384))] * 4,
        [pl.BlockSpec((step, width), along)] + [pl.BlockSpec((step, 384), along)] * 4,
        [pltpu.VMEM((4, step, 384), LOW)],
    )


def own_lanes(rows, head):
    lane = lax.broadcasted_iota(jnp.int32, (1, 128), 1)
    inside = (lane < HEAD_DIM) if head == 0 else (lane >= HEAD_DIM)
    return jnp.where(inside, rows, jnp.zeros_like(rows))


def attend_kernel(ix, r0, r1, r2, r3, o0, o1, o2, o3, raw_ref, lse_ref, held, sems):
    me = ix[ME]
    turn = pl.program_id(0)
    stretch = r0.shape[0]
    per = stretch // BLOCK
    here = ((turn // per) ^ me) * per + turn % per

    @pl.when(turn == 0)
    def _():
        copy_all(
            [(r, held.at[pl.ds((me ^ k) * stretch, stretch)]) for k, r in enumerate((r0, r1, r2, r3))],
            sems,
        )

    query = held[pl.ds(here * BLOCK, BLOCK), 0:128]
    queries = [own_lanes(query, head) for head in range(2)]

    def step(at, carry, diagonal):
        rows = pl.ds(at * BLOCK, BLOCK)
        keys, values = held[rows, 128:256], held[rows, 256:384]
        out = []
        for head in range(2):
            peak, mass, total = carry[3 * head : 3 * head + 3]
            scores = against(queries[head], keys)
            if diagonal:
                down = lax.broadcasted_iota(jnp.int32, (BLOCK, BLOCK), 0)
                along = lax.broadcasted_iota(jnp.int32, (BLOCK, BLOCK), 1)
                scores = jnp.where(down >= along, scores, -1e30)
            top = jnp.maximum(peak, jnp.max(scores, axis=-1, keepdims=True))
            weights = jnp.exp(scores - top)
            fade = jnp.exp(peak - top)
            mass = mass * fade + jnp.sum(weights, axis=-1, keepdims=True)
            total = total * fade + dot(weights.astype(LOW), values)
            out += [top, mass, total]
        return tuple(out)

    start = (
        jnp.full((BLOCK, 1), -1e30, F32),
        jnp.zeros((BLOCK, 1), F32),
        jnp.zeros((BLOCK, 128), F32),
    ) * 2
    carry = lax.fori_loop(0, here, lambda at, c: step(at, c, False), start)
    peak0, mass0, total0, peak1, mass1, total1 = step(here, carry, True)
    lane = lax.broadcasted_iota(jnp.int32, (1, 128), 1)
    mixed = jnp.where(lane < HEAD_DIM, total0 / mass0, total1 / mass1)
    raw_ref[...] = mixed
    for slot, out in enumerate((o0, o1, o2, o3)):

        @pl.when(turn // per == slot)
        def _():
            out[...] = mixed.astype(LOW)

    turned = jnp.where(lane < HEAD_DIM, peak0 + jnp.log(mass0), peak1 + jnp.log(mass1)).T
    lse_ref[0, 0:8] = turned[0:8]
    lse_ref[0, 8:16] = turned[64:72]


def attend(ix, pieces, after):
    stretch = pieces[0].shape[0]
    length = 4 * stretch
    per = stretch // BLOCK
    count = length // BLOCK

    def place(i, m):
        return ((i // per) ^ m[ME]) * per + i % per

    def slot_spec(slot):
        return pl.BlockSpec((BLOCK, 128), lambda i, m: (jnp.clip(i - slot * per, 0, per - 1), 0))

    return call(
        attend_kernel, "attend", ix, (count,), list(pieces), [ANY] * 4,
        [shaped((stretch, 128))] * 4 + [shaped((length, 128), F32), shaped((count, 16, BLOCK), F32)],
        [slot_spec(slot) for slot in range(4)]
        + [
            pl.BlockSpec((BLOCK, 128), lambda i, m: (place(i, m), 0)),
            pl.BlockSpec((1, 16, BLOCK), lambda i, m: (place(i, m), 0, 0)),
        ],
        [pltpu.VMEM((length, 384), LOW), pltpu.SemaphoreType.DMA((4,))],
        after=after,
    )


def attend_back_kernel(
    ix, r0, r1, r2, r3, u0, u1, u2, u3, raw_ref, lse_ref, cos_ref, sin_ref, o0, o1, o2, o3,
    held, up, query_at, up_at, delta, query_sum, key_sum, value_sum, sems,
):
    me = ix[ME]
    turn = pl.program_id(0)
    count = pl.num_programs(0)
    stretch = r0.shape[0]
    per = stretch // BLOCK
    here = ((turn // per) ^ me) * per + turn % per

    @pl.when(turn == 0)
    def _():
        rows = [pl.ds((me ^ k) * stretch, stretch) for k in range(4)]
        copy_all(
            [(ref, held.at[rows[k]]) for k, ref in enumerate((r0, r1, r2, r3))]
            + [(ref, up.at[rows[k]]) for k, ref in enumerate((u0, u1, u2, u3))],
            sems,
        )
        query_sum[...] = jnp.zeros_like(query_sum)

        def prepare(at, _):
            rows = pl.ds(at * BLOCK, BLOCK)
            query, upstream = held[rows, 0:128], up[rows, :]
            turned = (upstream.astype(F32) * raw_ref[rows, :]).T
            for head in range(2):
                query_at[head, rows, :] = own_lanes(query, head)
                up_at[head, rows, :] = own_lanes(upstream, head)
                total = jnp.sum(turned[head * 64 : head * 64 + 64], axis=0, keepdims=True)
                delta[at, head * 8 : head * 8 + 8, :] = jnp.broadcast_to(total, (8, BLOCK))
            return 0

        lax.fori_loop(0, count, prepare, 0)

    here_rows = pl.ds(here * BLOCK, BLOCK)
    key, value = held[here_rows, 128:256], held[here_rows, 256:384]
    keys = [own_lanes(key, head) for head in range(2)]
    values = [own_lanes(value, head) for head in range(2)]

    def step(at, diagonal):
        rows = pl.ds(at * BLOCK, BLOCK)
        query, upstream = held[rows, 0:128], up[rows, :]
        key_total = value_total = query_total = None
        for head in range(2):
            scores = against(keys[head], query)
            lse = lse_ref[at, head * 8 : head * 8 + 1, :]
            chance = jnp.exp(scores - lse)
            if diagonal:
                down = lax.broadcasted_iota(jnp.int32, (BLOCK, BLOCK), 0)
                along = lax.broadcasted_iota(jnp.int32, (BLOCK, BLOCK), 1)
                chance = jnp.where(along >= down, chance, 0.0)
            chance_back = against(values[head], upstream)
            shift = delta[at, head * 8 : head * 8 + 1, :]
            score_back = (chance * (chance_back - shift)).astype(LOW)
            value_part = dot(chance.astype(LOW), up_at[head, rows, :])
            key_part = dot(score_back, query_at[head, rows, :])
            query_part = across(score_back, keys[head])
            if head == 0:
                value_total, key_total, query_total = value_part, key_part, query_part
            else:
                value_total += value_part
                key_total += key_part
                query_total += query_part
        query_sum[rows, :] += query_total
        return key_total, value_total

    key_sum[...], value_sum[...] = step(here, True)

    def later(at, _):
        key_total, value_total = step(at, False)
        key_sum[...] += key_total
        value_sum[...] += value_total
        return 0

    lax.fori_loop(here + 1, count, later, 0)

    def back_rope(rows, at):
        places = pl.ds(at * BLOCK, BLOCK)
        return rows * cos_ref[places, :] - half_turn(rows) * sin_ref[places, :]

    inner = pl.ds(pl.multiple_of((turn % per) * BLOCK, BLOCK), BLOCK)
    key_low, value_low = back_rope(key_sum[...], here).astype(LOW), value_sum[...].astype(LOW)
    for slot, out in enumerate((o0, o1, o2, o3)):

        @pl.when(turn // per == slot)
        def _():
            out[inner, 128:256] = key_low
            out[inner, 256:384] = value_low

    @pl.when(turn == count - 1)
    def _():
        for slot, out in enumerate((o0, o1, o2, o3)):
            for block in range(per):
                at = (slot ^ me) * per + block
                rows = query_sum[pl.ds(at * BLOCK, BLOCK), :] * HEAD_DIM**-0.5
                out[block * BLOCK : (block + 1) * BLOCK, 0:128] = back_rope(rows, at).astype(LOW)


def attend_back(ix, pieces, upstreams, raw, lse, tables, after):
    stretch = pieces[0].shape[0]
    length = 4 * stretch
    count = length // BLOCK
    whole = lambda i, m: (0, 0)
    return call(
        attend_back_kernel, "attend_back", ix, (count,), [*pieces, *upstreams, raw, lse, *tables],
        [ANY] * 8
        + [
            pl.BlockSpec((length, 128), whole),
            pl.BlockSpec((count, 16, BLOCK), lambda i, m: (0, 0, 0)),
            pl.BlockSpec((length, 128), whole),
            pl.BlockSpec((length, 128), whole),
        ],
        [shaped((stretch, 384))] * 4,
        [pl.BlockSpec((stretch, 384), whole)] * 4,
        [
            pltpu.VMEM((length, 384), LOW),
            pltpu.VMEM((length, 128), LOW),
            pltpu.VMEM((2, length, 128), LOW),
            pltpu.VMEM((2, length, 128), LOW),
            pltpu.VMEM((count, 16, BLOCK), F32),
            pltpu.VMEM((length, 128), F32),
            pltpu.VMEM((BLOCK, 128), F32),
            pltpu.VMEM((BLOCK, 128), F32),
            pltpu.SemaphoreType.DMA((8,)),
        ],
        after=after,
    )


def store_quarters(total, t, keep_ref, send_ref):
    rows = keep_ref.shape[1]
    for quarter in range(4):
        part = total[quarter * rows : (quarter + 1) * rows].astype(LOW)
        slot = quarter ^ t

        @pl.when(slot % 2 == 0)
        def _():
            keep_ref[slot // 2] = part

        @pl.when(slot % 2 == 1)
        def _():
            send_ref[slot // 2] = part


def quarter_outs(rows, width, step):
    return (
        [shaped((2, rows // 4, width))] * 2,
        [pl.BlockSpec((2, rows // 4, step), lambda i, m: (0, 0, i))] * 2,
    )


def quarters_kernel(ix, *refs, count, turned):
    total = None
    for left, right in zip(refs[:count], refs[count : 2 * count]):
        part = (against if turned else dot)(left[...], right[...])
        total = part if total is None else total + part
    store_quarters(total, ix[T], *refs[2 * count :])


def feed_quarters(ix, lefts, rights, turned, name, after=()):
    rows, depth = lefts[0].shape
    step = 256
    if turned:
        width = rights[0].shape[0]
        spec = pl.BlockSpec((step, depth), lambda i, m: (i, m[ME] % 2))
    else:
        width = rights[0].shape[1]
        spec = pl.BlockSpec((depth, step), lambda i, m: (m[ME] % 2, i))
    count = len(lefts)
    outs, out_specs = quarter_outs(rows, width, step)
    return call(
        functools.partial(quarters_kernel, count=count, turned=turned), name, ix, (width // step,),
        [*lefts, *rights],
        [pl.BlockSpec((rows, depth), lambda i, m: (0, 0))] * count + [spec] * count,
        outs, out_specs, after=after,
    )


def join_heads_kernel(ix, a0, a1, a2, a3, w0, w1, w2, w3, keep_ref, send_ref):
    left = jnp.concatenate([a0[...], a1[...], a2[...], a3[...]], axis=1)
    right = jnp.concatenate([w0[...], w1[...], w2[...], w3[...]], axis=0)
    store_quarters(dot(left, right), ix[T], keep_ref, send_ref)


def join_heads(ix, mixed, w_out, after=()):
    rows = mixed[0].shape[0]
    width = w_out.shape[1]
    step = 512

    def heads(slot):
        return pl.BlockSpec((128, step), lambda i, m: (m[ME] ^ slot, i))

    outs, out_specs = quarter_outs(rows, width, step)
    return call(
        join_heads_kernel, "join_heads", ix, (width // step,), [*mixed] + [w_out] * 4,
        [pl.BlockSpec((rows, 128), lambda i, m: (0, 0))] * 4 + [heads(slot) for slot in range(4)],
        outs, out_specs, after=after,
    )


def project_back_kernel(ix, *refs):
    left = jnp.concatenate([ref[...] for ref in refs[:4]], axis=1)
    right = jnp.concatenate([ref[...] for ref in refs[4:16]], axis=1)
    store_quarters(against(left, right), ix[T], *refs[16:])


def project_back(ix, back, weights, after):
    rows = back[0].shape[0]
    width = weights[0].shape[0]
    step = 256

    def heads(slot):
        return pl.BlockSpec((step, 128), lambda i, m: (i, m[ME] ^ slot))

    outs, out_specs = quarter_outs(rows, width, step)
    return call(
        project_back_kernel, "project_back", ix, (width // step,),
        [*back] + [w for slot in range(4) for w in weights],
        [pl.BlockSpec((rows, 384), lambda i, m: (0, 0))] * 4
        + [heads(slot) for slot in range(4) for w in weights],
        outs, out_specs, after=after,
    )


def rows_call(kernel, name, ix, quarters, others, outs, sums=0, after=()):
    rows, width = quarters[0].shape[-2:]
    step = rows // 2

    def spec(array):
        if array.ndim == 3:
            return pl.BlockSpec((2, step, width), lambda i, m: (0, i, 0))
        if array.shape[0] == 1:
            return pl.BlockSpec((1, width), lambda i, m: (0, 0))
        if array.shape[0] == rows:
            return pl.BlockSpec((step, width), lambda i, m: (i, 0))
        return pl.BlockSpec((step, width), lambda i, m: (2 * m[T] + i, 0))

    return call(
        kernel, name, ix, (2,), [*quarters, *others], [spec(a) for a in (*quarters, *others)],
        [shaped((rows, width), dtype) for dtype in outs] + [shaped((1, width), F32)] * sums,
        [pl.BlockSpec((step, width), lambda i, m: (i, 0))] * len(outs)
        + [pl.BlockSpec((1, width), lambda i, m: (0, 0))] * sums,
        after=after,
    )


def pair_kernel(ix, keep_ref, other_ref, own_ref, send_ref):
    own_ref[...] = keep_ref[0].astype(F32) + other_ref[0].astype(F32)
    send_ref[...] = (keep_ref[1].astype(F32) + other_ref[1].astype(F32)).astype(LOW)


def pair_sums(ix, keep, other, after=()):
    return rows_call(pair_kernel, "pair_sums", ix, [keep, other], [], [F32, LOW], after=after)


def add_kernel(ix, own_ref, other_ref, out_ref):
    out_ref[...] = (own_ref[...] + other_ref[...].astype(F32)).astype(LOW)


def middle_kernel(ix, own_ref, other_ref, tok_ref, gain_ref, middle_ref, second_ref):
    middle = tok_ref[...].astype(F32) + (own_ref[...] + other_ref[...].astype(F32))
    middle_ref[...] = middle
    normed, _ = normalize(middle)
    second_ref[...] = (normed * gain_ref[...]).astype(LOW)


def add_rows(out_ref, rows):
    part = jnp.sum(rows, axis=0, keepdims=True)

    @pl.when(pl.program_id(0) == 0)
    def _():
        out_ref[...] = part

    @pl.when(pl.program_id(0) != 0)
    def _():
        out_ref[...] += part


def middle_back_kernel(ix, own_ref, y_ref, z_ref, middle_ref, cot_ref, gain_ref, grad_ref, low_ref, sum_ref):
    second_sum = own_ref[...] + y_ref[...].astype(F32) + z_ref[...].astype(F32)
    normed, inverse = normalize(middle_ref[...])
    grad = cot_ref[...].astype(F32) + norm_back(second_sum, normed, inverse, gain_ref[...])
    grad_ref[...] = grad
    low_ref[...] = grad.astype(LOW)
    add_rows(sum_ref, second_sum * normed)


def output_kernel(ix, own_ref, y_ref, z_ref, middle_ref, out_ref):
    branch = own_ref[...] + y_ref[...].astype(F32) + z_ref[...].astype(F32)
    out_ref[...] = (middle_ref[...] + branch).astype(LOW)


def input_kernel(ix, own_ref, y_ref, grad_ref, tok_ref, gain_ref, out_ref, sum_ref):
    first_sum = own_ref[...] + y_ref[...].astype(F32)
    normed, inverse = normalize(tok_ref[...].astype(F32))
    out_ref[...] = (grad_ref[...] + norm_back(first_sum, normed, inverse, gain_ref[...])).astype(LOW)
    add_rows(sum_ref, first_sum * normed)


def normalize(vector):
    inverse = lax.rsqrt(jnp.mean(vector * vector, axis=-1, keepdims=True) + EPS)
    return (vector * inverse, inverse)


def norm_back(grad_rows, normed, inverse, gain):
    scaled = grad_rows * gain
    return inverse * (scaled - normed * jnp.mean(scaled * normed, axis=-1, keepdims=True))


def tie(ix, value, after):
    return pl.pallas_call(
        lambda *refs: None,
        grid_spec=pltpu.PrefetchScalarGridSpec(
            num_scalar_prefetch=1, grid=(1,), in_specs=[ANY] * (1 + len(after)), out_specs=ANY
        ),
        out_shape=shaped(value.shape, value.dtype),
        input_output_aliases={1: 0},
        cost_estimate=pl.CostEstimate(flops=0, bytes_accessed=0, transcendentals=0),
        name="tie",
    )(ix, value, *after)


def spread(quarter, hold=lambda two: two, late=lambda quarter: quarter):
    two = hold(swap(quarter, TENSOR, 2))
    one = swap(late(quarter), TENSOR, 1)
    three = swap(two, TENSOR, 1)
    return (quarter, one, two, three)


def quarter_copies(t, pieces, held):
    rows = pieces[0].shape[0]
    return [(ref, held.at[pl.ds((t ^ k) * rows, rows)]) for k, ref in enumerate(pieces)]


def join_kernel(ix, q0, q1, q2, q3, out_ref, held, sems):
    rows = q0.shape[0]
    ins, outs = [], []
    for k, ref in enumerate((q0, q1, q2, q3)):
        ins.append(pltpu.make_async_copy(ref, held.at[k], sems.at[k]))
        at = pl.ds((ix[T] ^ k) * rows, rows)
        outs.append(pltpu.make_async_copy(held.at[k], out_ref.at[at], sems.at[4 + k]))
    for copy in ins:
        copy.start()
    for one, two in zip(ins, outs):
        one.wait()
        two.start()
    for copy in outs:
        copy.wait()


def join(ix, pieces, after=()):
    rows, width = pieces[0].shape
    return call(
        join_kernel, "join", ix, (1,), list(pieces), [ANY] * 4,
        shaped((4 * rows, width)), ANY,
        [pltpu.VMEM((4, rows, width), LOW), pltpu.SemaphoreType.DMA((8,))], after=after,
    )


def mine_kernel(ix, a_ref, b_ref, a_out, b_out, sems):
    rows = a_out.shape[0]
    at = pl.ds(ix[T] * rows, rows)
    copy_all([(a_ref.at[at], a_out), (b_ref.at[at], b_out)], sems)


def mine(ix, arrays, after):
    count, width = arrays[0].shape
    return call(
        mine_kernel, "quarter", ix, (1,), list(arrays), [ANY] * 2, [shaped((count // 4, width))] * 2,
        [pl.BlockSpec((count // 4, width), lambda i, m: (0, 0))] * 2, [pltpu.SemaphoreType.DMA((2,))], after=after,
    )


def stack_kernel(ix, a, b, c, out_ref, sems):
    copy_all([(ref, out_ref.at[k]) for k, ref in enumerate((a, b, c))], sems)


def stack(ix, arrays, after):
    shape = (3,) + arrays[0].shape
    return call(
        stack_kernel, "stack", ix, (1,), list(arrays), [ANY] * 3, shaped(shape),
        pl.BlockSpec(shape, lambda i, m: (0, 0, 0)), [pltpu.SemaphoreType.DMA((3,))], after=after,
    )


def tables_kernel(ix, freq_ref, cos_ref, sin_ref):
    rows = cos_ref.shape[0]
    lane = lax.broadcasted_iota(jnp.int32, (1, 128), 1)
    place = pl.program_id(0) * rows + lax.broadcasted_iota(jnp.int32, (rows, 128), 0)
    angle = place.astype(F32) * freq_ref[0:1, :]
    cos_ref[...] = jnp.cos(angle)
    sin_ref[...] = jnp.where((lane % HEAD_DIM) < HEAD_DIM // 2, -1.0, 1.0) * jnp.sin(angle)


def all_rope_tables(ix, count, after):
    step = 768
    return call(
        tables_kernel, "rope_tables", ix, (count // step,), [rope_freq().reshape(1, 128)],
        [pl.BlockSpec((1, 128), lambda i, m: (0, 0))], [shaped((count, 128), F32)] * 2,
        [pl.BlockSpec((step, 128), lambda i, m: (i, 0))] * 2, after=after,
    )


def hidden_back_kernel(ix, cot_ref, w_ref, out_ref):
    out_ref[...] = against(cot_ref[...], w_ref[...])


def hidden_back(ix, cotangent, w_down, after=()):
    rows, width = cotangent.shape
    units = w_down.shape[0] // 2
    step = 256
    return call(
        hidden_back_kernel, "hidden_back", ix, (units // step,), [cotangent, w_down],
        [
            pl.BlockSpec((rows, width), lambda i, m: (0, 0)),
            pl.BlockSpec((step, width), lambda i, m: ((m[ME] % 2) * (units // step) + i, 0)),
        ],
        shaped((rows, units), F32), pl.BlockSpec((rows, step), lambda i, m: (0, i)), after=after,
    )


def feed_kernel(ix, q0, q1, q2, q3, wg_ref, wu_ref, hb_ref, rows_ref, hid_ref, gb_ref, ub_ref, held, sems):
    here = pl.program_id(0)

    @pl.when(here == 0)
    def _():
        copy_all(quarter_copies(ix[T], (q0, q1, q2, q3), held), sems)
        pltpu.make_async_copy(held, rows_ref, sems.at[4]).start()

    for part in range(3):
        at = slice(part * 256, (part + 1) * 256)
        second = held[at, :]
        gate = dot(second, wg_ref[...])
        up = dot(second, wu_ref[...])
        back = hb_ref[at, :]
        sig = 0.5 + 0.5 * jnp.tanh(0.5 * gate)
        swish = gate * sig
        hid_ref[at, :] = (swish * up).astype(LOW)
        gb_ref[at, :] = (back * up * (sig + swish * (1.0 - sig))).astype(LOW)
        ub_ref[at, :] = (back * swish).astype(LOW)

    @pl.when(here == pl.num_programs(0) - 1)
    def _():
        pltpu.make_async_copy(held, rows_ref, sems.at[4]).wait()


def feed(ix, pieces, w_gate, w_up, back, after=()):
    rows, width = pieces[0].shape
    rows = 4 * rows
    units = w_gate.shape[1] // 2
    step = 256
    weight = pl.BlockSpec((width, step), lambda i, m: (0, (m[ME] % 2) * (units // step) + i))
    block = pl.BlockSpec((rows, step), lambda i, m: (0, i))
    return call(
        feed_kernel, "feed", ix, (units // step,), [*pieces, w_gate, w_up, back],
        [ANY] * 4 + [weight] * 2 + [block],
        [shaped((rows, width))] + [shaped((rows, units))] * 3, [ANY, block, block, block],
        [pltpu.VMEM((rows, width), LOW), pltpu.SemaphoreType.DMA((5,))], after=after,
    )


def branch_back_kernel(ix, q0, q1, q2, q3, w0, w1, w2, w3, rows_ref, o0, o1, o2, o3, held, sems):
    copy_all(quarter_copies(ix[T], (q0, q1, q2, q3), held), sems)
    keep = pltpu.make_async_copy(held, rows_ref, sems.at[4])
    keep.start()
    weight = jnp.concatenate([w0[...], w1[...], w2[...], w3[...]], axis=0)
    for part in range(3):
        at = slice(part * 256, (part + 1) * 256)
        flat = against(held[at, :], weight).astype(LOW)
        for slot, out in enumerate((o0, o1, o2, o3)):
            out[at, :] = flat[:, slot * 128 : (slot + 1) * 128]
    keep.wait()


def branch_back(ix, pieces, w_out, after):
    rows, width = pieces[0].shape
    rows = 4 * rows

    def heads(slot):
        return pl.BlockSpec((128, width), lambda i, m: (m[ME] ^ slot, 0))

    return call(
        branch_back_kernel, "branch_back", ix, (1,), [*pieces] + [w_out] * 4,
        [ANY] * 4 + [heads(slot) for slot in range(4)],
        [shaped((rows, width))] + [shaped((rows, 128))] * 4,
        [ANY] + [pl.BlockSpec((rows, 128), lambda i, m: (0, 0))] * 4,
        [pltpu.VMEM((rows, width), LOW), pltpu.SemaphoreType.DMA((5,))], after=after,
    )


def wgrad_kernel(ix, l0, l1, r0, r1, out_ref):
    out_ref[0] = (across(l0[...], r0[...]) + across(l1[...], r1[...])).astype(LOW)


def wide_spec(rows, share, pair):
    return pl.BlockSpec((rows, share), lambda i, m: (0, (i % 4 // 2) * 4 + (m[ME] ^ (i % 2 + 2 * pair))))


def wgrad(ix, wide, free, after=()):
    rows, units = free[0].shape
    share = 256
    return call(
        wgrad_kernel, "wgrad", ix, (4,), [*wide, *free],
        [wide_spec(rows, share, 1)] * 2 + [pl.BlockSpec((rows, units), lambda i, m: (0, 0))] * 2,
        shaped((4, share, units)), pl.BlockSpec((1, share, units), lambda i, m: (i, 0, 0)), after=after,
    )


def wgrads_kernel(ix, c0, c1, s0, s1, h0, h1, g0, g1, u0, u1, out_ref):
    turn = pl.program_id(0) // 4
    for k, (l0, l1, r0, r1) in enumerate(((c0, c1, h0, h1), (s0, s1, g0, g1), (s0, s1, u0, u1))):

        @pl.when(turn == k)
        def _():
            out_ref[0, 0, 0] = (across(l0[...], r0[...]) + across(l1[...], r1[...])).astype(LOW)


def wgrads(ix, cots, seconds, frees, after=()):
    rows, units = frees[0][0].shape
    share = 256
    return call(
        wgrads_kernel, "wgrads", ix, (12,), [*cots, *seconds, *frees[0], *frees[1], *frees[2]],
        [wide_spec(rows, share, 0)] * 4 + [pl.BlockSpec((rows, units), lambda i, m: (0, 0))] * 6,
        shaped((2, 3, 2, share, units)),
        pl.BlockSpec((1, 1, 1, share, units), lambda i, m: (i % 4 // 2, i // 4, i % 2, 0, 0)), after=after,
    )


def add_pairs_kernel(ix, a_ref, b_ref, own_ref, other_ref):
    own_ref[...] = (a_ref[0].astype(F32) + b_ref[0].astype(F32)).astype(LOW)
    other_ref[...] = (a_ref[1].astype(F32) + b_ref[1].astype(F32)).astype(LOW)


def add_pairs(ix, one, which, two, after=()):
    share, units = two.shape[1:]
    step = units // 2
    return call(
        add_pairs_kernel, "add_pairs", ix, (2,), [one, two],
        [
            pl.BlockSpec((2, share, step), lambda i, m: (which, 0, i)),
            pl.BlockSpec((2, share, step), lambda i, m: (0, 0, i)),
        ],
        [shaped((share, units))] * 2, [pl.BlockSpec((share, step), lambda i, m: (0, i))] * 2, after=after,
    )


def halves_kernel(ix, own_ref, other_ref, out_ref, *, axis):
    which = ix[ME] % 2
    for place, ref in ((which, own_ref), (1 - which, other_ref)):
        value = ref[...].astype(F32)
        if axis == 0:
            value = value.T
        size = value.shape[axis]
        at = pl.ds(pl.multiple_of(place * size, size), size)
        if axis == 0:
            out_ref[at, :] = value
        else:
            out_ref[:, at] = value


def halves(ix, own, other, axis, after=()):
    share, units = own.shape
    shape = (2 * units, share) if axis == 0 else (share, 2 * units)
    whole = lambda i, m: (0, 0)
    return call(
        functools.partial(halves_kernel, axis=axis), "halves", ix, (1,), [own, other],
        [pl.BlockSpec((share, units), whole)] * 2, shaped(shape, F32), pl.BlockSpec(shape, whole),
        after=after,
    )


def out_wgrad_kernel(ix, a0, a1, a2, a3, rows_ref, out_ref):
    for slot, ref in enumerate((a0, a1, a2, a3)):
        at = pl.ds(pl.multiple_of((slot ^ ix[ME]) * 128, 128), 128)
        out_ref[0, at, :] = across(ref[...], rows_ref[...]).astype(LOW)


def out_wgrad(ix, mixed, rows, after=()):
    count, width = rows.shape
    share = 256
    return call(
        out_wgrad_kernel, "out_wgrad", ix, (width // share,), [*mixed, rows],
        [pl.BlockSpec((count, 128), lambda i, m: (0, 0))] * 4
        + [pl.BlockSpec((count, share), lambda i, m: (0, i))],
        shaped((8, 512, share)), pl.BlockSpec((1, 512, share), lambda i, m: (i, 0, 0)), after=after,
    )


def project_wgrad_kernel(ix, first_ref, f0, f1, f2, f3, b0, b1, b2, b3, out_ref, held, total, sems):
    me, t = ix[ME], ix[T]
    turn = pl.program_id(0)
    quarter = f0.shape[1]

    def copies(slot):
        if slot == 0:
            return [pltpu.make_async_copy(first_ref, held.at[0], sems.at[0, 0])]
        return [
            pltpu.make_async_copy(
                ref.at[slot - 1], held.at[slot, pl.ds((t ^ k) * quarter, quarter)], sems.at[slot, k]
            )
            for k, ref in enumerate((f0, f1, f2, f3))
        ]

    @pl.when(turn == 0)
    def _():
        for slot in range(4):
            for copy in copies(slot):
                copy.start()

    for slot, back in enumerate((b0, b1, b2, b3)):

        @pl.when(turn == slot)
        def _():
            for copy in copies(slot):
                copy.wait()
            for block in range(8):
                at = slice(block * 256, (block + 1) * 256)
                part = across(held[slot, :, at], back[...])
                if slot == 0:
                    total[at, :] = part
                elif slot < 3:
                    total[at, :] += part
                else:
                    out_ref[block // 4, (block % 4) ^ me] = (total[at, :] + part).astype(LOW)


def project_wgrad(ix, first_in, far, back, after=()):
    rows, width = first_in.shape
    whole = lambda i, m: (0, 0)
    return call(
        project_wgrad_kernel, "project_wgrad", ix, (4,), [first_in, *far, *back],
        [ANY] * 5 + [pl.BlockSpec((rows, 384), whole)] * 4,
        shaped((2, 4, 256, 384)), pl.BlockSpec((2, 4, 256, 384), lambda i, m: (0, 0, 0, 0)),
        [
            pltpu.VMEM((4, rows, width), LOW),
            pltpu.VMEM((width, 384), F32),
            pltpu.SemaphoreType.DMA((4, 4)),
        ],
        after=after,
    )


def project_last_kernel(ix, p0, p1, p2, p3, q_ref, k_ref, v_ref):
    for slot, ref in enumerate((p0, p1, p2, p3)):
        at = pl.ds(pl.multiple_of((slot ^ ix[ME]) * 128, 128), 128)
        for place, out in enumerate((q_ref, k_ref, v_ref)):
            out[:, at] = ref[:, place * 128 : (place + 1) * 128].astype(F32)


def project_last(ix, pieces):
    share = pieces[0].shape[0]
    whole = lambda i, m: (0, 0)
    return call(
        project_last_kernel, "project_last", ix, (1,), list(pieces),
        [pl.BlockSpec((share, 384), whole)] * 4,
        [shaped((share, 512), F32)] * 3, [pl.BlockSpec((share, 512), whole)] * 3,
    )


def over_ctx(slots):
    return [slots[0]] + [swap(slots[k], CTX, k) for k in range(1, 4)]


def per_device(
    dp_size, tokens, attn_gain, w_query, w_key, w_value, w_out, mlp_gain, w_gate, w_up, w_down, cotangent
):
    rows_here, width = tokens.shape
    share = width // (4 * dp_size)
    me, t, d = lax.axis_index(CTX), lax.axis_index(TENSOR), lax.axis_index("dp")
    two_dp = dp_size == 2
    ix = jnp.stack([me, t]).astype(jnp.int32)
    order = me ^ jnp.arange(4)
    projections = (w_query, w_key, w_value)
    attn_gain, mlp_gain = attn_gain.reshape(1, -1), mlp_gain.reshape(1, -1)

    tables = rope_tables(me * rows_here + jnp.arange(rows_here, dtype=jnp.int32))
    first_in, *slots = project(ix, tokens, attn_gain, tables, projections)
    pieces = over_ctx(slots)

    back_own = hidden_back(ix, cotangent, w_down, (slots[0],))
    all_tables = all_rope_tables(ix, 4 * rows_here, (back_own,))
    cot_mine, first_mine = mine(ix, [cotangent, first_in], (*pieces[1:], all_tables[0]))
    cot_z, first_two = swap(cot_mine, CTX, 1), swap(first_mine, CTX, 2)

    *mixed_slots, raw, lse = attend(ix, pieces, (first_mine,))
    mixed = over_ctx(mixed_slots)
    cot_z, first_two = tie(ix, cot_z, (raw,)), tie(ix, first_two, (raw,))
    cot_one, cot_two = swap(cot_z, TENSOR, 1), swap(cot_z, TENSOR, 2)
    keep, send = join_heads(ix, mixed, w_out, (cot_one, cot_two, first_two))
    own, low = pair_sums(ix, keep, swap(send, TENSOR, 1))
    cot_three = swap(tie(ix, cot_two, (keep,)), TENSOR, 1)
    first_mine = tie(ix, first_mine, (keep,))
    first_one, first_three = swap(first_mine, CTX, 1), swap(first_mine, CTX, 3)
    cot_far = join(ix, (cot_z, cot_one, cot_two, cot_three), (low,))
    back_far = hidden_back(ix, cot_far, w_down, (low,))
    middle, second_mine = rows_call(
        middle_kernel, "middle", ix, [own, swap(low, TENSOR, 2)], [tokens, mlp_gain], [F32, LOW],
        after=(back_far, first_one, first_three),
    )

    second_far = swap(second_mine, CTX, 1)
    second_own, hid_own, gb_own, ub_own = feed(ix, spread(second_mine), w_gate, w_up, back_own)
    keep, send = feed_quarters(ix, [gb_own, ub_own], [w_gate, w_up], True, "feed_back")
    second_far, hid_far, gb_far, ub_far = feed(
        ix, spread(second_far, lambda two: tie(ix, two, (hid_own,))), w_gate, w_up, back_far, (keep,)
    )
    own, low = pair_sums(ix, keep, swap(send, TENSOR, 1), (hid_far,))
    own_y = swap(low, TENSOR, 2)
    keep, send = feed_quarters(ix, [gb_far, ub_far], [w_gate, w_up], True, "feed_back", (low,))

    cots, seconds = (cotangent, cot_far), (second_own, second_far)
    frees = ((hid_own, hid_far), (gb_own, gb_far), (ub_own, ub_far))

    def over_dp(part):
        return lax.psum_scatter(part, "dp", scatter_dimension=0, tiled=True) if two_dp else part

    def over_pairs(part, after):
        return swap(tie(ix, part, after), CTX, 2) if two_dp else part

    far_own, far_low = pair_sums(ix, keep, swap(send, TENSOR, 1))
    part_down = wgrad(ix, cots, frees[0], (far_low,))
    part_gate = wgrad(ix, seconds, frees[1], (part_down,))
    part_up = wgrad(ix, seconds, frees[2], (part_gate,))
    sum_down = over_dp(part_down)
    (far_low,) = rows_call(
        add_kernel, "add_low", ix, [far_own, swap(far_low, TENSOR, 2)], [], [LOW], after=(part_up,)
    )
    far_z = swap(far_low, CTX, 1)
    own_pair = wgrads(ix, cots, seconds, frees, (far_low,))
    sum_gate = over_dp(part_gate)
    middle_grad, branch_mine, mlp_gain_part = rows_call(
        middle_back_kernel, "middle_back", ix, [own, own_y, far_z, middle],
        [cotangent, mlp_gain], [F32, LOW], 1, (own_pair,),
    )
    cross_down = over_pairs(sum_down, (branch_mine,))
    down_own = feed_quarters(ix, [hid_own], [w_down], False, "feed_down", (branch_mine,))
    down_far = feed_quarters(ix, [hid_far], [w_down], False, "feed_down", (down_own[0],))
    sum_up = over_dp(part_up)
    own_sum = over_dp(own_pair)
    branch_low, *slots = branch_back(
        ix, spread(branch_mine, lambda two: tie(ix, two, (down_far[0],))), w_out, (down_far[0],)
    )
    upstreams = over_ctx(slots)
    first_far = stack(ix, [first_one, first_two, first_three], (branch_low, cross_down))
    out_part = out_wgrad(ix, mixed, branch_low, (first_far,))
    down_own_far, down_far_far = (swap(tie(ix, send, (branch_low,)), TENSOR, 1) for _, send in (down_own, down_far))
    sums = []
    token = out_part
    if two_dp:
        own_sum = own_sum.reshape(6, 256, -1)
        sums.append(add_pairs(ix, own_sum, 0, cross_down, (token,)))
        token = sums[0][0]
    cross_gate = over_pairs(sum_gate, (token, *upstreams[1:]))

    back_slots = attend_back(
        ix, pieces, upstreams, raw, lse, all_tables, (token, down_own_far, down_far_far)
    )
    back = over_ctx(back_slots)

    own, low = pair_sums(ix, down_own[0], down_own_far, (back_slots[0], cross_gate))
    own_y = swap(low, TENSOR, 2)
    far_own, far_low = pair_sums(ix, down_far[0], down_far_far, (low,))
    far_y = swap(far_low, TENSOR, 2)
    token = far_low
    if two_dp:
        sums.append(add_pairs(ix, own_sum, 1, cross_gate, (token,)))
        token = sums[1][0]
        out_part = lax.psum_scatter(out_part, ("dp", *CTX), scatter_dimension=0, tiled=True)

    cross_up = over_pairs(sum_up, (token, *back[1:]))
    keep, send = project_back(ix, back, projections, (token, out_part))
    first_own, first_low = pair_sums(ix, keep, swap(send, TENSOR, 1))
    first_spread = spread(
        first_far, lambda two: tie(ix, two, (back_slots[0],)), lambda quarter: tie(ix, quarter, (back_slots[0],))
    )
    qkv_part = project_wgrad(ix, first_in, first_spread, back_slots, (first_low,))
    input_mine, attn_gain_part = rows_call(
        input_kernel, "input_back", ix, [first_own, swap(first_low, TENSOR, 2), middle_grad],
        [tokens, attn_gain], [LOW], 1, (qkv_part,),
    )
    (far_low,) = rows_call(add_kernel, "add_low", ix, [far_own, far_y], [], [LOW], after=(input_mine,))
    far_z = swap(far_low, CTX, 1)
    if two_dp:
        sums.append(add_pairs(ix, own_sum, 2, cross_up, (far_low,)))
    (output_mine,) = rows_call(output_kernel, "output", ix, [own, own_y, far_z, middle], [], [LOW], after=(input_mine,))
    input_grad = join(ix, spread(input_mine), (far_low,))
    output = join(ix, spread(output_mine), (input_grad,))

    if two_dp:
        out_grad = out_part[0].astype(F32)
        qkv_part = over_dp(qkv_part)[0]
    else:
        def scattered(blocks, axis):
            blocks = jnp.moveaxis(blocks, 0, axis)
            shape = blocks.shape[:axis] + (width,) + blocks.shape[axis + 2 :]
            part = lax.psum_scatter(blocks.reshape(shape), "dp", scatter_dimension=axis, tiled=True)
            shape = part.shape[:axis] + (4, share) + part.shape[axis + 1 :]
            return jnp.moveaxis(part.reshape(shape), axis, 0)

        def in_order(blocks):
            return blocks[:, order].reshape(8, *blocks.shape[2:])

        for k, far in enumerate((part_down, part_gate, part_up)):
            blocks = jnp.concatenate([own_pair[:, k], far.reshape(2, 2, 256, -1)], axis=1)
            part = scattered(in_order(blocks), 0)[order].astype(F32)
            part = (part[:2] + swap(part[2:].astype(LOW), CTX, 2).astype(F32)).astype(LOW)
            sums.append((part[0], part[1]))
        qkv_part = scattered(in_order(qkv_part), 0)[order]
        out_grad = scattered(out_part, 1).astype(F32)
        out_grad = lax.psum_scatter(out_grad, CTX, scatter_dimension=0, tiled=True)[0]

    down_grad, gate_grad, up_grad = (
        halves(ix, own, swap(other, CTX, 1), axis) for (own, other), axis in zip(sums, (0, 1, 1))
    )
    qkv = project_last(ix, over_ctx(qkv_part))

    gains = jnp.concatenate([attn_gain_part, mlp_gain_part])
    gains = gains + swap(gains, TENSOR, 1)
    gains = gains + swap(gains, TENSOR, 2)
    if two_dp:
        halved = gains.reshape(2, 2, width // 2)[:, d ^ jnp.arange(2)]
        gains = halved[:, 0] + swap(halved[:, 1], "dp", 1)
    else:
        gains = lax.psum_scatter(gains, "dp", scatter_dimension=1, tiled=True)
    gains = gains.reshape(2, 4, share).transpose(1, 0, 2)[order]
    gains = sum(over_ctx(gains))

    return (
        output,
        input_grad,
        gains[0],
        qkv[0],
        qkv[1],
        qkv[2],
        out_grad,
        gains[1],
        gate_grad,
        up_grad,
        down_grad,
    )


def solution(mesh):
    dp_size = mesh.shape["dp"]
    mesh = jax.sharding.Mesh(mesh.devices.reshape(dp_size, 2, 2, 2, 2), ("dp", *CTX, *TENSOR))
    rows, tensor = ("dp", *CTX), TENSOR
    columns = P(None, tensor)
    in_specs = (
        P(rows, None), P(), columns, columns, columns, P(tensor, None),
        P(), columns, columns, P(tensor, None), P(rows, None),
    )
    out_specs = (
        P(rows, None), P(rows, None), P(rows), P(rows, tensor), P(rows, tensor), P(rows, tensor),
        P(tensor, rows), P(rows), P(rows, tensor), P(rows, tensor), P(tensor, rows),
    )
    return jax.shard_map(
        functools.partial(per_device, dp_size),
        mesh=mesh,
        in_specs=in_specs,
        out_specs=out_specs,
        check_vma=False,
    )
```

time: 1750 us -> 775 us (0.44)
  waiting for transfers between devices: 1090 us -> 244 us
  matrix products: 410 us -> 0 us
  Pallas kernels: 0 us -> 384 us
  other arithmetic: 174 us -> 5.82 us
  starting transfers between devices: 1.51 us -> 88.9 us
  blocking collectives: 22.2 us -> 0 us
    reduce_scatter x9 -> x6, waiting for transfers between devices: 720 us -> 6.79 us  [the longest x1 6.65 us: per_device(): lax.psum_scatter(out_part, ('dp', *CTX), scatter_dimension=0, tiled=True)]
    dot_general x77 -> x0, matrix products: 410 us -> none  [the longest x31 166 us: against(): lax.dot_general(left, right, (((1,), (1,)), ((), ())), preferred_element_...]
    pallas_call x0 -> x58, Pallas kernels: none -> 384 us  [the longest x45 375 us: call(): pl.pallas_call(body, grid_spec=pltpu.PrefetchScalarGridSpec(num_scalar_pr...]
    psum x3 -> x0, waiting for transfers between devices: 255 us -> none  [the longest x1 120 us: per_device(): lax.psum(jnp.dot(hidden, w_down, preferred_element_type=jnp.float32).asty...]
    ppermute x0 -> x67, waiting for transfers between devices: none -> 236 us  [swap(): return lax.ppermute(value, axis, [(i, i ^ distance) for i in range(size)])]
    convert_element_type x20 -> x2, other arithmetic: 119 us -> 1.78 us  [the longest x1 1.78 us: per_device(): out_grad = out_part[0].astype(F32)]
    all_gather x2 -> x0, waiting for transfers between devices: 116 us -> none  [the longest x1 57.8 us: per_device(): lax.all_gather(key_rot.reshape(rows_here, local_width), 'ctx', axis=0, ti...]
    ppermute x0 -> x67, starting transfers between devices: none -> 88.6 us  [swap(): return lax.ppermute(value, axis, [(i, i ^ distance) for i in range(size)])]
  transfers between devices with their start and end apart: 14 -> 73, of which waited for: 14 -> 31; matrix products, arithmetic and copies ran while one was open for 8% -> 1% of each run, Pallas kernels for 0% -> 43%
where the time goes in v2:
time: 775 us; the launch traced here: 764 us
  Pallas kernels  384 us (50%)
  waiting for transfers between devices  244 us (31%)
  starting transfers between devices  88.9 us (11%)
  local copies, waits for them, and re-layouts  25.9 us (3%)
  between operations  15.2 us (2%)
    pallas_call x45, Pallas kernels, call(): pl.pallas_call(body, grid_spec=pltpu.PrefetchScalarGridSpec(num_scalar_pr...  375 us
    ppermute x67, waiting for transfers between devices, swap(): return lax.ppermute(value, axis, [(i, i ^ distance) for i in range(size)])  236 us
    ppermute x67, starting transfers between devices, swap(): return lax.ppermute(value, axis, [(i, i ^ distance) for i in range(size)])  88.6 us
    unnamed x94, local copies, waits for them, and re-layouts  22.1 us
  transfers between devices with their start and end apart: 73, of which 31 were waited for; matrix products, arithmetic and copies ran while one was open for 1% of the time, Pallas kernels for 43%

profile of v2, /device:TPU:0, one launch (start us, length us, event | category | flops | bytes accessed | tf_op | source)
XLA Modules:
  0.0 763.6 jit_solution(13160190526487393072)
XLA Ops:
  10.5 11.2 %project.1 = (bf16[768,2048]{1,0:T(8,128)(2,1)}, bf16[768,384]{1,0:T(8,128)(2,1)}, bf16[768,384]{1,0:T(8,128)(2,1)}, bf16[768,384]{1,0:T(8,128)(2,1)}, bf16[768,384]{1,0:T(8,128)(2,1)}) custom-call(s32[2]{0:T(128)} %pad_add_fusion.index_ref.refs_0_, bf16[768,2048]{1,0:T(8,128)(2,1)} %refs_3_.5, f32[1,2048]{1,0:T(1,128)} %bitcast.57, ...), custom_call_target="tpu_custom_call" | custom-call | tf_op jit(solution)/shard_map/project/pallas_call | solution.py:55
  27.4 8.4 %hidden_back.2.refs_1_.refs_6_ = f32[768,1024]{1,0:T(8,128)} custom-call(s32[2]{0:T(128)} %pad_add_fusion.index_ref.refs_0_, bf16[768,2048]{1,0:T(8,128)(2,1)} %refs_4_.11, bf16[2048,2048]{1,0:T(8,128)(2,1)} %refs_1_.7, bf16[768,384]{1,0:T(8,128)(2,1)} %get-tuple-element.83.refs_2_.refs_0_), custom_call_target="tpu_custom_call" | custom-call | bytes 14680064 | tf_op jit(solution)/shard_map/hidden_back/pallas_call | solution.py:55
  35.8 8.0 %rope_tables.1 = (f32[3072,128]{1,0:T(8,128)}, f32[3072,128]{1,0:T(8,128)}) custom-call(s32[2]{0:T(128)} %pad_add_fusion.index_ref.refs_0_, f32[1,128]{1,0:T(1,128)} %bitcast.59, f32[768,1024]{1,0:T(8,128)} %hidden_back.2.refs_1_.refs_6_), custom_call_target="tpu_custom_call" | custom-call | bytes 11010048 | tf_op jit(solution)/shard_map/rope_tables/pallas_call | solution.py:55
  43.8 6.4 collective-permute-done.refs_2_.refs_1_
  50.2 17.2 %collective-permute-done.1.refs_3_.refs_2_ = bf16[768,384]{1,0:T(8,128)(2,1)S(1)} collective-permute-done((bf16[768,384]{1,0:T(8,128)(2,1)}, bf16[768,384]{1,0:T(8,128)(2,1)S(1)}, u32[]{:S(2)}, u32[]{:S(2)}) %collective-permute-start.1) | collective-permute-done | bytes 589856 | tf_op jit(solution)/shard_map/ppermute | solution.py:30
  68.5 3.2 quarter.1
  71.7 11.6 %collective-permute-start.6 = (bf16[192,2048]{1,0:T(8,128)(2,1)}, bf16[192,2048]{1,0:T(8,128)(2,1)S(1)}, u32[]{:S(2)}, u32[]{:S(2)}) collective-permute-start(bf16[192,2048]{1,0:T(8,128)(2,1)} %get-tuple-element.94), channel_id=1, source_target_pairs={{0,4},{4,0},{8,12},{12,8},{1,5},{5,1},{9,13},{13,9},{2,6},{6,2},{1... | collective-permute-start | bytes 2359304 | tf_op jit(solution)/shard_map/ppermute | solution.py:30
  84.4 39.1 %attend.1 = (bf16[768,128]{1,0:T(8,128)(2,1)}, bf16[768,128]{1,0:T(8,128)(2,1)}, bf16[768,128]{1,0:T(8,128)(2,1)}, bf16[768,128]{1,0:T(8,128)(2,1)}, f32[3072,128]{1,0:T(8,128)}, /*index=5*/f32[8,16,384]{2,1,0:T(8,128)}) custom-call(s32[2]{0:T(128)} %pad_add_fusion.index_ref.refs_0_, bf16[768,384]{1,0:T(8,128)(2,1)} %get-tuple-element.83.refs_2_.refs_0_, ...), custom_call_target="tpu_custom_call" | custom-call | bytes 73400320 | tf_op jit(solution)/shard_map/attend/pallas_call | solution.py:55
  131.9 5.3 collective-permute-done.3.refs_1_
  137.3 8.6 %collective-permute-done.4.refs_2_ = bf16[768,128]{1,0:T(8,128)(2,1)S(1)} collective-permute-done((bf16[768,128]{1,0:T(8,128)(2,1)S(1)}, bf16[768,128]{1,0:T(8,128)(2,1)S(1)}, u32[]{:S(2)}, u32[]{:S(2)}) %collective-permute-start.4) | collective-permute-done | bytes 196640 | tf_op jit(solution)/shard_map/ppermute | solution.py:30
  147.5 6.6 join_heads.1
  161.8 3.6 pair_sums.6
  165.9 3.6 join.3.refs_0_.refs_1_
  169.5 8.5 %hidden_back.3.refs_4_.refs_6_ = f32[768,1024]{1,0:T(8,128)} custom-call(s32[2]{0:T(128)} %pad_add_fusion.index_ref.refs_0_, bf16[768,2048]{1,0:T(8,128)(2,1)} %join.3.refs_0_.refs_1_, bf16[2048,2048]{1,0:T(8,128)(2,1)} %refs_1_.7, bf16[192,2048]{1,0:T(8,128)(2,1)} %get-tuple-element.99.refs_4_.refs_2_), custom_call_target="tpu_custom_call" | custom-call | bytes 14680064 | tf_op jit(solution)/shard_map/hidden_back/pallas_call | solution.py:55
  179.8 15.9 %collective-permute-done.13.refs_5_.refs_0_ = bf16[192,2048]{1,0:T(8,128)(2,1)S(1)} collective-permute-done((bf16[192,2048]{1,0:T(8,128)(2,1)}, bf16[192,2048]{1,0:T(8,128)(2,1)S(1)}, u32[]{:S(2)}, u32[]{:S(2)}) %collective-permute-start.13) | collective-permute-done | bytes 786464 | tf_op jit(solution)/shard_map/ppermute | solution.py:30
  196.6 3.7 middle.1
  201.7 18.3 %collective-permute-done.16.refs_2_ = bf16[192,2048]{1,0:T(8,128)(2,1)S(1)} collective-permute-done((bf16[192,2048]{1,0:T(8,128)(2,1)}, bf16[192,2048]{1,0:T(8,128)(2,1)S(1)}, u32[]{:S(2)}, u32[]{:S(2)}) %collective-permute-start.16) | collective-permute-done | bytes 786464 | tf_op jit(solution)/shard_map/ppermute | solution.py:30
  222.4 14.2 %feed.2 = (bf16[768,2048]{1,0:T(8,128)(2,1)}, bf16[768,1024]{1,0:T(8,128)(2,1)}, bf16[768,1024]{1,0:T(8,128)(2,1)}, bf16[768,1024]{1,0:T(8,128)(2,1)}) custom-call(s32[2]{0:T(128)} %pad_add_fusion.index_ref.refs_0_, bf16[192,2048]{1,0:T(8,128)(2,1)} %get-tuple-element.100.refs_0_, bf16[192,2048]{1,0:T(8,128)(2,1)} %collective-permute-done.15.refs_1_, ...), custom_call_target="tpu_custom_call" | custom-call | bytes 22020096 | tf_op jit(solution)/shard_map/feed/pallas_call | solution.py:55
  236.6 13.4 %feed_back.2 = (bf16[2,192,2048]{2,1,0:T(8,128)(2,1)}, bf16[2,192,2048]{2,1,0:T(8,128)(2,1)}) custom-call(s32[2]{0:T(128)} %pad_add_fusion.index_ref.refs_0_, bf16[768,1024]{1,0:T(8,128)(2,1)} %get-tuple-element.102.refs_0_.refs_2_.refs_6_, bf16[768,1024]{1,0:T(8,128)(2,1)} %get-tuple-element.103.refs_1_.refs_2_.refs_8_, bf16[2048,2048]{1,0:T(8,128)(2,1)} %refs_2_.5, ...), custom_call_target="tpu_custom_call" | custom-call | bytes 22020096 | tf_op jit(solution)/shard_map/feed_back/pallas_call | solution.py:55
  256.8 14.0 %feed.3 = (bf16[768,2048]{1,0:T(8,128)(2,1)}, bf16[768,1024]{1,0:T(8,128)(2,1)}, bf16[768,1024]{1,0:T(8,128)(2,1)}, bf16[768,1024]{1,0:T(8,128)(2,1)}) custom-call(s32[2]{0:T(128)} %pad_add_fusion.index_ref.refs_0_, bf16[192,2048]{1,0:T(8,128)(2,1)} %collective-permute-done.19.refs_0_, bf16[192,2048]{1,0:T(8,128)(2,1)} %copy-done.29, ...), custom_call_target="tpu_custom_call" | custom-call | bytes 22020096 | tf_op jit(solution)/shard_map/feed/pallas_call | solution.py:55
  270.8 3.7 pair_sums.7
  274.4 13.4 %feed_back.3 = (bf16[2,192,2048]{2,1,0:T(8,128)(2,1)}, bf16[2,192,2048]{2,1,0:T(8,128)(2,1)}) custom-call(s32[2]{0:T(128)} %pad_add_fusion.index_ref.refs_0_, bf16[768,1024]{1,0:T(8,128)(2,1)} %get-tuple-element.109.refs_0_.refs_3_.refs_7_, bf16[768,1024]{1,0:T(8,128)(2,1)} %get-tuple-element.110.refs_1_.refs_3_.refs_9_, bf16[2048,2048]{1,0:T(8,128)(2,1)} %refs_2_.5, ...), custom_call_target="tpu_custom_call" | custom-call | bytes 22020096 | tf_op jit(solution)/shard_map/feed_back/pallas_call | solution.py:55
  288.0 3.5 collective-permute-done.24.refs_1_
  292.6 3.6 pair_sums.8
  296.2 8.1 %wgrad.3.refs_4_ = bf16[4,256,1024]{2,1,0:T(8,128)(2,1)} custom-call(s32[2]{0:T(128)} %pad_add_fusion.index_ref.refs_0_, bf16[768,2048]{1,0:T(8,128)(2,1)} %refs_4_.11, bf16[768,2048]{1,0:T(8,128)(2,1)} %join.3.refs_0_.refs_1_, bf16[768,1024]{1,0:T(8,128)(2,1)} %get-tuple-element.101.refs_2_.refs_4_.refs_0_, ...), custom_call_target="tpu_custom_call" | custom-call | bytes 14680064 | tf_op jit(solution)/shard_map/wgrad/pallas_call | solution.py:55
  306.0 8.5 %wgrad.4.refs_4_ = bf16[4,256,1024]{2,1,0:T(8,128)(2,1)} custom-call(s32[2]{0:T(128)} %pad_add_fusion.index_ref.refs_0_, bf16[768,2048]{1,0:T(8,128)(2,1)} %get-tuple-element.115.refs_0_.refs_2_, bf16[768,2048]{1,0:T(8,128)(2,1)} %get-tuple-element.116.refs_1_.refs_3_, bf16[768,1024]{1,0:T(8,128)(2,1)} %get-tuple-element.102.refs_0_.refs_2_.refs_6_, ...), custom_call_target="tpu_custom_call" | custom-call | bytes 14680064 | tf_op jit(solution)/shard_map/wgrad/pallas_call | solution.py:55
  314.5 8.1 %wgrad.5.refs_2_ = bf16[4,256,1024]{2,1,0:T(8,128)(2,1)} custom-call(s32[2]{0:T(128)} %pad_add_fusion.index_ref.refs_0_, bf16[768,2048]{1,0:T(8,128)(2,1)} %get-tuple-element.115.refs_0_.refs_2_, bf16[768,2048]{1,0:T(8,128)(2,1)} %get-tuple-element.116.refs_1_.refs_3_, bf16[768,1024]{1,0:T(8,128)(2,1)} %get-tuple-element.103.refs_1_.refs_2_.refs_8_, ...), custom_call_target="tpu_custom_call" | custom-call | bytes 14680064 | tf_op jit(solution)/shard_map/wgrad/pallas_call | solution.py:55
  329.0 21.3 %wgrads.1.refs_6_ = bf16[2,3,2,256,1024]{4,3,2,1,0:T(8,128)(2,1)} custom-call(s32[2]{0:T(128)} %pad_add_fusion.index_ref.refs_0_, bf16[768,2048]{1,0:T(8,128)(2,1)} %refs_4_.11, bf16[768,2048]{1,0:T(8,128)(2,1)} %join.3.refs_0_.refs_1_, bf16[768,2048]{1,0:T(8,128)(2,1)} %get-tuple-element.115.refs_0_.refs_2_, ...), custom_call_target="tpu_custom_call" | custom-call | bytes 36700160 | tf_op jit(solution)/shard_map/wgrads/pallas_call | solution.py:55
  353.0 17.4 %collective-permute-done.23.refs_1_ = bf16[192,2048]{1,0:T(8,128)(2,1)S(1)} collective-permute-done((bf16[192,2048]{1,0:T(8,128)(2,1)S(1)}, bf16[192,2048]{1,0:T(8,128)(2,1)S(1)}, u32[]{:S(2)}, u32[]{:S(2)}) %collective-permute-start.23) | collective-permute-done | bytes 786464 | tf_op jit(solution)/shard_map/ppermute | solution.py:30
  371.5 5.3 middle_back.1
  379.9 10.2 %feed_down.2 = (bf16[2,192,2048]{2,1,0:T(8,128)(2,1)}, bf16[2,192,2048]{2,1,0:T(8,128)(2,1)}) custom-call(s32[2]{0:T(128)} %pad_add_fusion.index_ref.refs_0_, bf16[768,1024]{1,0:T(8,128)(2,1)} %get-tuple-element.101.refs_2_.refs_4_.refs_0_, bf16[2048,2048]{1,0:T(8,128)(2,1)} %refs_1_.7, bf16[192,2048]{1,0:T(8,128)(2,1)} %get-tuple-element.118.refs_2_.refs_0_), custom_call_target="tpu_custom_call" | custom-call | bytes 18350080 | tf_op jit(solution)/shard_map/feed_down/pallas_call | solution.py:55
  390.1 10.3 %feed_down.3 = (bf16[2,192,2048]{2,1,0:T(8,128)(2,1)}, bf16[2,192,2048]{2,1,0:T(8,128)(2,1)}) custom-call(s32[2]{0:T(128)} %pad_add_fusion.index_ref.refs_0_, bf16[768,1024]{1,0:T(8,128)(2,1)} %get-tuple-element.106.refs_2_.refs_3_.refs_5_.refs_0_, bf16[2048,2048]{1,0:T(8,128)(2,1)} %refs_1_.7, bf16[2,192,2048]{2,1,0:T(8,128)(2,1)} %get-tuple-element.119.refs_2_.refs_0_), custom_call_target="tpu_custom_call" | custom-call | bytes 18350080 | tf_op jit(solution)/shard_map/feed_down/pallas_call | solution.py:55
  403.8 6.8 branch_back.1
  410.6 15.1 %collective-permute-done.34.refs_4_.refs_1_ = bf16[2,256,1024]{2,1,0:T(8,128)(2,1)S(1)} collective-permute-done((bf16[2,256,1024]{2,1,0:T(8,128)(2,1)}, bf16[2,256,1024]{2,1,0:T(8,128)(2,1)S(1)}, u32[]{:S(2)}, u32[]{:S(2)}) %collective-permute-start.34) | collective-permute-done | bytes 1048608 | tf_op jit(solution)/shard_map/ppermute | solution.py:30
  426.7 3.8 stack.13.refs_5_.refs_1_
  430.5 8.4 %out_wgrad.1.refs_2_ = bf16[8,512,256]{2,1,0:T(8,128)(2,1)} custom-call(s32[2]{0:T(128)} %pad_add_fusion.index_ref.refs_0_, bf16[768,128]{1,0:T(8,128)(2,1)} %get-tuple-element.90.refs_0_, bf16[768,128]{1,0:T(8,128)(2,1)} %copy-done.33, bf16[768,128]{1,0:T(8,128)(2,1)} %copy-done.34, bf16[768,128]{1,0:T(8,128)(2,1)} %copy-done.35, ...), custom_call_target="tpu_custom_call" | custom-call | bytes 14680064 | tf_op jit(solution)/shard_map/out_wgrad/pallas_call | solution.py:55
  444.1 7.7 %collective-permute-done.31.refs_5_.refs_3_ = bf16[768,128]{1,0:T(8,128)(2,1)S(1)} collective-permute-done((bf16[768,128]{1,0:T(8,128)(2,1)S(1)}, bf16[768,128]{1,0:T(8,128)(2,1)S(1)}, u32[]{:S(2)}, u32[]{:S(2)}) %collective-permute-start.31) | collective-permute-done | bytes 196640 | tf_op jit(solution)/shard_map/ppermute | solution.py:30
  461.0 3.2 collective-permute-start.36
  465.3 45.6 %attend_back.1 = (bf16[768,384]{1,0:T(8,128)(2,1)}, bf16[768,384]{1,0:T(8,128)(2,1)}, bf16[768,384]{1,0:T(8,128)(2,1)}, bf16[768,384]{1,0:T(8,128)(2,1)}) custom-call(s32[2]{0:T(128)} %pad_add_fusion.index_ref.refs_0_, bf16[768,384]{1,0:T(8,128)(2,1)} %get-tuple-element.83.refs_2_.refs_0_, bf16[768,384]{1,0:T(8,128)(2,1)} %copy-done.5, ...), custom_call_target="tpu_custom_call" | custom-call | bytes 80740352 | tf_op jit(solution)/shard_map/attend_back/pallas_call | solution.py:55
  515.4 3.4 copy.51.refs_1_
  520.2 35.4 %collective-permute-done.36.refs_3_.refs_1_ = bf16[2,256,1024]{2,1,0:T(8,128)(2,1)} collective-permute-done((bf16[2,256,1024]{2,1,0:T(8,128)(2,1)}, bf16[2,256,1024]{2,1,0:T(8,128)(2,1)}, u32[]{:S(2)}, u32[]{:S(2)}) %collective-permute-start.36) | collective-permute-done | bytes 1048608 | tf_op jit(solution)/shard_map/ppermute | solution.py:30
  555.6 3.7 pair_sums.9
  559.3 3.7 pair_sums.10
  566.0 6.6 reduce-scatter.13.cloned.1.call-done.refs_17_
  575.2 12.3 %project_back.1 = (bf16[2,192,2048]{2,1,0:T(8,128)(2,1)}, bf16[2,192,2048]{2,1,0:T(8,128)(2,1)}) custom-call(s32[2]{0:T(128)} %pad_add_fusion.index_ref.refs_0_, bf16[768,384]{1,0:T(8,128)(2,1)} %get-tuple-element.131.refs_2_.refs_0_.refs_5_, bf16[768,384]{1,0:T(8,128)(2,1)} %copy-done.15, bf16[768,384]{1,0:T(8,128)(2,1)} %copy-done.16, ...), custom_call_target="tpu_custom_call" | custom-call | bytes 18350080 | tf_op jit(solution)/shard_map/project_back/pallas_call | solution.py:55
  587.6 3.6 collective-permute-done.42.refs_1_
  592.3 3.7 pair_sums.11
  598.0 13.2 %project_wgrad.1.refs_5_ = bf16[2,4,256,384]{3,2,1,0:T(8,128)(2,1)} custom-call(s32[2]{0:T(128)} %pad_add_fusion.index_ref.refs_0_, bf16[768,2048]{1,0:T(8,128)(2,1)} %get-tuple-element.87.refs_1_.refs_0_, bf16[3,192,2048]{2,1,0:T(8,128)(2,1)} %stack.13.refs_5_.refs_1_, bf16[3,192,2048]{2,1,0:T(8,128)(2,1)} %collective-permute-done.44.refs_2_, ...), custom_call_target="tpu_custom_call" | custom-call | tf_op jit(solution)/shard_map/project_wgrad/pallas_call | solution.py:55
  611.3 5.3 collective-permute-done.43.refs_1_
  617.5 4.5 input_back.1
  624.3 9.1 %collective-permute-done.38.refs_1_ = bf16[192,2048]{1,0:T(8,128)(2,1)S(1)} collective-permute-done((bf16[192,2048]{1,0:T(8,128)(2,1)}, bf16[192,2048]{1,0:T(8,128)(2,1)S(1)}, u32[]{:S(2)}, u32[]{:S(2)}) %collective-permute-start.38) | collective-permute-done | bytes 786464 | tf_op jit(solution)/shard_map/ppermute | solution.py:30
  634.3 3.2 add_low.3.refs_4_.refs_2_
  637.6 11.8 %collective-permute-start.47 = (bf16[192,2048]{1,0:T(8,128)(2,1)}, bf16[192,2048]{1,0:T(8,128)(2,1)}, u32[]{:S(2)}, u32[]{:S(2)}) collective-permute-start(bf16[192,2048]{1,0:T(8,128)(2,1)} %add_low.3.refs_4_.refs_2_), channel_id=1, source_target_pairs={{0,4},{4,0},{8,12},{12,8},{1,5},{5,1},{9,13},{13,9},{2,6},{6,2},{1... | collective-permute-start | bytes 2359304 | tf_op jit(solution)/shard_map/ppermute | solution.py:30
  651.7 3.7 collective-permute-start.64
  656.5 34.1 %collective-permute-done.47.refs_2_ = bf16[192,2048]{1,0:T(8,128)(2,1)} collective-permute-done((bf16[192,2048]{1,0:T(8,128)(2,1)}, bf16[192,2048]{1,0:T(8,128)(2,1)}, u32[]{:S(2)}, u32[]{:S(2)}) %collective-permute-start.47) | collective-permute-done | bytes 786464 | tf_op jit(solution)/shard_map/ppermute | solution.py:30
  690.6 3.9 output.1.refs_0_
  702.4 8.4 %collective-permute-done.63.refs_1_ = bf16[256,1024]{1,0:T(8,128)(2,1)S(1)} collective-permute-done((bf16[256,1024]{1,0:T(8,128)(2,1)}, bf16[256,1024]{1,0:T(8,128)(2,1)S(1)}, u32[]{:S(2)}, u32[]{:S(2)}) %collective-permute-start.63) | collective-permute-done | bytes 524320 | tf_op jit(solution)/shard_map/ppermute | solution.py:30
  723.7 3.5 halves.5
  727.2 3.3 halves.3
  737.6 3.3 halves.4
  740.9 3.5 join.4.refs_4_
  745.3 3.5 join.5
  748.9 4.2 collective-permute-done.61.refs_2_
  753.1 3.2 project_last.1
  (261 shorter events, 129.4 us)
Async XLA Ops:
  7.2 371.2 %reduce-scatter.9.cloned.1.call-start = ((), (), s32[]{:S(2)}) async-start(), calls=%async_computation.7 | async-start | bytes 3145728 | tf_op jit(solution)/shard_map/reduce_scatter | solution.py:941
  21.7 28.5 %collective-permute-start = (bf16[768,384]{1,0:T(8,128)(2,1)}, bf16[768,384]{1,0:T(8,128)(2,1)S(1)}, u32[]{:S(2)}, u32[]{:S(2)}) collective-permute-start(bf16[768,384]{1,0:T(8,128)(2,1)} %get-tuple-element.84), channel_id=1, source_target_pairs={{0,4},{4,0},{8,12},{12,8},{1,5},{5,1},{9,13},{13,9},{2,6},{6,2},{1... | collective-permute-start | bytes 1769480 | tf_op jit(solution)/shard_map/ppermute | solution.py:30
  24.8 42.6 %collective-permute-start.1 = (bf16[768,384]{1,0:T(8,128)(2,1)}, bf16[768,384]{1,0:T(8,128)(2,1)S(1)}, u32[]{:S(2)}, u32[]{:S(2)}) collective-permute-start(bf16[768,384]{1,0:T(8,128)(2,1)} %get-tuple-element.85), channel_id=1, source_target_pairs={{0,8},{4,12},{8,0},{12,4},{1,9},{5,13},{9,1},{13,5},{2,10},{6,14},... | collective-permute-start | bytes 1769480 | tf_op jit(solution)/shard_map/ppermute | solution.py:30
  27.4 40.1 %collective-permute-start.2 = (bf16[768,384]{1,0:T(8,128)(2,1)}, bf16[768,384]{1,0:T(8,128)(2,1)S(1)}, u32[]{:S(2)}, u32[]{:S(2)}) collective-permute-start(bf16[768,384]{1,0:T(8,128)(2,1)} %get-tuple-element.86), channel_id=1, source_target_pairs={{0,12},{4,8},{8,4},{12,0},{1,13},{5,9},{9,5},{13,1},{2,14},{6,10},... | collective-permute-start | bytes 1769480 | tf_op jit(solution)/shard_map/ppermute | solution.py:30
  71.7 51.8 %collective-permute-start.6 = (bf16[192,2048]{1,0:T(8,128)(2,1)}, bf16[192,2048]{1,0:T(8,128)(2,1)S(1)}, u32[]{:S(2)}, u32[]{:S(2)}) collective-permute-start(bf16[192,2048]{1,0:T(8,128)(2,1)} %get-tuple-element.94), channel_id=1, source_target_pairs={{0,4},{4,0},{8,12},{12,8},{1,5},{5,1},{9,13},{13,9},{2,6},{6,2},{1... | collective-permute-start | bytes 2359304 | tf_op jit(solution)/shard_map/ppermute | solution.py:30
  83.3 45.4 %collective-permute-start.9 = (bf16[192,2048]{1,0:T(8,128)(2,1)}, bf16[192,2048]{1,0:T(8,128)(2,1)S(1)}, u32[]{:S(2)}, u32[]{:S(2)}) collective-permute-start(bf16[192,2048]{1,0:T(8,128)(2,1)} %get-tuple-element.89.refs_4_.refs_1_), channel_id=1, source_target_pairs={{0,8},{4,12},{8,0},{12,4},{1,9},{5,13},{9,1},{13,5},{2,10},{6,14},... | collective-permute-start | bytes 2359304 | tf_op jit(solution)/shard_map/ppermute | solution.py:30
  125.2 20.7 %collective-permute-start.8 = (bf16[192,2048]{1,0:T(8,128)(2,1)}, bf16[192,2048]{1,0:T(8,128)(2,1)S(1)}, u32[]{:S(2)}, u32[]{:S(2)}) collective-permute-start(bf16[192,2048]{1,0:T(8,128)(2,1)} %tie.13.refs_0_), channel_id=1, source_target_pairs={{0,2},{1,3},{2,0},{3,1},{4,6},{5,7},{6,4},{7,5},{8,10},{9,11},{10,... | collective-permute-start | bytes 2359304 | tf_op jit(solution)/shard_map/ppermute | solution.py:30
  126.8 19.8 %collective-permute-start.7 = (bf16[192,2048]{1,0:T(8,128)(2,1)}, bf16[192,2048]{1,0:T(8,128)(2,1)}, u32[]{:S(2)}, u32[]{:S(2)}) collective-permute-start(bf16[192,2048]{1,0:T(8,128)(2,1)} %tie.13.refs_0_), channel_id=1, source_target_pairs={{0,1},{1,0},{2,3},{3,2},{4,5},{5,4},{6,7},{7,6},{8,9},{9,8},{10,11... | collective-permute-start | bytes 2359304 | tf_op jit(solution)/shard_map/ppermute | solution.py:30
  126.8 10.5 %collective-permute-start.3 = (bf16[768,128]{1,0:T(8,128)(2,1)S(1)}, bf16[768,128]{1,0:T(8,128)(2,1)S(1)}, u32[]{:S(2)}, u32[]{:S(2)}) collective-permute-start(bf16[768,128]{1,0:T(8,128)(2,1)S(1)} %copy-done.45), channel_id=1, source_target_pairs={{0,4},{4,0},{8,12},{12,8},{1,5},{5,1},{9,13},{13,9},{2,6},{6,2},{1... | collective-permute-start | bytes 589832 | tf_op jit(solution)/shard_map/ppermute | solution.py:30
  128.8 17.1 %collective-permute-start.4 = (bf16[768,128]{1,0:T(8,128)(2,1)S(1)}, bf16[768,128]{1,0:T(8,128)(2,1)S(1)}, u32[]{:S(2)}, u32[]{:S(2)}) collective-permute-start(bf16[768,128]{1,0:T(8,128)(2,1)S(1)} %copy-done.44), channel_id=1, source_target_pairs={{0,8},{4,12},{8,0},{12,4},{1,9},{5,13},{9,1},{13,5},{2,10},{6,14},... | collective-permute-start | bytes 589832 | tf_op jit(solution)/shard_map/ppermute | solution.py:30
  128.8 17.1 %collective-permute-start.5 = (bf16[768,128]{1,0:T(8,128)(2,1)S(1)}, bf16[768,128]{1,0:T(8,128)(2,1)S(1)}, u32[]{:S(2)}, u32[]{:S(2)}) collective-permute-start(bf16[768,128]{1,0:T(8,128)(2,1)S(1)} %copy-done.43), channel_id=1, source_target_pairs={{0,12},{4,8},{8,4},{12,0},{1,13},{5,9},{9,5},{13,1},{2,14},{6,10},... | collective-permute-start | bytes 589832 | tf_op jit(solution)/shard_map/ppermute | solution.py:30
  154.0 7.8 %collective-permute-start.10 = (bf16[2,192,2048]{2,1,0:T(8,128)(2,1)}, bf16[2,192,2048]{2,1,0:T(8,128)(2,1)}, u32[]{:S(2)}, u32[]{:S(2)}) collective-permute-start(bf16[2,192,2048]{2,1,0:T(8,128)(2,1)} %get-tuple-element.97), channel_id=1, source_target_pairs={{0,1},{1,0},{2,3},{3,2},{4,5},{5,4},{6,7},{7,6},{8,9},{9,8},{10,11... | collective-permute-start | bytes 4718600 | tf_op jit(solution)/shard_map/ppermute | solution.py:30
  156.8 9.2 %collective-permute-start.12 = (bf16[192,2048]{1,0:T(8,128)(2,1)}, bf16[192,2048]{1,0:T(8,128)(2,1)}, u32[]{:S(2)}, u32[]{:S(2)}) collective-permute-start(bf16[192,2048]{1,0:T(8,128)(2,1)} %tie.15), channel_id=1, source_target_pairs={{0,1},{1,0},{2,3},{3,2},{4,5},{5,4},{6,7},{7,6},{8,9},{9,8},{10,11... | collective-permute-start | bytes 2359304 | tf_op jit(solution)/shard_map/ppermute | solution.py:30
  157.3 22.5 %collective-permute-start.14 = (bf16[192,2048]{1,0:T(8,128)(2,1)}, bf16[192,2048]{1,0:T(8,128)(2,1)S(1)}, u32[]{:S(2)}, u32[]{:S(2)}) collective-permute-start(bf16[192,2048]{1,0:T(8,128)(2,1)} %tie.16), channel_id=1, source_target_pairs={{0,12},{4,8},{8,4},{12,0},{1,13},{5,9},{9,5},{13,1},{2,14},{6,10},... | collective-permute-start | bytes 2359304 | tf_op jit(solution)/shard_map/ppermute | solution.py:30
  158.7 37.1 %collective-permute-start.13 = (bf16[192,2048]{1,0:T(8,128)(2,1)}, bf16[192,2048]{1,0:T(8,128)(2,1)S(1)}, u32[]{:S(2)}, u32[]{:S(2)}) collective-permute-start(bf16[192,2048]{1,0:T(8,128)(2,1)} %tie.16), channel_id=1, source_target_pairs={{0,4},{4,0},{8,12},{12,8},{1,5},{5,1},{9,13},{13,9},{2,6},{6,2},{1... | collective-permute-start | bytes 2359304 | tf_op jit(solution)/shard_map/ppermute | solution.py:30
  165.4 30.3 %collective-permute-start.11 = (bf16[192,2048]{1,0:T(8,128)(2,1)}, bf16[192,2048]{1,0:T(8,128)(2,1)}, u32[]{:S(2)}, u32[]{:S(2)}) collective-permute-start(bf16[192,2048]{1,0:T(8,128)(2,1)} %get-tuple-element.99.refs_4_.refs_2_), channel_id=1, source_target_pairs={{0,2},{1,3},{2,0},{3,1},{4,6},{5,7},{6,4},{7,5},{8,10},{9,11},{10,... | collective-permute-start | bytes 2359304 | tf_op jit(solution)/shard_map/ppermute | solution.py:30
  200.3 19.7 %collective-permute-start.16 = (bf16[192,2048]{1,0:T(8,128)(2,1)}, bf16[192,2048]{1,0:T(8,128)(2,1)S(1)}, u32[]{:S(2)}, u32[]{:S(2)}) collective-permute-start(bf16[192,2048]{1,0:T(8,128)(2,1)} %get-tuple-element.100.refs_0_), channel_id=1, source_target_pairs={{0,2},{1,3},{2,0},{3,1},{4,6},{5,7},{6,4},{7,5},{8,10},{9,11},{10,... | collective-permute-start | bytes 2359304 | tf_op jit(solution)/shard_map/ppermute | solution.py:30
  200.8 19.5 %collective-permute-start.19 = (bf16[192,2048]{1,0:T(8,128)(2,1)}, bf16[192,2048]{1,0:T(8,128)(2,1)}, u32[]{:S(2)}, u32[]{:S(2)}) collective-permute-start(bf16[192,2048]{1,0:T(8,128)(2,1)} %get-tuple-element.100.refs_0_), channel_id=1, source_target_pairs={{0,4},{4,0},{8,12},{12,8},{1,5},{5,1},{9,13},{13,9},{2,6},{6,2},{1... | collective-permute-start | bytes 2359304 | tf_op jit(solution)/shard_map/ppermute | solution.py:30
  201.7 20.2 %collective-permute-start.15 = (bf16[192,2048]{1,0:T(8,128)(2,1)}, bf16[192,2048]{1,0:T(8,128)(2,1)}, u32[]{:S(2)}, u32[]{:S(2)}) collective-permute-start(bf16[192,2048]{1,0:T(8,128)(2,1)} %get-tuple-element.100.refs_0_), channel_id=1, source_target_pairs={{0,1},{1,0},{2,3},{3,2},{4,5},{5,4},{6,7},{7,6},{8,9},{9,8},{10,11... | collective-permute-start | bytes 2359304 | tf_op jit(solution)/shard_map/ppermute | solution.py:30
  220.3 30.2 %collective-permute-start.21 = (bf16[192,2048]{1,0:T(8,128)(2,1)}, bf16[192,2048]{1,0:T(8,128)(2,1)S(1)}, u32[]{:S(2)}, u32[]{:S(2)}) collective-permute-start(bf16[192,2048]{1,0:T(8,128)(2,1)} %collective-permute-done.19.refs_0_), channel_id=1, source_target_pairs={{0,2},{1,3},{2,0},{3,1},{4,6},{5,7},{6,4},{7,5},{8,10},{9,11},{10,... | collective-permute-start | bytes 2359304 | tf_op jit(solution)/shard_map/ppermute | solution.py:30
  250.0 20.7 %collective-permute-start.18 = (bf16[2,192,2048]{2,1,0:T(8,128)(2,1)}, bf16[2,192,2048]{2,1,0:T(8,128)(2,1)}, u32[]{:S(2)}, u32[]{:S(2)}) collective-permute-start(bf16[2,192,2048]{2,1,0:T(8,128)(2,1)} %get-tuple-element.105), channel_id=1, source_target_pairs={{0,1},{1,0},{2,3},{3,2},{4,5},{5,4},{6,7},{7,6},{8,9},{9,8},{10,11... | collective-permute-start | bytes 4718600 | tf_op jit(solution)/shard_map/ppermute | solution.py:30
  304.4 149.8 %reduce-scatter.7.cloned.1.call-start = ((), (), s32[]{:S(2)}) async-start(), calls=%async_computation.6 | async-start | bytes 9437184 | tf_op jit(solution)/shard_map/reduce_scatter | solution.py:941
  305.5 19.6 %collective-permute-start.25 = (bf16[192,2048]{1,0:T(8,128)(2,1)S(1)}, bf16[192,2048]{1,0:T(8,128)(2,1)S(1)}, u32[]{:S(2)}, u32[]{:S(2)}) collective-permute-start(bf16[192,2048]{1,0:T(8,128)(2,1)S(1)} %copy-done.26), channel_id=1, source_target_pairs={{0,2},{1,3},{2,0},{3,1},{4,6},{5,7},{6,4},{7,5},{8,10},{9,11},{10,... | collective-permute-start | bytes 2359304 | tf_op jit(solution)/shard_map/ppermute | solution.py:30
  350.4 109.9 %reduce-scatter.11.cloned.1.call-start = ((), (), s32[]{:S(2)}) async-start(), calls=%async_computation.8 | async-start | bytes 3145728 | tf_op jit(solution)/shard_map/reduce_scatter | solution.py:941
  351.1 221.5 %reduce-scatter.13.cloned.1.call-start = ((), (), s32[]{:S(2)}) async-start(), calls=%async_computation.9 | async-start | bytes 2359296 | tf_op jit(solution)/shard_map/reduce_scatter | solution.py:994
  351.5 18.8 %collective-permute-start.23 = (bf16[192,2048]{1,0:T(8,128)(2,1)S(1)}, bf16[192,2048]{1,0:T(8,128)(2,1)S(1)}, u32[]{:S(2)}, u32[]{:S(2)}) collective-permute-start(bf16[192,2048]{1,0:T(8,128)(2,1)S(1)} %copy-done.21), channel_id=1, source_target_pairs={{0,2},{1,3},{2,0},{3,1},{4,6},{5,7},{6,4},{7,5},{8,10},{9,11},{10,... | collective-permute-start | bytes 2359304 | tf_op jit(solution)/shard_map/ppermute | solution.py:30
  352.0 18.6 %collective-permute-start.26 = (bf16[192,2048]{1,0:T(8,128)(2,1)S(1)}, bf16[192,2048]{1,0:T(8,128)(2,1)S(1)}, u32[]{:S(2)}, u32[]{:S(2)}) collective-permute-start(bf16[192,2048]{1,0:T(8,128)(2,1)S(1)} %copy-done.13), channel_id=1, source_target_pairs={{0,4},{4,0},{8,12},{12,8},{1,5},{5,1},{9,13},{13,9},{2,6},{6,2},{1... | collective-permute-start | bytes 2359304 | tf_op jit(solution)/shard_map/ppermute | solution.py:30
  376.8 23.6 %collective-permute-start.28 = (bf16[192,2048]{1,0:T(8,128)(2,1)}, bf16[192,2048]{1,0:T(8,128)(2,1)}, u32[]{:S(2)}, u32[]{:S(2)}) collective-permute-start(bf16[192,2048]{1,0:T(8,128)(2,1)} %get-tuple-element.118.refs_2_.refs_0_), channel_id=1, source_target_pairs={{0,2},{1,3},{2,0},{3,1},{4,6},{5,7},{6,4},{7,5},{8,10},{9,11},{10,... | collective-permute-start | bytes 2359304 | tf_op jit(solution)/shard_map/ppermute | solution.py:30
  379.0 46.7 %collective-permute-start.34 = (bf16[2,256,1024]{2,1,0:T(8,128)(2,1)}, bf16[2,256,1024]{2,1,0:T(8,128)(2,1)S(1)}, u32[]{:S(2)}, u32[]{:S(2)}) collective-permute-start(bf16[2,256,1024]{2,1,0:T(8,128)(2,1)} %tie.20), channel_id=1, source_target_pairs={{0,8},{4,12},{8,0},{12,4},{1,9},{5,13},{9,1},{13,5},{2,10},{6,14},... | collective-permute-start | bytes 3145736 | tf_op jit(solution)/shard_map/ppermute | solution.py:30
  379.9 21.7 %collective-permute-start.27 = (bf16[192,2048]{1,0:T(8,128)(2,1)S(1)}, bf16[192,2048]{1,0:T(8,128)(2,1)}, u32[]{:S(2)}, u32[]{:S(2)}) collective-permute-start(bf16[192,2048]{1,0:T(8,128)(2,1)S(1)} %copy-done.3), channel_id=1, source_target_pairs={{0,1},{1,0},{2,3},{3,2},{4,5},{5,4},{6,7},{7,6},{8,9},{9,8},{10,11... | collective-permute-start | bytes 2359304 | tf_op jit(solution)/shard_map/ppermute | solution.py:30
  439.0 212.1 %reduce-scatter.17.cloned.1.call-start = ((), (), s32[]{:S(2)}) async-start(), calls=%async_computation.11 | async-start | bytes 3145728 | tf_op jit(solution)/shard_map/reduce_scatter | solution.py:941
  439.0 80.4 %collective-permute-start.45 = (bf16[3,192,2048]{2,1,0:T(8,128)(2,1)}, bf16[3,192,2048]{2,1,0:T(8,128)(2,1)}, u32[]{:S(2)}, u32[]{:S(2)}) collective-permute-start(bf16[3,192,2048]{2,1,0:T(8,128)(2,1)} %stack.13.refs_5_.refs_1_), channel_id=1, source_target_pairs={{0,2},{1,3},{2,0},{3,1},{4,6},{5,7},{6,4},{7,5},{8,10},{9,11},{10,... | collective-permute-start | bytes 7077896 | tf_op jit(solution)/shard_map/ppermute | solution.py:30
  440.0 290.6 %reduce-scatter.15.cloned.1.call-start = ((), (), s32[]{:S(2)}) async-start(), calls=%async_computation.10 | async-start | bytes 2359296 | tf_op jit(solution)/shard_map/reduce_scatter | solution.py:941
  441.5 22.7 %collective-permute-start.30 = (bf16[2,192,2048]{2,1,0:T(8,128)(2,1)}, bf16[2,192,2048]{2,1,0:T(8,128)(2,1)S(1)}, u32[]{:S(2)}, u32[]{:S(2)}) collective-permute-start(bf16[2,192,2048]{2,1,0:T(8,128)(2,1)} %tie.19), channel_id=1, source_target_pairs={{0,1},{1,0},{2,3},{3,2},{4,5},{5,4},{6,7},{7,6},{8,9},{9,8},{10,11... | collective-permute-start | bytes 4718600 | tf_op jit(solution)/shard_map/ppermute | solution.py:30
  441.6 22.6 %collective-permute-start.35 = (bf16[2,192,2048]{2,1,0:T(8,128)(2,1)}, bf16[2,192,2048]{2,1,0:T(8,128)(2,1)}, u32[]{:S(2)}, u32[]{:S(2)}) collective-permute-start(bf16[2,192,2048]{2,1,0:T(8,128)(2,1)} %tie.21), channel_id=1, source_target_pairs={{0,1},{1,0},{2,3},{3,2},{4,5},{5,4},{6,7},{7,6},{8,9},{9,8},{10,11... | collective-permute-start | bytes 4718600 | tf_op jit(solution)/shard_map/ppermute | solution.py:30
  442.1 9.8 %collective-permute-start.31 = (bf16[768,128]{1,0:T(8,128)(2,1)S(1)}, bf16[768,128]{1,0:T(8,128)(2,1)S(1)}, u32[]{:S(2)}, u32[]{:S(2)}) collective-permute-start(bf16[768,128]{1,0:T(8,128)(2,1)S(1)} %copy-done.42), channel_id=1, source_target_pairs={{0,4},{4,0},{8,12},{12,8},{1,5},{5,1},{9,13},{13,9},{2,6},{6,2},{1... | collective-permute-start | bytes 589832 | tf_op jit(solution)/shard_map/ppermute | solution.py:30
  442.1 15.2 %collective-permute-start.32 = (bf16[768,128]{1,0:T(8,128)(2,1)}, bf16[768,128]{1,0:T(8,128)(2,1)S(1)}, u32[]{:S(2)}, u32[]{:S(2)}) collective-permute-start(bf16[768,128]{1,0:T(8,128)(2,1)} %get-tuple-element.125), channel_id=1, source_target_pairs={{0,8},{4,12},{8,0},{12,4},{1,9},{5,13},{9,1},{13,5},{2,10},{6,14},... | collective-permute-start | bytes 589832 | tf_op jit(solution)/shard_map/ppermute | solution.py:30
  451.8 8.4 %collective-permute-start.33 = (bf16[768,128]{1,0:T(8,128)(2,1)}, bf16[768,128]{1,0:T(8,128)(2,1)}, u32[]{:S(2)}, u32[]{:S(2)}) collective-permute-start(bf16[768,128]{1,0:T(8,128)(2,1)} %get-tuple-element.126), channel_id=1, source_target_pairs={{0,12},{4,8},{8,4},{12,0},{1,13},{5,9},{9,5},{13,1},{2,14},{6,10},... | collective-permute-start | bytes 589832 | tf_op jit(solution)/shard_map/ppermute | solution.py:30
  461.0 94.6 %collective-permute-start.36 = (bf16[2,256,1024]{2,1,0:T(8,128)(2,1)}, bf16[2,256,1024]{2,1,0:T(8,128)(2,1)}, u32[]{:S(2)}, u32[]{:S(2)}) collective-permute-start(bf16[2,256,1024]{2,1,0:T(8,128)(2,1)} %tie.22), channel_id=1, source_target_pairs={{0,8},{4,12},{8,0},{12,4},{1,9},{5,13},{9,1},{13,5},{2,10},{6,14},... | collective-permute-start | bytes 3145736 | tf_op jit(solution)/shard_map/ppermute | solution.py:30
  510.9 61.7 %collective-permute-start.39 = (bf16[768,384]{1,0:T(8,128)(2,1)}, bf16[768,384]{1,0:T(8,128)(2,1)S(1)}, u32[]{:S(2)}, u32[]{:S(2)}) collective-permute-start(bf16[768,384]{1,0:T(8,128)(2,1)} %get-tuple-element.136.refs_6_), channel_id=1, source_target_pairs={{0,4},{4,0},{8,12},{12,8},{1,5},{5,1},{9,13},{13,9},{2,6},{6,2},{1... | collective-permute-start | bytes 1769480 | tf_op jit(solution)/shard_map/ppermute | solution.py:30
  511.8 62.3 %collective-permute-start.40 = (bf16[768,384]{1,0:T(8,128)(2,1)}, bf16[768,384]{1,0:T(8,128)(2,1)S(1)}, u32[]{:S(2)}, u32[]{:S(2)}) collective-permute-start(bf16[768,384]{1,0:T(8,128)(2,1)} %get-tuple-element.137.refs_7_), channel_id=1, source_target_pairs={{0,8},{4,12},{8,0},{12,4},{1,9},{5,13},{9,1},{13,5},{2,10},{6,14},... | collective-permute-start | bytes 1769480 | tf_op jit(solution)/shard_map/ppermute | solution.py:30
  514.0 60.2 %collective-permute-start.41 = (bf16[768,384]{1,0:T(8,128)(2,1)}, bf16[768,384]{1,0:T(8,128)(2,1)S(1)}, u32[]{:S(2)}, u32[]{:S(2)}) collective-permute-start(bf16[768,384]{1,0:T(8,128)(2,1)} %get-tuple-element.138.refs_8_), channel_id=1, source_target_pairs={{0,12},{4,8},{8,4},{12,0},{1,13},{5,9},{9,5},{13,1},{2,14},{6,10},... | collective-permute-start | bytes 1769480 | tf_op jit(solution)/shard_map/ppermute | solution.py:30
  519.4 78.6 %collective-permute-start.44 = (bf16[3,192,2048]{2,1,0:T(8,128)(2,1)}, bf16[3,192,2048]{2,1,0:T(8,128)(2,1)}, u32[]{:S(2)}, u32[]{:S(2)}) collective-permute-start(bf16[3,192,2048]{2,1,0:T(8,128)(2,1)} %tie.23), channel_id=1, source_target_pairs={{0,1},{1,0},{2,3},{3,2},{4,5},{5,4},{6,7},{7,6},{8,9},{9,8},{10,11... | collective-permute-start | bytes 7077896 | tf_op jit(solution)/shard_map/ppermute | solution.py:30
  555.6 42.5 %collective-permute-start.46 = (bf16[3,192,2048]{2,1,0:T(8,128)(2,1)}, bf16[3,192,2048]{2,1,0:T(8,128)(2,1)}, u32[]{:S(2)}, u32[]{:S(2)}) collective-permute-start(bf16[3,192,2048]{2,1,0:T(8,128)(2,1)} %tie.24.refs_3_), channel_id=1, source_target_pairs={{0,1},{1,0},{2,3},{3,2},{4,5},{5,4},{6,7},{7,6},{8,9},{9,8},{10,11... | collective-permute-start | bytes 7077896 | tf_op jit(solution)/shard_map/ppermute | solution.py:30
  596.0 20.6 %collective-permute-start.43 = (bf16[192,2048]{1,0:T(8,128)(2,1)}, bf16[192,2048]{1,0:T(8,128)(2,1)S(1)}, u32[]{:S(2)}, u32[]{:S(2)}) collective-permute-start(bf16[192,2048]{1,0:T(8,128)(2,1)} %get-tuple-element.143.refs_9_), channel_id=1, source_target_pairs={{0,2},{1,3},{2,0},{3,1},{4,6},{5,7},{6,4},{7,5},{8,10},{9,11},{10,... | collective-permute-start | bytes 2359304 | tf_op jit(solution)/shard_map/ppermute | solution.py:30
  597.5 36.0 %collective-permute-start.38 = (bf16[192,2048]{1,0:T(8,128)(2,1)}, bf16[192,2048]{1,0:T(8,128)(2,1)S(1)}, u32[]{:S(2)}, u32[]{:S(2)}) collective-permute-start(bf16[192,2048]{1,0:T(8,128)(2,1)} %get-tuple-element.135.refs_2_), channel_id=1, source_target_pairs={{0,2},{1,3},{2,0},{3,1},{4,6},{5,7},{6,4},{7,5},{8,10},{9,11},{10,... | collective-permute-start | bytes 2359304 | tf_op jit(solution)/shard_map/ppermute | solution.py:30
  622.7 26.7 %collective-permute-start.54 = (f32[2,2048]{1,0:T(2,128)S(1)}, f32[2,2048]{1,0:T(2,128)S(1)}, u32[]{:S(2)}, u32[]{:S(2)}) collective-permute-start(f32[2,2048]{1,0:T(2,128)S(1)} %pad_maximum_fusion), channel_id=1, source_target_pairs={{0,1},{1,0},{2,3},{3,2},{4,5},{5,4},{6,7},{7,6},{8,9},{9,8},{10,11... | collective-permute-start | bytes 49160 | tf_op jit(solution)/shard_map/ppermute | solution.py:30
  622.8 33.7 %collective-permute-start.37 = (bf16[192,2048]{1,0:T(8,128)(2,1)}, bf16[192,2048]{1,0:T(8,128)(2,1)S(1)}, u32[]{:S(2)}, u32[]{:S(2)}) collective-permute-start(bf16[192,2048]{1,0:T(8,128)(2,1)} %get-tuple-element.133.refs_2_), channel_id=1, source_target_pairs={{0,2},{1,3},{2,0},{3,1},{4,6},{5,7},{6,4},{7,5},{8,10},{9,11},{10,... | collective-permute-start | bytes 2359304 | tf_op jit(solution)/shard_map/ppermute | solution.py:30
  637.6 53.1 %collective-permute-start.47 = (bf16[192,2048]{1,0:T(8,128)(2,1)}, bf16[192,2048]{1,0:T(8,128)(2,1)}, u32[]{:S(2)}, u32[]{:S(2)}) collective-permute-start(bf16[192,2048]{1,0:T(8,128)(2,1)} %add_low.3.refs_4_.refs_2_), channel_id=1, source_target_pairs={{0,4},{4,0},{8,12},{12,8},{1,5},{5,1},{9,13},{13,9},{2,6},{6,2},{1... | collective-permute-start | bytes 2359304 | tf_op jit(solution)/shard_map/ppermute | solution.py:30
  651.0 50.9 %collective-permute-start.66 = (bf16[256,1024]{1,0:T(8,128)(2,1)}, bf16[256,1024]{1,0:T(8,128)(2,1)}, u32[]{:S(2)}, u32[]{:S(2)}) collective-permute-start(bf16[256,1024]{1,0:T(8,128)(2,1)} %get-tuple-element.154), channel_id=1, source_target_pairs={{0,4},{4,0},{8,12},{12,8},{1,5},{5,1},{9,13},{13,9},{2,6},{6,2},{1... | collective-permute-start | bytes 1572872 | tf_op jit(solution)/shard_map/ppermute | solution.py:30
  651.7 60.8 %collective-permute-start.64 = (bf16[2,256,1024]{2,1,0:T(8,128)(2,1)}, bf16[2,256,1024]{2,1,0:T(8,128)(2,1)S(1)}, u32[]{:S(2)}, u32[]{:S(2)}) collective-permute-start(bf16[2,256,1024]{2,1,0:T(8,128)(2,1)} %tie.25), channel_id=1, source_target_pairs={{0,8},{4,12},{8,0},{12,4},{1,9},{5,13},{9,1},{13,5},{2,10},{6,14},... | collective-permute-start | bytes 3145736 | tf_op jit(solution)/shard_map/ppermute | solution.py:30
  655.4 46.5 %collective-permute-start.52 = (bf16[192,2048]{1,0:T(8,128)(2,1)}, bf16[192,2048]{1,0:T(8,128)(2,1)}, u32[]{:S(2)}, u32[]{:S(2)}) collective-permute-start(bf16[192,2048]{1,0:T(8,128)(2,1)} %get-tuple-element.145.refs_2_.refs_4_.refs_0_), channel_id=1, source_target_pairs={{0,2},{1,3},{2,0},{3,1},{4,6},{5,7},{6,4},{7,5},{8,10},{9,11},{10,... | collective-permute-start | bytes 2359304 | tf_op jit(solution)/shard_map/ppermute | solution.py:30
  694.5 26.9 %collective-permute-start.49 = (bf16[192,2048]{1,0:T(8,128)(2,1)}, bf16[192,2048]{1,0:T(8,128)(2,1)}, u32[]{:S(2)}, u32[]{:S(2)}) collective-permute-start(bf16[192,2048]{1,0:T(8,128)(2,1)} %output.1.refs_0_), channel_id=1, source_target_pairs={{0,2},{1,3},{2,0},{3,1},{4,6},{5,7},{6,4},{7,5},{8,10},{9,11},{10,... | collective-permute-start | bytes 2359304 | tf_op jit(solution)/shard_map/ppermute | solution.py:30
  699.7 11.1 %collective-permute-start.63 = (bf16[256,1024]{1,0:T(8,128)(2,1)}, bf16[256,1024]{1,0:T(8,128)(2,1)S(1)}, u32[]{:S(2)}, u32[]{:S(2)}) collective-permute-start(bf16[256,1024]{1,0:T(8,128)(2,1)} %get-tuple-element.151), channel_id=1, source_target_pairs={{0,4},{4,0},{8,12},{12,8},{1,5},{5,1},{9,13},{13,9},{2,6},{6,2},{1... | collective-permute-start | bytes 1572872 | tf_op jit(solution)/shard_map/ppermute | solution.py:30
  701.9 32.4 %collective-permute-start.51 = (bf16[192,2048]{1,0:T(8,128)(2,1)}, bf16[192,2048]{1,0:T(8,128)(2,1)}, u32[]{:S(2)}, u32[]{:S(2)}) collective-permute-start(bf16[192,2048]{1,0:T(8,128)(2,1)} %get-tuple-element.145.refs_2_.refs_4_.refs_0_), channel_id=1, source_target_pairs={{0,1},{1,0},{2,3},{3,2},{4,5},{5,4},{6,7},{7,6},{8,9},{9,8},{10,11... | collective-permute-start | bytes 2359304 | tf_op jit(solution)/shard_map/ppermute | solution.py:30
  701.9 33.4 %collective-permute-start.53 = (bf16[192,2048]{1,0:T(8,128)(2,1)}, bf16[192,2048]{1,0:T(8,128)(2,1)}, u32[]{:S(2)}, u32[]{:S(2)}) collective-permute-start(bf16[192,2048]{1,0:T(8,128)(2,1)} %collective-permute-done.52.refs_2_), channel_id=1, source_target_pairs={{0,1},{1,0},{2,3},{3,2},{4,5},{5,4},{6,7},{7,6},{8,9},{9,8},{10,11... | collective-permute-start | bytes 2359304 | tf_op jit(solution)/shard_map/ppermute | solution.py:30
  712.5 8.0 %collective-permute-start.58 = (f32[2,256]{1,0:T(2,128)S(1)}, f32[2,256]{1,0:T(2,128)S(1)}, u32[]{:S(2)}, u32[]{:S(2)}) collective-permute-start(f32[2,256]{1,0:T(2,128)S(1)} %get-tuple-element.160), channel_id=1, source_target_pairs={{0,8},{4,12},{8,0},{12,4},{1,9},{5,13},{9,1},{13,5},{2,10},{6,14},... | collective-permute-start | bytes 6152 | tf_op jit(solution)/shard_map/ppermute | solution.py:30
  714.5 6.9 collective-permute-start.59
  720.6 12.1 %collective-permute-start.65 = (bf16[256,1024]{1,0:T(8,128)(2,1)}, bf16[256,1024]{1,0:T(8,128)(2,1)}, u32[]{:S(2)}, u32[]{:S(2)}) collective-permute-start(bf16[256,1024]{1,0:T(8,128)(2,1)} %get-tuple-element.153), channel_id=1, source_target_pairs={{0,4},{4,0},{8,12},{12,8},{1,5},{5,1},{9,13},{13,9},{2,6},{6,2},{1... | collective-permute-start | bytes 1572872 | tf_op jit(solution)/shard_map/ppermute | solution.py:30
  721.4 23.0 %collective-permute-start.48 = (bf16[192,2048]{1,0:T(8,128)(2,1)S(1)}, bf16[192,2048]{1,0:T(8,128)(2,1)S(1)}, u32[]{:S(2)}, u32[]{:S(2)}) collective-permute-start(bf16[192,2048]{1,0:T(8,128)(2,1)S(1)} %copy-done.11), channel_id=1, source_target_pairs={{0,1},{1,0},{2,3},{3,2},{4,5},{5,4},{6,7},{7,6},{8,9},{9,8},{10,11... | collective-permute-start | bytes 2359304 | tf_op jit(solution)/shard_map/ppermute | solution.py:30
  721.5 23.0 %collective-permute-start.50 = (bf16[192,2048]{1,0:T(8,128)(2,1)}, bf16[192,2048]{1,0:T(8,128)(2,1)}, u32[]{:S(2)}, u32[]{:S(2)}) collective-permute-start(bf16[192,2048]{1,0:T(8,128)(2,1)} %collective-permute-done.49.refs_2_), channel_id=1, source_target_pairs={{0,1},{1,0},{2,3},{3,2},{4,5},{5,4},{6,7},{7,6},{8,9},{9,8},{10,11... | collective-permute-start | bytes 2359304 | tf_op jit(solution)/shard_map/ppermute | solution.py:30
  732.6 16.2 %collective-permute-start.62 = (bf16[256,384]{1,0:T(8,128)(2,1)}, bf16[256,384]{1,0:T(8,128)(2,1)}, u32[]{:S(2)}, u32[]{:S(2)}) collective-permute-start(bf16[256,384]{1,0:T(8,128)(2,1)} %get-tuple-element.155), channel_id=1, source_target_pairs={{0,12},{4,8},{8,4},{12,0},{1,13},{5,9},{9,5},{13,1},{2,14},{6,10},... | collective-permute-start | bytes 589832 | tf_op jit(solution)/shard_map/ppermute | solution.py:30
  734.2 18.9 %collective-permute-start.61 = (bf16[256,384]{1,0:T(8,128)(2,1)S(1)}, bf16[256,384]{1,0:T(8,128)(2,1)}, u32[]{:S(2)}, u32[]{:S(2)}) collective-permute-start(bf16[256,384]{1,0:T(8,128)(2,1)S(1)} %get-tuple-element.156), channel_id=1, source_target_pairs={{0,8},{4,12},{8,0},{12,4},{1,9},{5,13},{9,1},{13,5},{2,10},{6,14},... | collective-permute-start | bytes 589832 | tf_op jit(solution)/shard_map/ppermute | solution.py:30
  735.3 17.8 %collective-permute-start.60 = (bf16[256,384]{1,0:T(8,128)(2,1)S(1)}, bf16[256,384]{1,0:T(8,128)(2,1)}, u32[]{:S(2)}, u32[]{:S(2)}) collective-permute-start(bf16[256,384]{1,0:T(8,128)(2,1)S(1)} %get-tuple-element.157), channel_id=1, source_target_pairs={{0,4},{4,0},{8,12},{12,8},{1,5},{5,1},{9,13},{13,9},{2,6},{6,2},{1... | collective-permute-start | bytes 589832 | tf_op jit(solution)/shard_map/ppermute | solution.py:30
  (55 other events, 216.5 us)
Sparse Core Ops, SparseCore 0:
  304.5 29.8 reduce-scatter.8
  350.5 75.1 reduce-scatter.6
  428.5 31.8 reduce-scatter.10
  464.7 107.9 reduce-scatter.12
  575.4 28.7 reduce-scatter.16
  611.4 36.2 reduce-scatter.14

commit v3 on v2

v3 whole, which is shorter than its diff:
```python
import functools

import jax
import jax.numpy as jnp
from jax import lax
from jax.experimental import pallas as pl
from jax.experimental.pallas import tpu as pltpu
from jax.sharding import PartitionSpec as P

HEAD_DIM = 64
EPS = 1e-05
THETA = 130000.0
MIB = 1 << 20
MOST = 64
COSTS = {
    "project": 11, "hidden_back": 8.5, "rope_tables": 8, "attend": 28, "quarter": 3,
    "join_heads": 6.5, "sums": 3, "join": 3.5, "middle": 4, "feed": 24, "wgrad_down": 14, "wgrad_gate": 14, "wgrad_up": 14,
    "middle_back": 5, "branch_back": 7, "others": 4, "feed_down": 9, "attend_back": 40, "project_wgrad": 13,
    "out_wgrad": 8.5, "add_pairs": 4, "project_back": 11, "input_back": 5, "output": 4, "halves": 3.5,
    "project_last": 3, "add_blocks": 3, "one_block": 2,
}
SCALE = 2
LOW = jnp.bfloat16
F32 = jnp.float32
ANY = pl.BlockSpec(memory_space=pl.ANY)


CTX, TENSOR = ("hi", "lo"), ("y", "core")


def swap(value, axis, distance):
    size = 2 if axis == "dp" else 4
    return lax.ppermute(value, axis, [(i, i ^ distance) for i in range(size)])


def dot(left, right):
    return jnp.dot(left, right, preferred_element_type=F32)


def against(left, right):
    return lax.dot_general(left, right, (((1,), (1,)), ((), ())), preferred_element_type=F32)


def across(left, right):
    return lax.dot_general(left, right, (((0,), (0,)), ((), ())), preferred_element_type=F32)


def shaped(shape, dtype=LOW):
    return jax.ShapeDtypeStruct(shape, dtype)


def call(kernel, name, index, grid, inputs, in_specs, outs, out_specs, scratch=(), mib=MOST, after=()):
    count = len(inputs)

    def body(index_ref, *refs):
        kernel(index_ref, *refs[:count], *refs[count + len(after) :])

    return pl.pallas_call(
        body,
        grid_spec=pltpu.PrefetchScalarGridSpec(
            num_scalar_prefetch=1,
            grid=grid,
            in_specs=list(in_specs) + [ANY] * len(after),
            out_specs=out_specs,
            scratch_shapes=list(scratch),
        ),
        out_shape=outs,
        compiler_params=pltpu.CompilerParams(
            vmem_limit_bytes=mib * MIB, dimension_semantics=("arbitrary",) * len(grid)
        ),
        cost_estimate=pl.CostEstimate(flops=0, bytes_accessed=int(COSTS.get(name, 0) * SCALE * 3.5 * MIB), transcendentals=0),
        name=name,
    )(index, *inputs, *after)


ME, T, DP = 0, 1, 2


def copy_all(pairs, sems):
    copies = [pltpu.make_async_copy(a, b, sems.at[k]) for k, (a, b) in enumerate(pairs)]
    for copy in copies:
        copy.start()
    for copy in copies:
        copy.wait()


def half_turn(rows):
    lane = lax.broadcasted_iota(jnp.int32, (1, 128), 1)
    first = (lane % HEAD_DIM) < HEAD_DIM // 2
    return jnp.where(first, pltpu.roll(rows, 96, 1), pltpu.roll(rows, 32, 1))


def rope_freq():
    half = HEAD_DIM // 2
    freq = jnp.power(THETA, -jnp.arange(half, dtype=F32) * (2.0 / HEAD_DIM))
    return jnp.concatenate([freq] * 4)


def rope_tables(positions):
    sign = jnp.where((jnp.arange(128) % HEAD_DIM) < HEAD_DIM // 2, -1.0, 1.0)
    angle = positions.astype(F32)[:, None] * rope_freq()[None, :]
    return jnp.cos(angle), jnp.sin(angle) * sign


def project_kernel(ix, tok_ref, gain_ref, cos_ref, sin_ref, wq_ref, wk_ref, wv_ref, first_ref, o0, o1, o2, o3, held):
    me = ix[ME]
    rows = tok_ref[...].astype(F32)
    inverse = lax.rsqrt(jnp.mean(rows * rows, axis=-1, keepdims=True) + EPS)
    first = (rows * inverse * gain_ref[...]).astype(LOW)
    first_ref[...] = first
    cosine, sine = cos_ref[...], sin_ref[...]
    for place, weight in enumerate((wq_ref, wk_ref, wv_ref)):
        flat = dot(first, weight[...])
        for group in range(4):
            part = flat[:, group * 128 : (group + 1) * 128]
            if place < 2:
                part = part * cosine + half_turn(part) * sine
            if place == 0:
                part = part * HEAD_DIM**-0.5
            held[group, :, place * 128 : (place + 1) * 128] = part.astype(LOW)
    for slot, out in enumerate((o0, o1, o2, o3)):
        out[...] = held[slot ^ me]


def project(ix, tokens, gain, tables, weights):
    rows, width = tokens.shape
    local = weights[0].shape[1]
    step = 256
    whole = lambda i, m: (0, 0)
    along = lambda i, m: (i, 0)
    return call(
        project_kernel, "project", ix, (rows // step,),
        [tokens, gain, *tables, *weights],
        [pl.BlockSpec((step, width), along), pl.BlockSpec((1, width), whole)]
        + [pl.BlockSpec((step, 128), along)] * 2 + [pl.BlockSpec((width, local), whole)] * 3,
        [shaped((rows, width))] + [shaped((rows, 384))] * 4,
        [pl.BlockSpec((step, width), along)] + [pl.BlockSpec((step, 384), along)] * 4,
        [pltpu.VMEM((4, step, 384), LOW)],
    )


def own_lanes(rows, head):
    lane = lax.broadcasted_iota(jnp.int32, (1, 128), 1)
    inside = (lane < HEAD_DIM) if head == 0 else (lane >= HEAD_DIM)
    return jnp.where(inside, rows, jnp.zeros_like(rows))


def attend_kernel(ix, r0, r1, r2, r3, o0, o1, o2, o3, raw_ref, lse_ref, held, sems):
    me = ix[ME]
    turn = pl.program_id(0)
    here = turn ^ me
    stretch = r0.shape[0]
    half = stretch // 2
    lane = lax.broadcasted_iota(jnp.int32, (1, 128), 1)

    @pl.when(turn == 0)
    def _():
        copy_all(
            [(ref, held.at[pl.ds((me ^ k) * stretch, stretch)]) for k, ref in enumerate((r0, r1, r2, r3))], sems
        )

    query = held[pl.ds(here * stretch, stretch), 0:128]
    queries = [own_lanes(query, head) for head in range(2)]

    def step(queries, rows, carry, offset):
        keys, values = held[rows, 128:256], held[rows, 256:384]
        out = []
        for head in range(2):
            peak, mass, total = carry[3 * head : 3 * head + 3]
            scores = against(queries[head], keys)
            if offset is not None:
                down = lax.broadcasted_iota(jnp.int32, scores.shape, 0) + offset
                along = lax.broadcasted_iota(jnp.int32, scores.shape, 1)
                scores = jnp.where(down >= along, scores, -1e30)
            top = jnp.maximum(peak, jnp.max(scores, axis=-1, keepdims=True))
            weights = jnp.exp(scores - top)
            fade = jnp.exp(peak - top)
            mass = mass * fade + jnp.sum(weights, axis=-1, keepdims=True)
            out += [top, mass, total * fade + dot(weights.astype(LOW), values)]
        return tuple(out)

    start = (
        jnp.full((stretch, 1), -1e30, F32),
        jnp.zeros((stretch, 1), F32),
        jnp.zeros((stretch, 128), F32),
    ) * 2
    carry = lax.fori_loop(0, here, lambda at, c: step(queries, pl.ds(at * stretch, stretch), c, None), start)
    for part in range(2):
        at = slice(part * half, (part + 1) * half)
        rows = pl.ds(here * stretch, (part + 1) * half)
        done = step([query[at] for query in queries], rows, [c[at] for c in carry], part * half)
        peak0, mass0, total0, peak1, mass1, total1 = done
        mixed = jnp.where(lane < HEAD_DIM, total0 / mass0, total1 / mass1)
        raw_ref[at, :] = mixed
        for slot, out in enumerate((o0, o1, o2, o3)):

            @pl.when(turn == slot)
            def _():
                out[at, :] = mixed.astype(LOW)

        turned = jnp.where(lane < HEAD_DIM, peak0 + jnp.log(mass0), peak1 + jnp.log(mass1)).T
        lse_ref[0, 0:8, at] = turned[0:8]
        lse_ref[0, 8:16, at] = turned[64:72]


def attend(ix, pieces, after):
    stretch = pieces[0].shape[0]
    length = 4 * stretch
    return call(
        attend_kernel, "attend", ix, (4,), list(pieces), [ANY] * 4,
        [shaped((stretch, 128))] * 4 + [shaped((length, 128), F32), shaped((4, 16, stretch), F32)],
        [pl.BlockSpec((stretch, 128), lambda i, m: (0, 0))] * 4
        + [
            pl.BlockSpec((stretch, 128), lambda i, m: (i ^ m[ME], 0)),
            pl.BlockSpec((1, 16, stretch), lambda i, m: (i ^ m[ME], 0, 0)),
        ],
        [pltpu.VMEM((length, 384), LOW), pltpu.SemaphoreType.DMA((4,))], after=after,
    )


def attend_back_kernel(
    ix, p0, p1, p2, p3, u0, u1, u2, u3, raw_ref, lse_ref, cos_ref, sin_ref, o0, o1, o2, o3,
    held, up, query_at, up_at, delta, query_sum, key_sum, value_sum, sems,
):
    me = ix[ME]
    turn = pl.program_id(0)
    count = pl.num_programs(0)
    stretch = p0.shape[0]
    half = stretch // 2
    here = turn ^ me

    @pl.when(turn == 0)
    def _():
        rows = [pl.ds((me ^ k) * stretch, stretch) for k in range(4)]
        copy_all(
            [(ref, held.at[rows[k]]) for k, ref in enumerate((p0, p1, p2, p3))]
            + [(ref, up.at[rows[k]]) for k, ref in enumerate((u0, u1, u2, u3))],
            sems,
        )
        query_sum[...] = jnp.zeros_like(query_sum)

        def prepare(at, _):
            rows = pl.ds(at * stretch, stretch)
            query, upstream = held[rows, 0:128], up[rows, :]
            turned = (upstream.astype(F32) * raw_ref[rows, :]).T
            for head in range(2):
                query_at[head, rows, :] = own_lanes(query, head)
                up_at[head, rows, :] = own_lanes(upstream, head)
                total = jnp.sum(turned[head * 64 : head * 64 + 64], axis=0, keepdims=True)
                delta[at, head * 8 : head * 8 + 8, :] = jnp.broadcast_to(total, (8, stretch))
            return 0

        lax.fori_loop(0, count, prepare, 0)

    here_rows = pl.ds(here * stretch, stretch)
    key, value = held[here_rows, 128:256], held[here_rows, 256:384]
    keys = [own_lanes(key, head) for head in range(2)]
    values = [own_lanes(value, head) for head in range(2)]

    def step(at, queries, kept, diagonal):
        size = queries.stop - queries.start
        rows = pl.ds(at * stretch + queries.start, size)
        query, upstream = held[rows, 0:128], up[rows, :]
        key_total = value_total = query_total = None
        for head in range(2):
            scores = against(keys[head][:kept], query)
            lse = lse_ref[at, head * 8 : head * 8 + 1, queries]
            chance = jnp.exp(scores - lse)
            if diagonal:
                down = lax.broadcasted_iota(jnp.int32, scores.shape, 0)
                along = lax.broadcasted_iota(jnp.int32, scores.shape, 1) + queries.start
                chance = jnp.where(along >= down, chance, 0.0)
            chance_back = against(values[head][:kept], upstream)
            shift = delta[at, head * 8 : head * 8 + 1, queries]
            score_back = (chance * (chance_back - shift)).astype(LOW)
            value_part = dot(chance.astype(LOW), up_at[head, rows, :])
            key_part = dot(score_back, query_at[head, rows, :])
            query_part = across(score_back, keys[head][:kept])
            if head == 0:
                value_total, key_total, query_total = value_part, key_part, query_part
            else:
                value_total += value_part
                key_total += key_part
                query_total += query_part
        query_sum[rows, :] += query_total
        return key_total, value_total

    key_sum[...], value_sum[...] = step(here, slice(half, stretch), stretch, True)
    key_total, value_total = step(here, slice(0, half), half, True)
    key_sum[:half] += key_total
    value_sum[:half] += value_total

    def later(at, _):
        key_total, value_total = step(at, slice(0, stretch), stretch, False)
        key_sum[...] += key_total
        value_sum[...] += value_total
        return 0

    lax.fori_loop(here + 1, count, later, 0)

    def back_rope(rows, at):
        places = pl.ds(at * stretch, stretch)
        return rows * cos_ref[places, :] - half_turn(rows) * sin_ref[places, :]

    key_low, value_low = back_rope(key_sum[...], here).astype(LOW), value_sum[...].astype(LOW)
    for slot, out in enumerate((o0, o1, o2, o3)):

        @pl.when(turn == slot)
        def _():
            out[:, 128:256] = key_low
            out[:, 256:384] = value_low

    @pl.when(turn == count - 1)
    def _():
        for slot, out in enumerate((o0, o1, o2, o3)):
            rows = query_sum[pl.ds((slot ^ me) * stretch, stretch), :] * HEAD_DIM**-0.5
            out[:, 0:128] = back_rope(rows, slot ^ me).astype(LOW)


def attend_back(ix, pieces, upstreams, raw, lse, tables, after):
    stretch = pieces[0].shape[0]
    length = 4 * stretch
    whole = lambda i, m: (0, 0)
    return call(
        attend_back_kernel, "attend_back", ix, (4,), [*pieces, *upstreams, raw, lse, *tables],
        [ANY] * 8
        + [pl.BlockSpec((length, 128), whole), pl.BlockSpec((4, 16, stretch), lambda i, m: (0, 0, 0))]
        + [pl.BlockSpec((length, 128), whole)] * 2,
        [shaped((stretch, 384))] * 4,
        [pl.BlockSpec((stretch, 384), whole)] * 4,
        [
            pltpu.VMEM((length, 384), LOW),
            pltpu.VMEM((length, 128), LOW),
            pltpu.VMEM((2, length, 128), LOW),
            pltpu.VMEM((2, length, 128), LOW),
            pltpu.VMEM((4, 16, stretch), F32),
            pltpu.VMEM((length, 128), F32),
            pltpu.VMEM((stretch, 128), F32),
            pltpu.VMEM((stretch, 128), F32),
            pltpu.SemaphoreType.DMA((8,)),
        ],
        after=after,
    )


def quarter_outs(rows, width, step):
    return (
        [shaped((2, rows // 4, width))] * 2,
        [pl.BlockSpec((2, rows // 4, step), lambda i, m: (0, 0, i))] * 2,
    )


def in_quarters(t, ref, held, columns=slice(None)):
    rows = ref.shape[0] // 4
    return [
        (ref.at[pl.ds((t ^ k) * rows, rows)], held.at[pl.ds(place * rows, rows), columns])
        for place, k in enumerate((0, 2, 1, 3))
    ]


def store_quarters(total, keep_ref, send_ref):
    rows = keep_ref.shape[1]
    for k in range(2):
        keep_ref[k] = total[k * rows : (k + 1) * rows].astype(LOW)
        send_ref[k] = total[(2 + k) * rows : (3 + k) * rows].astype(LOW)


def feed_down_kernel(ix, left_ref, right_ref, keep_ref, send_ref, held, sems):
    @pl.when(pl.program_id(0) == 0)
    def _():
        copy_all(in_quarters(ix[T], left_ref, held), sems)

    store_quarters(dot(held[...], right_ref[...]), keep_ref, send_ref)


def feed_down(ix, hidden, w_down, after=()):
    rows, units = hidden.shape
    width = w_down.shape[1]
    step = 512
    outs, out_specs = quarter_outs(rows, width, step)
    return call(
        feed_down_kernel, "feed_down", ix, (width // step,), [hidden, w_down],
        [ANY, pl.BlockSpec((units, step), lambda i, m: (m[ME] % 2, i))], outs, out_specs,
        [pltpu.VMEM((rows, units), LOW), pltpu.SemaphoreType.DMA((4,))], after=after,
    )


def join_heads_kernel(ix, a0, a1, a2, a3, w0, w1, w2, w3, keep_ref, send_ref, held, sems):
    @pl.when(pl.program_id(0) == 0)
    def _():
        copy_all(
            [
                pair
                for k, ref in enumerate((a0, a1, a2, a3))
                for pair in in_quarters(ix[T], ref, held, slice(k * 128, (k + 1) * 128))
            ],
            sems,
        )

    right = jnp.concatenate([w0[...], w1[...], w2[...], w3[...]], axis=0)
    store_quarters(dot(held[...], right), keep_ref, send_ref)


def join_heads(ix, mixed, w_out, after=()):
    rows = mixed[0].shape[0]
    width = w_out.shape[1]
    step = 1024

    def heads(slot):
        return pl.BlockSpec((128, step), lambda i, m: (m[ME] ^ slot, i))

    outs, out_specs = quarter_outs(rows, width, step)
    return call(
        join_heads_kernel, "join_heads", ix, (width // step,), [*mixed] + [w_out] * 4,
        [ANY] * 4 + [heads(slot) for slot in range(4)], outs, out_specs,
        [pltpu.VMEM((rows, 512), LOW), pltpu.SemaphoreType.DMA((16,))], after=after,
    )


def project_back_kernel(ix, *refs):
    keep_ref, send_ref, held, sems = refs[16:]

    @pl.when(pl.program_id(0) == 0)
    def _():
        copy_all(
            [
                pair
                for k, ref in enumerate(refs[:4])
                for pair in in_quarters(ix[T], ref, held, slice(k * 384, (k + 1) * 384))
            ],
            sems,
        )

    right = jnp.concatenate([ref[...] for ref in refs[4:16]], axis=1)
    store_quarters(against(held[...], right), keep_ref, send_ref)


def project_back(ix, back, weights, after):
    rows = back[0].shape[0]
    width = weights[0].shape[0]
    step = 512

    def heads(slot):
        return pl.BlockSpec((step, 128), lambda i, m: (i, m[ME] ^ slot))

    outs, out_specs = quarter_outs(rows, width, step)
    return call(
        project_back_kernel, "project_back", ix, (width // step,),
        [*back] + [w for slot in range(4) for w in weights],
        [ANY] * 4 + [heads(slot) for slot in range(4) for w in weights], outs, out_specs,
        [pltpu.VMEM((rows, 1536), LOW), pltpu.SemaphoreType.DMA((16,))], after=after,
    )


def rows_call(kernel, name, ix, quarters, others, outs, sums=0, after=()):
    arrays = [a if isinstance(a, tuple) else (a, None) for a in (*quarters, *others)]
    rows, width = arrays[0][0].shape[-2:]
    step = rows // 2

    def spec(array, which):
        if which is not None:
            return pl.BlockSpec((None, step, width), lambda i, m: (which, i, 0))
        if array.shape[0] == 1:
            return pl.BlockSpec((1, width), lambda i, m: (0, 0))
        if array.shape[0] == rows:
            return pl.BlockSpec((step, width), lambda i, m: (i, 0))
        return pl.BlockSpec((step, width), lambda i, m: (2 * m[T] + i, 0))

    return call(
        kernel, name, ix, (2,), [array for array, _ in arrays], [spec(*pair) for pair in arrays],
        [shaped((rows, width), dtype) for dtype in outs] + [shaped((1, width), F32)] * sums,
        [pl.BlockSpec((step, width), lambda i, m: (i, 0))] * len(outs)
        + [pl.BlockSpec((1, width), lambda i, m: (0, 0))] * sums,
        after=after,
    )


def wide_sum(*refs):
    return sum(ref[...].astype(F32) for ref in refs)


def sum_kernel(ix, *refs):
    refs[-1][...] = wide_sum(*refs[:-1]).astype(LOW)


def sums_to_send(ix, arrays, after=()):
    return rows_call(sum_kernel, "sums", ix, arrays, [], [LOW], after=after)[0]


def middle_kernel(ix, one, two, y_ref, tok_ref, gain_ref, middle_ref, second_ref):
    middle = tok_ref[...].astype(F32) + wide_sum(one, two, y_ref)
    middle_ref[...] = middle
    normed, _ = normalize(middle)
    second_ref[...] = (normed * gain_ref[...]).astype(LOW)


def add_rows(out_ref, rows):
    part = jnp.sum(rows, axis=0, keepdims=True)

    @pl.when(pl.program_id(0) == 0)
    def _():
        out_ref[...] = part

    @pl.when(pl.program_id(0) != 0)
    def _():
        out_ref[...] += part


def middle_back_kernel(ix, one, two, y_ref, z_ref, middle_ref, cot_ref, gain_ref, grad_ref, low_ref, sum_ref):
    second_sum = wide_sum(one, two, y_ref, z_ref)
    normed, inverse = normalize(middle_ref[...])
    grad = cot_ref[...].astype(F32) + norm_back(second_sum, normed, inverse, gain_ref[...])
    grad_ref[...] = grad
    low_ref[...] = grad.astype(LOW)
    add_rows(sum_ref, second_sum * normed)


def output_kernel(ix, one, two, y_ref, z_ref, middle_ref, out_ref):
    out_ref[...] = (middle_ref[...] + wide_sum(one, two, y_ref, z_ref)).astype(LOW)


def input_kernel(ix, one, two, y_ref, grad_ref, tok_ref, gain_ref, mlp_ref, out_ref, total):
    here, last = pl.program_id(0), pl.num_programs(0) - 1

    @pl.when(here < last)
    def _():
        first_sum = wide_sum(one, two, y_ref)
        normed, inverse = normalize(tok_ref[...].astype(F32))
        out_ref[...] = (grad_ref[...] + norm_back(first_sum, normed, inverse, gain_ref[...])).astype(LOW)
        add_rows(total, first_sum * normed)

    @pl.when(here == last)
    def _():
        sums = jnp.concatenate([total[...], mlp_ref[...], jnp.zeros((14, total.shape[1]), F32)], axis=0)
        out_ref[0:16, :] = sums.astype(LOW)


def input_back(ix, keep, core, y, grad, tokens, gain, mlp_sum, after):
    rows, width = grad.shape
    step = rows // 2
    at = lambda i: jnp.minimum(i, 1)
    block = pl.BlockSpec((None, step, width), lambda i, m: (0, at(i), 0))
    row = pl.BlockSpec((step, width), lambda i, m: (at(i), 0))
    single = pl.BlockSpec((1, width), lambda i, m: (0, 0))
    return call(
        input_kernel, "input_back", ix, (3,), [keep, core, y, grad, tokens, gain, mlp_sum],
        [block, block, row, row, pl.BlockSpec((step, width), lambda i, m: (2 * m[T] + at(i), 0)), single, single],
        shaped((rows + 16, width)), pl.BlockSpec((step, width), lambda i, m: (i, 0)),
        [pltpu.VMEM((1, width), F32)], after=after,
    )


def join_input_kernel(ix, q0, q1, q2, q3, out_ref, sum_ref, held, sems):
    rows = out_ref.shape[0] // 4
    ins, outs = [], []
    for k, ref in enumerate((q0, q1, q2, q3)):
        ins.append(pltpu.make_async_copy(ref, held.at[k], sems.at[k]))
        at = pl.ds((ix[T] ^ k) * rows, rows)
        outs.append(pltpu.make_async_copy(held.at[k, pl.ds(0, rows)], out_ref.at[at], sems.at[4 + k]))
    for copy in ins:
        copy.start()
    total = jnp.zeros(sum_ref.shape, F32)
    for k, (one, two) in enumerate(zip(ins, outs)):
        one.wait()
        two.start()
        total = total + held[k, rows : rows + 16, :].astype(F32)
    sum_ref[...] = total
    for copy in outs:
        copy.wait()


def join_input(ix, pieces, after):
    rows, width = pieces[0].shape
    rows -= 16
    return call(
        join_input_kernel, "join", ix, (1,), list(pieces), [ANY] * 4,
        [shaped((4 * rows, width)), shaped((16, width), F32)],
        [ANY, pl.BlockSpec((16, width), lambda i, m: (0, 0))],
        [pltpu.VMEM((4, rows + 16, width), LOW), pltpu.SemaphoreType.DMA((8,))], after=after,
    )


def normalize(vector):
    inverse = lax.rsqrt(jnp.mean(vector * vector, axis=-1, keepdims=True) + EPS)
    return (vector * inverse, inverse)


def norm_back(grad_rows, normed, inverse, gain):
    scaled = grad_rows * gain
    return inverse * (scaled - normed * jnp.mean(scaled * normed, axis=-1, keepdims=True))


def tie(ix, value, after):
    return pl.pallas_call(
        lambda *refs: None,
        grid_spec=pltpu.PrefetchScalarGridSpec(
            num_scalar_prefetch=1, grid=(1,), in_specs=[ANY] * (1 + len(after)), out_specs=ANY
        ),
        out_shape=shaped(value.shape, value.dtype),
        input_output_aliases={1: 0},
        cost_estimate=pl.CostEstimate(flops=0, bytes_accessed=0, transcendentals=0),
        name="tie",
    )(ix, value, *after)


def spread(quarter, hold=lambda two: two, late=lambda quarter: quarter):
    two = hold(swap(quarter, TENSOR, 2))
    one = swap(late(quarter), TENSOR, 1)
    three = swap(two, TENSOR, 1)
    return (quarter, one, two, three)


def quarter_copies(t, pieces, held):
    rows = pieces[0].shape[0]
    return [(ref, held.at[pl.ds((t ^ k) * rows, rows)]) for k, ref in enumerate(pieces)]


def join_kernel(ix, q0, q1, q2, q3, out_ref, held, sems):
    rows = q0.shape[0]
    ins, outs = [], []
    for k, ref in enumerate((q0, q1, q2, q3)):
        ins.append(pltpu.make_async_copy(ref, held.at[k], sems.at[k]))
        at = pl.ds((ix[T] ^ k) * rows, rows)
        outs.append(pltpu.make_async_copy(held.at[k], out_ref.at[at], sems.at[4 + k]))
    for copy in ins:
        copy.start()
    for one, two in zip(ins, outs):
        one.wait()
        two.start()
    for copy in outs:
        copy.wait()


def join(ix, pieces, after=()):
    rows, width = pieces[0].shape
    return call(
        join_kernel, "join", ix, (1,), list(pieces), [ANY] * 4,
        shaped((4 * rows, width)), ANY,
        [pltpu.VMEM((4, rows, width), LOW), pltpu.SemaphoreType.DMA((8,))], after=after,
    )


def mine_kernel(ix, *refs):
    count = len(refs) // 2
    rows = refs[count].shape[0]
    at = pl.ds(ix[T] * rows, rows)
    copy_all([(refs[k].at[at], refs[count + k]) for k in range(count)], refs[-1])


def mine(ix, arrays, after):
    count, width = arrays[0].shape
    size = len(arrays)
    return call(
        mine_kernel, "quarter", ix, (1,), list(arrays), [ANY] * size, [shaped((count // 4, width))] * size,
        [pl.BlockSpec((count // 4, width), lambda i, m: (0, 0))] * size, [pltpu.SemaphoreType.DMA((size,))],
        after=after,
    )


def others_kernel(ix, rows_ref, out_ref, sems):
    copy_all([(rows_ref.at[ix[ME] ^ k], out_ref.at[k - 1]) for k in range(1, 4)], sems)


def others(ix, rows, after):
    shape = (3,) + rows.shape[1:]
    return call(
        others_kernel, "others", ix, (1,), [rows], [ANY], shaped(shape),
        pl.BlockSpec(shape, lambda i, m: (0, 0, 0)), [pltpu.SemaphoreType.DMA((3,))], after=after,
    )


def tables_kernel(ix, freq_ref, cos_ref, sin_ref):
    rows = cos_ref.shape[0]
    lane = lax.broadcasted_iota(jnp.int32, (1, 128), 1)
    place = pl.program_id(0) * rows + lax.broadcasted_iota(jnp.int32, (rows, 128), 0)
    angle = place.astype(F32) * freq_ref[0:1, :]
    cos_ref[...] = jnp.cos(angle)
    sin_ref[...] = jnp.where((lane % HEAD_DIM) < HEAD_DIM // 2, -1.0, 1.0) * jnp.sin(angle)


def all_rope_tables(ix, count, after):
    step = 768
    return call(
        tables_kernel, "rope_tables", ix, (count // step,), [rope_freq().reshape(1, 128)],
        [pl.BlockSpec((1, 128), lambda i, m: (0, 0))], [shaped((count, 128), F32)] * 2,
        [pl.BlockSpec((step, 128), lambda i, m: (i, 0))] * 2, after=after,
    )


def hidden_back_kernel(ix, cot_ref, w_ref, out_ref):
    out_ref[...] = against(cot_ref[...], w_ref[...])


def far_rows(array, rows):
    return (lambda m: (m[ME] % 2) ^ 1) if array.shape[0] > rows else (lambda m: 0)


def hidden_back(ix, cotangent, rows, w_down, after=()):
    width = cotangent.shape[1]
    units = w_down.shape[0] // 2
    step = 512
    block = far_rows(cotangent, rows)
    return call(
        hidden_back_kernel, "hidden_back", ix, (units // step,), [cotangent, w_down],
        [
            pl.BlockSpec((rows, width), lambda i, m: (block(m), 0)),
            pl.BlockSpec((step, width), lambda i, m: ((m[ME] % 2) * (units // step) + i, 0)),
        ],
        shaped((rows, units), F32), pl.BlockSpec((rows, step), lambda i, m: (0, i)), after=after,
    )


def feed_kernel(ix, *refs, count):
    pieces = refs[:count]
    wg_ref, wu_ref, hb_ref, wg_rows, wu_rows, rows_ref, hid_ref, gb_ref, ub_ref, keep_ref, send_ref = refs[count:-4]
    held, gate_back, up_back, sems = refs[-4:]
    t = ix[T]
    here = pl.program_id(0)
    rows, units = gate_back.shape
    step = wg_ref.shape[1]
    forward = units // step
    quarter = rows // 4

    @pl.when(here == 0)
    def _():
        if count == 1:
            copy_all([(pieces[0].at[pl.ds((1 - ix[ME] % 2) * rows, rows)], held)], sems)
        else:
            copy_all(quarter_copies(t, pieces, held), sems)
        pltpu.make_async_copy(held, rows_ref, sems.at[4]).start()

    @pl.when(here < forward)
    def _():
        second = held[...]
        gate = dot(second, wg_ref[...])
        up = dot(second, wu_ref[...])
        back = hb_ref[...]
        sig = 0.5 + 0.5 * jnp.tanh(0.5 * gate)
        swish = gate * sig
        hid_ref[...] = (swish * up).astype(LOW)
        gate_low = (back * up * (sig + swish * (1.0 - sig))).astype(LOW)
        up_low = (back * swish).astype(LOW)
        gb_ref[...] = gate_low
        ub_ref[...] = up_low
        columns = pl.ds(pl.multiple_of(here * step, step), step)
        for k in range(4):
            slot = k ^ t
            place = pl.ds(pl.multiple_of(((slot & 1) * 2 + (slot >> 1)) * quarter, quarter), quarter)
            gate_back[place, columns] = gate_low[k * quarter : (k + 1) * quarter]
            up_back[place, columns] = up_low[k * quarter : (k + 1) * quarter]

    @pl.when(here >= forward)
    def _():
        total = against(gate_back[...], wg_rows[...]) + against(up_back[...], wu_rows[...])
        store_quarters(total, keep_ref, send_ref)

    @pl.when(here == pl.num_programs(0) - 1)
    def _():
        pltpu.make_async_copy(held, rows_ref, sems.at[4]).wait()


def feed(ix, pieces, w_gate, w_up, back, after=()):
    rows, width = back.shape[0], pieces[0].shape[1]
    units = w_gate.shape[1] // 2
    step, wide = 256, 512
    forward = units // step
    first = lambda i: jnp.minimum(i, forward - 1)
    then = lambda i: jnp.maximum(i - forward, 0)
    weight = pl.BlockSpec((width, step), lambda i, m: (0, (m[ME] % 2) * forward + first(i)))
    weight_rows = pl.BlockSpec((wide, units), lambda i, m: (then(i), m[ME] % 2))
    block = pl.BlockSpec((rows, step), lambda i, m: (0, first(i)))
    return call(
        functools.partial(feed_kernel, count=len(pieces)), "feed", ix, (forward + width // wide,),
        [*pieces, w_gate, w_up, back, w_gate, w_up],
        [ANY] * len(pieces) + [weight] * 2 + [block] + [weight_rows] * 2,
        [shaped((rows, width))] + [shaped((rows, units))] * 3 + [shaped((2, rows // 4, width))] * 2,
        [ANY, block, block, block] + [pl.BlockSpec((2, rows // 4, wide), lambda i, m: (0, 0, then(i)))] * 2,
        [
            pltpu.VMEM((rows, width), LOW),
            pltpu.VMEM((rows, units), LOW),
            pltpu.VMEM((rows, units), LOW),
            pltpu.SemaphoreType.DMA((5,)),
        ],
        after=after,
    )


def branch_back_kernel(ix, q0, q1, q2, q3, w0, w1, w2, w3, rows_ref, o0, o1, o2, o3, held, sems):
    copy_all(quarter_copies(ix[T], (q0, q1, q2, q3), held), sems)
    keep = pltpu.make_async_copy(held, rows_ref, sems.at[4])
    keep.start()
    weight = jnp.concatenate([w0[...], w1[...], w2[...], w3[...]], axis=0)
    for part in range(3):
        at = slice(part * 256, (part + 1) * 256)
        flat = against(held[at, :], weight).astype(LOW)
        for slot, out in enumerate((o0, o1, o2, o3)):
            out[at, :] = flat[:, slot * 128 : (slot + 1) * 128]
    keep.wait()


def branch_back(ix, pieces, w_out, after):
    rows, width = pieces[0].shape
    rows = 4 * rows

    def heads(slot):
        return pl.BlockSpec((128, width), lambda i, m: (m[ME] ^ slot, 0))

    return call(
        branch_back_kernel, "branch_back", ix, (1,), [*pieces] + [w_out] * 4,
        [ANY] * 4 + [heads(slot) for slot in range(4)],
        [shaped((rows, width))] + [shaped((rows, 128))] * 4,
        [ANY] + [pl.BlockSpec((rows, 128), lambda i, m: (0, 0))] * 4,
        [pltpu.VMEM((rows, width), LOW), pltpu.SemaphoreType.DMA((5,))], after=after,
    )


def wgrad_kernel(ix, l0, l1, r0, r1, out_ref):
    out_ref[0] = (across(l0[...], r0[...]) + across(l1[...], r1[...])).astype(LOW)


def wgrad_kernel(ix, l0, l1, r0, r1, out_ref):
    out_ref[0] = (across(l0[...], r0[...]) + across(l1[...], r1[...])).astype(LOW)


def wgrad(ix, wide, free, name, after=()):
    rows, units = free[0].shape
    share = 256

    def wide_spec(array):
        block = far_rows(array, rows)
        return pl.BlockSpec((rows, share), lambda i, m: (block(m), i ^ (m[ME] % 2)))

    return call(
        wgrad_kernel, name, ix, (8,), [*wide, *free],
        [wide_spec(array) for array in wide] + [pl.BlockSpec((rows, units), lambda i, m: (0, 0))] * 2,
        shaped((8, share, units)), pl.BlockSpec((1, share, units), lambda i, m: (i, 0, 0)), after=after,
    )


def add_blocks_kernel(ix, a_ref, b_ref, *refs):
    total = (a_ref[...].astype(F32) + b_ref[...].astype(F32)).astype(LOW)
    size = refs[0].shape[0]
    for k, ref in enumerate(refs):
        ref[...] = total[k * size : (k + 1) * size]


def add_blocks(ix, one, two, parts, after=()):
    shape = (one.shape[0] // parts,) + one.shape[1:]
    whole = pl.BlockSpec(one.shape, lambda i, m: (0, 0, 0))
    return call(
        add_blocks_kernel, "add_blocks", ix, (1,), [one, two], [whole] * 2,
        [shaped(shape)] * parts, [pl.BlockSpec(shape, lambda i, m: (0, 0, 0))] * parts, after=after,
    )


def one_block_kernel(ix, in_ref, out_ref):
    out_ref[...] = in_ref[...]


def one_block(ix, blocks, which, after=()):
    shape = (1,) + blocks.shape[1:]
    return call(
        one_block_kernel, "one_block", ix, (1,), [blocks],
        [pl.BlockSpec(shape, lambda i, m: (which, 0, 0))], shaped(shape),
        pl.BlockSpec(shape, lambda i, m: (0, 0, 0)), after=after,
    )


def halves_kernel(ix, own_ref, other_ref, out_ref, *, axis):
    which = ix[ME] % 2
    for place, ref in ((which, own_ref), (1 - which, other_ref)):
        value = ref[...].astype(F32)
        if axis == 0:
            value = value.T
        size = value.shape[axis]
        at = pl.ds(pl.multiple_of(place * size, size), size)
        if axis == 0:
            out_ref[at, :] = value
        else:
            out_ref[:, at] = value


def halves(ix, blocks, other, axis, after=()):
    share, units = blocks.shape[1:]
    shape = (2 * units, share) if axis == 0 else (share, 2 * units)
    whole = lambda i, m: (0, 0)
    return call(
        functools.partial(halves_kernel, axis=axis), "halves", ix, (1,), [blocks, other],
        [pl.BlockSpec((None, share, units), lambda i, m: (0, 0, 0))] * 2,
        shaped(shape, F32), pl.BlockSpec(shape, whole), after=after,
    )


def out_wgrad_kernel(ix, a0, a1, a2, a3, rows_ref, own_ref, far_ref, held):
    for slot, ref in enumerate((a0, a1, a2, a3)):
        at = pl.ds(pl.multiple_of((slot ^ ix[ME]) * 128, 128), 128)
        held[at, :] = across(ref[...], rows_ref[...]).astype(LOW)
    for half, out in enumerate((own_ref, far_ref)):

        @pl.when(pl.program_id(0) // 4 == half)
        def _():
            out[0] = held[...]


def out_wgrad(ix, mixed, rows, after=()):
    count, width = rows.shape
    share = 256
    return call(
        out_wgrad_kernel, "out_wgrad", ix, (width // share,), [*mixed, rows],
        [pl.BlockSpec((count, 128), lambda i, m: (0, 0))] * 4
        + [pl.BlockSpec((count, share), lambda i, m: (0, i ^ (m[DP] * 4 + m[ME])))],
        [shaped((4, 512, share))] * 2,
        [
            pl.BlockSpec((1, 512, share), lambda i, m: (jnp.minimum(i, 3), 0, 0)),
            pl.BlockSpec((1, 512, share), lambda i, m: (jnp.maximum(i - 4, 0), 0, 0)),
        ],
        [pltpu.VMEM((512, share), LOW)], after=after,
    )


def project_wgrad_kernel(ix, first_ref, f0, f1, f2, f3, b0, b1, b2, b3, own_ref, far_ref, held, total, sems):
    me, t = ix[ME], ix[T]
    turn = pl.program_id(0)
    quarter = f0.shape[1]

    def copies(slot):
        if slot == 0:
            return [pltpu.make_async_copy(first_ref, held.at[0], sems.at[0, 0])]
        return [
            pltpu.make_async_copy(
                ref.at[slot - 1], held.at[slot, pl.ds((t ^ k) * quarter, quarter)], sems.at[slot, k]
            )
            for k, ref in enumerate((f0, f1, f2, f3))
        ]

    @pl.when(turn == 0)
    def _():
        for slot in range(4):
            for copy in copies(slot):
                copy.start()

    for slot, back in enumerate((b0, b1, b2, b3)):

        @pl.when(turn == slot)
        def _():
            for copy in copies(slot):
                copy.wait()
            for block in range(8):
                at = slice(block * 256, (block + 1) * 256)
                part = across(held[slot, :, at], back[...])
                if slot == 0:
                    total[at, :] = part
                elif slot < 3:
                    total[at, :] += part
                else:
                    done = (total[at, :] + part).astype(LOW)

                    @pl.when(ix[DP] == block // 4)
                    def _():
                        own_ref[(block % 4) ^ me] = done

                    @pl.when(ix[DP] != block // 4)
                    def _():
                        far_ref[(block % 4) ^ me] = done


def project_wgrad(ix, first_in, far, back, after=()):
    rows, width = first_in.shape
    whole = lambda i, m: (0, 0)
    return call(
        project_wgrad_kernel, "project_wgrad", ix, (4,), [first_in, *far, *back],
        [ANY] * 5 + [pl.BlockSpec((rows, 384), whole)] * 4,
        [shaped((4, 256, 384))] * 2, [pl.BlockSpec((4, 256, 384), lambda i, m: (0, 0, 0))] * 2,
        [
            pltpu.VMEM((4, rows, width), LOW),
            pltpu.VMEM((width, 384), F32),
            pltpu.SemaphoreType.DMA((4, 4)),
        ],
        after=after,
    )


def project_last_kernel(ix, p0, p1, p2, p3, q_ref, k_ref, v_ref):
    for slot, ref in enumerate((p0, p1, p2, p3)):
        at = pl.ds(pl.multiple_of((slot ^ ix[ME]) * 128, 128), 128)
        for place, out in enumerate((q_ref, k_ref, v_ref)):
            out[:, at] = ref[:, place * 128 : (place + 1) * 128].astype(F32)


def project_last(ix, pieces):
    share = pieces[0].shape[0]
    whole = lambda i, m: (0, 0)
    return call(
        project_last_kernel, "project_last", ix, (1,), list(pieces),
        [pl.BlockSpec((share, 384), whole)] * 4,
        [shaped((share, 512), F32)] * 3, [pl.BlockSpec((share, 512), whole)] * 3,
    )


def over_ctx(slots):
    return [slots[0]] + [swap(slots[k], CTX, k) for k in range(1, 4)]


def per_device(
    dp_size, tokens, attn_gain, w_query, w_key, w_value, w_out, mlp_gain, w_gate, w_up, w_down, cotangent
):
    rows_here, width = tokens.shape
    share = width // (4 * dp_size)
    me, t, d = lax.axis_index(CTX), lax.axis_index(TENSOR), lax.axis_index("dp")
    two_dp = dp_size == 2
    ix = jnp.stack([me, t, d if two_dp else jnp.zeros_like(d)]).astype(jnp.int32)
    order = me ^ jnp.arange(4)
    projections = (w_query, w_key, w_value)
    attn_gain, mlp_gain = attn_gain.reshape(1, -1), mlp_gain.reshape(1, -1)

    cot_mine = lax.dynamic_slice_in_dim(cotangent, t * (rows_here // 4), rows_here // 4, 0)
    tables = rope_tables(me * rows_here + jnp.arange(rows_here, dtype=jnp.int32))
    first_in, *slots = project(ix, tokens, attn_gain, tables, projections)
    pieces = over_ctx(slots)

    back_own = hidden_back(ix, cotangent, rows_here, w_down, (slots[0],))
    all_tables = all_rope_tables(ix, 4 * rows_here, (back_own,))
    (first_mine,) = mine(ix, [first_in], (all_tables[0],))
    cot_mine = tie(ix, cot_mine, (*pieces[1:], first_mine))
    cot_both = lax.all_gather(cot_mine, ("lo", *TENSOR), axis=0, tiled=True)

    *mixed_slots, raw, lse = attend(ix, pieces, (first_mine,))
    mixed = over_ctx(mixed_slots)
    keep, send = join_heads(ix, mixed, w_out, (cot_both,))
    core = swap(send, TENSOR, 1)
    low = sums_to_send(ix, [(keep, 1), (core, 1)])
    middle, second_mine = rows_call(
        middle_kernel, "middle", ix, [(keep, 0), (core, 0), swap(low, TENSOR, 2)], [tokens, mlp_gain], [F32, LOW]
    )

    second_both = lax.all_gather(second_mine, ("lo", *TENSOR), axis=0, tiled=True)
    back_far = hidden_back(ix, cot_both, rows_here, w_down, (second_mine,))
    own_pieces = spread(second_mine, lambda two: tie(ix, two, (back_far,)))
    second_own, hid_own, gb_own, ub_own, keep_own, send = feed(ix, own_pieces, w_gate, w_up, back_own)
    first_all = lax.all_gather(tie(ix, first_mine, (hid_own,)), CTX, axis=0, tiled=False)
    core_own = swap(send, TENSOR, 1)
    second_far, hid_far, gb_far, ub_far, keep, send = feed(ix, [second_both], w_gate, w_up, back_far, (hid_own,))

    seconds = (second_own, second_far)

    def over_pairs(part):
        return lax.psum_scatter(part, ("dp", "hi"), scatter_dimension=0, tiled=True) if two_dp else part

    core = swap(send, TENSOR, 1)
    part_down = wgrad(ix, (cotangent, cot_both), (hid_own, hid_far), "wgrad_down")
    sum_down = over_pairs(part_down)
    low = sums_to_send(ix, [(keep, 1), (core, 1)], (part_down,))
    far_y = swap(low, TENSOR, 2)
    down_far = feed_down(ix, hid_far, w_down, (low,))
    low = sums_to_send(ix, [(keep, 0), (core, 0), far_y], (down_far[0],))
    far_z = swap(low, CTX, 1)
    low = sums_to_send(ix, [(keep_own, 1), (core_own, 1)], (low,))
    own_sums = [(keep_own, 0), (core_own, 0), swap(low, TENSOR, 2)]
    core_far = swap(down_far[1], TENSOR, 1)
    down_own = feed_down(ix, hid_own, w_down, (low,))
    low = sums_to_send(ix, [(down_far[0], 1), (core_far, 1)], (down_own[0],))
    far_down = [(down_far[0], 0), (core_far, 0), swap(low, TENSOR, 2)]
    middle_grad, branch_mine, mlp_gain_part = rows_call(
        middle_back_kernel, "middle_back", ix, [*own_sums, far_z, middle], [cotangent, mlp_gain], [F32, LOW], 1,
        (low,),
    )
    part_gate = wgrad(ix, seconds, (gb_own, gb_far), "wgrad_gate", (branch_mine,))
    sum_gate = over_pairs(part_gate)
    core_own = swap(tie(ix, down_own[1], (branch_mine,)), TENSOR, 1)
    branch_low, *slots = branch_back(
        ix, spread(branch_mine, lambda two: tie(ix, two, (part_gate,))), w_out, (part_gate,)
    )
    upstreams = over_ctx(slots)
    first_far = others(ix, first_all, (branch_low,))
    out_own, out_far = out_wgrad(ix, mixed, branch_low, (first_far,))
    low = sums_to_send(ix, [(down_own[0], 1), (core_own, 1)], (out_own,))
    own_y = swap(low, TENSOR, 2)

    def for_partner(blocks, after):
        return swap(blocks[1:] if after is None else one_block(ix, blocks, 1, after), CTX, 1)

    arrived = [far_down[2], own_y]
    if two_dp:
        out_other = swap(out_far, "dp", 1)
        down_other = for_partner(sum_down, (low,))
        arrived += [out_other, down_other]
    back_slots = attend_back(ix, pieces, upstreams, raw, lse, all_tables, (low,))
    back = over_ctx(back_slots)

    arrived = (back_slots[0], *arrived)
    first_spread = spread(first_far, lambda two: tie(ix, two, arrived), lambda quarter: tie(ix, quarter, arrived))
    qkv_own, qkv_far = project_wgrad(ix, first_in, first_spread, back_slots)
    far_low = sums_to_send(ix, far_down, (qkv_own,))
    part_up = wgrad(ix, seconds, (ub_own, ub_far), "wgrad_up", (far_low,))
    sum_up = over_pairs(tie(ix, part_up, back[1:]))
    token = part_up
    if two_dp:
        out_part = add_blocks(ix, out_own, out_other, 2, (part_up,))
        down_grad = halves(ix, sum_down, down_other, 0, (out_part[0],))
        token = down_grad
    keep, send = project_back(ix, back, projections, (token,))
    core = swap(send, TENSOR, 1)
    low = sums_to_send(ix, [(keep, 1), (core, 1)])
    low_y = swap(low, TENSOR, 2)
    far_z = swap(tie(ix, far_low, (low,)), CTX, 1)
    token = low
    if two_dp:
        gate_low = one_block(ix, sum_gate, 1, (low,))
        token = gate_low
    input_mine = input_back(ix, keep, core, low_y, middle_grad, tokens, attn_gain, mlp_gain_part, (token,))
    input_pieces = spread(input_mine)
    token = input_mine
    if two_dp:
        (qkv_part,) = add_blocks(ix, qkv_own, swap(qkv_far, "dp", 1), 1, (input_mine,))
        out_z = swap(tie(ix, out_part[1], (keep,)), CTX, 2)
        token = qkv_part
    (output_mine,) = rows_call(
        output_kernel, "output", ix, [(down_own[0], 0), (core_own, 0), own_y, far_z, middle], [], [LOW], after=(token,)
    )
    input_grad, gains = join_input(ix, input_pieces, (output_mine,))
    output_pieces = spread(output_mine, late=lambda quarter: tie(ix, quarter, (input_grad,)))
    if two_dp:
        qkv_parts = over_ctx(qkv_part)
        out_part = add_blocks(ix, out_part[0], out_z, 2, (input_grad,))
        out_other = swap(out_part[1], CTX, 1)
        gate_grad = halves(ix, sum_gate, swap(gate_low, CTX, 1), 1, (out_part[0],))
        up_low = one_block(ix, sum_up, 1, (gate_grad,))
        output = join(ix, output_pieces, (up_low,))
        up_grad = halves(ix, sum_up, swap(up_low, CTX, 1), 1, (output,))
        out_grad = out_part[0][0].astype(F32) + out_other[0].astype(F32)
    else:
        output = join(ix, output_pieces)

        def scattered(blocks, axis):
            blocks = jnp.moveaxis(blocks, 0, axis)
            shape = blocks.shape[:axis] + (width,) + blocks.shape[axis + 2 :]
            part = lax.psum_scatter(blocks.reshape(shape), "dp", scatter_dimension=axis, tiled=True)
            shape = part.shape[:axis] + (4, share) + part.shape[axis + 1 :]
            return jnp.moveaxis(part.reshape(shape), axis, 0)

        def in_order(blocks):
            return blocks.reshape(2, 4, *blocks.shape[1:])[:, order].reshape(blocks.shape)

        grads = []
        low_bit = me % 2 ^ jnp.arange(2)
        for k, blocks in enumerate((sum_down, sum_gate, sum_up)):
            blocks = blocks.reshape(4, 2, *blocks.shape[1:])[:, low_bit].reshape(blocks.shape)
            part = scattered(blocks, 0)[order].astype(F32)
            part = (part[:2] + swap(part[2:].astype(LOW), CTX, 2).astype(F32)).astype(LOW)
            grads.append(halves(ix, part, for_partner(part, None), min(k, 1)))
        down_grad, gate_grad, up_grad = grads
        qkv_parts = over_ctx(scattered(in_order(jnp.concatenate([qkv_own, qkv_far])), 0)[order])
        out_part = scattered(in_order(jnp.concatenate([out_own, out_far])), 1)[order]
        out_part = out_part[:2].astype(F32) + swap(out_part[2:], CTX, 2).astype(F32)
        out_grad = out_part[0] + swap(out_part[1].astype(LOW), CTX, 1).astype(F32)
    qkv = project_last(ix, qkv_parts)

    gains = gains[:2]
    if two_dp:
        halved = gains.reshape(2, 2, width // 2)[:, d ^ jnp.arange(2)]
        gains = halved[:, 0] + swap(halved[:, 1], "dp", 1)
    else:
        gains = lax.psum_scatter(gains, "dp", scatter_dimension=1, tiled=True)
    gains = sum(over_ctx(gains.reshape(2, 4, share).transpose(1, 0, 2)[order]))

    return (
        output,
        input_grad,
        gains[0],
        qkv[0],
        qkv[1],
        qkv[2],
        out_grad,
        gains[1],
        gate_grad,
        up_grad,
        down_grad,
    )


def solution(mesh):
    dp_size = mesh.shape["dp"]
    mesh = jax.sharding.Mesh(mesh.devices.reshape(dp_size, 2, 2, 2, 2), ("dp", *CTX, *TENSOR))
    rows, tensor = ("dp", *CTX), TENSOR
    columns = P(None, tensor)
    in_specs = (
        P(rows, None), P(), columns, columns, columns, P(tensor, None),
        P(), columns, columns, P(tensor, None), P(rows, None),
    )
    out_specs = (
        P(rows, None), P(rows, None), P(rows), P(rows, tensor), P(rows, tensor), P(rows, tensor),
        P(tensor, rows), P(rows), P(rows, tensor), P(rows, tensor), P(tensor, rows),
    )
    return jax.shard_map(
        functools.partial(per_device, dp_size),
        mesh=mesh,
        in_specs=in_specs,
        out_specs=out_specs,
        check_vma=False,
    )
```

time: 775 us -> 717 us (0.925)
  Pallas kernels: 384 us -> 346 us
  waiting for transfers between devices: 244 us -> 231 us
    pallas_call x45 -> x44, Pallas kernels: 375 us -> 339 us  [call(): pl.pallas_call(body, grid_spec=pltpu.PrefetchScalarGridSpec(num_scalar_pr...]
    unnamed x94 -> x23, local copies, waits for them, and re-layouts: 22.1 us -> 13.3 us
    ppermute x67 -> x55, waiting for transfers between devices: 236 us -> 231 us  [swap(): return lax.ppermute(value, axis, [(i, i ^ distance) for i in range(size)])]
    ppermute x67 -> x55, starting transfers between devices: 88.6 us -> 86.3 us  [swap(): return lax.ppermute(value, axis, [(i, i ^ distance) for i in range(size)])]
  transfers between devices with their start and end apart: 73 -> 61, of which waited for: 31 -> 30; matrix products, arithmetic and copies ran while one was open for 1% -> 3% of each run, Pallas kernels for 43% -> 45%
where the time goes in v3:
time: 717 us; the launch traced here: 709 us
  Pallas kernels  346 us (48%)
  waiting for transfers between devices  231 us (32%)
  starting transfers between devices  87.4 us (12%)
  local copies, waits for them, and re-layouts  20.9 us (3%)
  between operations  14.8 us (2%)
  other arithmetic  8.14 us (1%)
    pallas_call x44, Pallas kernels, call(): pl.pallas_call(body, grid_spec=pltpu.PrefetchScalarGridSpec(num_scalar_pr...  339 us
    ppermute x55, waiting for transfers between devices, swap(): return lax.ppermute(value, axis, [(i, i ^ distance) for i in range(size)])  231 us
    ppermute x55, starting transfers between devices, swap(): return lax.ppermute(value, axis, [(i, i ^ distance) for i in range(size)])  86.3 us
  transfers between devices with their start and end apart: 61, of which 30 were waited for; matrix products, arithmetic and copies ran while one was open for 3% of the time, Pallas kernels for 45%

profile of v3, /device:TPU:0, one launch (start us, length us, event | category | flops | bytes accessed | tf_op | source)
XLA Modules:
  0.0 708.6 jit_solution(1515091822098507646)
XLA Ops:
  10.5 11.2 %project.1 = (bf16[768,2048]{1,0:T(8,128)(2,1)}, bf16[768,384]{1,0:T(8,128)(2,1)}, bf16[768,384]{1,0:T(8,128)(2,1)}, bf16[768,384]{1,0:T(8,128)(2,1)}, bf16[768,384]{1,0:T(8,128)(2,1)}) custom-call(s32[3]{0:T(128)} %pad_add_fusion.index_ref.refs_0_, bf16[768,2048]{1,0:T(8,128)(2,1)} %refs_4_.13, f32[1,2048]{1,0:T(1,128)} %bitcast.53, ...), custom_call_target="tpu_custom_call" | custom-call | bytes 80740352 | tf_op jit(solution)/shard_map/project/pallas_call | solution.py:58
  21.7 3.0 collective-permute-start
  27.3 8.0 %hidden_back.2.refs_1_.refs_6_ = f32[768,1024]{1,0:T(8,128)} custom-call(s32[3]{0:T(128)} %pad_add_fusion.index_ref.refs_0_, bf16[768,2048]{1,0:T(8,128)(2,1)} %refs_5_.11, bf16[2048,2048]{1,0:T(8,128)(2,1)} %refs_1_.9, bf16[768,384]{1,0:T(8,128)(2,1)} %get-tuple-element.71.refs_2_.refs_0_), custom_call_target="tpu_custom_call" | custom-call | bytes 62390272 | tf_op jit(solution)/shard_map/hidden_back/pallas_call | solution.py:58
  35.4 8.0 %rope_tables.1 = (f32[3072,128]{1,0:T(8,128)}, f32[3072,128]{1,0:T(8,128)}) custom-call(s32[3]{0:T(128)} %pad_add_fusion.index_ref.refs_0_, f32[1,128]{1,0:T(1,128)} %bitcast.57, f32[768,1024]{1,0:T(8,128)} %hidden_back.2.refs_1_.refs_6_), custom_call_target="tpu_custom_call" | custom-call | bytes 58720256 | tf_op jit(solution)/shard_map/rope_tables/pallas_call | solution.py:58
  50.3 17.2 %collective-permute-done.1.refs_2_.refs_3_ = bf16[768,384]{1,0:T(8,128)(2,1)} collective-permute-done((bf16[768,384]{1,0:T(8,128)(2,1)}, bf16[768,384]{1,0:T(8,128)(2,1)}, u32[]{:S(2)}, u32[]{:S(2)}) %collective-permute-start.1) | collective-permute-done | bytes 589856 | tf_op jit(solution)/shard_map/ppermute | solution.py:33
  68.5 27.7 %attend.1 = (bf16[768,128]{1,0:T(8,128)(2,1)}, bf16[768,128]{1,0:T(8,128)(2,1)}, bf16[768,128]{1,0:T(8,128)(2,1)}, bf16[768,128]{1,0:T(8,128)(2,1)}, f32[3072,128]{1,0:T(8,128)}, /*index=5*/f32[4,16,768]{2,1,0:T(8,128)}) custom-call(s32[3]{0:T(128)} %pad_add_fusion.index_ref.refs_0_, bf16[768,384]{1,0:T(8,128)(2,1)} %get-tuple-element.71.refs_2_.refs_0_, ...), custom_call_target="tpu_custom_call" | custom-call | bytes 205520896 | tf_op jit(solution)/shard_map/attend/pallas_call | solution.py:58
  96.2 11.8 %collective-permute-start.3 = (bf16[768,128]{1,0:T(8,128)(2,1)}, bf16[768,128]{1,0:T(8,128)(2,1)}, u32[]{:S(2)}, u32[]{:S(2)}) collective-permute-start(bf16[768,128]{1,0:T(8,128)(2,1)} %get-tuple-element.78), channel_id=1, source_target_pairs={{0,4},{4,0},{8,12},{12,8},{1,5},{5,1},{9,13},{13,9},{2,6},{6,2},{1... | collective-permute-start | bytes 589832 | tf_op jit(solution)/shard_map/ppermute | solution.py:33
  110.5 11.3 %collective-permute-done.3.refs_1_ = bf16[768,128]{1,0:T(8,128)(2,1)} collective-permute-done((bf16[768,128]{1,0:T(8,128)(2,1)}, bf16[768,128]{1,0:T(8,128)(2,1)}, u32[]{:S(2)}, u32[]{:S(2)}) %collective-permute-start.3) | collective-permute-done | bytes 196640 | tf_op jit(solution)/shard_map/ppermute | solution.py:33
  122.3 7.0 collective-permute-done.5.refs_3_
  129.4 6.3 join_heads.1
  135.7 3.7 collective-permute-done.6.refs_1_
  144.3 18.2 %collective-permute-done.7.refs_2_ = bf16[192,2048]{1,0:T(8,128)(2,1)} collective-permute-done((bf16[192,2048]{1,0:T(8,128)(2,1)}, bf16[192,2048]{1,0:T(8,128)(2,1)}, u32[]{:S(2)}, u32[]{:S(2)}) %collective-permute-start.7) | collective-permute-done | bytes 786464 | tf_op jit(solution)/shard_map/ppermute | solution.py:33
  162.4 3.8 middle.1
  168.1 8.1 %hidden_back.3.refs_2_.refs_3_ = f32[768,1024]{1,0:T(8,128)} custom-call(s32[3]{0:T(128)} %pad_add_fusion.index_ref.refs_0_, bf16[1536,2048]{1,0:T(8,128)(2,1)} %all-gather.5.cloned.1.call-done.refs_8_.refs_0_.refs_1_, bf16[2048,2048]{1,0:T(8,128)(2,1)} %refs_1_.9, bf16[192,2048]{1,0:T(8,128)(2,1)} %get-tuple-element.83.refs_2_.refs_0_), custom_call_target="tpu_custom_call" | custom-call | bytes 62390272 | tf_op jit(solution)/shard_map/hidden_back/pallas_call | solution.py:58
  176.3 21.3 %collective-permute-done.9.refs_1_ = bf16[192,2048]{1,0:T(8,128)(2,1)} collective-permute-done((bf16[192,2048]{1,0:T(8,128)(2,1)}, bf16[192,2048]{1,0:T(8,128)(2,1)}, u32[]{:S(2)}, u32[]{:S(2)}) %collective-permute-start.9) | collective-permute-done | bytes 786464 | tf_op jit(solution)/shard_map/ppermute | solution.py:33
  201.1 22.9 %feed.2 = (bf16[768,2048]{1,0:T(8,128)(2,1)}, bf16[768,1024]{1,0:T(8,128)(2,1)}, bf16[768,1024]{1,0:T(8,128)(2,1)}, bf16[768,1024]{1,0:T(8,128)(2,1)}, bf16[2,19...) custom-call(s32[3]{0:T(128)} %pad_add_fusion.index_ref.refs_0_, bf16[192,2048]{1,0:T(8,128)(2,1)} %get-tuple-element.83.refs_2_.refs_0_, ...), custom_call_target="tpu_custom_call" | custom-call | bytes 176160768 | tf_op jit(solution)/shard_map/feed/pallas_call | solution.py:58
  225.1 22.9 %feed.3 = (bf16[768,2048]{1,0:T(8,128)(2,1)}, bf16[768,1024]{1,0:T(8,128)(2,1)}, bf16[768,1024]{1,0:T(8,128)(2,1)}, bf16[768,1024]{1,0:T(8,128)(2,1)}, bf16[2,19...) custom-call(s32[3]{0:T(128)} %pad_add_fusion.index_ref.refs_0_, ...), custom_call_target="tpu_custom_call" | custom-call | bytes 176160768 | tf_op jit(solution)/shard_map/feed/pallas_call | solution.py:58
  248.0 12.9 %wgrad_down.1.refs_2_ = bf16[8,256,1024]{2,1,0:T(8,128)(2,1)} custom-call(s32[3]{0:T(128)} %pad_add_fusion.index_ref.refs_0_, bf16[768,2048]{1,0:T(8,128)(2,1)} %refs_5_.11, bf16[1536,2048]{1,0:T(8,128)(2,1)} %all-gather.5.cloned.1.call-done.refs_8_.refs_0_.refs_1_, bf16[768,1024]{1,0:T(8,128)(2,1)} %get-tuple-element.84.refs_6_.refs_2_.refs_0_, ...), custom_call_target="tpu_custom_call" | custom-call | bytes 102760448 | tf_op jit(solution)/shard_map/wgrad_down/pallas_call | solution.py:58
  262.8 3.8 collective-permute-done.12.refs_1_
  272.3 8.7 %feed_down.2 = (bf16[2,192,2048]{2,1,0:T(8,128)(2,1)}, bf16[2,192,2048]{2,1,0:T(8,128)(2,1)}) custom-call(s32[3]{0:T(128)} %pad_add_fusion.index_ref.refs_0_, bf16[768,1024]{1,0:T(8,128)(2,1)} %get-tuple-element.89.refs_3_.refs_0_, bf16[2048,2048]{1,0:T(8,128)(2,1)} %refs_1_.9, bf16[192,2048]{1,0:T(8,128)(2,1)} %sums.9.refs_2_), custom_call_target="tpu_custom_call" | custom-call | bytes 66060288 | tf_op jit(solution)/shard_map/feed_down/pallas_call | solution.py:58
  281.1 9.4 %collective-permute-done.13.refs_2_ = bf16[192,2048]{1,0:T(8,128)(2,1)} collective-permute-done((bf16[192,2048]{1,0:T(8,128)(2,1)}, bf16[192,2048]{1,0:T(8,128)(2,1)}, u32[]{:S(2)}, u32[]{:S(2)}) %collective-permute-start.13) | collective-permute-done | bytes 786464 | tf_op jit(solution)/shard_map/ppermute | solution.py:33
  290.4 3.2 sums.10.refs_2_
  293.6 3.3 sums.11.refs_2_
  298.6 8.8 %feed_down.3 = (bf16[2,192,2048]{2,1,0:T(8,128)(2,1)}, bf16[2,192,2048]{2,1,0:T(8,128)(2,1)}) custom-call(s32[3]{0:T(128)} %pad_add_fusion.index_ref.refs_0_, bf16[768,1024]{1,0:T(8,128)(2,1)} %get-tuple-element.84.refs_6_.refs_2_.refs_0_, bf16[2048,2048]{1,0:T(8,128)(2,1)} %refs_1_.9, bf16[192,2048]{1,0:T(8,128)(2,1)} %sums.11.refs_2_), custom_call_target="tpu_custom_call" | custom-call | bytes 66060288 | tf_op jit(solution)/shard_map/feed_down/pallas_call | solution.py:58
  310.3 5.5 collective-permute-done.14.refs_2_
  315.9 17.1 %collective-permute-done.15.refs_3_ = bf16[192,2048]{1,0:T(8,128)(2,1)} collective-permute-done((bf16[192,2048]{1,0:T(8,128)(2,1)}, bf16[192,2048]{1,0:T(8,128)(2,1)}, u32[]{:S(2)}, u32[]{:S(2)}) %collective-permute-start.15) | collective-permute-done | bytes 786464 | tf_op jit(solution)/shard_map/ppermute | solution.py:33
  333.0 5.3 middle_back.1
  338.3 13.1 %wgrad_gate.1.refs_2_.refs_8_ = bf16[8,256,1024]{2,1,0:T(8,128)(2,1)} custom-call(s32[3]{0:T(128)} %pad_add_fusion.index_ref.refs_0_, bf16[768,2048]{1,0:T(8,128)(2,1)} %get-tuple-element.96.refs_0_, bf16[768,2048]{1,0:T(8,128)(2,1)} %get-tuple-element.97.refs_1_, bf16[768,1024]{1,0:T(8,128)(2,1)} %get-tuple-element.98.refs_2_, ...), custom_call_target="tpu_custom_call" | custom-call | bytes 102760448 | tf_op jit(solution)/shard_map/wgrad_gate/pallas_call | solution.py:58
  352.9 17.2 %collective-permute-done.19.refs_1_ = bf16[192,2048]{1,0:T(8,128)(2,1)S(1)} collective-permute-done((bf16[192,2048]{1,0:T(8,128)(2,1)S(1)}, bf16[192,2048]{1,0:T(8,128)(2,1)S(1)}, u32[]{:S(2)}, u32[]{:S(2)}) %collective-permute-start.19) | collective-permute-done | bytes 786464 | tf_op jit(solution)/shard_map/ppermute | solution.py:33
  374.3 6.8 branch_back.1
  381.1 3.8 others.1.refs_5_.refs_1_
  385.5 8.5 %out_wgrad.1 = (bf16[4,512,256]{2,1,0:T(8,128)(2,1)}, bf16[4,512,256]{2,1,0:T(8,128)(2,1)}) custom-call(s32[3]{0:T(128)} %pad_add_fusion.index_ref.refs_0_, bf16[768,128]{1,0:T(8,128)(2,1)} %get-tuple-element.77.refs_0_, bf16[768,128]{1,0:T(8,128)(2,1)} %collective-permute-done.3.refs_1_, bf16[768,128]{1,0:T(8,128)(2,1)} %collective-permute-done.4.refs_2_, ...), custom_call_target="tpu_custom_call" | custom-call | bytes 62390272 | tf_op jit(solution)/shard_map/out_wgrad/pallas_call | solution.py:58
  401.9 3.5 collective-permute-done.23.refs_5_
  406.8 15.3 %collective-permute-done.24.refs_6_ = bf16[768,128]{1,0:T(8,128)(2,1)} collective-permute-done((bf16[768,128]{1,0:T(8,128)(2,1)}, bf16[768,128]{1,0:T(8,128)(2,1)}, u32[]{:S(2)}, u32[]{:S(2)}) %collective-permute-start.24) | collective-permute-done | bytes 196640 | tf_op jit(solution)/shard_map/ppermute | solution.py:33
  424.6 6.7 collective-permute-done.25.refs_7_
  431.4 10.0 %collective-permute-start.27 = (bf16[1,256,1024]{2,1,0:T(8,128)(2,1)}, bf16[1,256,1024]{2,1,0:T(8,128)(2,1)}, u32[]{:S(2)}, u32[]{:S(2)}) collective-permute-start(bf16[1,256,1024]{2,1,0:T(8,128)(2,1)} %one_block.3), channel_id=1, source_target_pairs={{0,4},{4,0},{8,12},{12,8},{1,5},{5,1},{9,13},{13,9},{2,6},{6,2},{1... | collective-permute-start | bytes 1572872 | tf_op jit(solution)/shard_map/ppermute | solution.py:33
  441.3 3.5 copy.44.refs_1_
  444.8 39.8 %attend_back.1 = (bf16[768,384]{1,0:T(8,128)(2,1)}, bf16[768,384]{1,0:T(8,128)(2,1)}, bf16[768,384]{1,0:T(8,128)(2,1)}, bf16[768,384]{1,0:T(8,128)(2,1)}) custom-call(s32[3]{0:T(128)} %pad_add_fusion.index_ref.refs_0_, bf16[768,384]{1,0:T(8,128)(2,1)} %get-tuple-element.71.refs_2_.refs_0_, bf16[768,384]{1,0:T(8,128)(2,1)} %collective-permute-done.refs_1_.refs_2_, ...), custom_call_target="tpu_custom_call" | custom-call | bytes 293601280 | tf_op jit(solution)/shard_map/attend_back/pallas_call | solution.py:58
  487.5 3.5 collective-permute-start.33
  493.7 14.7 %project_wgrad.1 = (bf16[4,256,384]{2,1,0:T(8,128)(2,1)}, bf16[4,256,384]{2,1,0:T(8,128)(2,1)}) custom-call(s32[3]{0:T(128)} %pad_add_fusion.index_ref.refs_0_, bf16[768,2048]{1,0:T(8,128)(2,1)} %get-tuple-element.75.refs_0_, bf16[3,192,2048]{2,1,0:T(8,128)(2,1)} %others.1.refs_5_.refs_1_, bf16[3,192,2048]{2,1,0:T(8,128)(2,1)} %collective-permute-done.28.refs_2_, ...), custom_call_target="tpu_custom_call" | custom-call | bytes 95420416 | tf_op jit(solution)/shard_map/project_wgrad/pallas_call | solution.py:58
  508.4 3.2 sums.14.refs_4_.refs_1_
  511.5 12.9 %wgrad_up.1.refs_2_ = bf16[8,256,1024]{2,1,0:T(8,128)(2,1)} custom-call(s32[3]{0:T(128)} %pad_add_fusion.index_ref.refs_0_, bf16[768,2048]{1,0:T(8,128)(2,1)} %get-tuple-element.96.refs_0_, bf16[768,2048]{1,0:T(8,128)(2,1)} %get-tuple-element.97.refs_1_, bf16[768,1024]{1,0:T(8,128)(2,1)} %get-tuple-element.115.refs_2_, ...), custom_call_target="tpu_custom_call" | custom-call | bytes 102760448 | tf_op jit(solution)/shard_map/wgrad_up/pallas_call | solution.py:58
  524.4 4.7 copy.48.refs_1_
  530.1 3.3 add_blocks.3
  533.4 3.5 halves.3.refs_16_
  536.9 11.2 %project_back.1 = (bf16[2,192,2048]{2,1,0:T(8,128)(2,1)}, bf16[2,192,2048]{2,1,0:T(8,128)(2,1)}) custom-call(s32[3]{0:T(128)} %pad_add_fusion.index_ref.refs_0_, bf16[768,384]{1,0:T(8,128)(2,1)} %get-tuple-element.109.refs_2_.refs_5_.refs_0_, bf16[768,384]{1,0:T(8,128)(2,1)} %collective-permute-done.31.refs_1_.refs_2_, ...), custom_call_target="tpu_custom_call" | custom-call | bytes 80740352 | tf_op jit(solution)/shard_map/project_back/pallas_call | solution.py:58
  548.2 3.7 collective-permute-done.34.refs_1_
  559.0 15.7 %collective-permute-done.37.refs_2_ = bf16[192,2048]{1,0:T(8,128)(2,1)} collective-permute-done((bf16[192,2048]{1,0:T(8,128)(2,1)}, bf16[192,2048]{1,0:T(8,128)(2,1)}, u32[]{:S(2)}, u32[]{:S(2)}) %collective-permute-start.37) | collective-permute-done | bytes 786464 | tf_op jit(solution)/shard_map/ppermute | solution.py:33
  574.7 5.0 input_back.1.refs_2_.refs_0_
  582.6 12.2 %collective-permute-start.35 = (bf16[192,2048]{1,0:T(8,128)(2,1)}, bf16[192,2048]{1,0:T(8,128)(2,1)}, u32[]{:S(2)}, u32[]{:S(2)}) collective-permute-start(bf16[192,2048]{1,0:T(8,128)(2,1)} %tie.18), channel_id=1, source_target_pairs={{0,4},{4,0},{8,12},{12,8},{1,5},{5,1},{9,13},{13,9},{2,6},{6,2},{1... | collective-permute-start | bytes 2359304 | tf_op jit(solution)/shard_map/ppermute | solution.py:33
  594.8 5.5 collective-permute-done.39.refs_2_
  603.5 3.1 add_blocks.4.refs_5_
  606.6 15.5 %collective-permute-done.35.refs_3_ = bf16[192,2048]{1,0:T(8,128)(2,1)} collective-permute-done((bf16[192,2048]{1,0:T(8,128)(2,1)}, bf16[192,2048]{1,0:T(8,128)(2,1)}, u32[]{:S(2)}, u32[]{:S(2)}) %collective-permute-start.35) | collective-permute-done | bytes 786464 | tf_op jit(solution)/shard_map/ppermute | solution.py:33
  622.1 4.0 output.1.refs_4_.refs_0_
  628.6 3.0 collective-permute-start.45
  632.9 4.2 join.2
  646.0 9.3 %collective-permute-done.45.refs_1_ = bf16[2,512,256]{2,1,0:T(8,128)(2,1)} collective-permute-done((bf16[2,512,256]{2,1,0:T(8,128)(2,1)}, bf16[2,512,256]{2,1,0:T(8,128)(2,1)}, u32[]{:S(2)}, u32[]{:S(2)}) %collective-permute-start.45) | collective-permute-done | bytes 524320 | tf_op jit(solution)/shard_map/ppermute | solution.py:33
  660.5 6.9 collective-permute-start.48
  668.0 3.2 project_last.1
  673.9 3.3 halves.4.refs_1_
  683.1 6.1 collective-permute-done.53
  691.0 3.5 join.3.refs_2_
  694.6 3.6 collective-permute-done.54.refs_1_
  698.2 3.3 halves.5
  (162 shorter events, 106.7 us)
Async XLA Ops:
  7.2 122.2 %all-gather.5.cloned.1.call-start = ((), (), s32[]{:S(2)}) async-start(), calls=%async_computation.3 | async-start | bytes 7077888 | tf_op jit(solution)/shard_map/all_gather | solution.py:1025
  21.7 28.6 %collective-permute-start = (bf16[768,384]{1,0:T(8,128)(2,1)}, bf16[768,384]{1,0:T(8,128)(2,1)}, u32[]{:S(2)}, u32[]{:S(2)}) collective-permute-start(bf16[768,384]{1,0:T(8,128)(2,1)} %get-tuple-element.72), channel_id=1, source_target_pairs={{0,4},{4,0},{8,12},{12,8},{1,5},{5,1},{9,13},{13,9},{2,6},{6,2},{1... | collective-permute-start | bytes 1769480 | tf_op jit(solution)/shard_map/ppermute | solution.py:33
  24.8 42.8 %collective-permute-start.1 = (bf16[768,384]{1,0:T(8,128)(2,1)}, bf16[768,384]{1,0:T(8,128)(2,1)}, u32[]{:S(2)}, u32[]{:S(2)}) collective-permute-start(bf16[768,384]{1,0:T(8,128)(2,1)} %get-tuple-element.73), channel_id=1, source_target_pairs={{0,8},{4,12},{8,0},{12,4},{1,9},{5,13},{9,1},{13,5},{2,10},{6,14},... | collective-permute-start | bytes 1769480 | tf_op jit(solution)/shard_map/ppermute | solution.py:33
  27.3 40.2 %collective-permute-start.2 = (bf16[768,384]{1,0:T(8,128)(2,1)}, bf16[768,384]{1,0:T(8,128)(2,1)}, u32[]{:S(2)}, u32[]{:S(2)}) collective-permute-start(bf16[768,384]{1,0:T(8,128)(2,1)} %get-tuple-element.74), channel_id=1, source_target_pairs={{0,12},{4,8},{8,4},{12,0},{1,13},{5,9},{9,5},{13,1},{2,14},{6,10},... | collective-permute-start | bytes 1769480 | tf_op jit(solution)/shard_map/ppermute | solution.py:33
  68.2 156.9 %all-gather.7.cloned.1.call-start = ((), (), s32[]{:S(2)}) async-start(), calls=%async_computation.4 | async-start | bytes 7077888 | tf_op jit(solution)/shard_map/all_gather | solution.py:1036
  96.2 25.6 %collective-permute-start.3 = (bf16[768,128]{1,0:T(8,128)(2,1)}, bf16[768,128]{1,0:T(8,128)(2,1)}, u32[]{:S(2)}, u32[]{:S(2)}) collective-permute-start(bf16[768,128]{1,0:T(8,128)(2,1)} %get-tuple-element.78), channel_id=1, source_target_pairs={{0,4},{4,0},{8,12},{12,8},{1,5},{5,1},{9,13},{13,9},{2,6},{6,2},{1... | collective-permute-start | bytes 589832 | tf_op jit(solution)/shard_map/ppermute | solution.py:33
  108.0 14.3 %collective-permute-start.4 = (bf16[768,128]{1,0:T(8,128)(2,1)}, bf16[768,128]{1,0:T(8,128)(2,1)}, u32[]{:S(2)}, u32[]{:S(2)}) collective-permute-start(bf16[768,128]{1,0:T(8,128)(2,1)} %get-tuple-element.79), channel_id=1, source_target_pairs={{0,8},{4,12},{8,0},{12,4},{1,9},{5,13},{9,1},{13,5},{2,10},{6,14},... | collective-permute-start | bytes 589832 | tf_op jit(solution)/shard_map/ppermute | solution.py:33
  109.1 20.2 %collective-permute-start.5 = (bf16[768,128]{1,0:T(8,128)(2,1)}, bf16[768,128]{1,0:T(8,128)(2,1)}, u32[]{:S(2)}, u32[]{:S(2)}) collective-permute-start(bf16[768,128]{1,0:T(8,128)(2,1)} %get-tuple-element.80), channel_id=1, source_target_pairs={{0,12},{4,8},{8,4},{12,0},{1,13},{5,9},{9,5},{13,1},{2,14},{6,10},... | collective-permute-start | bytes 589832 | tf_op jit(solution)/shard_map/ppermute | solution.py:33
  135.6 3.8 collective-permute-start.6
  142.3 20.1 %collective-permute-start.7 = (bf16[192,2048]{1,0:T(8,128)(2,1)}, bf16[192,2048]{1,0:T(8,128)(2,1)}, u32[]{:S(2)}, u32[]{:S(2)}) collective-permute-start(bf16[192,2048]{1,0:T(8,128)(2,1)} %sums.8), channel_id=1, source_target_pairs={{0,2},{1,3},{2,0},{3,1},{4,6},{5,7},{6,4},{7,5},{8,10},{9,11},{10,... | collective-permute-start | bytes 2359304 | tf_op jit(solution)/shard_map/ppermute | solution.py:33
  166.3 214.9 %all-gather.9.cloned.1.call-start = ((), (), s32[]{:S(2)}) async-start(), calls=%async_computation.8 | async-start | bytes 3932160 | tf_op jit(solution)/shard_map/all_gather | solution.py:1040
  166.3 31.2 %collective-permute-start.9 = (bf16[192,2048]{1,0:T(8,128)(2,1)}, bf16[192,2048]{1,0:T(8,128)(2,1)}, u32[]{:S(2)}, u32[]{:S(2)}) collective-permute-start(bf16[192,2048]{1,0:T(8,128)(2,1)} %get-tuple-element.83.refs_2_.refs_0_), channel_id=1, source_target_pairs={{0,2},{1,3},{2,0},{3,1},{4,6},{5,7},{6,4},{7,5},{8,10},{9,11},{10,... | collective-permute-start | bytes 2359304 | tf_op jit(solution)/shard_map/ppermute | solution.py:33
  168.1 30.2 %collective-permute-start.8 = (bf16[192,2048]{1,0:T(8,128)(2,1)}, bf16[192,2048]{1,0:T(8,128)(2,1)}, u32[]{:S(2)}, u32[]{:S(2)}) collective-permute-start(bf16[192,2048]{1,0:T(8,128)(2,1)} %get-tuple-element.83.refs_2_.refs_0_), channel_id=1, source_target_pairs={{0,1},{1,0},{2,3},{3,2},{4,5},{5,4},{6,7},{7,6},{8,9},{9,8},{10,11... | collective-permute-start | bytes 2359304 | tf_op jit(solution)/shard_map/ppermute | solution.py:33
  198.2 2.9 collective-permute-start.10
  224.8 197.3 %reduce-scatter.4.cloned.1.call-start = ((), (), s32[]{:S(2)}) async-start(), calls=%async_computation.5 | async-start | bytes 5242880 | tf_op jit(solution)/shard_map/reduce_scatter | solution.py:1047
  260.9 295.5 %reduce-scatter.6.cloned.1.call-start = ((), (), s32[]{:S(2)}) async-start(), calls=%async_computation.6 | async-start | bytes 5242880 | tf_op jit(solution)/shard_map/reduce_scatter | solution.py:1047
  262.3 4.3 collective-permute-start.12
  262.5 31.2 %collective-permute-start.11 = (bf16[2,192,2048]{2,1,0:T(8,128)(2,1)}, bf16[2,192,2048]{2,1,0:T(8,128)(2,1)}, u32[]{:S(2)}, u32[]{:S(2)}) collective-permute-start(bf16[2,192,2048]{2,1,0:T(8,128)(2,1)} %get-tuple-element.86), channel_id=1, source_target_pairs={{0,1},{1,0},{2,3},{3,2},{4,5},{5,4},{6,7},{7,6},{8,9},{9,8},{10,11... | collective-permute-start | bytes 4718600 | tf_op jit(solution)/shard_map/ppermute | solution.py:33
  269.5 20.9 %collective-permute-start.13 = (bf16[192,2048]{1,0:T(8,128)(2,1)}, bf16[192,2048]{1,0:T(8,128)(2,1)}, u32[]{:S(2)}, u32[]{:S(2)}) collective-permute-start(bf16[192,2048]{1,0:T(8,128)(2,1)} %sums.9.refs_2_), channel_id=1, source_target_pairs={{0,2},{1,3},{2,0},{3,1},{4,6},{5,7},{6,4},{7,5},{8,10},{9,11},{10,... | collective-permute-start | bytes 2359304 | tf_op jit(solution)/shard_map/ppermute | solution.py:33
  281.0 26.4 %collective-permute-start.16 = (bf16[2,192,2048]{2,1,0:T(8,128)(2,1)}, bf16[2,192,2048]{2,1,0:T(8,128)(2,1)}, u32[]{:S(2)}, u32[]{:S(2)}) collective-permute-start(bf16[2,192,2048]{2,1,0:T(8,128)(2,1)} %get-tuple-element.94), channel_id=1, source_target_pairs={{0,1},{1,0},{2,3},{3,2},{4,5},{5,4},{6,7},{7,6},{8,9},{9,8},{10,11... | collective-permute-start | bytes 4718600 | tf_op jit(solution)/shard_map/ppermute | solution.py:33
  296.9 18.9 %collective-permute-start.14 = (bf16[192,2048]{1,0:T(8,128)(2,1)}, bf16[192,2048]{1,0:T(8,128)(2,1)}, u32[]{:S(2)}, u32[]{:S(2)}) collective-permute-start(bf16[192,2048]{1,0:T(8,128)(2,1)} %sums.11.refs_2_), channel_id=1, source_target_pairs={{0,2},{1,3},{2,0},{3,1},{4,6},{5,7},{6,4},{7,5},{8,10},{9,11},{10,... | collective-permute-start | bytes 2359304 | tf_op jit(solution)/shard_map/ppermute | solution.py:33
  298.6 34.4 %collective-permute-start.15 = (bf16[192,2048]{1,0:T(8,128)(2,1)}, bf16[192,2048]{1,0:T(8,128)(2,1)}, u32[]{:S(2)}, u32[]{:S(2)}) collective-permute-start(bf16[192,2048]{1,0:T(8,128)(2,1)} %sums.10.refs_2_), channel_id=1, source_target_pairs={{0,4},{4,0},{8,12},{12,8},{1,5},{5,1},{9,13},{13,9},{2,6},{6,2},{1... | collective-permute-start | bytes 2359304 | tf_op jit(solution)/shard_map/ppermute | solution.py:33
  351.4 325.8 %reduce-scatter.8.cloned.1.call-start = ((), (), s32[]{:S(2)}) async-start(), calls=%async_computation.7 | async-start | bytes 5242880 | tf_op jit(solution)/shard_map/reduce_scatter | solution.py:1047
  352.5 17.5 %collective-permute-start.19 = (bf16[192,2048]{1,0:T(8,128)(2,1)S(1)}, bf16[192,2048]{1,0:T(8,128)(2,1)S(1)}, u32[]{:S(2)}, u32[]{:S(2)}) collective-permute-start(bf16[192,2048]{1,0:T(8,128)(2,1)S(1)} %copy-done.1), channel_id=1, source_target_pairs={{0,2},{1,3},{2,0},{3,1},{4,6},{5,7},{6,4},{7,5},{8,10},{9,11},{10,... | collective-permute-start | bytes 2359304 | tf_op jit(solution)/shard_map/ppermute | solution.py:33
  352.9 20.0 %collective-permute-start.18 = (bf16[192,2048]{1,0:T(8,128)(2,1)S(1)}, bf16[192,2048]{1,0:T(8,128)(2,1)S(1)}, u32[]{:S(2)}, u32[]{:S(2)}) collective-permute-start(bf16[192,2048]{1,0:T(8,128)(2,1)S(1)} %copy-done.1), channel_id=1, source_target_pairs={{0,1},{1,0},{2,3},{3,2},{4,5},{5,4},{6,7},{7,6},{8,9},{9,8},{10,11... | collective-permute-start | bytes 2359304 | tf_op jit(solution)/shard_map/ppermute | solution.py:33
  371.6 2.7 collective-permute-start.20
  372.3 25.4 %collective-permute-start.17 = (bf16[2,192,2048]{2,1,0:T(8,128)(2,1)}, bf16[2,192,2048]{2,1,0:T(8,128)(2,1)}, u32[]{:S(2)}, u32[]{:S(2)}) collective-permute-start(bf16[2,192,2048]{2,1,0:T(8,128)(2,1)} %tie.13), channel_id=1, source_target_pairs={{0,1},{1,0},{2,3},{3,2},{4,5},{5,4},{6,7},{7,6},{8,9},{9,8},{10,11... | collective-permute-start | bytes 4718600 | tf_op jit(solution)/shard_map/ppermute | solution.py:33
  384.9 99.7 %collective-permute-start.29 = (bf16[3,192,2048]{2,1,0:T(8,128)(2,1)}, bf16[3,192,2048]{2,1,0:T(8,128)(2,1)}, u32[]{:S(2)}, u32[]{:S(2)}) collective-permute-start(bf16[3,192,2048]{2,1,0:T(8,128)(2,1)} %others.1.refs_5_.refs_1_), channel_id=1, source_target_pairs={{0,2},{1,3},{2,0},{3,1},{4,6},{5,7},{6,4},{7,5},{8,10},{9,11},{10,... | collective-permute-start | bytes 7077896 | tf_op jit(solution)/shard_map/ppermute | solution.py:33
  394.0 90.7 %collective-permute-start.26 = (bf16[4,512,256]{2,1,0:T(8,128)(2,1)}, bf16[4,512,256]{2,1,0:T(8,128)(2,1)}, u32[]{:S(2)}, u32[]{:S(2)}) collective-permute-start(bf16[4,512,256]{2,1,0:T(8,128)(2,1)} %get-tuple-element.110), channel_id=1, source_target_pairs={{0,16},{16,0},{1,17},{17,1},{2,18},{18,2},{3,19},{19,3},{4,20},{20... | collective-permute-start | bytes 3145736 | tf_op jit(solution)/shard_map/ppermute | solution.py:33
  395.1 10.4 %collective-permute-start.23 = (bf16[768,128]{1,0:T(8,128)(2,1)}, bf16[768,128]{1,0:T(8,128)(2,1)}, u32[]{:S(2)}, u32[]{:S(2)}) collective-permute-start(bf16[768,128]{1,0:T(8,128)(2,1)} %get-tuple-element.103), channel_id=1, source_target_pairs={{0,4},{4,0},{8,12},{12,8},{1,5},{5,1},{9,13},{13,9},{2,6},{6,2},{1... | collective-permute-start | bytes 589832 | tf_op jit(solution)/shard_map/ppermute | solution.py:33
  397.7 24.3 %collective-permute-start.24 = (bf16[768,128]{1,0:T(8,128)(2,1)}, bf16[768,128]{1,0:T(8,128)(2,1)}, u32[]{:S(2)}, u32[]{:S(2)}) collective-permute-start(bf16[768,128]{1,0:T(8,128)(2,1)} %get-tuple-element.104), channel_id=1, source_target_pairs={{0,8},{4,12},{8,0},{12,4},{1,9},{5,13},{9,1},{13,5},{2,10},{6,14},... | collective-permute-start | bytes 589832 | tf_op jit(solution)/shard_map/ppermute | solution.py:33
  397.7 86.9 %collective-permute-start.22 = (bf16[192,2048]{1,0:T(8,128)(2,1)}, bf16[192,2048]{1,0:T(8,128)(2,1)}, u32[]{:S(2)}, u32[]{:S(2)}) collective-permute-start(bf16[192,2048]{1,0:T(8,128)(2,1)} %sums.12.refs_7_), channel_id=1, source_target_pairs={{0,2},{1,3},{2,0},{3,1},{4,6},{5,7},{6,4},{7,5},{8,10},{9,11},{10,... | collective-permute-start | bytes 2359304 | tf_op jit(solution)/shard_map/ppermute | solution.py:33
  405.5 79.2 %collective-permute-start.21 = (bf16[192,2048]{1,0:T(8,128)(2,1)}, bf16[192,2048]{1,0:T(8,128)(2,1)}, u32[]{:S(2)}, u32[]{:S(2)}) collective-permute-start(bf16[192,2048]{1,0:T(8,128)(2,1)} %sums.13.refs_12_.refs_1_), channel_id=1, source_target_pairs={{0,2},{1,3},{2,0},{3,1},{4,6},{5,7},{6,4},{7,5},{8,10},{9,11},{10,... | collective-permute-start | bytes 2359304 | tf_op jit(solution)/shard_map/ppermute | solution.py:33
  422.1 9.3 %collective-permute-start.25 = (bf16[768,128]{1,0:T(8,128)(2,1)}, bf16[768,128]{1,0:T(8,128)(2,1)}, u32[]{:S(2)}, u32[]{:S(2)}) collective-permute-start(bf16[768,128]{1,0:T(8,128)(2,1)} %get-tuple-element.105), channel_id=1, source_target_pairs={{0,12},{4,8},{8,4},{12,0},{1,13},{5,9},{9,5},{13,1},{2,14},{6,10},... | collective-permute-start | bytes 589832 | tf_op jit(solution)/shard_map/ppermute | solution.py:33
  431.4 53.3 %collective-permute-start.27 = (bf16[1,256,1024]{2,1,0:T(8,128)(2,1)}, bf16[1,256,1024]{2,1,0:T(8,128)(2,1)}, u32[]{:S(2)}, u32[]{:S(2)}) collective-permute-start(bf16[1,256,1024]{2,1,0:T(8,128)(2,1)} %one_block.3), channel_id=1, source_target_pairs={{0,4},{4,0},{8,12},{12,8},{1,5},{5,1},{9,13},{13,9},{2,6},{6,2},{1... | collective-permute-start | bytes 1572872 | tf_op jit(solution)/shard_map/ppermute | solution.py:33
  485.3 5.7 collective-permute-start.30
  486.1 7.6 %collective-permute-start.28 = (bf16[3,192,2048]{2,1,0:T(8,128)(2,1)}, bf16[3,192,2048]{2,1,0:T(8,128)(2,1)}, u32[]{:S(2)}, u32[]{:S(2)}) collective-permute-start(bf16[3,192,2048]{2,1,0:T(8,128)(2,1)} %tie.16), channel_id=1, source_target_pairs={{0,1},{1,0},{2,3},{3,2},{4,5},{5,4},{6,7},{7,6},{8,9},{9,8},{10,11... | collective-permute-start | bytes 7077896 | tf_op jit(solution)/shard_map/ppermute | solution.py:33
  486.7 42.4 %collective-permute-start.31 = (bf16[768,384]{1,0:T(8,128)(2,1)}, bf16[768,384]{1,0:T(8,128)(2,1)}, u32[]{:S(2)}, u32[]{:S(2)}) collective-permute-start(bf16[768,384]{1,0:T(8,128)(2,1)} %get-tuple-element.111.refs_6_), channel_id=1, source_target_pairs={{0,4},{4,0},{8,12},{12,8},{1,5},{5,1},{9,13},{13,9},{2,6},{6,2},{1... | collective-permute-start | bytes 1769480 | tf_op jit(solution)/shard_map/ppermute | solution.py:33
  486.7 42.7 %collective-permute-start.32 = (bf16[768,384]{1,0:T(8,128)(2,1)}, bf16[768,384]{1,0:T(8,128)(2,1)}, u32[]{:S(2)}, u32[]{:S(2)}) collective-permute-start(bf16[768,384]{1,0:T(8,128)(2,1)} %get-tuple-element.112.refs_7_), channel_id=1, source_target_pairs={{0,8},{4,12},{8,0},{12,4},{1,9},{5,13},{9,1},{13,5},{2,10},{6,14},... | collective-permute-start | bytes 1769480 | tf_op jit(solution)/shard_map/ppermute | solution.py:33
  487.5 41.9 %collective-permute-start.33 = (bf16[768,384]{1,0:T(8,128)(2,1)}, bf16[768,384]{1,0:T(8,128)(2,1)}, u32[]{:S(2)}, u32[]{:S(2)}) collective-permute-start(bf16[768,384]{1,0:T(8,128)(2,1)} %get-tuple-element.113.refs_8_), channel_id=1, source_target_pairs={{0,12},{4,8},{8,4},{12,0},{1,13},{5,9},{9,5},{13,1},{2,14},{6,10},... | collective-permute-start | bytes 1769480 | tf_op jit(solution)/shard_map/ppermute | solution.py:33
  548.1 3.8 collective-permute-start.34
  554.8 19.9 %collective-permute-start.37 = (bf16[192,2048]{1,0:T(8,128)(2,1)}, bf16[192,2048]{1,0:T(8,128)(2,1)}, u32[]{:S(2)}, u32[]{:S(2)}) collective-permute-start(bf16[192,2048]{1,0:T(8,128)(2,1)} %sums.15.refs_2_.refs_1_), channel_id=1, source_target_pairs={{0,2},{1,3},{2,0},{3,1},{4,6},{5,7},{6,4},{7,5},{8,10},{9,11},{10,... | collective-permute-start | bytes 2359304 | tf_op jit(solution)/shard_map/ppermute | solution.py:33
  579.8 20.6 %collective-permute-start.39 = (bf16[208,2048]{1,0:T(8,128)(2,1)}, bf16[208,2048]{1,0:T(8,128)(2,1)}, u32[]{:S(2)}, u32[]{:S(2)}) collective-permute-start(bf16[208,2048]{1,0:T(8,128)(2,1)} %input_back.1.refs_2_.refs_0_), channel_id=1, source_target_pairs={{0,2},{1,3},{2,0},{3,1},{4,6},{5,7},{6,4},{7,5},{8,10},{9,11},{10,... | collective-permute-start | bytes 2555912 | tf_op jit(solution)/shard_map/ppermute | solution.py:33
  581.3 22.1 %collective-permute-start.36 = (bf16[4,256,384]{2,1,0:T(8,128)(2,1)}, bf16[4,256,384]{2,1,0:T(8,128)(2,1)}, u32[]{:S(2)}, u32[]{:S(2)}) collective-permute-start(bf16[4,256,384]{2,1,0:T(8,128)(2,1)} %get-tuple-element.120), channel_id=1, source_target_pairs={{0,16},{16,0},{1,17},{17,1},{2,18},{18,2},{3,19},{19,3},{4,20},{20... | collective-permute-start | bytes 2359304 | tf_op jit(solution)/shard_map/ppermute | solution.py:33
  582.6 39.5 %collective-permute-start.35 = (bf16[192,2048]{1,0:T(8,128)(2,1)}, bf16[192,2048]{1,0:T(8,128)(2,1)}, u32[]{:S(2)}, u32[]{:S(2)}) collective-permute-start(bf16[192,2048]{1,0:T(8,128)(2,1)} %tie.18), channel_id=1, source_target_pairs={{0,4},{4,0},{8,12},{12,8},{1,5},{5,1},{9,13},{13,9},{2,6},{6,2},{1... | collective-permute-start | bytes 2359304 | tf_op jit(solution)/shard_map/ppermute | solution.py:33
  594.8 38.0 %collective-permute-start.38 = (bf16[208,2048]{1,0:T(8,128)(2,1)}, bf16[208,2048]{1,0:T(8,128)(2,1)}, u32[]{:S(2)}, u32[]{:S(2)}) collective-permute-start(bf16[208,2048]{1,0:T(8,128)(2,1)} %input_back.1.refs_2_.refs_0_), channel_id=1, source_target_pairs={{0,1},{1,0},{2,3},{3,2},{4,5},{5,4},{6,7},{7,6},{8,9},{9,8},{10,11... | collective-permute-start | bytes 2555912 | tf_op jit(solution)/shard_map/ppermute | solution.py:33
  600.3 32.5 %collective-permute-start.40 = (bf16[208,2048]{1,0:T(8,128)(2,1)}, bf16[208,2048]{1,0:T(8,128)(2,1)}, u32[]{:S(2)}, u32[]{:S(2)}) collective-permute-start(bf16[208,2048]{1,0:T(8,128)(2,1)} %collective-permute-done.39.refs_2_), channel_id=1, source_target_pairs={{0,1},{1,0},{2,3},{3,2},{4,5},{5,4},{6,7},{7,6},{8,9},{9,8},{10,11... | collective-permute-start | bytes 2555912 | tf_op jit(solution)/shard_map/ppermute | solution.py:33
  626.1 30.0 %collective-permute-start.42 = (bf16[192,2048]{1,0:T(8,128)(2,1)}, bf16[192,2048]{1,0:T(8,128)(2,1)}, u32[]{:S(2)}, u32[]{:S(2)}) collective-permute-start(bf16[192,2048]{1,0:T(8,128)(2,1)} %output.1.refs_4_.refs_0_), channel_id=1, source_target_pairs={{0,2},{1,3},{2,0},{3,1},{4,6},{5,7},{6,4},{7,5},{8,10},{9,11},{10,... | collective-permute-start | bytes 2359304 | tf_op jit(solution)/shard_map/ppermute | solution.py:33
  628.6 26.7 %collective-permute-start.45 = (bf16[2,512,256]{2,1,0:T(8,128)(2,1)}, bf16[2,512,256]{2,1,0:T(8,128)(2,1)}, u32[]{:S(2)}, u32[]{:S(2)}) collective-permute-start(bf16[2,512,256]{2,1,0:T(8,128)(2,1)} %tie.21), channel_id=1, source_target_pairs={{0,8},{4,12},{8,0},{12,4},{1,9},{5,13},{9,1},{13,5},{2,10},{6,14},... | collective-permute-start | bytes 1572872 | tf_op jit(solution)/shard_map/ppermute | solution.py:33
  631.6 24.5 %collective-permute-start.44 = (bf16[1,256,1024]{2,1,0:T(8,128)(2,1)}, bf16[1,256,1024]{2,1,0:T(8,128)(2,1)}, u32[]{:S(2)}, u32[]{:S(2)}) collective-permute-start(bf16[1,256,1024]{2,1,0:T(8,128)(2,1)} %one_block.4.refs_7_), channel_id=1, source_target_pairs={{0,4},{4,0},{8,12},{12,8},{1,5},{5,1},{9,13},{13,9},{2,6},{6,2},{1... | collective-permute-start | bytes 1572872 | tf_op jit(solution)/shard_map/ppermute | solution.py:33
  638.7 4.9 collective-permute-start.46
  641.7 17.8 %collective-permute-start.50 = (bf16[256,384]{1,0:T(8,128)(2,1)S(1)}, bf16[256,384]{1,0:T(8,128)(2,1)S(1)}, u32[]{:S(2)}, u32[]{:S(2)}) collective-permute-start(bf16[256,384]{1,0:T(8,128)(2,1)S(1)} %get-tuple-element.133), channel_id=1, source_target_pairs={{0,4},{4,0},{8,12},{12,8},{1,5},{5,1},{9,13},{13,9},{2,6},{6,2},{1... | collective-permute-start | bytes 589832 | tf_op jit(solution)/shard_map/ppermute | solution.py:33
  643.7 16.8 %collective-permute-start.51 = (bf16[256,384]{1,0:T(8,128)(2,1)S(1)}, bf16[256,384]{1,0:T(8,128)(2,1)S(1)}, u32[]{:S(2)}, u32[]{:S(2)}) collective-permute-start(bf16[256,384]{1,0:T(8,128)(2,1)S(1)} %get-tuple-element.132), channel_id=1, source_target_pairs={{0,8},{4,12},{8,0},{12,4},{1,9},{5,13},{9,1},{13,5},{2,10},{6,14},... | collective-permute-start | bytes 589832 | tf_op jit(solution)/shard_map/ppermute | solution.py:33
  646.0 21.5 %copy-start.7 = (f32[4,2,256]{2,1,0:T(2,128)}, f32[4,2,256]{2,1,0:T(2,128)S(1)}, u32[]{:S(2)}) copy-start(f32[4,2,256]{2,1,0:T(2,128)S(1)} %gather_fusion.1) | copy-start | bytes 24580
  655.3 12.0 %collective-permute-start.52 = (bf16[256,384]{1,0:T(8,128)(2,1)S(1)}, bf16[256,384]{1,0:T(8,128)(2,1)S(1)}, u32[]{:S(2)}, u32[]{:S(2)}) collective-permute-start(bf16[256,384]{1,0:T(8,128)(2,1)S(1)} %get-tuple-element.131), channel_id=1, source_target_pairs={{0,12},{4,8},{8,4},{12,0},{1,13},{5,9},{9,5},{13,1},{2,14},{6,10},... | collective-permute-start | bytes 589832 | tf_op jit(solution)/shard_map/ppermute | solution.py:33
  656.1 34.9 %collective-permute-start.43 = (bf16[192,2048]{1,0:T(8,128)(2,1)}, bf16[192,2048]{1,0:T(8,128)(2,1)}, u32[]{:S(2)}, u32[]{:S(2)}) collective-permute-start(bf16[192,2048]{1,0:T(8,128)(2,1)} %collective-permute-done.42.refs_2_), channel_id=1, source_target_pairs={{0,1},{1,0},{2,3},{3,2},{4,5},{5,4},{6,7},{7,6},{8,9},{9,8},{10,11... | collective-permute-start | bytes 2359304 | tf_op jit(solution)/shard_map/ppermute | solution.py:33
  656.1 34.9 %collective-permute-start.41 = (bf16[192,2048]{1,0:T(8,128)(2,1)}, bf16[192,2048]{1,0:T(8,128)(2,1)}, u32[]{:S(2)}, u32[]{:S(2)}) collective-permute-start(bf16[192,2048]{1,0:T(8,128)(2,1)} %tie.19), channel_id=1, source_target_pairs={{0,1},{1,0},{2,3},{3,2},{4,5},{5,4},{6,7},{7,6},{8,9},{9,8},{10,11... | collective-permute-start | bytes 2359304 | tf_op jit(solution)/shard_map/ppermute | solution.py:33
  659.6 7.8 %copy-start.4 = (bf16[256,384]{1,0:T(8,128)(2,1)}, bf16[256,384]{1,0:T(8,128)(2,1)S(1)}, u32[]{:S(2)}) copy-start(bf16[256,384]{1,0:T(8,128)(2,1)S(1)} %collective-permute-done.50.refs_1_) | copy-start | bytes 589828
  659.6 20.2 %collective-permute-start.47 = (f32[2,256]{1,0:T(2,128)}, f32[2,256]{1,0:T(2,128)}, u32[]{:S(2)}, u32[]{:S(2)}) collective-permute-start(f32[2,256]{1,0:T(2,128)} %get-tuple-element.135), channel_id=1, source_target_pairs={{0,4},{4,0},{8,12},{12,8},{1,5},{5,1},{9,13},{13,9},{2,6},{6,2},{1... | collective-permute-start | bytes 6152 | tf_op jit(solution)/shard_map/ppermute | solution.py:33
  660.5 6.9 copy-start.5
  660.5 20.9 %collective-permute-start.48 = (f32[2,256]{1,0:T(2,128)}, f32[2,256]{1,0:T(2,128)}, u32[]{:S(2)}, u32[]{:S(2)}) collective-permute-start(f32[2,256]{1,0:T(2,128)} %get-tuple-element.136), channel_id=1, source_target_pairs={{0,8},{4,12},{8,0},{12,4},{1,9},{5,13},{9,1},{13,5},{2,10},{6,14},... | collective-permute-start | bytes 6152 | tf_op jit(solution)/shard_map/ppermute | solution.py:33
  667.3 14.5 %collective-permute-start.49 = (f32[2,256]{1,0:T(2,128)}, f32[2,256]{1,0:T(2,128)}, u32[]{:S(2)}, u32[]{:S(2)}) collective-permute-start(f32[2,256]{1,0:T(2,128)} %get-tuple-element.137), channel_id=1, source_target_pairs={{0,12},{4,8},{8,4},{12,0},{1,13},{5,9},{9,5},{13,1},{2,14},{6,10},... | collective-permute-start | bytes 6152 | tf_op jit(solution)/shard_map/ppermute | solution.py:33
  679.8 9.5 %collective-permute-start.53 = (bf16[1,512,256]{2,1,0:T(8,128)(2,1)}, bf16[1,512,256]{2,1,0:T(8,128)(2,1)S(1)}, u32[]{:S(2)}, u32[]{:S(2)}) collective-permute-start(bf16[1,512,256]{2,1,0:T(8,128)(2,1)} %get-tuple-element.130), channel_id=1, source_target_pairs={{0,4},{4,0},{8,12},{12,8},{1,5},{5,1},{9,13},{13,9},{2,6},{6,2},{1... | collective-permute-start | bytes 786440 | tf_op jit(solution)/shard_map/ppermute | solution.py:33
  681.4 16.8 %collective-permute-start.54 = (bf16[1,256,1024]{2,1,0:T(8,128)(2,1)}, bf16[1,256,1024]{2,1,0:T(8,128)(2,1)}, u32[]{:S(2)}, u32[]{:S(2)}) collective-permute-start(bf16[1,256,1024]{2,1,0:T(8,128)(2,1)} %one_block.5.refs_4_), channel_id=1, source_target_pairs={{0,4},{4,0},{8,12},{12,8},{1,5},{5,1},{9,13},{13,9},{2,6},{6,2},{1... | collective-permute-start | bytes 1572872 | tf_op jit(solution)/shard_map/ppermute | solution.py:33
  (7 other events, 11.9 us)
Sparse Core Ops, SparseCore 0:
  68.3 56.5 all-gather.4
  166.4 46.0 all-gather.6
  224.9 62.2 all-gather.8
  290.0 85.7 reduce-scatter.3
  378.8 103.0 reduce-scatter.5
  530.2 96.3 reduce-scatter.7

commit v4 on v3

--- a/solution.py
+++ b/solution.py
@@ -980,20 +980,54 @@
     )
 
 
-def project_last_kernel(ix, p0, p1, p2, p3, q_ref, k_ref, v_ref):
+def add_parts_kernel(ix, a_ref, b_ref, gain_ref, *refs):
+    rows = a_ref.shape[1]
+    for k, out in enumerate(refs):
+        out[0:rows, :] = (a_ref[k].astype(F32) + b_ref[k].astype(F32)).astype(LOW)
+        gains = jnp.concatenate([gain_ref[k], jnp.zeros((14, gain_ref.shape[2]), F32)], axis=0)
+        out[rows : rows + 16, 0 : gains.shape[1]] = gains.astype(LOW)
+        out[rows : rows + 16, gains.shape[1] :] = jnp.zeros((16, out.shape[1] - gains.shape[1]), LOW)
+
+
+def add_parts(ix, one, two, gains, after=()):
+    count, rows, width = one.shape
+    whole = lambda shape: pl.BlockSpec(shape, lambda i, m: (0,) * len(shape))
+    shape = (rows + 16, width)
+    return call(
+        add_parts_kernel, "add_blocks", ix, (1,), [one, two, gains], [whole(a.shape) for a in (one, two, gains)],
+        [shaped(shape)] * count, [whole(shape)] * count, after=after,
+    )
+
+
+def add_last_kernel(ix, a_ref, b_ref, out_ref):
+    out_ref[...] = a_ref[...].astype(F32) + b_ref[...].astype(F32)
+
+
+def add_last(ix, one, two, after):
+    shape = one.shape[1:]
+    block = pl.BlockSpec((None, *shape), lambda i, m: (0, 0, 0))
+    return call(
+        add_last_kernel, "add_last", ix, (1,), [one, two], [block] * 2, shaped(shape, F32),
+        pl.BlockSpec(shape, lambda i, m: (0, 0)), after=after,
+    )
+
+
+def project_last_kernel(ix, p0, p1, p2, p3, q_ref, k_ref, v_ref, *gain_refs):
+    share = q_ref.shape[0]
     for slot, ref in enumerate((p0, p1, p2, p3)):
         at = pl.ds(pl.multiple_of((slot ^ ix[ME]) * 128, 128), 128)
         for place, out in enumerate((q_ref, k_ref, v_ref)):
-            out[:, at] = ref[:, place * 128 : (place + 1) * 128].astype(F32)
-
-
-def project_last(ix, pieces):
-    share = pieces[0].shape[0]
+            out[:, at] = ref[0:share, place * 128 : (place + 1) * 128].astype(F32)
+    for out in gain_refs:
+        out[...] = sum(ref[share : share + 16, 0 : out.shape[1]].astype(F32) for ref in (p0, p1, p2, p3))
+
+
+def project_last(ix, pieces, share, after=()):
     whole = lambda i, m: (0, 0)
-    return call(
-        project_last_kernel, "project_last", ix, (1,), list(pieces),
-        [pl.BlockSpec((share, 384), whole)] * 4,
-        [shaped((share, 512), F32)] * 3, [pl.BlockSpec((share, 512), whole)] * 3,
+    shapes = [(share, 512)] * 3 + ([(16, share)] if pieces[0].shape[0] > share else [])
+    return call(
+        project_last_kernel, "project_last", ix, (1,), list(pieces), [pl.BlockSpec(pieces[0].shape, whole)] * 4,
+        [shaped(shape, F32) for shape in shapes], [pl.BlockSpec(shape, whole) for shape in shapes], after=after,
     )
 
 
@@ -1048,12 +1082,12 @@
 
     core = swap(send, TENSOR, 1)
     part_down = wgrad(ix, (cotangent, cot_both), (hid_own, hid_far), "wgrad_down")
-    sum_down = over_pairs(part_down)
-    low = sums_to_send(ix, [(keep, 1), (core, 1)], (part_down,))
+    low = sums_to_send(ix, [(keep, 1), (core, 1)])
     far_y = swap(low, TENSOR, 2)
     down_far = feed_down(ix, hid_far, w_down, (low,))
     low = sums_to_send(ix, [(keep, 0), (core, 0), far_y], (down_far[0],))
     far_z = swap(low, CTX, 1)
+    sum_down = over_pairs(tie(ix, part_down, (far_z,)))
     low = sums_to_send(ix, [(keep_own, 1), (core_own, 1)], (low,))
     own_sums = [(keep_own, 0), (core_own, 0), swap(low, TENSOR, 2)]
     core_far = swap(down_far[1], TENSOR, 1)
@@ -1064,41 +1098,42 @@
         middle_back_kernel, "middle_back", ix, [*own_sums, far_z, middle], [cotangent, mlp_gain], [F32, LOW], 1,
         (low,),
     )
-    part_gate = wgrad(ix, seconds, (gb_own, gb_far), "wgrad_gate", (branch_mine,))
-    sum_gate = over_pairs(part_gate)
-    core_own = swap(tie(ix, down_own[1], (branch_mine,)), TENSOR, 1)
-    branch_low, *slots = branch_back(
-        ix, spread(branch_mine, lambda two: tie(ix, two, (part_gate,))), w_out, (part_gate,)
-    )
+    core_own = swap(down_own[1], TENSOR, 1)
+    low = sums_to_send(ix, [(down_own[0], 1), (core_own, 1)], (branch_mine,))
+    own_y = swap(low, TENSOR, 2)
+    branch_low, *slots = branch_back(ix, spread(branch_mine), w_out, (low,))
     upstreams = over_ctx(slots)
     first_far = others(ix, first_all, (branch_low,))
     out_own, out_far = out_wgrad(ix, mixed, branch_low, (first_far,))
-    low = sums_to_send(ix, [(down_own[0], 1), (core_own, 1)], (out_own,))
-    own_y = swap(low, TENSOR, 2)
+    part_gate = wgrad(ix, seconds, (gb_own, gb_far), "wgrad_gate", (out_own, own_y))
+    sum_gate = over_pairs(tie(ix, part_gate, upstreams[1:]))
 
     def for_partner(blocks, after):
         return swap(blocks[1:] if after is None else one_block(ix, blocks, 1, after), CTX, 1)
 
-    arrived = [far_down[2], own_y]
+    token, arrived = own_y, []
     if two_dp:
         out_other = swap(out_far, "dp", 1)
-        down_other = for_partner(sum_down, (low,))
-        arrived += [out_other, down_other]
-    back_slots = attend_back(ix, pieces, upstreams, raw, lse, all_tables, (low,))
+        token = one_block(ix, sum_down, 1, (out_own, *upstreams[1:]))
+        down_other = swap(token, CTX, 1)
+        arrived = [out_other, down_other]
+    back_slots = attend_back(ix, pieces, upstreams, raw, lse, all_tables, (token, out_own, own_y))
     back = over_ctx(back_slots)
 
     arrived = (back_slots[0], *arrived)
-    first_spread = spread(first_far, lambda two: tie(ix, two, arrived), lambda quarter: tie(ix, quarter, arrived))
+    first_spread = spread(first_far, lambda two: tie(ix, two, arrived))
     qkv_own, qkv_far = project_wgrad(ix, first_in, first_spread, back_slots)
     far_low = sums_to_send(ix, far_down, (qkv_own,))
-    part_up = wgrad(ix, seconds, (ub_own, ub_far), "wgrad_up", (far_low,))
-    sum_up = over_pairs(tie(ix, part_up, back[1:]))
-    token = part_up
+    token = far_low
     if two_dp:
-        out_part = add_blocks(ix, out_own, out_other, 2, (part_up,))
+        qkv_other = swap(qkv_far, "dp", 1)
+        out_part = add_blocks(ix, out_own, out_other, 2, (far_low,))
         down_grad = halves(ix, sum_down, down_other, 0, (out_part[0],))
         token = down_grad
-    keep, send = project_back(ix, back, projections, (token,))
+    part_up = wgrad(ix, seconds, (ub_own, ub_far), "wgrad_up", (token,))
+    part_up = tie(ix, part_up, back[1:])
+    sum_up = over_pairs(part_up)
+    keep, send = project_back(ix, back, projections, (part_up,))
     core = swap(send, TENSOR, 1)
     low = sums_to_send(ix, [(keep, 1), (core, 1)])
     low_y = swap(low, TENSOR, 2)
@@ -1106,31 +1141,35 @@
     token = low
     if two_dp:
         gate_low = one_block(ix, sum_gate, 1, (low,))
+        gate_other = swap(gate_low, CTX, 1)
         token = gate_low
     input_mine = input_back(ix, keep, core, low_y, middle_grad, tokens, attn_gain, mlp_gain_part, (token,))
-    input_pieces = spread(input_mine)
-    token = input_mine
+    arrived = (far_z,)
     if two_dp:
-        (qkv_part,) = add_blocks(ix, qkv_own, swap(qkv_far, "dp", 1), 1, (input_mine,))
         out_z = swap(tie(ix, out_part[1], (keep,)), CTX, 2)
-        token = qkv_part
+        arrived = (far_z, qkv_other, out_z)
+    input_grad, gains = join_input(ix, spread(input_mine, lambda two: tie(ix, two, arrived)), (input_mine,))
+    gains = gains[:2]
+    if two_dp:
+        halved = gains.reshape(2, 2, width // 2)[:, d ^ jnp.arange(2)]
+        gains = halved[:, 0] + swap(halved[:, 1], "dp", 1)
+        gains = gains.reshape(2, 4, share).transpose(1, 0, 2)[order]
     (output_mine,) = rows_call(
-        output_kernel, "output", ix, [(down_own[0], 0), (core_own, 0), own_y, far_z, middle], [], [LOW], after=(token,)
-    )
-    input_grad, gains = join_input(ix, input_pieces, (output_mine,))
-    output_pieces = spread(output_mine, late=lambda quarter: tie(ix, quarter, (input_grad,)))
+        output_kernel, "output", ix, [(down_own[0], 0), (core_own, 0), own_y, far_z, middle], [], [LOW],
+        after=(input_grad,),
+    )
+    output = lax.all_gather(output_mine, TENSOR, axis=0, tiled=True)
     if two_dp:
-        qkv_parts = over_ctx(qkv_part)
-        out_part = add_blocks(ix, out_part[0], out_z, 2, (input_grad,))
+        up_low = one_block(ix, sum_up, 1, (output_mine,))
+        up_other = swap(up_low, CTX, 1)
+        out_part = add_blocks(ix, out_part[0], out_z, 2, (up_low,))
         out_other = swap(out_part[1], CTX, 1)
-        gate_grad = halves(ix, sum_gate, swap(gate_low, CTX, 1), 1, (out_part[0],))
-        up_low = one_block(ix, sum_up, 1, (gate_grad,))
-        output = join(ix, output_pieces, (up_low,))
-        up_grad = halves(ix, sum_up, swap(up_low, CTX, 1), 1, (output,))
-        out_grad = out_part[0][0].astype(F32) + out_other[0].astype(F32)
+        qkv_parts = over_ctx(add_parts(ix, qkv_own, qkv_other, gains, (out_part[0],)))
+        gate_grad = halves(ix, sum_gate, gate_other, 1, (qkv_parts[0],))
+        up_grad = halves(ix, sum_up, up_other, 1, (gate_grad,))
+        *qkv, gains = project_last(ix, qkv_parts, share, (up_grad,))
+        out_grad = add_last(ix, out_part[0], out_other, (qkv[0],))
     else:
-        output = join(ix, output_pieces)
-
         def scattered(blocks, axis):
             blocks = jnp.moveaxis(blocks, 0, axis)
             shape = blocks.shape[:axis] + (width,) + blocks.shape[axis + 2 :]
@@ -1142,9 +1181,9 @@
             return blocks.reshape(2, 4, *blocks.shape[1:])[:, order].reshape(blocks.shape)
 
         grads = []
-        low_bit = me % 2 ^ jnp.arange(2)
+        own_first = me % 2 ^ jnp.arange(2)
         for k, blocks in enumerate((sum_down, sum_gate, sum_up)):
-            blocks = blocks.reshape(4, 2, *blocks.shape[1:])[:, low_bit].reshape(blocks.shape)
+            blocks = blocks.reshape(4, 2, *blocks.shape[1:])[:, own_first].reshape(blocks.shape)
             part = scattered(blocks, 0)[order].astype(F32)
             part = (part[:2] + swap(part[2:].astype(LOW), CTX, 2).astype(F32)).astype(LOW)
             grads.append(halves(ix, part, for_partner(part, None), min(k, 1)))
@@ -1153,15 +1192,9 @@
         out_part = scattered(in_order(jnp.concatenate([out_own, out_far])), 1)[order]
         out_part = out_part[:2].astype(F32) + swap(out_part[2:], CTX, 2).astype(F32)
         out_grad = out_part[0] + swap(out_part[1].astype(LOW), CTX, 1).astype(F32)
-    qkv = project_last(ix, qkv_parts)
-
-    gains = gains[:2]
-    if two_dp:
-        halved = gains.reshape(2, 2, width // 2)[:, d ^ jnp.arange(2)]
-        gains = halved[:, 0] + swap(halved[:, 1], "dp", 1)
-    else:
+        qkv = project_last(ix, qkv_parts, share)
         gains = lax.psum_scatter(gains, "dp", scatter_dimension=1, tiled=True)
-    gains = sum(over_ctx(gains.reshape(2, 4, share).transpose(1, 0, 2)[order]))
+        gains = sum(over_ctx(gains.reshape(2, 4, share).transpose(1, 0, 2)[order]))
 
     return (
         output,

time: 717 us -> 707 us (0.986)
    ppermute x55 -> x49, starting transfers between devices: 86.3 us -> 80.7 us  [swap(): return lax.ppermute(value, axis, [(i, i ^ distance) for i in range(size)])]
    ppermute x55 -> x49, waiting for transfers between devices: 231 us -> 230 us  [swap(): return lax.ppermute(value, axis, [(i, i ^ distance) for i in range(size)])]
  transfers between devices with their start and end apart: 61 -> 56, of which waited for: 30 -> 26; matrix products, arithmetic and copies ran while one was open for 3% -> 1% of each run, Pallas kernels for 45% -> 45%
where the time goes in v4:
time: 707 us; the launch traced here: 699 us
  Pallas kernels  345 us (49%)
  waiting for transfers between devices  238 us (34%)
  starting transfers between devices  81.9 us (12%)
  local copies, waits for them, and re-layouts  15.1 us (2%)
  between operations  14.8 us (2%)
    pallas_call x44, Pallas kernels, call(): pl.pallas_call(body, grid_spec=pltpu.PrefetchScalarGridSpec(num_scalar_pr...  338 us
    ppermute x49, waiting for transfers between devices, swap(): return lax.ppermute(value, axis, [(i, i ^ distance) for i in range(size)])  230 us
    ppermute x49, starting transfers between devices, swap(): return lax.ppermute(value, axis, [(i, i ^ distance) for i in range(size)])  80.7 us
  transfers between devices with their start and end apart: 56, of which 26 were waited for; matrix products, arithmetic and copies ran while one was open for 1% of the time, Pallas kernels for 45%

profile of v4, /device:TPU:0, one launch (start us, length us, event | category | flops | bytes accessed | tf_op | source)
XLA Modules:
  0.0 699.1 jit_solution(4971108561456338044)
XLA Ops:
  10.4 11.2 %project.1 = (bf16[768,2048]{1,0:T(8,128)(2,1)}, bf16[768,384]{1,0:T(8,128)(2,1)}, bf16[768,384]{1,0:T(8,128)(2,1)}, bf16[768,384]{1,0:T(8,128)(2,1)}, bf16[768,384]{1,0:T(8,128)(2,1)}) custom-call(s32[3]{0:T(128)} %pad_add_fusion.index_ref.refs_0_, bf16[768,2048]{1,0:T(8,128)(2,1)} %refs_4_.13, f32[1,2048]{1,0:T(1,128)} %bitcast.29, ...), custom_call_target="tpu_custom_call" | custom-call | bytes 80740352 | tf_op jit(solution)/shard_map/project/pallas_call | solution.py:58
  21.7 3.0 collective-permute-start
  27.3 8.0 %hidden_back.2.refs_1_.refs_6_ = f32[768,1024]{1,0:T(8,128)} custom-call(s32[3]{0:T(128)} %pad_add_fusion.index_ref.refs_0_, bf16[768,2048]{1,0:T(8,128)(2,1)} %refs_0_.5, bf16[2048,2048]{1,0:T(8,128)(2,1)} %refs_1_.9, bf16[768,384]{1,0:T(8,128)(2,1)} %get-tuple-element.76.refs_2_.refs_0_), custom_call_target="tpu_custom_call" | custom-call | bytes 62390272 | tf_op jit(solution)/shard_map/hidden_back/pallas_call | solution.py:58
  35.3 8.0 %rope_tables.1 = (f32[3072,128]{1,0:T(8,128)}, f32[3072,128]{1,0:T(8,128)}) custom-call(s32[3]{0:T(128)} %pad_add_fusion.index_ref.refs_0_, f32[1,128]{1,0:T(1,128)} %bitcast.33, f32[768,1024]{1,0:T(8,128)} %hidden_back.2.refs_1_.refs_6_), custom_call_target="tpu_custom_call" | custom-call | bytes 58720256 | tf_op jit(solution)/shard_map/rope_tables/pallas_call | solution.py:58
  50.2 17.2 %collective-permute-done.1.refs_2_.refs_3_ = bf16[768,384]{1,0:T(8,128)(2,1)} collective-permute-done((bf16[768,384]{1,0:T(8,128)(2,1)}, bf16[768,384]{1,0:T(8,128)(2,1)}, u32[]{:S(2)}, u32[]{:S(2)}) %collective-permute-start.1) | collective-permute-done | bytes 589856 | tf_op jit(solution)/shard_map/ppermute | solution.py:33
  68.4 27.7 %attend.1 = (bf16[768,128]{1,0:T(8,128)(2,1)}, bf16[768,128]{1,0:T(8,128)(2,1)}, bf16[768,128]{1,0:T(8,128)(2,1)}, bf16[768,128]{1,0:T(8,128)(2,1)}, f32[3072,128]{1,0:T(8,128)}, /*index=5*/f32[4,16,768]{2,1,0:T(8,128)}) custom-call(s32[3]{0:T(128)} %pad_add_fusion.index_ref.refs_0_, bf16[768,384]{1,0:T(8,128)(2,1)} %get-tuple-element.76.refs_2_.refs_0_, ...), custom_call_target="tpu_custom_call" | custom-call | bytes 205520896 | tf_op jit(solution)/shard_map/attend/pallas_call | solution.py:58
  96.2 11.8 %collective-permute-start.3 = (bf16[768,128]{1,0:T(8,128)(2,1)}, bf16[768,128]{1,0:T(8,128)(2,1)}, u32[]{:S(2)}, u32[]{:S(2)}) collective-permute-start(bf16[768,128]{1,0:T(8,128)(2,1)} %get-tuple-element.83), channel_id=1, source_target_pairs={{0,4},{4,0},{8,12},{12,8},{1,5},{5,1},{9,13},{13,9},{2,6},{6,2},{1... | collective-permute-start | bytes 589832 | tf_op jit(solution)/shard_map/ppermute | solution.py:33
  110.5 11.3 %collective-permute-done.3.refs_1_ = bf16[768,128]{1,0:T(8,128)(2,1)} collective-permute-done((bf16[768,128]{1,0:T(8,128)(2,1)}, bf16[768,128]{1,0:T(8,128)(2,1)}, u32[]{:S(2)}, u32[]{:S(2)}) %collective-permute-start.3) | collective-permute-done | bytes 196640 | tf_op jit(solution)/shard_map/ppermute | solution.py:33
  122.3 7.0 %collective-permute-done.5.refs_3_ = bf16[768,128]{1,0:T(8,128)(2,1)} collective-permute-done((bf16[768,128]{1,0:T(8,128)(2,1)}, bf16[768,128]{1,0:T(8,128)(2,1)}, u32[]{:S(2)}, u32[]{:S(2)}) %collective-permute-start.5) | collective-permute-done | bytes 196640 | tf_op jit(solution)/shard_map/ppermute | solution.py:33
  129.3 6.3 join_heads.1
  135.7 3.7 collective-permute-done.6.refs_1_
  139.4 2.9 sums.8
  144.2 18.2 %collective-permute-done.7.refs_2_ = bf16[192,2048]{1,0:T(8,128)(2,1)} collective-permute-done((bf16[192,2048]{1,0:T(8,128)(2,1)}, bf16[192,2048]{1,0:T(8,128)(2,1)}, u32[]{:S(2)}, u32[]{:S(2)}) %collective-permute-start.7) | collective-permute-done | bytes 786464 | tf_op jit(solution)/shard_map/ppermute | solution.py:33
  162.4 3.8 middle.1
  168.1 8.1 %hidden_back.3.refs_2_.refs_3_ = f32[768,1024]{1,0:T(8,128)} custom-call(s32[3]{0:T(128)} %pad_add_fusion.index_ref.refs_0_, bf16[1536,2048]{1,0:T(8,128)(2,1)} %all-gather.6.cloned.1.call-done.refs_8_.refs_0_.refs_1_, bf16[2048,2048]{1,0:T(8,128)(2,1)} %refs_1_.9, bf16[192,2048]{1,0:T(8,128)(2,1)} %get-tuple-element.88.refs_2_.refs_0_), custom_call_target="tpu_custom_call" | custom-call | bytes 62390272 | tf_op jit(solution)/shard_map/hidden_back/pallas_call | solution.py:58
  176.2 21.3 %collective-permute-done.9.refs_1_ = bf16[192,2048]{1,0:T(8,128)(2,1)} collective-permute-done((bf16[192,2048]{1,0:T(8,128)(2,1)}, bf16[192,2048]{1,0:T(8,128)(2,1)}, u32[]{:S(2)}, u32[]{:S(2)}) %collective-permute-start.9) | collective-permute-done | bytes 786464 | tf_op jit(solution)/shard_map/ppermute | solution.py:33
  198.3 2.8 collective-permute-done.10.refs_3_
  201.1 22.9 %feed.2 = (bf16[768,2048]{1,0:T(8,128)(2,1)}, bf16[768,1024]{1,0:T(8,128)(2,1)}, bf16[768,1024]{1,0:T(8,128)(2,1)}, bf16[768,1024]{1,0:T(8,128)(2,1)}, bf16[2,19...) custom-call(s32[3]{0:T(128)} %pad_add_fusion.index_ref.refs_0_, bf16[192,2048]{1,0:T(8,128)(2,1)} %get-tuple-element.88.refs_2_.refs_0_, ...), custom_call_target="tpu_custom_call" | custom-call | bytes 176160768 | tf_op jit(solution)/shard_map/feed/pallas_call | solution.py:58
  225.0 22.8 %feed.3 = (bf16[768,2048]{1,0:T(8,128)(2,1)}, bf16[768,1024]{1,0:T(8,128)(2,1)}, bf16[768,1024]{1,0:T(8,128)(2,1)}, bf16[768,1024]{1,0:T(8,128)(2,1)}, bf16[2,19...) custom-call(s32[3]{0:T(128)} %pad_add_fusion.index_ref.refs_0_, ...), custom_call_target="tpu_custom_call" | custom-call | bytes 176160768 | tf_op jit(solution)/shard_map/feed/pallas_call | solution.py:58
  248.0 3.6 collective-permute-done.12.refs_1_
  251.6 2.9 sums.9.refs_2_
  256.9 8.7 %feed_down.2 = (bf16[2,192,2048]{2,1,0:T(8,128)(2,1)}, bf16[2,192,2048]{2,1,0:T(8,128)(2,1)}) custom-call(s32[3]{0:T(128)} %pad_add_fusion.index_ref.refs_0_, bf16[768,1024]{1,0:T(8,128)(2,1)} %get-tuple-element.94.refs_0_.refs_3_, bf16[2048,2048]{1,0:T(8,128)(2,1)} %refs_1_.9, bf16[192,2048]{1,0:T(8,128)(2,1)} %sums.9.refs_2_), custom_call_target="tpu_custom_call" | custom-call | bytes 66060288 | tf_op jit(solution)/shard_map/feed_down/pallas_call | solution.py:58
  265.7 9.4 %collective-permute-done.13.refs_2_ = bf16[192,2048]{1,0:T(8,128)(2,1)} collective-permute-done((bf16[192,2048]{1,0:T(8,128)(2,1)}, bf16[192,2048]{1,0:T(8,128)(2,1)}, u32[]{:S(2)}, u32[]{:S(2)}) %collective-permute-start.13) | collective-permute-done | bytes 786464 | tf_op jit(solution)/shard_map/ppermute | solution.py:33
  275.1 3.2 sums.10.refs_2_
  278.3 12.9 %wgrad_down.1.refs_1_ = bf16[8,256,1024]{2,1,0:T(8,128)(2,1)} custom-call(s32[3]{0:T(128)} %pad_add_fusion.index_ref.refs_0_, bf16[768,2048]{1,0:T(8,128)(2,1)} %refs_0_.5, bf16[1536,2048]{1,0:T(8,128)(2,1)} %all-gather.6.cloned.1.call-done.refs_8_.refs_0_.refs_1_, bf16[768,1024]{1,0:T(8,128)(2,1)} %get-tuple-element.89.refs_6_.refs_0_.refs_2_, ...), custom_call_target="tpu_custom_call" | custom-call | bytes 102760448 | tf_op jit(solution)/shard_map/wgrad_down/pallas_call | solution.py:58
  291.2 10.6 %collective-permute-done.16.refs_3_.refs_2_ = bf16[192,2048]{1,0:T(8,128)(2,1)} collective-permute-done((bf16[192,2048]{1,0:T(8,128)(2,1)}, bf16[192,2048]{1,0:T(8,128)(2,1)}, u32[]{:S(2)}, u32[]{:S(2)}) %collective-permute-start.16) | collective-permute-done | bytes 786464 | tf_op jit(solution)/shard_map/ppermute | solution.py:33
  304.4 5.2 collective-permute-done.11.refs_1_
  309.6 2.9 sums.11.refs_2_
  314.0 8.7 %feed_down.3 = (bf16[2,192,2048]{2,1,0:T(8,128)(2,1)}, bf16[2,192,2048]{2,1,0:T(8,128)(2,1)}) custom-call(s32[3]{0:T(128)} %pad_add_fusion.index_ref.refs_0_, bf16[768,1024]{1,0:T(8,128)(2,1)} %get-tuple-element.89.refs_6_.refs_0_.refs_2_, bf16[2048,2048]{1,0:T(8,128)(2,1)} %refs_1_.9, bf16[192,2048]{1,0:T(8,128)(2,1)} %sums.11.refs_2_), custom_call_target="tpu_custom_call" | custom-call | bytes 66060288 | tf_op jit(solution)/shard_map/feed_down/pallas_call | solution.py:58
  322.8 2.9 sums.12.refs_7_
  325.7 6.7 collective-permute-done.15.refs_2_
  332.4 5.3 middle_back.1
  339.3 17.5 %collective-permute-done.21.refs_2_ = bf16[192,2048]{1,0:T(8,128)(2,1)} collective-permute-done((bf16[192,2048]{1,0:T(8,128)(2,1)}, bf16[192,2048]{1,0:T(8,128)(2,1)}, u32[]{:S(2)}, u32[]{:S(2)}) %collective-permute-start.21) | collective-permute-done | bytes 786464 | tf_op jit(solution)/shard_map/ppermute | solution.py:33
  356.8 2.9 sums.13.refs_8_
  361.2 7.0 %branch_back.1 = (bf16[768,2048]{1,0:T(8,128)(2,1)}, bf16[768,128]{1,0:T(8,128)(2,1)}, bf16[768,128]{1,0:T(8,128)(2,1)}, bf16[768,128]{1,0:T(8,128)(2,1)}, bf16[768,128]{1,0:T(8,128)(2,1)}) custom-call(s32[3]{0:T(128)} %pad_add_fusion.index_ref.refs_0_, bf16[192,2048]{1,0:T(8,128)(2,1)} %get-tuple-element.100.refs_2_.refs_0_, ...), custom_call_target="tpu_custom_call" | custom-call | bytes 51380224 | tf_op jit(solution)/shard_map/branch_back/pallas_call | solution.py:58
  372.7 3.7 others.1.refs_5_.refs_1_
  376.4 8.5 %out_wgrad.1 = (bf16[4,512,256]{2,1,0:T(8,128)(2,1)}, bf16[4,512,256]{2,1,0:T(8,128)(2,1)}) custom-call(s32[3]{0:T(128)} %pad_add_fusion.index_ref.refs_0_, bf16[768,128]{1,0:T(8,128)(2,1)} %get-tuple-element.82.refs_0_, bf16[768,128]{1,0:T(8,128)(2,1)} %collective-permute-done.3.refs_1_, bf16[768,128]{1,0:T(8,128)(2,1)} %collective-permute-done.4.refs_2_, ...), custom_call_target="tpu_custom_call" | custom-call | bytes 62390272 | tf_op jit(solution)/shard_map/out_wgrad/pallas_call | solution.py:58
  385.0 12.9 %wgrad_gate.1.refs_1_ = bf16[8,256,1024]{2,1,0:T(8,128)(2,1)} custom-call(s32[3]{0:T(128)} %pad_add_fusion.index_ref.refs_0_, bf16[768,2048]{1,0:T(8,128)(2,1)} %get-tuple-element.116.refs_0_, bf16[768,2048]{1,0:T(8,128)(2,1)} %get-tuple-element.117.refs_1_, bf16[768,1024]{1,0:T(8,128)(2,1)} %get-tuple-element.125.refs_2_, ...), custom_call_target="tpu_custom_call" | custom-call | bytes 102760448 | tf_op jit(solution)/shard_map/wgrad_gate/pallas_call | solution.py:58
  401.4 5.6 reduce-scatter.4.cloned.1.call-done.refs_0_
  411.2 40.4 %attend_back.1 = (bf16[768,384]{1,0:T(8,128)(2,1)}, bf16[768,384]{1,0:T(8,128)(2,1)}, bf16[768,384]{1,0:T(8,128)(2,1)}, bf16[768,384]{1,0:T(8,128)(2,1)}) custom-call(s32[3]{0:T(128)} %pad_add_fusion.index_ref.refs_0_, bf16[768,384]{1,0:T(8,128)(2,1)} %get-tuple-element.76.refs_2_.refs_0_, bf16[768,384]{1,0:T(8,128)(2,1)} %collective-permute-done.refs_1_.refs_2_, ...), custom_call_target="tpu_custom_call" | custom-call | bytes 293601280 | tf_op jit(solution)/shard_map/attend_back/pallas_call | solution.py:58
  453.8 7.6 %collective-permute-start.31 = (bf16[768,384]{1,0:T(8,128)(2,1)}, bf16[768,384]{1,0:T(8,128)(2,1)}, u32[]{:S(2)}, u32[]{:S(2)}) collective-permute-start(bf16[768,384]{1,0:T(8,128)(2,1)} %get-tuple-element.112.refs_6_), channel_id=1, source_target_pairs={{0,4},{4,0},{8,12},{12,8},{1,5},{5,1},{9,13},{13,9},{2,6},{6,2},{1... | collective-permute-start | bytes 1769480 | tf_op jit(solution)/shard_map/ppermute | solution.py:33
  463.9 14.7 %project_wgrad.1 = (bf16[4,256,384]{2,1,0:T(8,128)(2,1)}, bf16[4,256,384]{2,1,0:T(8,128)(2,1)}) custom-call(s32[3]{0:T(128)} %pad_add_fusion.index_ref.refs_0_, bf16[768,2048]{1,0:T(8,128)(2,1)} %get-tuple-element.80.refs_0_, bf16[3,192,2048]{2,1,0:T(8,128)(2,1)} %others.1.refs_5_.refs_1_, bf16[3,192,2048]{2,1,0:T(8,128)(2,1)} %collective-permute-done.23.refs_2_, ...), custom_call_target="tpu_custom_call" | custom-call | bytes 95420416 | tf_op jit(solution)/shard_map/project_wgrad/pallas_call | solution.py:58
  478.5 3.2 sums.14.refs_2_.refs_1_
  481.7 3.3 add_blocks.3
  485.0 3.5 halves.3.refs_4_
  488.5 12.9 %wgrad_up.1.refs_1_ = bf16[8,256,1024]{2,1,0:T(8,128)(2,1)} custom-call(s32[3]{0:T(128)} %pad_add_fusion.index_ref.refs_0_, bf16[768,2048]{1,0:T(8,128)(2,1)} %get-tuple-element.116.refs_0_, bf16[768,2048]{1,0:T(8,128)(2,1)} %get-tuple-element.117.refs_1_, bf16[768,1024]{1,0:T(8,128)(2,1)} %get-tuple-element.118.refs_2_, ...), custom_call_target="tpu_custom_call" | custom-call | bytes 102760448 | tf_op jit(solution)/shard_map/wgrad_up/pallas_call | solution.py:58
  501.4 20.4 %collective-permute-done.32.refs_3_.refs_2_ = bf16[768,384]{1,0:T(8,128)(2,1)} collective-permute-done((bf16[768,384]{1,0:T(8,128)(2,1)}, bf16[768,384]{1,0:T(8,128)(2,1)}, u32[]{:S(2)}, u32[]{:S(2)}) %collective-permute-start.32) | collective-permute-done | bytes 589856 | tf_op jit(solution)/shard_map/ppermute | solution.py:33
  522.5 11.5 %project_back.1 = (bf16[2,192,2048]{2,1,0:T(8,128)(2,1)}, bf16[2,192,2048]{2,1,0:T(8,128)(2,1)}) custom-call(s32[3]{0:T(128)} %pad_add_fusion.index_ref.refs_0_, bf16[768,384]{1,0:T(8,128)(2,1)} %get-tuple-element.110.refs_2_.refs_5_.refs_0_, bf16[768,384]{1,0:T(8,128)(2,1)} %collective-permute-done.31.refs_2_.refs_1_, ...), custom_call_target="tpu_custom_call" | custom-call | bytes 80740352 | tf_op jit(solution)/shard_map/project_back/pallas_call | solution.py:58
  534.1 3.7 collective-permute-done.34.refs_1_
  537.8 2.9 sums.15.refs_2_.refs_1_
  543.2 17.4 %collective-permute-done.36.refs_2_ = bf16[192,2048]{1,0:T(8,128)(2,1)} collective-permute-done((bf16[192,2048]{1,0:T(8,128)(2,1)}, bf16[192,2048]{1,0:T(8,128)(2,1)}, u32[]{:S(2)}, u32[]{:S(2)}) %collective-permute-start.36) | collective-permute-done | bytes 786464 | tf_op jit(solution)/shard_map/ppermute | solution.py:33
  560.6 4.8 input_back.1.refs_0_.refs_4_
  567.9 17.3 %collective-permute-start.35 = (bf16[192,2048]{1,0:T(8,128)(2,1)}, bf16[192,2048]{1,0:T(8,128)(2,1)S(1)}, u32[]{:S(2)}, u32[]{:S(2)}) collective-permute-start(bf16[192,2048]{1,0:T(8,128)(2,1)} %tie.16), channel_id=1, source_target_pairs={{0,4},{4,0},{8,12},{12,8},{1,5},{5,1},{9,13},{13,9},{2,6},{6,2},{1... | collective-permute-start | bytes 2359304 | tf_op jit(solution)/shard_map/ppermute | solution.py:33
  586.1 37.6 %collective-permute-done.40.refs_4_.refs_1_ = bf16[2,512,256]{2,1,0:T(8,128)(2,1)S(1)} collective-permute-done((bf16[2,512,256]{2,1,0:T(8,128)(2,1)}, bf16[2,512,256]{2,1,0:T(8,128)(2,1)S(1)}, u32[]{:S(2)}, u32[]{:S(2)}) %collective-permute-start.40) | collective-permute-done | bytes 524320 | tf_op jit(solution)/shard_map/ppermute | solution.py:33
  629.7 4.3 join.1
  634.0 4.0 output.1.refs_1_
  652.2 2.7 add_blocks.4
  654.9 3.0 add_blocks.5
  658.0 4.3 collective-permute-start.45
  662.3 3.3 halves.4.refs_2_
  669.8 3.3 halves.5.refs_4_
  674.3 6.7 collective-permute-done.45.refs_3_
  681.0 3.2 project_last.1
  688.1 4.0 copy.46
  (142 shorter events, 84.9 us)
Async XLA Ops:
  7.2 122.2 %all-gather.6.cloned.1.call-start = ((), (), s32[]{:S(2)}) async-start(), calls=%async_computation.3 | async-start | bytes 7077888 | tf_op jit(solution)/shard_map/all_gather | solution.py:1059
  7.3 3.1 copy-start.6
  21.7 28.5 %collective-permute-start = (bf16[768,384]{1,0:T(8,128)(2,1)}, bf16[768,384]{1,0:T(8,128)(2,1)}, u32[]{:S(2)}, u32[]{:S(2)}) collective-permute-start(bf16[768,384]{1,0:T(8,128)(2,1)} %get-tuple-element.77), channel_id=1, source_target_pairs={{0,4},{4,0},{8,12},{12,8},{1,5},{5,1},{9,13},{13,9},{2,6},{6,2},{1... | collective-permute-start | bytes 1769480 | tf_op jit(solution)/shard_map/ppermute | solution.py:33
  24.7 42.8 %collective-permute-start.1 = (bf16[768,384]{1,0:T(8,128)(2,1)}, bf16[768,384]{1,0:T(8,128)(2,1)}, u32[]{:S(2)}, u32[]{:S(2)}) collective-permute-start(bf16[768,384]{1,0:T(8,128)(2,1)} %get-tuple-element.78), channel_id=1, source_target_pairs={{0,8},{4,12},{8,0},{12,4},{1,9},{5,13},{9,1},{13,5},{2,10},{6,14},... | collective-permute-start | bytes 1769480 | tf_op jit(solution)/shard_map/ppermute | solution.py:33
  27.3 40.2 %collective-permute-start.2 = (bf16[768,384]{1,0:T(8,128)(2,1)}, bf16[768,384]{1,0:T(8,128)(2,1)}, u32[]{:S(2)}, u32[]{:S(2)}) collective-permute-start(bf16[768,384]{1,0:T(8,128)(2,1)} %get-tuple-element.79), channel_id=1, source_target_pairs={{0,12},{4,8},{8,4},{12,0},{1,13},{5,9},{9,5},{13,1},{2,14},{6,10},... | collective-permute-start | bytes 1769480 | tf_op jit(solution)/shard_map/ppermute | solution.py:33
  68.2 156.8 %all-gather.8.cloned.1.call-start = ((), (), s32[]{:S(2)}) async-start(), calls=%async_computation.4 | async-start | bytes 7077888 | tf_op jit(solution)/shard_map/all_gather | solution.py:1070
  96.2 25.6 %collective-permute-start.3 = (bf16[768,128]{1,0:T(8,128)(2,1)}, bf16[768,128]{1,0:T(8,128)(2,1)}, u32[]{:S(2)}, u32[]{:S(2)}) collective-permute-start(bf16[768,128]{1,0:T(8,128)(2,1)} %get-tuple-element.83), channel_id=1, source_target_pairs={{0,4},{4,0},{8,12},{12,8},{1,5},{5,1},{9,13},{13,9},{2,6},{6,2},{1... | collective-permute-start | bytes 589832 | tf_op jit(solution)/shard_map/ppermute | solution.py:33
  108.0 14.3 %collective-permute-start.4 = (bf16[768,128]{1,0:T(8,128)(2,1)}, bf16[768,128]{1,0:T(8,128)(2,1)}, u32[]{:S(2)}, u32[]{:S(2)}) collective-permute-start(bf16[768,128]{1,0:T(8,128)(2,1)} %get-tuple-element.84), channel_id=1, source_target_pairs={{0,8},{4,12},{8,0},{12,4},{1,9},{5,13},{9,1},{13,5},{2,10},{6,14},... | collective-permute-start | bytes 589832 | tf_op jit(solution)/shard_map/ppermute | solution.py:33
  109.1 20.2 %collective-permute-start.5 = (bf16[768,128]{1,0:T(8,128)(2,1)}, bf16[768,128]{1,0:T(8,128)(2,1)}, u32[]{:S(2)}, u32[]{:S(2)}) collective-permute-start(bf16[768,128]{1,0:T(8,128)(2,1)} %get-tuple-element.85), channel_id=1, source_target_pairs={{0,12},{4,8},{8,4},{12,0},{1,13},{5,9},{9,5},{13,1},{2,14},{6,10},... | collective-permute-start | bytes 589832 | tf_op jit(solution)/shard_map/ppermute | solution.py:33
  135.6 3.8 collective-permute-start.6
  142.3 20.1 %collective-permute-start.7 = (bf16[192,2048]{1,0:T(8,128)(2,1)}, bf16[192,2048]{1,0:T(8,128)(2,1)}, u32[]{:S(2)}, u32[]{:S(2)}) collective-permute-start(bf16[192,2048]{1,0:T(8,128)(2,1)} %sums.8), channel_id=1, source_target_pairs={{0,2},{1,3},{2,0},{3,1},{4,6},{5,7},{6,4},{7,5},{8,10},{9,11},{10,... | collective-permute-start | bytes 2359304 | tf_op jit(solution)/shard_map/ppermute | solution.py:33
  166.3 206.4 %all-gather.12.cloned.1.call-start = ((), (), s32[]{:S(2)}) async-start(), calls=%async_computation.9 | async-start | bytes 3932160 | tf_op jit(solution)/shard_map/all_gather | solution.py:1074
  166.3 31.2 %collective-permute-start.9 = (bf16[192,2048]{1,0:T(8,128)(2,1)}, bf16[192,2048]{1,0:T(8,128)(2,1)}, u32[]{:S(2)}, u32[]{:S(2)}) collective-permute-start(bf16[192,2048]{1,0:T(8,128)(2,1)} %get-tuple-element.88.refs_2_.refs_0_), channel_id=1, source_target_pairs={{0,2},{1,3},{2,0},{3,1},{4,6},{5,7},{6,4},{7,5},{8,10},{9,11},{10,... | collective-permute-start | bytes 2359304 | tf_op jit(solution)/shard_map/ppermute | solution.py:33
  168.1 30.2 %collective-permute-start.8 = (bf16[192,2048]{1,0:T(8,128)(2,1)}, bf16[192,2048]{1,0:T(8,128)(2,1)}, u32[]{:S(2)}, u32[]{:S(2)}) collective-permute-start(bf16[192,2048]{1,0:T(8,128)(2,1)} %get-tuple-element.88.refs_2_.refs_0_), channel_id=1, source_target_pairs={{0,1},{1,0},{2,3},{3,2},{4,5},{5,4},{6,7},{7,6},{8,9},{9,8},{10,11... | collective-permute-start | bytes 2359304 | tf_op jit(solution)/shard_map/ppermute | solution.py:33
  198.2 2.9 collective-permute-start.10
  224.7 182.3 %reduce-scatter.4.cloned.1.call-start = ((), (), s32[]{:S(2)}) async-start(), calls=%async_computation.5 | async-start | bytes 5242880 | tf_op jit(solution)/shard_map/reduce_scatter | solution.py:1081
  247.8 3.8 collective-permute-start.12
  254.5 20.5 %collective-permute-start.13 = (bf16[192,2048]{1,0:T(8,128)(2,1)}, bf16[192,2048]{1,0:T(8,128)(2,1)}, u32[]{:S(2)}, u32[]{:S(2)}) collective-permute-start(bf16[192,2048]{1,0:T(8,128)(2,1)} %sums.9.refs_2_), channel_id=1, source_target_pairs={{0,2},{1,3},{2,0},{3,1},{4,6},{5,7},{6,4},{7,5},{8,10},{9,11},{10,... | collective-permute-start | bytes 2359304 | tf_op jit(solution)/shard_map/ppermute | solution.py:33
  278.3 23.5 %collective-permute-start.16 = (bf16[192,2048]{1,0:T(8,128)(2,1)}, bf16[192,2048]{1,0:T(8,128)(2,1)}, u32[]{:S(2)}, u32[]{:S(2)}) collective-permute-start(bf16[192,2048]{1,0:T(8,128)(2,1)} %sums.10.refs_2_), channel_id=1, source_target_pairs={{0,4},{4,0},{8,12},{12,8},{1,5},{5,1},{9,13},{13,9},{2,6},{6,2},{1... | collective-permute-start | bytes 2359304 | tf_op jit(solution)/shard_map/ppermute | solution.py:33
  302.5 1.4 copy-start.7
  302.5 238.2 %reduce-scatter.6.cloned.1.call-start = ((), (), s32[]{:S(2)}) async-start(), calls=%async_computation.6 | async-start | bytes 5242880 | tf_op jit(solution)/shard_map/reduce_scatter | solution.py:1081
  303.9 5.8 collective-permute-start.11
  303.9 18.9 %collective-permute-start.17 = (bf16[2,192,2048]{2,1,0:T(8,128)(2,1)}, bf16[2,192,2048]{2,1,0:T(8,128)(2,1)}, u32[]{:S(2)}, u32[]{:S(2)}) collective-permute-start(bf16[2,192,2048]{2,1,0:T(8,128)(2,1)} %get-tuple-element.99), channel_id=1, source_target_pairs={{0,1},{1,0},{2,3},{3,2},{4,5},{5,4},{6,7},{7,6},{8,9},{9,8},{10,11... | collective-permute-start | bytes 4718600 | tf_op jit(solution)/shard_map/ppermute | solution.py:33
  312.5 19.9 %collective-permute-start.15 = (bf16[192,2048]{1,0:T(8,128)(2,1)}, bf16[192,2048]{1,0:T(8,128)(2,1)}, u32[]{:S(2)}, u32[]{:S(2)}) collective-permute-start(bf16[192,2048]{1,0:T(8,128)(2,1)} %sums.11.refs_2_), channel_id=1, source_target_pairs={{0,2},{1,3},{2,0},{3,1},{4,6},{5,7},{6,4},{7,5},{8,10},{9,11},{10,... | collective-permute-start | bytes 2359304 | tf_op jit(solution)/shard_map/ppermute | solution.py:33
  322.7 34.2 %collective-permute-start.14 = (bf16[2,192,2048]{2,1,0:T(8,128)(2,1)}, bf16[2,192,2048]{2,1,0:T(8,128)(2,1)}, u32[]{:S(2)}, u32[]{:S(2)}) collective-permute-start(bf16[2,192,2048]{2,1,0:T(8,128)(2,1)} %get-tuple-element.97), channel_id=1, source_target_pairs={{0,1},{1,0},{2,3},{3,2},{4,5},{5,4},{6,7},{7,6},{8,9},{9,8},{10,11... | collective-permute-start | bytes 4718600 | tf_op jit(solution)/shard_map/ppermute | solution.py:33
  337.7 19.1 %collective-permute-start.21 = (bf16[192,2048]{1,0:T(8,128)(2,1)}, bf16[192,2048]{1,0:T(8,128)(2,1)}, u32[]{:S(2)}, u32[]{:S(2)}) collective-permute-start(bf16[192,2048]{1,0:T(8,128)(2,1)} %get-tuple-element.100.refs_2_.refs_0_), channel_id=1, source_target_pairs={{0,2},{1,3},{2,0},{3,1},{4,6},{5,7},{6,4},{7,5},{8,10},{9,11},{10,... | collective-permute-start | bytes 2359304 | tf_op jit(solution)/shard_map/ppermute | solution.py:33
  339.3 21.9 %collective-permute-start.20 = (bf16[192,2048]{1,0:T(8,128)(2,1)}, bf16[192,2048]{1,0:T(8,128)(2,1)}, u32[]{:S(2)}, u32[]{:S(2)}) collective-permute-start(bf16[192,2048]{1,0:T(8,128)(2,1)} %get-tuple-element.100.refs_2_.refs_0_), channel_id=1, source_target_pairs={{0,1},{1,0},{2,3},{3,2},{4,5},{5,4},{6,7},{7,6},{8,9},{9,8},{10,11... | collective-permute-start | bytes 2359304 | tf_op jit(solution)/shard_map/ppermute | solution.py:33
  356.8 4.4 collective-permute-start.22
  359.7 25.3 %collective-permute-start.18 = (bf16[192,2048]{1,0:T(8,128)(2,1)}, bf16[192,2048]{1,0:T(8,128)(2,1)}, u32[]{:S(2)}, u32[]{:S(2)}) collective-permute-start(bf16[192,2048]{1,0:T(8,128)(2,1)} %sums.13.refs_8_), channel_id=1, source_target_pairs={{0,2},{1,3},{2,0},{3,1},{4,6},{5,7},{6,4},{7,5},{8,10},{9,11},{10,... | collective-permute-start | bytes 2359304 | tf_op jit(solution)/shard_map/ppermute | solution.py:33
  368.2 29.6 %collective-permute-start.25 = (bf16[768,128]{1,0:T(8,128)(2,1)}, bf16[768,128]{1,0:T(8,128)(2,1)}, u32[]{:S(2)}, u32[]{:S(2)}) collective-permute-start(bf16[768,128]{1,0:T(8,128)(2,1)} %get-tuple-element.103), channel_id=1, source_target_pairs={{0,4},{4,0},{8,12},{12,8},{1,5},{5,1},{9,13},{13,9},{2,6},{6,2},{1... | collective-permute-start | bytes 589832 | tf_op jit(solution)/shard_map/ppermute | solution.py:33
  369.7 28.2 %collective-permute-start.26 = (bf16[768,128]{1,0:T(8,128)(2,1)}, bf16[768,128]{1,0:T(8,128)(2,1)}, u32[]{:S(2)}, u32[]{:S(2)}) collective-permute-start(bf16[768,128]{1,0:T(8,128)(2,1)} %get-tuple-element.104), channel_id=1, source_target_pairs={{0,8},{4,12},{8,0},{12,4},{1,9},{5,13},{9,1},{13,5},{2,10},{6,14},... | collective-permute-start | bytes 589832 | tf_op jit(solution)/shard_map/ppermute | solution.py:33
  372.0 25.8 %collective-permute-start.27 = (bf16[768,128]{1,0:T(8,128)(2,1)}, bf16[768,128]{1,0:T(8,128)(2,1)}, u32[]{:S(2)}, u32[]{:S(2)}) collective-permute-start(bf16[768,128]{1,0:T(8,128)(2,1)} %get-tuple-element.105), channel_id=1, source_target_pairs={{0,12},{4,8},{8,4},{12,0},{1,13},{5,9},{9,5},{13,1},{2,14},{6,10},... | collective-permute-start | bytes 589832 | tf_op jit(solution)/shard_map/ppermute | solution.py:33
  398.5 246.5 %reduce-scatter.8.cloned.1.call-start = ((), (), s32[]{:S(2)}) async-start(), calls=%async_computation.8 | async-start | bytes 5242880 | tf_op jit(solution)/shard_map/reduce_scatter | solution.py:1081
  399.1 53.1 %collective-permute-start.24 = (bf16[3,192,2048]{2,1,0:T(8,128)(2,1)}, bf16[3,192,2048]{2,1,0:T(8,128)(2,1)}, u32[]{:S(2)}, u32[]{:S(2)}) collective-permute-start(bf16[3,192,2048]{2,1,0:T(8,128)(2,1)} %others.1.refs_5_.refs_1_), channel_id=1, source_target_pairs={{0,2},{1,3},{2,0},{3,1},{4,6},{5,7},{6,4},{7,5},{8,10},{9,11},{10,... | collective-permute-start | bytes 7077896 | tf_op jit(solution)/shard_map/ppermute | solution.py:33
  400.1 51.5 %collective-permute-start.28 = (bf16[4,512,256]{2,1,0:T(8,128)(2,1)}, bf16[4,512,256]{2,1,0:T(8,128)(2,1)}, u32[]{:S(2)}, u32[]{:S(2)}) collective-permute-start(bf16[4,512,256]{2,1,0:T(8,128)(2,1)} %get-tuple-element.111), channel_id=1, source_target_pairs={{0,16},{16,0},{1,17},{17,1},{2,18},{18,2},{3,19},{19,3},{4,20},{20... | collective-permute-start | bytes 3145736 | tf_op jit(solution)/shard_map/ppermute | solution.py:33
  401.4 60.1 %collective-permute-start.23 = (bf16[3,192,2048]{2,1,0:T(8,128)(2,1)}, bf16[3,192,2048]{2,1,0:T(8,128)(2,1)}, u32[]{:S(2)}, u32[]{:S(2)}) collective-permute-start(bf16[3,192,2048]{2,1,0:T(8,128)(2,1)} %others.1.refs_5_.refs_1_), channel_id=1, source_target_pairs={{0,1},{1,0},{2,3},{3,2},{4,5},{5,4},{6,7},{7,6},{8,9},{9,8},{10,11... | collective-permute-start | bytes 7077896 | tf_op jit(solution)/shard_map/ppermute | solution.py:33
  409.5 42.7 %collective-permute-start.29 = (bf16[1,256,1024]{2,1,0:T(8,128)(2,1)}, bf16[1,256,1024]{2,1,0:T(8,128)(2,1)}, u32[]{:S(2)}, u32[]{:S(2)}) collective-permute-start(bf16[1,256,1024]{2,1,0:T(8,128)(2,1)} %one_block.3.refs_12_), channel_id=1, source_target_pairs={{0,4},{4,0},{8,12},{12,8},{1,5},{5,1},{9,13},{13,9},{2,6},{6,2},{1... | collective-permute-start | bytes 1572872 | tf_op jit(solution)/shard_map/ppermute | solution.py:33
  452.9 11.0 %collective-permute-start.30 = (bf16[3,192,2048]{2,1,0:T(8,128)(2,1)}, bf16[3,192,2048]{2,1,0:T(8,128)(2,1)}, u32[]{:S(2)}, u32[]{:S(2)}) collective-permute-start(bf16[3,192,2048]{2,1,0:T(8,128)(2,1)} %tie.14.refs_3_), channel_id=1, source_target_pairs={{0,1},{1,0},{2,3},{3,2},{4,5},{5,4},{6,7},{7,6},{8,9},{9,8},{10,11... | collective-permute-start | bytes 7077896 | tf_op jit(solution)/shard_map/ppermute | solution.py:33
  452.9 25.6 %collective-permute-start.19 = (bf16[192,2048]{1,0:T(8,128)(2,1)}, bf16[192,2048]{1,0:T(8,128)(2,1)}, u32[]{:S(2)}, u32[]{:S(2)}) collective-permute-start(bf16[192,2048]{1,0:T(8,128)(2,1)} %sums.12.refs_7_), channel_id=1, source_target_pairs={{0,2},{1,3},{2,0},{3,1},{4,6},{5,7},{6,4},{7,5},{8,10},{9,11},{10,... | collective-permute-start | bytes 2359304 | tf_op jit(solution)/shard_map/ppermute | solution.py:33
  453.8 47.5 %collective-permute-start.31 = (bf16[768,384]{1,0:T(8,128)(2,1)}, bf16[768,384]{1,0:T(8,128)(2,1)}, u32[]{:S(2)}, u32[]{:S(2)}) collective-permute-start(bf16[768,384]{1,0:T(8,128)(2,1)} %get-tuple-element.112.refs_6_), channel_id=1, source_target_pairs={{0,4},{4,0},{8,12},{12,8},{1,5},{5,1},{9,13},{13,9},{2,6},{6,2},{1... | collective-permute-start | bytes 1769480 | tf_op jit(solution)/shard_map/ppermute | solution.py:33
  461.5 60.3 %collective-permute-start.32 = (bf16[768,384]{1,0:T(8,128)(2,1)}, bf16[768,384]{1,0:T(8,128)(2,1)}, u32[]{:S(2)}, u32[]{:S(2)}) collective-permute-start(bf16[768,384]{1,0:T(8,128)(2,1)} %get-tuple-element.113.refs_7_), channel_id=1, source_target_pairs={{0,8},{4,12},{8,0},{12,4},{1,9},{5,13},{9,1},{13,5},{2,10},{6,14},... | collective-permute-start | bytes 1769480 | tf_op jit(solution)/shard_map/ppermute | solution.py:33
  461.5 60.3 %collective-permute-start.33 = (bf16[768,384]{1,0:T(8,128)(2,1)}, bf16[768,384]{1,0:T(8,128)(2,1)}, u32[]{:S(2)}, u32[]{:S(2)}) collective-permute-start(bf16[768,384]{1,0:T(8,128)(2,1)} %get-tuple-element.114.refs_8_), channel_id=1, source_target_pairs={{0,12},{4,8},{8,4},{12,0},{1,13},{5,9},{9,5},{13,1},{2,14},{6,10},... | collective-permute-start | bytes 1769480 | tf_op jit(solution)/shard_map/ppermute | solution.py:33
  522.5 144.7 %all-gather.10.cloned.1.call-start = ((), (), s32[]{:S(2)}) async-start(), calls=%async_computation.7 | async-start | bytes 3932160 | tf_op jit(solution)/shard_map/all_gather | solution.py:1161
  534.0 3.8 collective-permute-start.34
  540.7 19.9 %collective-permute-start.36 = (bf16[192,2048]{1,0:T(8,128)(2,1)}, bf16[192,2048]{1,0:T(8,128)(2,1)}, u32[]{:S(2)}, u32[]{:S(2)}) collective-permute-start(bf16[192,2048]{1,0:T(8,128)(2,1)} %sums.15.refs_2_.refs_1_), channel_id=1, source_target_pairs={{0,2},{1,3},{2,0},{3,1},{4,6},{5,7},{6,4},{7,5},{8,10},{9,11},{10,... | collective-permute-start | bytes 2359304 | tf_op jit(solution)/shard_map/ppermute | solution.py:33
  565.4 59.1 %collective-permute-start.38 = (bf16[208,2048]{1,0:T(8,128)(2,1)}, bf16[208,2048]{1,0:T(8,128)(2,1)S(1)}, u32[]{:S(2)}, u32[]{:S(2)}) collective-permute-start(bf16[208,2048]{1,0:T(8,128)(2,1)} %input_back.1.refs_0_.refs_4_), channel_id=1, source_target_pairs={{0,2},{1,3},{2,0},{3,1},{4,6},{5,7},{6,4},{7,5},{8,10},{9,11},{10,... | collective-permute-start | bytes 2555912 | tf_op jit(solution)/shard_map/ppermute | solution.py:33
  565.8 20.1 %copy-start = (bf16[208,2048]{1,0:T(8,128)(2,1)S(1)}, bf16[208,2048]{1,0:T(8,128)(2,1)}, u32[]{:S(2)}) copy-start(bf16[208,2048]{1,0:T(8,128)(2,1)} %input_back.1.refs_0_.refs_4_) | copy-start | bytes 2555908
  565.8 57.8 %collective-permute-start.39 = (bf16[4,256,384]{2,1,0:T(8,128)(2,1)}, bf16[4,256,384]{2,1,0:T(8,128)(2,1)S(1)}, u32[]{:S(2)}, u32[]{:S(2)}) collective-permute-start(bf16[4,256,384]{2,1,0:T(8,128)(2,1)} %get-tuple-element.127), channel_id=1, source_target_pairs={{0,16},{16,0},{1,17},{17,1},{2,18},{18,2},{3,19},{19,3},{4,20},{20... | collective-permute-start | bytes 2359304 | tf_op jit(solution)/shard_map/ppermute | solution.py:33
  567.9 55.8 %collective-permute-start.35 = (bf16[192,2048]{1,0:T(8,128)(2,1)}, bf16[192,2048]{1,0:T(8,128)(2,1)S(1)}, u32[]{:S(2)}, u32[]{:S(2)}) collective-permute-start(bf16[192,2048]{1,0:T(8,128)(2,1)} %tie.16), channel_id=1, source_target_pairs={{0,4},{4,0},{8,12},{12,8},{1,5},{5,1},{9,13},{13,9},{2,6},{6,2},{1... | collective-permute-start | bytes 2359304 | tf_op jit(solution)/shard_map/ppermute | solution.py:33
  585.9 37.8 %collective-permute-start.40 = (bf16[2,512,256]{2,1,0:T(8,128)(2,1)}, bf16[2,512,256]{2,1,0:T(8,128)(2,1)S(1)}, u32[]{:S(2)}, u32[]{:S(2)}) collective-permute-start(bf16[2,512,256]{2,1,0:T(8,128)(2,1)} %tie.18), channel_id=1, source_target_pairs={{0,8},{4,12},{8,0},{12,4},{1,9},{5,13},{9,1},{13,5},{2,10},{6,14},... | collective-permute-start | bytes 1572872 | tf_op jit(solution)/shard_map/ppermute | solution.py:33
  586.0 41.0 %collective-permute-start.37 = (bf16[208,2048]{1,0:T(8,128)(2,1)S(1)}, bf16[208,2048]{1,0:T(8,128)(2,1)}, u32[]{:S(2)}, u32[]{:S(2)}) collective-permute-start(bf16[208,2048]{1,0:T(8,128)(2,1)S(1)} %copy-done), channel_id=1, source_target_pairs={{0,1},{1,0},{2,3},{3,2},{4,5},{5,4},{6,7},{7,6},{8,9},{9,8},{10,11... | collective-permute-start | bytes 2555912 | tf_op jit(solution)/shard_map/ppermute | solution.py:33
  623.7 0.8 copy-start.4
  623.7 1.0 copy-start.3
  624.5 0.9 copy-start.2
  625.4 0.9 copy-start.1
  626.9 2.8 collective-permute-start.41
  638.5 23.8 %collective-permute-start.47 = (bf16[1,256,1024]{2,1,0:T(8,128)(2,1)}, bf16[1,256,1024]{2,1,0:T(8,128)(2,1)}, u32[]{:S(2)}, u32[]{:S(2)}) collective-permute-start(bf16[1,256,1024]{2,1,0:T(8,128)(2,1)} %one_block.4.refs_7_), channel_id=1, source_target_pairs={{0,4},{4,0},{8,12},{12,8},{1,5},{5,1},{9,13},{13,9},{2,6},{6,2},{1... | collective-permute-start | bytes 1572872 | tf_op jit(solution)/shard_map/ppermute | solution.py:33
  642.5 0.6 copy-start.5
  643.7 6.6 collective-permute-start.42
  647.6 22.1 %collective-permute-start.46 = (bf16[1,256,1024]{2,1,0:T(8,128)(2,1)}, bf16[1,256,1024]{2,1,0:T(8,128)(2,1)}, u32[]{:S(2)}, u32[]{:S(2)}) collective-permute-start(bf16[1,256,1024]{2,1,0:T(8,128)(2,1)} %one_block.5.refs_2_), channel_id=1, source_target_pairs={{0,4},{4,0},{8,12},{12,8},{1,5},{5,1},{9,13},{13,9},{2,6},{6,2},{1... | collective-permute-start | bytes 1572872 | tf_op jit(solution)/shard_map/ppermute | solution.py:33
  657.9 16.3 %collective-permute-start.43 = (bf16[272,384]{1,0:T(8,128)(2,1)}, bf16[272,384]{1,0:T(8,128)(2,1)}, u32[]{:S(2)}, u32[]{:S(2)}) collective-permute-start(bf16[272,384]{1,0:T(8,128)(2,1)} %get-tuple-element.133), channel_id=1, source_target_pairs={{0,4},{4,0},{8,12},{12,8},{1,5},{5,1},{9,13},{13,9},{2,6},{6,2},{1... | collective-permute-start | bytes 626696 | tf_op jit(solution)/shard_map/ppermute | solution.py:33
  657.9 16.3 %collective-permute-start.44 = (bf16[272,384]{1,0:T(8,128)(2,1)}, bf16[272,384]{1,0:T(8,128)(2,1)}, u32[]{:S(2)}, u32[]{:S(2)}) collective-permute-start(bf16[272,384]{1,0:T(8,128)(2,1)} %get-tuple-element.134), channel_id=1, source_target_pairs={{0,8},{4,12},{8,0},{12,4},{1,9},{5,13},{9,1},{13,5},{2,10},{6,14},... | collective-permute-start | bytes 626696 | tf_op jit(solution)/shard_map/ppermute | solution.py:33
  658.0 23.0 %collective-permute-start.45 = (bf16[272,384]{1,0:T(8,128)(2,1)}, bf16[272,384]{1,0:T(8,128)(2,1)}, u32[]{:S(2)}, u32[]{:S(2)}) collective-permute-start(bf16[272,384]{1,0:T(8,128)(2,1)} %get-tuple-element.135), channel_id=1, source_target_pairs={{0,12},{4,8},{8,4},{12,0},{1,13},{5,9},{9,5},{13,1},{2,14},{6,10},... | collective-permute-start | bytes 626696 | tf_op jit(solution)/shard_map/ppermute | solution.py:33
  662.3 23.2 %collective-permute-start.48 = (bf16[1,512,256]{2,1,0:T(8,128)(2,1)}, bf16[1,512,256]{2,1,0:T(8,128)(2,1)}, u32[]{:S(2)}, u32[]{:S(2)}) collective-permute-start(bf16[1,512,256]{2,1,0:T(8,128)(2,1)} %get-tuple-element.140), channel_id=1, source_target_pairs={{0,4},{4,0},{8,12},{12,8},{1,5},{5,1},{9,13},{13,9},{2,6},{6,2},{1... | collective-permute-start | bytes 786440 | tf_op jit(solution)/shard_map/ppermute | solution.py:33
Sparse Core Ops, SparseCore 0:
  68.3 56.5 all-gather.5
  166.4 46.0 all-gather.7
  224.8 62.7 all-gather.11
  302.6 104.2 reduce-scatter.3
  410.0 122.8 reduce-scatter.5
  535.7 101.4 reduce-scatter.7
  639.4 27.6 all-gather.9

commit v5 on v4

--- a/solution.py
+++ b/solution.py
@@ -97,9 +97,8 @@
 
 
 def rope_tables(positions):
-    sign = jnp.where((jnp.arange(128) % HEAD_DIM) < HEAD_DIM // 2, -1.0, 1.0)
-    angle = positions.astype(F32)[:, None] * rope_freq()[None, :]
-    return jnp.cos(angle), jnp.sin(angle) * sign
+    angle = rope_freq()[: HEAD_DIM // 2, None] * positions.astype(F32)[None, :]
+    return jnp.cos(angle), jnp.sin(angle)
 
 
 def project_kernel(ix, tok_ref, gain_ref, cos_ref, sin_ref, wq_ref, wk_ref, wv_ref, first_ref, o0, o1, o2, o3, held):
@@ -108,7 +107,9 @@
     inverse = lax.rsqrt(jnp.mean(rows * rows, axis=-1, keepdims=True) + EPS)
     first = (rows * inverse * gain_ref[...]).astype(LOW)
     first_ref[...] = first
-    cosine, sine = cos_ref[...], sin_ref[...]
+    half_cos, half_sin = cos_ref[...].T, sin_ref[...].T
+    cosine = jnp.concatenate([half_cos] * 4, axis=1)
+    sine = jnp.concatenate([-half_sin, half_sin] * 2, axis=1)
     for place, weight in enumerate((wq_ref, wk_ref, wv_ref)):
         flat = dot(first, weight[...])
         for group in range(4):
@@ -132,7 +133,7 @@
         project_kernel, "project", ix, (rows // step,),
         [tokens, gain, *tables, *weights],
         [pl.BlockSpec((step, width), along), pl.BlockSpec((1, width), whole)]
-        + [pl.BlockSpec((step, 128), along)] * 2 + [pl.BlockSpec((width, local), whole)] * 3,
+        + [pl.BlockSpec((HEAD_DIM // 2, step), lambda i, m: (0, i))] * 2 + [pl.BlockSpec((width, local), whole)] * 3,
         [shaped((rows, width))] + [shaped((rows, 384))] * 4,
         [pl.BlockSpec((step, width), along)] + [pl.BlockSpec((step, 384), along)] * 4,
         [pltpu.VMEM((4, step, 384), LOW)],
@@ -256,6 +257,7 @@
     key, value = held[here_rows, 128:256], held[here_rows, 256:384]
     keys = [own_lanes(key, head) for head in range(2)]
     values = [own_lanes(value, head) for head in range(2)]
+    keys_turned = [own.T for own in keys]
 
     def step(at, queries, kept, diagonal):
         size = queries.stop - queries.start
@@ -275,14 +277,15 @@
             score_back = (chance * (chance_back - shift)).astype(LOW)
             value_part = dot(chance.astype(LOW), up_at[head, rows, :])
             key_part = dot(score_back, query_at[head, rows, :])
-            query_part = across(score_back, keys[head][:kept])
+            query_part = dot(keys_turned[head][:, :kept], score_back)
             if head == 0:
                 value_total, key_total, query_total = value_part, key_part, query_part
             else:
                 value_total += value_part
                 key_total += key_part
                 query_total += query_part
-        query_sum[rows, :] += query_total
+        columns = pl.ds(pl.multiple_of(at * stretch + queries.start, 128), size)
+        query_sum[:, columns] += query_total
         return key_total, value_total
 
     key_sum[...], value_sum[...] = step(here, slice(half, stretch), stretch, True)
@@ -313,7 +316,8 @@
     @pl.when(turn == count - 1)
     def _():
         for slot, out in enumerate((o0, o1, o2, o3)):
-            rows = query_sum[pl.ds((slot ^ me) * stretch, stretch), :] * HEAD_DIM**-0.5
+            columns = pl.ds(pl.multiple_of((slot ^ me) * stretch, 128), stretch)
+            rows = query_sum[:, columns].T * HEAD_DIM**-0.5
             out[:, 0:128] = back_rope(rows, slot ^ me).astype(LOW)
 
 
@@ -334,7 +338,7 @@
             pltpu.VMEM((2, length, 128), LOW),
             pltpu.VMEM((2, length, 128), LOW),
             pltpu.VMEM((4, 16, stretch), F32),
-            pltpu.VMEM((length, 128), F32),
+            pltpu.VMEM((128, length), F32),
             pltpu.VMEM((stretch, 128), F32),
             pltpu.VMEM((stretch, 128), F32),
             pltpu.SemaphoreType.DMA((8,)),
@@ -548,6 +552,16 @@
         shaped((rows + 16, width)), pl.BlockSpec((step, width), lambda i, m: (i, 0)),
         [pltpu.VMEM((1, width), F32)], after=after,
     )
+
+
+def copied_kernel(ix, in_ref, out_ref):
+    out_ref[...] = in_ref[...]
+
+
+def copied(ix, rows, after=()):
+    count, width = rows.shape
+    spec = pl.BlockSpec((count // 2, width), lambda i, m: (i, 0))
+    return call(copied_kernel, "copied", ix, (2,), [rows], [spec], shaped((count, width)), spec, after=after)
 
 
 def join_input_kernel(ix, q0, q1, q2, q3, out_ref, sum_ref, held, sems):
@@ -1159,6 +1173,8 @@
         after=(input_grad,),
     )
     output = lax.all_gather(output_mine, TENSOR, axis=0, tiled=True)
+    if not two_dp:
+        output = copied(ix, output)
     if two_dp:
         up_low = one_block(ix, sum_up, 1, (output_mine,))
         up_other = swap(up_low, CTX, 1)
@@ -1167,7 +1183,8 @@
         qkv_parts = over_ctx(add_parts(ix, qkv_own, qkv_other, gains, (out_part[0],)))
         gate_grad = halves(ix, sum_gate, gate_other, 1, (qkv_parts[0],))
         up_grad = halves(ix, sum_up, up_other, 1, (gate_grad,))
-        *qkv, gains = project_last(ix, qkv_parts, share, (up_grad,))
+        output = copied(ix, output, (up_grad,))
+        *qkv, gains = project_last(ix, qkv_parts, share, (output,))
         out_grad = add_last(ix, out_part[0], out_other, (qkv[0],))
     else:
         def scattered(blocks, axis):

time: 707 us -> 701 us (level)
    pallas_call x44 -> x45, Pallas kernels: 338 us -> 340 us  [call(): pl.pallas_call(body, grid_spec=pltpu.PrefetchScalarGridSpec(num_scalar_pr...]
  transfers between devices with their start and end apart: 56 -> 56, of which waited for: 26 -> 24; matrix products, arithmetic and copies ran while one was open for 1% -> 1% of each run, Pallas kernels for 45% -> 46%
where the time goes in v5:
time: 701 us; the launch traced here: 694 us
  Pallas kernels  346 us (49%)
  waiting for transfers between devices  234 us (33%)
  starting transfers between devices  81.9 us (12%)
  between operations  14.8 us (2%)
  local copies, waits for them, and re-layouts  11.1 us (2%)
    pallas_call x45, Pallas kernels, call(): pl.pallas_call(body, grid_spec=pltpu.PrefetchScalarGridSpec(num_scalar_pr...  340 us
    ppermute x49, waiting for transfers between devices, swap(): return lax.ppermute(value, axis, [(i, i ^ distance) for i in range(size)])  229 us
    ppermute x49, starting transfers between devices, swap(): return lax.ppermute(value, axis, [(i, i ^ distance) for i in range(size)])  80.7 us
  transfers between devices with their start and end apart: 56, of which 24 were waited for; matrix products, arithmetic and copies ran while one was open for 1% of the time, Pallas kernels for 46%

profile of v5, /device:TPU:0, one launch (start us, length us, event | category | flops | bytes accessed | tf_op | source)
XLA Modules:
  0.0 693.7 jit_solution(3057203101594556084)
XLA Ops:
  9.0 11.2 %project.1 = (bf16[768,2048]{1,0:T(8,128)(2,1)}, bf16[768,384]{1,0:T(8,128)(2,1)}, bf16[768,384]{1,0:T(8,128)(2,1)}, bf16[768,384]{1,0:T(8,128)(2,1)}, bf16[768,384]{1,0:T(8,128)(2,1)}) custom-call(s32[3]{0:T(128)} %pad_add_fusion.index_ref.refs_0_, bf16[768,2048]{1,0:T(8,128)(2,1)} %refs_4_.13, f32[1,2048]{1,0:T(1,128)} %bitcast.30, ...), custom_call_target="tpu_custom_call" | custom-call | bytes 80740352 | tf_op jit(solution)/shard_map/project/pallas_call | solution.py:58
  20.2 3.0 collective-permute-start
  25.8 8.0 %hidden_back.2.refs_1_.refs_6_ = f32[768,1024]{1,0:T(8,128)} custom-call(s32[3]{0:T(128)} %pad_add_fusion.index_ref.refs_0_, bf16[768,2048]{1,0:T(8,128)(2,1)} %refs_0_.5, bf16[2048,2048]{1,0:T(8,128)(2,1)} %refs_1_.9, bf16[768,384]{1,0:T(8,128)(2,1)} %get-tuple-element.76.refs_2_.refs_0_), custom_call_target="tpu_custom_call" | custom-call | bytes 62390272 | tf_op jit(solution)/shard_map/hidden_back/pallas_call | solution.py:58
  35.2 8.0 %rope_tables.1 = (f32[3072,128]{1,0:T(8,128)}, f32[3072,128]{1,0:T(8,128)}) custom-call(s32[3]{0:T(128)} %pad_add_fusion.index_ref.refs_0_, f32[1,128]{1,0:T(1,128)} %maximum_bitcast_fusion.refs_0_, f32[768,1024]{1,0:T(8,128)} %hidden_back.2.refs_1_.refs_6_), custom_call_target="tpu_custom_call" | custom-call | bytes 58720256 | tf_op jit(solution)/shard_map/rope_tables/pallas_call | solution.py:58
  48.7 17.2 %collective-permute-done.1.refs_2_.refs_3_ = bf16[768,384]{1,0:T(8,128)(2,1)} collective-permute-done((bf16[768,384]{1,0:T(8,128)(2,1)}, bf16[768,384]{1,0:T(8,128)(2,1)}, u32[]{:S(2)}, u32[]{:S(2)}) %collective-permute-start.1) | collective-permute-done | bytes 589856 | tf_op jit(solution)/shard_map/ppermute | solution.py:33
  66.9 27.7 %attend.1 = (bf16[768,128]{1,0:T(8,128)(2,1)}, bf16[768,128]{1,0:T(8,128)(2,1)}, bf16[768,128]{1,0:T(8,128)(2,1)}, bf16[768,128]{1,0:T(8,128)(2,1)}, f32[3072,128]{1,0:T(8,128)}, /*index=5*/f32[4,16,768]{2,1,0:T(8,128)}) custom-call(s32[3]{0:T(128)} %pad_add_fusion.index_ref.refs_0_, bf16[768,384]{1,0:T(8,128)(2,1)} %get-tuple-element.76.refs_2_.refs_0_, ...), custom_call_target="tpu_custom_call" | custom-call | bytes 205520896 | tf_op jit(solution)/shard_map/attend/pallas_call | solution.py:58
  94.7 11.8 %collective-permute-start.3 = (bf16[768,128]{1,0:T(8,128)(2,1)}, bf16[768,128]{1,0:T(8,128)(2,1)}, u32[]{:S(2)}, u32[]{:S(2)}) collective-permute-start(bf16[768,128]{1,0:T(8,128)(2,1)} %get-tuple-element.83), channel_id=1, source_target_pairs={{0,4},{4,0},{8,12},{12,8},{1,5},{5,1},{9,13},{13,9},{2,6},{6,2},{1... | collective-permute-start | bytes 589832 | tf_op jit(solution)/shard_map/ppermute | solution.py:33
  109.0 11.3 %collective-permute-done.3.refs_1_ = bf16[768,128]{1,0:T(8,128)(2,1)} collective-permute-done((bf16[768,128]{1,0:T(8,128)(2,1)}, bf16[768,128]{1,0:T(8,128)(2,1)}, u32[]{:S(2)}, u32[]{:S(2)}) %collective-permute-start.3) | collective-permute-done | bytes 196640 | tf_op jit(solution)/shard_map/ppermute | solution.py:33
  120.8 7.0 %collective-permute-done.5.refs_3_ = bf16[768,128]{1,0:T(8,128)(2,1)} collective-permute-done((bf16[768,128]{1,0:T(8,128)(2,1)}, bf16[768,128]{1,0:T(8,128)(2,1)}, u32[]{:S(2)}, u32[]{:S(2)}) %collective-permute-start.5) | collective-permute-done | bytes 196640 | tf_op jit(solution)/shard_map/ppermute | solution.py:33
  127.8 6.3 join_heads.1
  134.2 3.7 collective-permute-done.6.refs_1_
  138.0 2.9 sums.8
  142.8 18.2 %collective-permute-done.7.refs_2_ = bf16[192,2048]{1,0:T(8,128)(2,1)} collective-permute-done((bf16[192,2048]{1,0:T(8,128)(2,1)}, bf16[192,2048]{1,0:T(8,128)(2,1)}, u32[]{:S(2)}, u32[]{:S(2)}) %collective-permute-start.7) | collective-permute-done | bytes 786464 | tf_op jit(solution)/shard_map/ppermute | solution.py:33
  160.9 3.8 middle.1
  166.6 8.1 %hidden_back.3.refs_2_.refs_3_ = f32[768,1024]{1,0:T(8,128)} custom-call(s32[3]{0:T(128)} %pad_add_fusion.index_ref.refs_0_, bf16[1536,2048]{1,0:T(8,128)(2,1)} %all-gather.6.cloned.1.call-done.refs_8_.refs_0_.refs_1_, bf16[2048,2048]{1,0:T(8,128)(2,1)} %refs_1_.9, bf16[192,2048]{1,0:T(8,128)(2,1)} %get-tuple-element.88.refs_2_.refs_0_), custom_call_target="tpu_custom_call" | custom-call | bytes 62390272 | tf_op jit(solution)/shard_map/hidden_back/pallas_call | solution.py:58
  174.8 21.3 %collective-permute-done.9.refs_1_ = bf16[192,2048]{1,0:T(8,128)(2,1)} collective-permute-done((bf16[192,2048]{1,0:T(8,128)(2,1)}, bf16[192,2048]{1,0:T(8,128)(2,1)}, u32[]{:S(2)}, u32[]{:S(2)}) %collective-permute-start.9) | collective-permute-done | bytes 786464 | tf_op jit(solution)/shard_map/ppermute | solution.py:33
  196.8 2.8 collective-permute-done.10.refs_3_
  199.6 22.9 %feed.2 = (bf16[768,2048]{1,0:T(8,128)(2,1)}, bf16[768,1024]{1,0:T(8,128)(2,1)}, bf16[768,1024]{1,0:T(8,128)(2,1)}, bf16[768,1024]{1,0:T(8,128)(2,1)}, bf16[2,19...) custom-call(s32[3]{0:T(128)} %pad_add_fusion.index_ref.refs_0_, bf16[192,2048]{1,0:T(8,128)(2,1)} %get-tuple-element.88.refs_2_.refs_0_, ...), custom_call_target="tpu_custom_call" | custom-call | bytes 176160768 | tf_op jit(solution)/shard_map/feed/pallas_call | solution.py:58
  223.6 22.8 %feed.3 = (bf16[768,2048]{1,0:T(8,128)(2,1)}, bf16[768,1024]{1,0:T(8,128)(2,1)}, bf16[768,1024]{1,0:T(8,128)(2,1)}, bf16[768,1024]{1,0:T(8,128)(2,1)}, bf16[2,19...) custom-call(s32[3]{0:T(128)} %pad_add_fusion.index_ref.refs_0_, ...), custom_call_target="tpu_custom_call" | custom-call | bytes 176160768 | tf_op jit(solution)/shard_map/feed/pallas_call | solution.py:58
  246.6 3.6 collective-permute-done.12.refs_1_
  250.2 2.9 sums.9.refs_2_
  255.5 8.7 %feed_down.2 = (bf16[2,192,2048]{2,1,0:T(8,128)(2,1)}, bf16[2,192,2048]{2,1,0:T(8,128)(2,1)}) custom-call(s32[3]{0:T(128)} %pad_add_fusion.index_ref.refs_0_, bf16[768,1024]{1,0:T(8,128)(2,1)} %get-tuple-element.94.refs_0_.refs_3_, bf16[2048,2048]{1,0:T(8,128)(2,1)} %refs_1_.9, bf16[192,2048]{1,0:T(8,128)(2,1)} %sums.9.refs_2_), custom_call_target="tpu_custom_call" | custom-call | bytes 66060288 | tf_op jit(solution)/shard_map/feed_down/pallas_call | solution.py:58
  264.2 9.4 %collective-permute-done.13.refs_2_ = bf16[192,2048]{1,0:T(8,128)(2,1)} collective-permute-done((bf16[192,2048]{1,0:T(8,128)(2,1)}, bf16[192,2048]{1,0:T(8,128)(2,1)}, u32[]{:S(2)}, u32[]{:S(2)}) %collective-permute-start.13) | collective-permute-done | bytes 786464 | tf_op jit(solution)/shard_map/ppermute | solution.py:33
  273.6 3.2 sums.10.refs_2_
  276.8 12.9 %wgrad_down.1.refs_1_ = bf16[8,256,1024]{2,1,0:T(8,128)(2,1)} custom-call(s32[3]{0:T(128)} %pad_add_fusion.index_ref.refs_0_, bf16[768,2048]{1,0:T(8,128)(2,1)} %refs_0_.5, bf16[1536,2048]{1,0:T(8,128)(2,1)} %all-gather.6.cloned.1.call-done.refs_8_.refs_0_.refs_1_, bf16[768,1024]{1,0:T(8,128)(2,1)} %get-tuple-element.89.refs_6_.refs_0_.refs_2_, ...), custom_call_target="tpu_custom_call" | custom-call | bytes 102760448 | tf_op jit(solution)/shard_map/wgrad_down/pallas_call | solution.py:58
  289.7 10.6 %collective-permute-done.16.refs_3_.refs_2_ = bf16[192,2048]{1,0:T(8,128)(2,1)} collective-permute-done((bf16[192,2048]{1,0:T(8,128)(2,1)}, bf16[192,2048]{1,0:T(8,128)(2,1)}, u32[]{:S(2)}, u32[]{:S(2)}) %collective-permute-start.16) | collective-permute-done | bytes 786464 | tf_op jit(solution)/shard_map/ppermute | solution.py:33
  303.0 5.2 collective-permute-done.11.refs_1_
  308.2 2.9 sums.11.refs_2_
  312.6 8.7 %feed_down.3 = (bf16[2,192,2048]{2,1,0:T(8,128)(2,1)}, bf16[2,192,2048]{2,1,0:T(8,128)(2,1)}) custom-call(s32[3]{0:T(128)} %pad_add_fusion.index_ref.refs_0_, bf16[768,1024]{1,0:T(8,128)(2,1)} %get-tuple-element.89.refs_6_.refs_0_.refs_2_, bf16[2048,2048]{1,0:T(8,128)(2,1)} %refs_1_.9, bf16[192,2048]{1,0:T(8,128)(2,1)} %sums.11.refs_2_), custom_call_target="tpu_custom_call" | custom-call | bytes 66060288 | tf_op jit(solution)/shard_map/feed_down/pallas_call | solution.py:58
  321.4 2.9 sums.12.refs_7_
  324.3 6.7 collective-permute-done.15.refs_2_
  331.0 5.3 middle_back.1
  337.8 17.5 %collective-permute-done.21.refs_2_ = bf16[192,2048]{1,0:T(8,128)(2,1)} collective-permute-done((bf16[192,2048]{1,0:T(8,128)(2,1)}, bf16[192,2048]{1,0:T(8,128)(2,1)}, u32[]{:S(2)}, u32[]{:S(2)}) %collective-permute-start.21) | collective-permute-done | bytes 786464 | tf_op jit(solution)/shard_map/ppermute | solution.py:33
  355.4 2.9 sums.13.refs_8_
  359.8 7.0 %branch_back.1 = (bf16[768,2048]{1,0:T(8,128)(2,1)}, bf16[768,128]{1,0:T(8,128)(2,1)}, bf16[768,128]{1,0:T(8,128)(2,1)}, bf16[768,128]{1,0:T(8,128)(2,1)}, bf16[768,128]{1,0:T(8,128)(2,1)}) custom-call(s32[3]{0:T(128)} %pad_add_fusion.index_ref.refs_0_, bf16[192,2048]{1,0:T(8,128)(2,1)} %get-tuple-element.100.refs_2_.refs_0_, ...), custom_call_target="tpu_custom_call" | custom-call | bytes 51380224 | tf_op jit(solution)/shard_map/branch_back/pallas_call | solution.py:58
  371.2 3.7 others.1.refs_5_.refs_1_
  375.0 8.5 %out_wgrad.1 = (bf16[4,512,256]{2,1,0:T(8,128)(2,1)}, bf16[4,512,256]{2,1,0:T(8,128)(2,1)}) custom-call(s32[3]{0:T(128)} %pad_add_fusion.index_ref.refs_0_, bf16[768,128]{1,0:T(8,128)(2,1)} %get-tuple-element.82.refs_0_, bf16[768,128]{1,0:T(8,128)(2,1)} %collective-permute-done.3.refs_1_, bf16[768,128]{1,0:T(8,128)(2,1)} %collective-permute-done.4.refs_2_, ...), custom_call_target="tpu_custom_call" | custom-call | bytes 62390272 | tf_op jit(solution)/shard_map/out_wgrad/pallas_call | solution.py:58
  383.5 12.9 %wgrad_gate.1.refs_1_ = bf16[8,256,1024]{2,1,0:T(8,128)(2,1)} custom-call(s32[3]{0:T(128)} %pad_add_fusion.index_ref.refs_0_, bf16[768,2048]{1,0:T(8,128)(2,1)} %get-tuple-element.116.refs_0_, bf16[768,2048]{1,0:T(8,128)(2,1)} %get-tuple-element.117.refs_1_, bf16[768,1024]{1,0:T(8,128)(2,1)} %get-tuple-element.125.refs_2_, ...), custom_call_target="tpu_custom_call" | custom-call | bytes 102760448 | tf_op jit(solution)/shard_map/wgrad_gate/pallas_call | solution.py:58
  399.9 5.7 reduce-scatter.4.cloned.1.call-done.refs_0_
  409.8 38.2 %attend_back.1 = (bf16[768,384]{1,0:T(8,128)(2,1)}, bf16[768,384]{1,0:T(8,128)(2,1)}, bf16[768,384]{1,0:T(8,128)(2,1)}, bf16[768,384]{1,0:T(8,128)(2,1)}) custom-call(s32[3]{0:T(128)} %pad_add_fusion.index_ref.refs_0_, bf16[768,384]{1,0:T(8,128)(2,1)} %get-tuple-element.76.refs_2_.refs_0_, bf16[768,384]{1,0:T(8,128)(2,1)} %collective-permute-done.refs_1_.refs_2_, ...), custom_call_target="tpu_custom_call" | custom-call | bytes 293601280 | tf_op jit(solution)/shard_map/attend_back/pallas_call | solution.py:58
  452.4 7.7 %collective-permute-start.31 = (bf16[768,384]{1,0:T(8,128)(2,1)}, bf16[768,384]{1,0:T(8,128)(2,1)}, u32[]{:S(2)}, u32[]{:S(2)}) collective-permute-start(bf16[768,384]{1,0:T(8,128)(2,1)} %get-tuple-element.112.refs_6_), channel_id=1, source_target_pairs={{0,4},{4,0},{8,12},{12,8},{1,5},{5,1},{9,13},{13,9},{2,6},{6,2},{1... | collective-permute-start | bytes 1769480 | tf_op jit(solution)/shard_map/ppermute | solution.py:33
  462.4 14.7 %project_wgrad.1 = (bf16[4,256,384]{2,1,0:T(8,128)(2,1)}, bf16[4,256,384]{2,1,0:T(8,128)(2,1)}) custom-call(s32[3]{0:T(128)} %pad_add_fusion.index_ref.refs_0_, bf16[768,2048]{1,0:T(8,128)(2,1)} %get-tuple-element.80.refs_0_, bf16[3,192,2048]{2,1,0:T(8,128)(2,1)} %others.1.refs_5_.refs_1_, bf16[3,192,2048]{2,1,0:T(8,128)(2,1)} %collective-permute-done.23.refs_2_, ...), custom_call_target="tpu_custom_call" | custom-call | bytes 95420416 | tf_op jit(solution)/shard_map/project_wgrad/pallas_call | solution.py:58
  477.2 3.2 sums.14.refs_2_.refs_1_
  480.3 3.3 add_blocks.3
  483.6 3.5 halves.3.refs_4_
  487.1 12.9 %wgrad_up.1.refs_1_ = bf16[8,256,1024]{2,1,0:T(8,128)(2,1)} custom-call(s32[3]{0:T(128)} %pad_add_fusion.index_ref.refs_0_, bf16[768,2048]{1,0:T(8,128)(2,1)} %get-tuple-element.116.refs_0_, bf16[768,2048]{1,0:T(8,128)(2,1)} %get-tuple-element.117.refs_1_, bf16[768,1024]{1,0:T(8,128)(2,1)} %get-tuple-element.118.refs_2_, ...), custom_call_target="tpu_custom_call" | custom-call | bytes 102760448 | tf_op jit(solution)/shard_map/wgrad_up/pallas_call | solution.py:58
  500.0 20.3 %collective-permute-done.32.refs_3_.refs_2_ = bf16[768,384]{1,0:T(8,128)(2,1)} collective-permute-done((bf16[768,384]{1,0:T(8,128)(2,1)}, bf16[768,384]{1,0:T(8,128)(2,1)}, u32[]{:S(2)}, u32[]{:S(2)}) %collective-permute-start.32) | collective-permute-done | bytes 589856 | tf_op jit(solution)/shard_map/ppermute | solution.py:33
  521.1 11.5 %project_back.1 = (bf16[2,192,2048]{2,1,0:T(8,128)(2,1)}, bf16[2,192,2048]{2,1,0:T(8,128)(2,1)}) custom-call(s32[3]{0:T(128)} %pad_add_fusion.index_ref.refs_0_, bf16[768,384]{1,0:T(8,128)(2,1)} %get-tuple-element.110.refs_2_.refs_5_.refs_0_, bf16[768,384]{1,0:T(8,128)(2,1)} %collective-permute-done.31.refs_2_.refs_1_, ...), custom_call_target="tpu_custom_call" | custom-call | bytes 80740352 | tf_op jit(solution)/shard_map/project_back/pallas_call | solution.py:58
  532.7 3.7 collective-permute-done.34.refs_1_
  536.4 2.9 sums.15.refs_2_.refs_1_
  541.8 17.4 %collective-permute-done.36.refs_2_ = bf16[192,2048]{1,0:T(8,128)(2,1)} collective-permute-done((bf16[192,2048]{1,0:T(8,128)(2,1)}, bf16[192,2048]{1,0:T(8,128)(2,1)}, u32[]{:S(2)}, u32[]{:S(2)}) %collective-permute-start.36) | collective-permute-done | bytes 786464 | tf_op jit(solution)/shard_map/ppermute | solution.py:33
  559.2 4.8 input_back.1.refs_0_.refs_4_
  566.5 17.3 %collective-permute-start.35 = (bf16[192,2048]{1,0:T(8,128)(2,1)}, bf16[192,2048]{1,0:T(8,128)(2,1)S(1)}, u32[]{:S(2)}, u32[]{:S(2)}) collective-permute-start(bf16[192,2048]{1,0:T(8,128)(2,1)} %tie.16), channel_id=1, source_target_pairs={{0,4},{4,0},{8,12},{12,8},{1,5},{5,1},{9,13},{13,9},{2,6},{6,2},{1... | collective-permute-start | bytes 2359304 | tf_op jit(solution)/shard_map/ppermute | solution.py:33
  584.7 37.6 %collective-permute-done.40.refs_4_.refs_1_ = bf16[2,512,256]{2,1,0:T(8,128)(2,1)S(1)} collective-permute-done((bf16[2,512,256]{2,1,0:T(8,128)(2,1)}, bf16[2,512,256]{2,1,0:T(8,128)(2,1)S(1)}, u32[]{:S(2)}, u32[]{:S(2)}) %collective-permute-start.40) | collective-permute-done | bytes 524320 | tf_op jit(solution)/shard_map/ppermute | solution.py:33
  628.3 4.3 join.1
  632.6 4.0 output.1.refs_1_
  653.5 3.0 add_blocks.5
  656.6 4.3 collective-permute-start.47
  660.9 3.3 halves.4.refs_2_
  664.3 4.1 collective-permute-done.42.refs_1_
  668.3 3.3 halves.5.refs_1_
  671.7 3.8 copied.1.refs_4_
  675.5 4.0 collective-permute-done.47.refs_3_
  679.6 3.2 project_last.1
  (142 shorter events, 83.0 us)
Async XLA Ops:
  7.2 120.7 %all-gather.6.cloned.1.call-start = ((), (), s32[]{:S(2)}) async-start(), calls=%async_computation.3 | async-start | bytes 7077888 | tf_op jit(solution)/shard_map/all_gather | solution.py:1073
  7.2 1.2 copy-start.6
  20.2 28.6 %collective-permute-start = (bf16[768,384]{1,0:T(8,128)(2,1)}, bf16[768,384]{1,0:T(8,128)(2,1)}, u32[]{:S(2)}, u32[]{:S(2)}) collective-permute-start(bf16[768,384]{1,0:T(8,128)(2,1)} %get-tuple-element.77), channel_id=1, source_target_pairs={{0,4},{4,0},{8,12},{12,8},{1,5},{5,1},{9,13},{13,9},{2,6},{6,2},{1... | collective-permute-start | bytes 1769480 | tf_op jit(solution)/shard_map/ppermute | solution.py:33
  23.2 42.7 %collective-permute-start.1 = (bf16[768,384]{1,0:T(8,128)(2,1)}, bf16[768,384]{1,0:T(8,128)(2,1)}, u32[]{:S(2)}, u32[]{:S(2)}) collective-permute-start(bf16[768,384]{1,0:T(8,128)(2,1)} %get-tuple-element.78), channel_id=1, source_target_pairs={{0,8},{4,12},{8,0},{12,4},{1,9},{5,13},{9,1},{13,5},{2,10},{6,14},... | collective-permute-start | bytes 1769480 | tf_op jit(solution)/shard_map/ppermute | solution.py:33
  25.8 40.2 %collective-permute-start.2 = (bf16[768,384]{1,0:T(8,128)(2,1)}, bf16[768,384]{1,0:T(8,128)(2,1)}, u32[]{:S(2)}, u32[]{:S(2)}) collective-permute-start(bf16[768,384]{1,0:T(8,128)(2,1)} %get-tuple-element.79), channel_id=1, source_target_pairs={{0,12},{4,8},{8,4},{12,0},{1,13},{5,9},{9,5},{13,1},{2,14},{6,10},... | collective-permute-start | bytes 1769480 | tf_op jit(solution)/shard_map/ppermute | solution.py:33
  66.7 156.9 %all-gather.8.cloned.1.call-start = ((), (), s32[]{:S(2)}) async-start(), calls=%async_computation.4 | async-start | bytes 7077888 | tf_op jit(solution)/shard_map/all_gather | solution.py:1084
  94.7 25.6 %collective-permute-start.3 = (bf16[768,128]{1,0:T(8,128)(2,1)}, bf16[768,128]{1,0:T(8,128)(2,1)}, u32[]{:S(2)}, u32[]{:S(2)}) collective-permute-start(bf16[768,128]{1,0:T(8,128)(2,1)} %get-tuple-element.83), channel_id=1, source_target_pairs={{0,4},{4,0},{8,12},{12,8},{1,5},{5,1},{9,13},{13,9},{2,6},{6,2},{1... | collective-permute-start | bytes 589832 | tf_op jit(solution)/shard_map/ppermute | solution.py:33
  106.5 14.3 %collective-permute-start.4 = (bf16[768,128]{1,0:T(8,128)(2,1)}, bf16[768,128]{1,0:T(8,128)(2,1)}, u32[]{:S(2)}, u32[]{:S(2)}) collective-permute-start(bf16[768,128]{1,0:T(8,128)(2,1)} %get-tuple-element.84), channel_id=1, source_target_pairs={{0,8},{4,12},{8,0},{12,4},{1,9},{5,13},{9,1},{13,5},{2,10},{6,14},... | collective-permute-start | bytes 589832 | tf_op jit(solution)/shard_map/ppermute | solution.py:33
  107.6 20.2 %collective-permute-start.5 = (bf16[768,128]{1,0:T(8,128)(2,1)}, bf16[768,128]{1,0:T(8,128)(2,1)}, u32[]{:S(2)}, u32[]{:S(2)}) collective-permute-start(bf16[768,128]{1,0:T(8,128)(2,1)} %get-tuple-element.85), channel_id=1, source_target_pairs={{0,12},{4,8},{8,4},{12,0},{1,13},{5,9},{9,5},{13,1},{2,14},{6,10},... | collective-permute-start | bytes 589832 | tf_op jit(solution)/shard_map/ppermute | solution.py:33
  134.1 3.8 collective-permute-start.6
  140.8 20.1 %collective-permute-start.7 = (bf16[192,2048]{1,0:T(8,128)(2,1)}, bf16[192,2048]{1,0:T(8,128)(2,1)}, u32[]{:S(2)}, u32[]{:S(2)}) collective-permute-start(bf16[192,2048]{1,0:T(8,128)(2,1)} %sums.8), channel_id=1, source_target_pairs={{0,2},{1,3},{2,0},{3,1},{4,6},{5,7},{6,4},{7,5},{8,10},{9,11},{10,... | collective-permute-start | bytes 2359304 | tf_op jit(solution)/shard_map/ppermute | solution.py:33
  164.8 206.5 %all-gather.12.cloned.1.call-start = ((), (), s32[]{:S(2)}) async-start(), calls=%async_computation.9 | async-start | bytes 3932160 | tf_op jit(solution)/shard_map/all_gather | solution.py:1088
  164.8 31.2 %collective-permute-start.9 = (bf16[192,2048]{1,0:T(8,128)(2,1)}, bf16[192,2048]{1,0:T(8,128)(2,1)}, u32[]{:S(2)}, u32[]{:S(2)}) collective-permute-start(bf16[192,2048]{1,0:T(8,128)(2,1)} %get-tuple-element.88.refs_2_.refs_0_), channel_id=1, source_target_pairs={{0,2},{1,3},{2,0},{3,1},{4,6},{5,7},{6,4},{7,5},{8,10},{9,11},{10,... | collective-permute-start | bytes 2359304 | tf_op jit(solution)/shard_map/ppermute | solution.py:33
  166.6 30.2 %collective-permute-start.8 = (bf16[192,2048]{1,0:T(8,128)(2,1)}, bf16[192,2048]{1,0:T(8,128)(2,1)}, u32[]{:S(2)}, u32[]{:S(2)}) collective-permute-start(bf16[192,2048]{1,0:T(8,128)(2,1)} %get-tuple-element.88.refs_2_.refs_0_), channel_id=1, source_target_pairs={{0,1},{1,0},{2,3},{3,2},{4,5},{5,4},{6,7},{7,6},{8,9},{9,8},{10,11... | collective-permute-start | bytes 2359304 | tf_op jit(solution)/shard_map/ppermute | solution.py:33
  196.7 2.9 collective-permute-start.10
  223.2 182.3 %reduce-scatter.4.cloned.1.call-start = ((), (), s32[]{:S(2)}) async-start(), calls=%async_computation.5 | async-start | bytes 5242880 | tf_op jit(solution)/shard_map/reduce_scatter | solution.py:1095
  246.4 3.8 collective-permute-start.12
  253.1 20.5 %collective-permute-start.13 = (bf16[192,2048]{1,0:T(8,128)(2,1)}, bf16[192,2048]{1,0:T(8,128)(2,1)}, u32[]{:S(2)}, u32[]{:S(2)}) collective-permute-start(bf16[192,2048]{1,0:T(8,128)(2,1)} %sums.9.refs_2_), channel_id=1, source_target_pairs={{0,2},{1,3},{2,0},{3,1},{4,6},{5,7},{6,4},{7,5},{8,10},{9,11},{10,... | collective-permute-start | bytes 2359304 | tf_op jit(solution)/shard_map/ppermute | solution.py:33
  276.8 23.5 %collective-permute-start.16 = (bf16[192,2048]{1,0:T(8,128)(2,1)}, bf16[192,2048]{1,0:T(8,128)(2,1)}, u32[]{:S(2)}, u32[]{:S(2)}) collective-permute-start(bf16[192,2048]{1,0:T(8,128)(2,1)} %sums.10.refs_2_), channel_id=1, source_target_pairs={{0,4},{4,0},{8,12},{12,8},{1,5},{5,1},{9,13},{13,9},{2,6},{6,2},{1... | collective-permute-start | bytes 2359304 | tf_op jit(solution)/shard_map/ppermute | solution.py:33
  301.0 1.4 copy-start.7
  301.1 238.2 %reduce-scatter.6.cloned.1.call-start = ((), (), s32[]{:S(2)}) async-start(), calls=%async_computation.6 | async-start | bytes 5242880 | tf_op jit(solution)/shard_map/reduce_scatter | solution.py:1095
  302.5 5.8 collective-permute-start.11
  302.5 18.9 %collective-permute-start.17 = (bf16[2,192,2048]{2,1,0:T(8,128)(2,1)}, bf16[2,192,2048]{2,1,0:T(8,128)(2,1)}, u32[]{:S(2)}, u32[]{:S(2)}) collective-permute-start(bf16[2,192,2048]{2,1,0:T(8,128)(2,1)} %get-tuple-element.99), channel_id=1, source_target_pairs={{0,1},{1,0},{2,3},{3,2},{4,5},{5,4},{6,7},{7,6},{8,9},{9,8},{10,11... | collective-permute-start | bytes 4718600 | tf_op jit(solution)/shard_map/ppermute | solution.py:33
  311.1 19.9 %collective-permute-start.15 = (bf16[192,2048]{1,0:T(8,128)(2,1)}, bf16[192,2048]{1,0:T(8,128)(2,1)}, u32[]{:S(2)}, u32[]{:S(2)}) collective-permute-start(bf16[192,2048]{1,0:T(8,128)(2,1)} %sums.11.refs_2_), channel_id=1, source_target_pairs={{0,2},{1,3},{2,0},{3,1},{4,6},{5,7},{6,4},{7,5},{8,10},{9,11},{10,... | collective-permute-start | bytes 2359304 | tf_op jit(solution)/shard_map/ppermute | solution.py:33
  321.3 34.1 %collective-permute-start.14 = (bf16[2,192,2048]{2,1,0:T(8,128)(2,1)}, bf16[2,192,2048]{2,1,0:T(8,128)(2,1)}, u32[]{:S(2)}, u32[]{:S(2)}) collective-permute-start(bf16[2,192,2048]{2,1,0:T(8,128)(2,1)} %get-tuple-element.97), channel_id=1, source_target_pairs={{0,1},{1,0},{2,3},{3,2},{4,5},{5,4},{6,7},{7,6},{8,9},{9,8},{10,11... | collective-permute-start | bytes 4718600 | tf_op jit(solution)/shard_map/ppermute | solution.py:33
  336.3 19.1 %collective-permute-start.21 = (bf16[192,2048]{1,0:T(8,128)(2,1)}, bf16[192,2048]{1,0:T(8,128)(2,1)}, u32[]{:S(2)}, u32[]{:S(2)}) collective-permute-start(bf16[192,2048]{1,0:T(8,128)(2,1)} %get-tuple-element.100.refs_2_.refs_0_), channel_id=1, source_target_pairs={{0,2},{1,3},{2,0},{3,1},{4,6},{5,7},{6,4},{7,5},{8,10},{9,11},{10,... | collective-permute-start | bytes 2359304 | tf_op jit(solution)/shard_map/ppermute | solution.py:33
  337.8 22.0 %collective-permute-start.20 = (bf16[192,2048]{1,0:T(8,128)(2,1)}, bf16[192,2048]{1,0:T(8,128)(2,1)}, u32[]{:S(2)}, u32[]{:S(2)}) collective-permute-start(bf16[192,2048]{1,0:T(8,128)(2,1)} %get-tuple-element.100.refs_2_.refs_0_), channel_id=1, source_target_pairs={{0,1},{1,0},{2,3},{3,2},{4,5},{5,4},{6,7},{7,6},{8,9},{9,8},{10,11... | collective-permute-start | bytes 2359304 | tf_op jit(solution)/shard_map/ppermute | solution.py:33
  355.4 4.4 collective-permute-start.22
  358.2 25.3 %collective-permute-start.18 = (bf16[192,2048]{1,0:T(8,128)(2,1)}, bf16[192,2048]{1,0:T(8,128)(2,1)}, u32[]{:S(2)}, u32[]{:S(2)}) collective-permute-start(bf16[192,2048]{1,0:T(8,128)(2,1)} %sums.13.refs_8_), channel_id=1, source_target_pairs={{0,2},{1,3},{2,0},{3,1},{4,6},{5,7},{6,4},{7,5},{8,10},{9,11},{10,... | collective-permute-start | bytes 2359304 | tf_op jit(solution)/shard_map/ppermute | solution.py:33
  366.8 29.6 %collective-permute-start.25 = (bf16[768,128]{1,0:T(8,128)(2,1)}, bf16[768,128]{1,0:T(8,128)(2,1)}, u32[]{:S(2)}, u32[]{:S(2)}) collective-permute-start(bf16[768,128]{1,0:T(8,128)(2,1)} %get-tuple-element.103), channel_id=1, source_target_pairs={{0,4},{4,0},{8,12},{12,8},{1,5},{5,1},{9,13},{13,9},{2,6},{6,2},{1... | collective-permute-start | bytes 589832 | tf_op jit(solution)/shard_map/ppermute | solution.py:33
  368.2 28.2 %collective-permute-start.26 = (bf16[768,128]{1,0:T(8,128)(2,1)}, bf16[768,128]{1,0:T(8,128)(2,1)}, u32[]{:S(2)}, u32[]{:S(2)}) collective-permute-start(bf16[768,128]{1,0:T(8,128)(2,1)} %get-tuple-element.104), channel_id=1, source_target_pairs={{0,8},{4,12},{8,0},{12,4},{1,9},{5,13},{9,1},{13,5},{2,10},{6,14},... | collective-permute-start | bytes 589832 | tf_op jit(solution)/shard_map/ppermute | solution.py:33
  370.6 25.8 %collective-permute-start.27 = (bf16[768,128]{1,0:T(8,128)(2,1)}, bf16[768,128]{1,0:T(8,128)(2,1)}, u32[]{:S(2)}, u32[]{:S(2)}) collective-permute-start(bf16[768,128]{1,0:T(8,128)(2,1)} %get-tuple-element.105), channel_id=1, source_target_pairs={{0,12},{4,8},{8,4},{12,0},{1,13},{5,9},{9,5},{13,1},{2,14},{6,10},... | collective-permute-start | bytes 589832 | tf_op jit(solution)/shard_map/ppermute | solution.py:33
  397.1 246.6 %reduce-scatter.8.cloned.1.call-start = ((), (), s32[]{:S(2)}) async-start(), calls=%async_computation.8 | async-start | bytes 5242880 | tf_op jit(solution)/shard_map/reduce_scatter | solution.py:1095
  397.6 53.1 %collective-permute-start.24 = (bf16[3,192,2048]{2,1,0:T(8,128)(2,1)}, bf16[3,192,2048]{2,1,0:T(8,128)(2,1)}, u32[]{:S(2)}, u32[]{:S(2)}) collective-permute-start(bf16[3,192,2048]{2,1,0:T(8,128)(2,1)} %others.1.refs_5_.refs_1_), channel_id=1, source_target_pairs={{0,2},{1,3},{2,0},{3,1},{4,6},{5,7},{6,4},{7,5},{8,10},{9,11},{10,... | collective-permute-start | bytes 7077896 | tf_op jit(solution)/shard_map/ppermute | solution.py:33
  398.6 49.4 %collective-permute-start.28 = (bf16[4,512,256]{2,1,0:T(8,128)(2,1)}, bf16[4,512,256]{2,1,0:T(8,128)(2,1)}, u32[]{:S(2)}, u32[]{:S(2)}) collective-permute-start(bf16[4,512,256]{2,1,0:T(8,128)(2,1)} %get-tuple-element.111), channel_id=1, source_target_pairs={{0,16},{16,0},{1,17},{17,1},{2,18},{18,2},{3,19},{19,3},{4,20},{20... | collective-permute-start | bytes 3145736 | tf_op jit(solution)/shard_map/ppermute | solution.py:33
  399.9 60.2 %collective-permute-start.23 = (bf16[3,192,2048]{2,1,0:T(8,128)(2,1)}, bf16[3,192,2048]{2,1,0:T(8,128)(2,1)}, u32[]{:S(2)}, u32[]{:S(2)}) collective-permute-start(bf16[3,192,2048]{2,1,0:T(8,128)(2,1)} %others.1.refs_5_.refs_1_), channel_id=1, source_target_pairs={{0,1},{1,0},{2,3},{3,2},{4,5},{5,4},{6,7},{7,6},{8,9},{9,8},{10,11... | collective-permute-start | bytes 7077896 | tf_op jit(solution)/shard_map/ppermute | solution.py:33
  408.1 42.7 %collective-permute-start.29 = (bf16[1,256,1024]{2,1,0:T(8,128)(2,1)}, bf16[1,256,1024]{2,1,0:T(8,128)(2,1)}, u32[]{:S(2)}, u32[]{:S(2)}) collective-permute-start(bf16[1,256,1024]{2,1,0:T(8,128)(2,1)} %one_block.3.refs_12_), channel_id=1, source_target_pairs={{0,4},{4,0},{8,12},{12,8},{1,5},{5,1},{9,13},{13,9},{2,6},{6,2},{1... | collective-permute-start | bytes 1572872 | tf_op jit(solution)/shard_map/ppermute | solution.py:33
  451.4 11.0 %collective-permute-start.30 = (bf16[3,192,2048]{2,1,0:T(8,128)(2,1)}, bf16[3,192,2048]{2,1,0:T(8,128)(2,1)}, u32[]{:S(2)}, u32[]{:S(2)}) collective-permute-start(bf16[3,192,2048]{2,1,0:T(8,128)(2,1)} %tie.14.refs_3_), channel_id=1, source_target_pairs={{0,1},{1,0},{2,3},{3,2},{4,5},{5,4},{6,7},{7,6},{8,9},{9,8},{10,11... | collective-permute-start | bytes 7077896 | tf_op jit(solution)/shard_map/ppermute | solution.py:33
  451.5 25.7 %collective-permute-start.19 = (bf16[192,2048]{1,0:T(8,128)(2,1)}, bf16[192,2048]{1,0:T(8,128)(2,1)}, u32[]{:S(2)}, u32[]{:S(2)}) collective-permute-start(bf16[192,2048]{1,0:T(8,128)(2,1)} %sums.12.refs_7_), channel_id=1, source_target_pairs={{0,2},{1,3},{2,0},{3,1},{4,6},{5,7},{6,4},{7,5},{8,10},{9,11},{10,... | collective-permute-start | bytes 2359304 | tf_op jit(solution)/shard_map/ppermute | solution.py:33
  452.4 47.6 %collective-permute-start.31 = (bf16[768,384]{1,0:T(8,128)(2,1)}, bf16[768,384]{1,0:T(8,128)(2,1)}, u32[]{:S(2)}, u32[]{:S(2)}) collective-permute-start(bf16[768,384]{1,0:T(8,128)(2,1)} %get-tuple-element.112.refs_6_), channel_id=1, source_target_pairs={{0,4},{4,0},{8,12},{12,8},{1,5},{5,1},{9,13},{13,9},{2,6},{6,2},{1... | collective-permute-start | bytes 1769480 | tf_op jit(solution)/shard_map/ppermute | solution.py:33
  460.1 60.3 %collective-permute-start.32 = (bf16[768,384]{1,0:T(8,128)(2,1)}, bf16[768,384]{1,0:T(8,128)(2,1)}, u32[]{:S(2)}, u32[]{:S(2)}) collective-permute-start(bf16[768,384]{1,0:T(8,128)(2,1)} %get-tuple-element.113.refs_7_), channel_id=1, source_target_pairs={{0,8},{4,12},{8,0},{12,4},{1,9},{5,13},{9,1},{13,5},{2,10},{6,14},... | collective-permute-start | bytes 1769480 | tf_op jit(solution)/shard_map/ppermute | solution.py:33
  460.1 60.3 %collective-permute-start.33 = (bf16[768,384]{1,0:T(8,128)(2,1)}, bf16[768,384]{1,0:T(8,128)(2,1)}, u32[]{:S(2)}, u32[]{:S(2)}) collective-permute-start(bf16[768,384]{1,0:T(8,128)(2,1)} %get-tuple-element.114.refs_8_), channel_id=1, source_target_pairs={{0,12},{4,8},{8,4},{12,0},{1,13},{5,9},{9,5},{13,1},{2,14},{6,10},... | collective-permute-start | bytes 1769480 | tf_op jit(solution)/shard_map/ppermute | solution.py:33
  521.0 150.6 %all-gather.10.cloned.1.call-start = ((), (), s32[]{:S(2)}) async-start(), calls=%async_computation.7 | async-start | bytes 3932160 | tf_op jit(solution)/shard_map/all_gather | solution.py:1175
  532.6 3.8 collective-permute-start.34
  539.3 19.9 %collective-permute-start.36 = (bf16[192,2048]{1,0:T(8,128)(2,1)}, bf16[192,2048]{1,0:T(8,128)(2,1)}, u32[]{:S(2)}, u32[]{:S(2)}) collective-permute-start(bf16[192,2048]{1,0:T(8,128)(2,1)} %sums.15.refs_2_.refs_1_), channel_id=1, source_target_pairs={{0,2},{1,3},{2,0},{3,1},{4,6},{5,7},{6,4},{7,5},{8,10},{9,11},{10,... | collective-permute-start | bytes 2359304 | tf_op jit(solution)/shard_map/ppermute | solution.py:33
  564.0 59.1 %collective-permute-start.38 = (bf16[208,2048]{1,0:T(8,128)(2,1)}, bf16[208,2048]{1,0:T(8,128)(2,1)S(1)}, u32[]{:S(2)}, u32[]{:S(2)}) collective-permute-start(bf16[208,2048]{1,0:T(8,128)(2,1)} %input_back.1.refs_0_.refs_4_), channel_id=1, source_target_pairs={{0,2},{1,3},{2,0},{3,1},{4,6},{5,7},{6,4},{7,5},{8,10},{9,11},{10,... | collective-permute-start | bytes 2555912 | tf_op jit(solution)/shard_map/ppermute | solution.py:33
  564.4 20.2 %copy-start = (bf16[208,2048]{1,0:T(8,128)(2,1)S(1)}, bf16[208,2048]{1,0:T(8,128)(2,1)}, u32[]{:S(2)}) copy-start(bf16[208,2048]{1,0:T(8,128)(2,1)} %input_back.1.refs_0_.refs_4_) | copy-start | bytes 2555908
  564.4 57.9 %collective-permute-start.39 = (bf16[4,256,384]{2,1,0:T(8,128)(2,1)}, bf16[4,256,384]{2,1,0:T(8,128)(2,1)S(1)}, u32[]{:S(2)}, u32[]{:S(2)}) collective-permute-start(bf16[4,256,384]{2,1,0:T(8,128)(2,1)} %get-tuple-element.127), channel_id=1, source_target_pairs={{0,16},{16,0},{1,17},{17,1},{2,18},{18,2},{3,19},{19,3},{4,20},{20... | collective-permute-start | bytes 2359304 | tf_op jit(solution)/shard_map/ppermute | solution.py:33
  566.5 55.8 %collective-permute-start.35 = (bf16[192,2048]{1,0:T(8,128)(2,1)}, bf16[192,2048]{1,0:T(8,128)(2,1)S(1)}, u32[]{:S(2)}, u32[]{:S(2)}) collective-permute-start(bf16[192,2048]{1,0:T(8,128)(2,1)} %tie.16), channel_id=1, source_target_pairs={{0,4},{4,0},{8,12},{12,8},{1,5},{5,1},{9,13},{13,9},{2,6},{6,2},{1... | collective-permute-start | bytes 2359304 | tf_op jit(solution)/shard_map/ppermute | solution.py:33
  584.5 37.8 %collective-permute-start.40 = (bf16[2,512,256]{2,1,0:T(8,128)(2,1)}, bf16[2,512,256]{2,1,0:T(8,128)(2,1)S(1)}, u32[]{:S(2)}, u32[]{:S(2)}) collective-permute-start(bf16[2,512,256]{2,1,0:T(8,128)(2,1)} %tie.18), channel_id=1, source_target_pairs={{0,8},{4,12},{8,0},{12,4},{1,9},{5,13},{9,1},{13,5},{2,10},{6,14},... | collective-permute-start | bytes 1572872 | tf_op jit(solution)/shard_map/ppermute | solution.py:33
  584.6 41.0 %collective-permute-start.37 = (bf16[208,2048]{1,0:T(8,128)(2,1)S(1)}, bf16[208,2048]{1,0:T(8,128)(2,1)}, u32[]{:S(2)}, u32[]{:S(2)}) collective-permute-start(bf16[208,2048]{1,0:T(8,128)(2,1)S(1)} %copy-done), channel_id=1, source_target_pairs={{0,1},{1,0},{2,3},{3,2},{4,5},{5,4},{6,7},{7,6},{8,9},{9,8},{10,11... | collective-permute-start | bytes 2555912 | tf_op jit(solution)/shard_map/ppermute | solution.py:33
  622.3 0.8 copy-start.4
  622.3 1.1 copy-start.3
  623.1 0.9 copy-start.2
  623.9 0.9 copy-start.1
  625.5 2.8 collective-permute-start.41
  637.1 23.8 %collective-permute-start.43 = (bf16[1,256,1024]{2,1,0:T(8,128)(2,1)}, bf16[1,256,1024]{2,1,0:T(8,128)(2,1)}, u32[]{:S(2)}, u32[]{:S(2)}) collective-permute-start(bf16[1,256,1024]{2,1,0:T(8,128)(2,1)} %one_block.4.refs_7_), channel_id=1, source_target_pairs={{0,4},{4,0},{8,12},{12,8},{1,5},{5,1},{9,13},{13,9},{2,6},{6,2},{1... | collective-permute-start | bytes 1572872 | tf_op jit(solution)/shard_map/ppermute | solution.py:33
  641.0 0.6 copy-start.5
  642.2 6.7 collective-permute-start.44
  646.2 22.1 %collective-permute-start.42 = (bf16[1,256,1024]{2,1,0:T(8,128)(2,1)}, bf16[1,256,1024]{2,1,0:T(8,128)(2,1)}, u32[]{:S(2)}, u32[]{:S(2)}) collective-permute-start(bf16[1,256,1024]{2,1,0:T(8,128)(2,1)} %one_block.5.refs_2_), channel_id=1, source_target_pairs={{0,4},{4,0},{8,12},{12,8},{1,5},{5,1},{9,13},{13,9},{2,6},{6,2},{1... | collective-permute-start | bytes 1572872 | tf_op jit(solution)/shard_map/ppermute | solution.py:33
  656.6 19.0 %collective-permute-start.45 = (bf16[272,384]{1,0:T(8,128)(2,1)}, bf16[272,384]{1,0:T(8,128)(2,1)}, u32[]{:S(2)}, u32[]{:S(2)}) collective-permute-start(bf16[272,384]{1,0:T(8,128)(2,1)} %get-tuple-element.133), channel_id=1, source_target_pairs={{0,4},{4,0},{8,12},{12,8},{1,5},{5,1},{9,13},{13,9},{2,6},{6,2},{1... | collective-permute-start | bytes 626696 | tf_op jit(solution)/shard_map/ppermute | solution.py:33
  656.6 19.0 %collective-permute-start.46 = (bf16[272,384]{1,0:T(8,128)(2,1)}, bf16[272,384]{1,0:T(8,128)(2,1)}, u32[]{:S(2)}, u32[]{:S(2)}) collective-permute-start(bf16[272,384]{1,0:T(8,128)(2,1)} %get-tuple-element.134), channel_id=1, source_target_pairs={{0,8},{4,12},{8,0},{12,4},{1,9},{5,13},{9,1},{13,5},{2,10},{6,14},... | collective-permute-start | bytes 626696 | tf_op jit(solution)/shard_map/ppermute | solution.py:33
  656.6 22.9 %collective-permute-start.47 = (bf16[272,384]{1,0:T(8,128)(2,1)}, bf16[272,384]{1,0:T(8,128)(2,1)}, u32[]{:S(2)}, u32[]{:S(2)}) collective-permute-start(bf16[272,384]{1,0:T(8,128)(2,1)} %get-tuple-element.135), channel_id=1, source_target_pairs={{0,12},{4,8},{8,4},{12,0},{1,13},{5,9},{9,5},{13,1},{2,14},{6,10},... | collective-permute-start | bytes 626696 | tf_op jit(solution)/shard_map/ppermute | solution.py:33
  660.9 23.2 %collective-permute-start.48 = (bf16[1,512,256]{2,1,0:T(8,128)(2,1)}, bf16[1,512,256]{2,1,0:T(8,128)(2,1)}, u32[]{:S(2)}, u32[]{:S(2)}) collective-permute-start(bf16[1,512,256]{2,1,0:T(8,128)(2,1)} %get-tuple-element.140), channel_id=1, source_target_pairs={{0,4},{4,0},{8,12},{12,8},{1,5},{5,1},{9,13},{13,9},{2,6},{6,2},{1... | collective-permute-start | bytes 786440 | tf_op jit(solution)/shard_map/ppermute | solution.py:33
Sparse Core Ops, SparseCore 0:
  66.8 56.5 all-gather.5
  164.9 46.0 all-gather.7
  223.4 62.7 all-gather.11
  301.2 104.3 reduce-scatter.3
  408.6 122.8 reduce-scatter.5
  534.3 101.4 reduce-scatter.7
  637.4 28.2 all-gather.9

commit v6 on v5

--- a/solution.py
+++ b/solution.py
@@ -800,15 +800,22 @@
 
 
 def branch_back_kernel(ix, q0, q1, q2, q3, w0, w1, w2, w3, rows_ref, o0, o1, o2, o3, held, sems):
-    copy_all(quarter_copies(ix[T], (q0, q1, q2, q3), held), sems)
-    keep = pltpu.make_async_copy(held, rows_ref, sems.at[4])
-    keep.start()
+    rows = q0.shape[0]
+    copies = [
+        pltpu.make_async_copy(a, b, sems.at[k])
+        for k, (a, b) in enumerate(quarter_copies(ix[T], (q0, q1, q2, q3), held))
+    ]
+    for copy in copies:
+        copy.start()
     weight = jnp.concatenate([w0[...], w1[...], w2[...], w3[...]], axis=0)
-    for part in range(3):
-        at = slice(part * 256, (part + 1) * 256)
+    for k, copy in enumerate(copies):
+        copy.wait()
+        at = pl.ds(pl.multiple_of((ix[T] ^ k) * rows, rows), rows)
         flat = against(held[at, :], weight).astype(LOW)
         for slot, out in enumerate((o0, o1, o2, o3)):
             out[at, :] = flat[:, slot * 128 : (slot + 1) * 128]
+    keep = pltpu.make_async_copy(held, rows_ref, sems.at[4])
+    keep.start()
     keep.wait()
 
 

time: 701 us -> 701 us (level)
  no operation moved by 1% of the time
where the time goes in v6:
time: 701 us; the launch traced here: 694 us
  Pallas kernels  348 us (50%)
  waiting for transfers between devices  235 us (34%)
  starting transfers between devices  79.8 us (11%)
  between operations  14.8 us (2%)
  local copies, waits for them, and re-layouts  11.1 us (2%)
    pallas_call x45, Pallas kernels, call(): pl.pallas_call(body, grid_spec=pltpu.PrefetchScalarGridSpec(num_scalar_pr...  341 us
    ppermute x49, waiting for transfers between devices, swap(): return lax.ppermute(value, axis, [(i, i ^ distance) for i in range(size)])  230 us
    ppermute x49, starting transfers between devices, swap(): return lax.ppermute(value, axis, [(i, i ^ distance) for i in range(size)])  78.6 us
  transfers between devices with their start and end apart: 56, of which 24 were waited for; matrix products, arithmetic and copies ran while one was open for 1% of the time, Pallas kernels for 46%

profile of v6, /device:TPU:0, one launch (start us, length us, event | category | flops | bytes accessed | tf_op | source)
XLA Modules:
  0.0 693.8 jit_solution(6429804036153541403)
XLA Ops:
  9.0 11.2 %project.1 = (bf16[768,2048]{1,0:T(8,128)(2,1)}, bf16[768,384]{1,0:T(8,128)(2,1)}, bf16[768,384]{1,0:T(8,128)(2,1)}, bf16[768,384]{1,0:T(8,128)(2,1)}, bf16[768,384]{1,0:T(8,128)(2,1)}) custom-call(s32[3]{0:T(128)} %pad_add_fusion.index_ref.refs_0_, bf16[768,2048]{1,0:T(8,128)(2,1)} %refs_4_.13, f32[1,2048]{1,0:T(1,128)} %bitcast.30, ...), custom_call_target="tpu_custom_call" | custom-call | bytes 80740352 | tf_op jit(solution)/shard_map/project/pallas_call | solution.py:58
  20.2 3.0 collective-permute-start
  25.8 8.0 %hidden_back.2.refs_1_.refs_6_ = f32[768,1024]{1,0:T(8,128)} custom-call(s32[3]{0:T(128)} %pad_add_fusion.index_ref.refs_0_, bf16[768,2048]{1,0:T(8,128)(2,1)} %refs_0_.5, bf16[2048,2048]{1,0:T(8,128)(2,1)} %refs_1_.9, bf16[768,384]{1,0:T(8,128)(2,1)} %get-tuple-element.76.refs_2_.refs_0_), custom_call_target="tpu_custom_call" | custom-call | bytes 62390272 | tf_op jit(solution)/shard_map/hidden_back/pallas_call | solution.py:58
  35.2 8.0 %rope_tables.1 = (f32[3072,128]{1,0:T(8,128)}, f32[3072,128]{1,0:T(8,128)}) custom-call(s32[3]{0:T(128)} %pad_add_fusion.index_ref.refs_0_, f32[1,128]{1,0:T(1,128)} %maximum_bitcast_fusion.refs_0_, f32[768,1024]{1,0:T(8,128)} %hidden_back.2.refs_1_.refs_6_), custom_call_target="tpu_custom_call" | custom-call | bytes 58720256 | tf_op jit(solution)/shard_map/rope_tables/pallas_call | solution.py:58
  48.7 17.2 %collective-permute-done.1.refs_2_.refs_3_ = bf16[768,384]{1,0:T(8,128)(2,1)} collective-permute-done((bf16[768,384]{1,0:T(8,128)(2,1)}, bf16[768,384]{1,0:T(8,128)(2,1)}, u32[]{:S(2)}, u32[]{:S(2)}) %collective-permute-start.1) | collective-permute-done | bytes 589856 | tf_op jit(solution)/shard_map/ppermute | solution.py:33
  66.9 27.7 %attend.1 = (bf16[768,128]{1,0:T(8,128)(2,1)}, bf16[768,128]{1,0:T(8,128)(2,1)}, bf16[768,128]{1,0:T(8,128)(2,1)}, bf16[768,128]{1,0:T(8,128)(2,1)}, f32[3072,128]{1,0:T(8,128)}, /*index=5*/f32[4,16,768]{2,1,0:T(8,128)}) custom-call(s32[3]{0:T(128)} %pad_add_fusion.index_ref.refs_0_, bf16[768,384]{1,0:T(8,128)(2,1)} %get-tuple-element.76.refs_2_.refs_0_, ...), custom_call_target="tpu_custom_call" | custom-call | bytes 205520896 | tf_op jit(solution)/shard_map/attend/pallas_call | solution.py:58
  94.7 11.8 %collective-permute-start.3 = (bf16[768,128]{1,0:T(8,128)(2,1)}, bf16[768,128]{1,0:T(8,128)(2,1)}, u32[]{:S(2)}, u32[]{:S(2)}) collective-permute-start(bf16[768,128]{1,0:T(8,128)(2,1)} %get-tuple-element.83), channel_id=1, source_target_pairs={{0,4},{4,0},{8,12},{12,8},{1,5},{5,1},{9,13},{13,9},{2,6},{6,2},{1... | collective-permute-start | bytes 589832 | tf_op jit(solution)/shard_map/ppermute | solution.py:33
  109.0 11.3 %collective-permute-done.3.refs_1_ = bf16[768,128]{1,0:T(8,128)(2,1)} collective-permute-done((bf16[768,128]{1,0:T(8,128)(2,1)}, bf16[768,128]{1,0:T(8,128)(2,1)}, u32[]{:S(2)}, u32[]{:S(2)}) %collective-permute-start.3) | collective-permute-done | bytes 196640 | tf_op jit(solution)/shard_map/ppermute | solution.py:33
  120.8 7.0 %collective-permute-done.5.refs_3_ = bf16[768,128]{1,0:T(8,128)(2,1)} collective-permute-done((bf16[768,128]{1,0:T(8,128)(2,1)}, bf16[768,128]{1,0:T(8,128)(2,1)}, u32[]{:S(2)}, u32[]{:S(2)}) %collective-permute-start.5) | collective-permute-done | bytes 196640 | tf_op jit(solution)/shard_map/ppermute | solution.py:33
  127.8 6.3 join_heads.1
  134.2 3.7 collective-permute-done.6.refs_1_
  138.0 2.9 sums.8
  142.8 18.2 %collective-permute-done.7.refs_2_ = bf16[192,2048]{1,0:T(8,128)(2,1)} collective-permute-done((bf16[192,2048]{1,0:T(8,128)(2,1)}, bf16[192,2048]{1,0:T(8,128)(2,1)}, u32[]{:S(2)}, u32[]{:S(2)}) %collective-permute-start.7) | collective-permute-done | bytes 786464 | tf_op jit(solution)/shard_map/ppermute | solution.py:33
  160.9 3.8 middle.1
  166.6 8.1 %hidden_back.3.refs_2_.refs_3_ = f32[768,1024]{1,0:T(8,128)} custom-call(s32[3]{0:T(128)} %pad_add_fusion.index_ref.refs_0_, bf16[1536,2048]{1,0:T(8,128)(2,1)} %all-gather.6.cloned.1.call-done.refs_8_.refs_0_.refs_1_, bf16[2048,2048]{1,0:T(8,128)(2,1)} %refs_1_.9, bf16[192,2048]{1,0:T(8,128)(2,1)} %get-tuple-element.88.refs_2_.refs_0_), custom_call_target="tpu_custom_call" | custom-call | bytes 62390272 | tf_op jit(solution)/shard_map/hidden_back/pallas_call | solution.py:58
  174.8 21.3 %collective-permute-done.9.refs_1_ = bf16[192,2048]{1,0:T(8,128)(2,1)} collective-permute-done((bf16[192,2048]{1,0:T(8,128)(2,1)}, bf16[192,2048]{1,0:T(8,128)(2,1)}, u32[]{:S(2)}, u32[]{:S(2)}) %collective-permute-start.9) | collective-permute-done | bytes 786464 | tf_op jit(solution)/shard_map/ppermute | solution.py:33
  199.6 22.9 %feed.2 = (bf16[768,2048]{1,0:T(8,128)(2,1)}, bf16[768,1024]{1,0:T(8,128)(2,1)}, bf16[768,1024]{1,0:T(8,128)(2,1)}, bf16[768,1024]{1,0:T(8,128)(2,1)}, bf16[2,19...) custom-call(s32[3]{0:T(128)} %pad_add_fusion.index_ref.refs_0_, bf16[192,2048]{1,0:T(8,128)(2,1)} %get-tuple-element.88.refs_2_.refs_0_, ...), custom_call_target="tpu_custom_call" | custom-call | bytes 176160768 | tf_op jit(solution)/shard_map/feed/pallas_call | solution.py:58
  223.6 22.8 %feed.3 = (bf16[768,2048]{1,0:T(8,128)(2,1)}, bf16[768,1024]{1,0:T(8,128)(2,1)}, bf16[768,1024]{1,0:T(8,128)(2,1)}, bf16[768,1024]{1,0:T(8,128)(2,1)}, bf16[2,19...) custom-call(s32[3]{0:T(128)} %pad_add_fusion.index_ref.refs_0_, ...), custom_call_target="tpu_custom_call" | custom-call | bytes 176160768 | tf_op jit(solution)/shard_map/feed/pallas_call | solution.py:58
  246.6 3.6 collective-permute-done.12.refs_1_
  250.2 2.9 sums.9.refs_2_
  255.5 8.7 %feed_down.2 = (bf16[2,192,2048]{2,1,0:T(8,128)(2,1)}, bf16[2,192,2048]{2,1,0:T(8,128)(2,1)}) custom-call(s32[3]{0:T(128)} %pad_add_fusion.index_ref.refs_0_, bf16[768,1024]{1,0:T(8,128)(2,1)} %get-tuple-element.94.refs_0_.refs_3_, bf16[2048,2048]{1,0:T(8,128)(2,1)} %refs_1_.9, bf16[192,2048]{1,0:T(8,128)(2,1)} %sums.9.refs_2_), custom_call_target="tpu_custom_call" | custom-call | bytes 66060288 | tf_op jit(solution)/shard_map/feed_down/pallas_call | solution.py:58
  264.2 9.4 %collective-permute-done.13.refs_2_ = bf16[192,2048]{1,0:T(8,128)(2,1)} collective-permute-done((bf16[192,2048]{1,0:T(8,128)(2,1)}, bf16[192,2048]{1,0:T(8,128)(2,1)}, u32[]{:S(2)}, u32[]{:S(2)}) %collective-permute-start.13) | collective-permute-done | bytes 786464 | tf_op jit(solution)/shard_map/ppermute | solution.py:33
  273.6 3.2 sums.10.refs_2_
  276.8 12.9 %wgrad_down.1.refs_1_ = bf16[8,256,1024]{2,1,0:T(8,128)(2,1)} custom-call(s32[3]{0:T(128)} %pad_add_fusion.index_ref.refs_0_, bf16[768,2048]{1,0:T(8,128)(2,1)} %refs_0_.5, bf16[1536,2048]{1,0:T(8,128)(2,1)} %all-gather.6.cloned.1.call-done.refs_8_.refs_0_.refs_1_, bf16[768,1024]{1,0:T(8,128)(2,1)} %get-tuple-element.89.refs_6_.refs_0_.refs_2_, ...), custom_call_target="tpu_custom_call" | custom-call | bytes 102760448 | tf_op jit(solution)/shard_map/wgrad_down/pallas_call | solution.py:58
  289.7 10.6 %collective-permute-done.16.refs_3_.refs_2_ = bf16[192,2048]{1,0:T(8,128)(2,1)} collective-permute-done((bf16[192,2048]{1,0:T(8,128)(2,1)}, bf16[192,2048]{1,0:T(8,128)(2,1)}, u32[]{:S(2)}, u32[]{:S(2)}) %collective-permute-start.16) | collective-permute-done | bytes 786464 | tf_op jit(solution)/shard_map/ppermute | solution.py:33
  303.0 5.2 collective-permute-done.11.refs_1_
  308.2 2.9 sums.11.refs_2_
  312.6 8.7 %feed_down.3 = (bf16[2,192,2048]{2,1,0:T(8,128)(2,1)}, bf16[2,192,2048]{2,1,0:T(8,128)(2,1)}) custom-call(s32[3]{0:T(128)} %pad_add_fusion.index_ref.refs_0_, bf16[768,1024]{1,0:T(8,128)(2,1)} %get-tuple-element.89.refs_6_.refs_0_.refs_2_, bf16[2048,2048]{1,0:T(8,128)(2,1)} %refs_1_.9, bf16[192,2048]{1,0:T(8,128)(2,1)} %sums.11.refs_2_), custom_call_target="tpu_custom_call" | custom-call | bytes 66060288 | tf_op jit(solution)/shard_map/feed_down/pallas_call | solution.py:58
  321.4 2.9 sums.12.refs_7_
  324.3 6.7 collective-permute-done.15.refs_2_
  331.0 5.3 middle_back.1
  337.8 17.5 %collective-permute-done.21.refs_2_ = bf16[192,2048]{1,0:T(8,128)(2,1)} collective-permute-done((bf16[192,2048]{1,0:T(8,128)(2,1)}, bf16[192,2048]{1,0:T(8,128)(2,1)}, u32[]{:S(2)}, u32[]{:S(2)}) %collective-permute-start.21) | collective-permute-done | bytes 786464 | tf_op jit(solution)/shard_map/ppermute | solution.py:33
  355.4 2.9 sums.13.refs_8_
  359.8 8.6 %branch_back.1 = (bf16[768,2048]{1,0:T(8,128)(2,1)}, bf16[768,128]{1,0:T(8,128)(2,1)}, bf16[768,128]{1,0:T(8,128)(2,1)}, bf16[768,128]{1,0:T(8,128)(2,1)}, bf16[768,128]{1,0:T(8,128)(2,1)}) custom-call(s32[3]{0:T(128)} %pad_add_fusion.index_ref.refs_0_, bf16[192,2048]{1,0:T(8,128)(2,1)} %get-tuple-element.100.refs_2_.refs_0_, ...), custom_call_target="tpu_custom_call" | custom-call | bytes 51380224 | tf_op jit(solution)/shard_map/branch_back/pallas_call | solution.py:58
  372.9 3.7 others.1.refs_5_.refs_1_
  376.6 8.5 %out_wgrad.1 = (bf16[4,512,256]{2,1,0:T(8,128)(2,1)}, bf16[4,512,256]{2,1,0:T(8,128)(2,1)}) custom-call(s32[3]{0:T(128)} %pad_add_fusion.index_ref.refs_0_, bf16[768,128]{1,0:T(8,128)(2,1)} %get-tuple-element.82.refs_0_, bf16[768,128]{1,0:T(8,128)(2,1)} %collective-permute-done.3.refs_1_, bf16[768,128]{1,0:T(8,128)(2,1)} %collective-permute-done.4.refs_2_, ...), custom_call_target="tpu_custom_call" | custom-call | bytes 62390272 | tf_op jit(solution)/shard_map/out_wgrad/pallas_call | solution.py:58
  385.1 12.9 %wgrad_gate.1.refs_1_ = bf16[8,256,1024]{2,1,0:T(8,128)(2,1)} custom-call(s32[3]{0:T(128)} %pad_add_fusion.index_ref.refs_0_, bf16[768,2048]{1,0:T(8,128)(2,1)} %get-tuple-element.116.refs_0_, bf16[768,2048]{1,0:T(8,128)(2,1)} %get-tuple-element.117.refs_1_, bf16[768,1024]{1,0:T(8,128)(2,1)} %get-tuple-element.125.refs_2_, ...), custom_call_target="tpu_custom_call" | custom-call | bytes 102760448 | tf_op jit(solution)/shard_map/wgrad_gate/pallas_call | solution.py:58
  401.1 4.4 reduce-scatter.4.cloned.1.call-done.refs_0_
  409.7 38.2 %attend_back.1 = (bf16[768,384]{1,0:T(8,128)(2,1)}, bf16[768,384]{1,0:T(8,128)(2,1)}, bf16[768,384]{1,0:T(8,128)(2,1)}, bf16[768,384]{1,0:T(8,128)(2,1)}) custom-call(s32[3]{0:T(128)} %pad_add_fusion.index_ref.refs_0_, bf16[768,384]{1,0:T(8,128)(2,1)} %get-tuple-element.76.refs_2_.refs_0_, bf16[768,384]{1,0:T(8,128)(2,1)} %collective-permute-done.refs_1_.refs_2_, ...), custom_call_target="tpu_custom_call" | custom-call | bytes 293601280 | tf_op jit(solution)/shard_map/attend_back/pallas_call | solution.py:58
  448.0 4.4 collective-permute-done.24.refs_1_
  453.7 6.4 collective-permute-start.31
  462.5 14.7 %project_wgrad.1 = (bf16[4,256,384]{2,1,0:T(8,128)(2,1)}, bf16[4,256,384]{2,1,0:T(8,128)(2,1)}) custom-call(s32[3]{0:T(128)} %pad_add_fusion.index_ref.refs_0_, bf16[768,2048]{1,0:T(8,128)(2,1)} %get-tuple-element.80.refs_0_, bf16[3,192,2048]{2,1,0:T(8,128)(2,1)} %others.1.refs_5_.refs_1_, bf16[3,192,2048]{2,1,0:T(8,128)(2,1)} %collective-permute-done.23.refs_2_, ...), custom_call_target="tpu_custom_call" | custom-call | bytes 95420416 | tf_op jit(solution)/shard_map/project_wgrad/pallas_call | solution.py:58
  477.2 3.2 sums.14.refs_2_.refs_1_
  480.3 3.3 add_blocks.3
  483.6 3.5 halves.3.refs_4_
  487.1 12.9 %wgrad_up.1.refs_1_ = bf16[8,256,1024]{2,1,0:T(8,128)(2,1)} custom-call(s32[3]{0:T(128)} %pad_add_fusion.index_ref.refs_0_, bf16[768,2048]{1,0:T(8,128)(2,1)} %get-tuple-element.116.refs_0_, bf16[768,2048]{1,0:T(8,128)(2,1)} %get-tuple-element.117.refs_1_, bf16[768,1024]{1,0:T(8,128)(2,1)} %get-tuple-element.118.refs_2_, ...), custom_call_target="tpu_custom_call" | custom-call | bytes 102760448 | tf_op jit(solution)/shard_map/wgrad_up/pallas_call | solution.py:58
  500.0 20.4 %collective-permute-done.32.refs_3_.refs_2_ = bf16[768,384]{1,0:T(8,128)(2,1)} collective-permute-done((bf16[768,384]{1,0:T(8,128)(2,1)}, bf16[768,384]{1,0:T(8,128)(2,1)}, u32[]{:S(2)}, u32[]{:S(2)}) %collective-permute-start.32) | collective-permute-done | bytes 589856 | tf_op jit(solution)/shard_map/ppermute | solution.py:33
  521.1 11.5 %project_back.1 = (bf16[2,192,2048]{2,1,0:T(8,128)(2,1)}, bf16[2,192,2048]{2,1,0:T(8,128)(2,1)}) custom-call(s32[3]{0:T(128)} %pad_add_fusion.index_ref.refs_0_, bf16[768,384]{1,0:T(8,128)(2,1)} %get-tuple-element.110.refs_2_.refs_5_.refs_0_, bf16[768,384]{1,0:T(8,128)(2,1)} %collective-permute-done.31.refs_2_.refs_1_, ...), custom_call_target="tpu_custom_call" | custom-call | bytes 80740352 | tf_op jit(solution)/shard_map/project_back/pallas_call | solution.py:58
  532.7 3.7 collective-permute-done.34.refs_1_
  536.4 2.9 sums.15.refs_2_.refs_1_
  541.8 17.4 %collective-permute-done.36.refs_2_ = bf16[192,2048]{1,0:T(8,128)(2,1)} collective-permute-done((bf16[192,2048]{1,0:T(8,128)(2,1)}, bf16[192,2048]{1,0:T(8,128)(2,1)}, u32[]{:S(2)}, u32[]{:S(2)}) %collective-permute-start.36) | collective-permute-done | bytes 786464 | tf_op jit(solution)/shard_map/ppermute | solution.py:33
  559.2 4.8 input_back.1.refs_0_.refs_4_
  566.5 17.3 %collective-permute-start.35 = (bf16[192,2048]{1,0:T(8,128)(2,1)}, bf16[192,2048]{1,0:T(8,128)(2,1)S(1)}, u32[]{:S(2)}, u32[]{:S(2)}) collective-permute-start(bf16[192,2048]{1,0:T(8,128)(2,1)} %tie.16), channel_id=1, source_target_pairs={{0,4},{4,0},{8,12},{12,8},{1,5},{5,1},{9,13},{13,9},{2,6},{6,2},{1... | collective-permute-start | bytes 2359304 | tf_op jit(solution)/shard_map/ppermute | solution.py:33
  584.7 37.6 %collective-permute-done.40.refs_4_.refs_1_ = bf16[2,512,256]{2,1,0:T(8,128)(2,1)S(1)} collective-permute-done((bf16[2,512,256]{2,1,0:T(8,128)(2,1)}, bf16[2,512,256]{2,1,0:T(8,128)(2,1)S(1)}, u32[]{:S(2)}, u32[]{:S(2)}) %collective-permute-start.40) | collective-permute-done | bytes 524320 | tf_op jit(solution)/shard_map/ppermute | solution.py:33
  628.3 4.3 join.1
  632.6 4.0 output.1.refs_1_
  653.4 3.0 add_blocks.5
  656.6 4.2 collective-permute-start.47
  660.8 3.3 halves.4.refs_2_
  664.2 4.2 collective-permute-done.42.refs_1_
  668.3 3.3 halves.5.refs_1_
  671.6 3.8 copied.1.refs_4_
  675.5 4.1 collective-permute-done.47.refs_3_
  679.6 3.2 project_last.1
  (142 shorter events, 82.4 us)
Async XLA Ops:
  7.2 120.7 %all-gather.6.cloned.1.call-start = ((), (), s32[]{:S(2)}) async-start(), calls=%async_computation.3 | async-start | bytes 7077888 | tf_op jit(solution)/shard_map/all_gather | solution.py:1080
  7.2 1.2 copy-start.6
  20.2 28.6 %collective-permute-start = (bf16[768,384]{1,0:T(8,128)(2,1)}, bf16[768,384]{1,0:T(8,128)(2,1)}, u32[]{:S(2)}, u32[]{:S(2)}) collective-permute-start(bf16[768,384]{1,0:T(8,128)(2,1)} %get-tuple-element.77), channel_id=1, source_target_pairs={{0,4},{4,0},{8,12},{12,8},{1,5},{5,1},{9,13},{13,9},{2,6},{6,2},{1... | collective-permute-start | bytes 1769480 | tf_op jit(solution)/shard_map/ppermute | solution.py:33
  23.2 42.7 %collective-permute-start.1 = (bf16[768,384]{1,0:T(8,128)(2,1)}, bf16[768,384]{1,0:T(8,128)(2,1)}, u32[]{:S(2)}, u32[]{:S(2)}) collective-permute-start(bf16[768,384]{1,0:T(8,128)(2,1)} %get-tuple-element.78), channel_id=1, source_target_pairs={{0,8},{4,12},{8,0},{12,4},{1,9},{5,13},{9,1},{13,5},{2,10},{6,14},... | collective-permute-start | bytes 1769480 | tf_op jit(solution)/shard_map/ppermute | solution.py:33
  25.8 40.2 %collective-permute-start.2 = (bf16[768,384]{1,0:T(8,128)(2,1)}, bf16[768,384]{1,0:T(8,128)(2,1)}, u32[]{:S(2)}, u32[]{:S(2)}) collective-permute-start(bf16[768,384]{1,0:T(8,128)(2,1)} %get-tuple-element.79), channel_id=1, source_target_pairs={{0,12},{4,8},{8,4},{12,0},{1,13},{5,9},{9,5},{13,1},{2,14},{6,10},... | collective-permute-start | bytes 1769480 | tf_op jit(solution)/shard_map/ppermute | solution.py:33
  66.7 156.9 %all-gather.8.cloned.1.call-start = ((), (), s32[]{:S(2)}) async-start(), calls=%async_computation.4 | async-start | bytes 7077888 | tf_op jit(solution)/shard_map/all_gather | solution.py:1091
  94.7 25.6 %collective-permute-start.3 = (bf16[768,128]{1,0:T(8,128)(2,1)}, bf16[768,128]{1,0:T(8,128)(2,1)}, u32[]{:S(2)}, u32[]{:S(2)}) collective-permute-start(bf16[768,128]{1,0:T(8,128)(2,1)} %get-tuple-element.83), channel_id=1, source_target_pairs={{0,4},{4,0},{8,12},{12,8},{1,5},{5,1},{9,13},{13,9},{2,6},{6,2},{1... | collective-permute-start | bytes 589832 | tf_op jit(solution)/shard_map/ppermute | solution.py:33
  106.5 14.3 %collective-permute-start.4 = (bf16[768,128]{1,0:T(8,128)(2,1)}, bf16[768,128]{1,0:T(8,128)(2,1)}, u32[]{:S(2)}, u32[]{:S(2)}) collective-permute-start(bf16[768,128]{1,0:T(8,128)(2,1)} %get-tuple-element.84), channel_id=1, source_target_pairs={{0,8},{4,12},{8,0},{12,4},{1,9},{5,13},{9,1},{13,5},{2,10},{6,14},... | collective-permute-start | bytes 589832 | tf_op jit(solution)/shard_map/ppermute | solution.py:33
  107.6 20.2 %collective-permute-start.5 = (bf16[768,128]{1,0:T(8,128)(2,1)}, bf16[768,128]{1,0:T(8,128)(2,1)}, u32[]{:S(2)}, u32[]{:S(2)}) collective-permute-start(bf16[768,128]{1,0:T(8,128)(2,1)} %get-tuple-element.85), channel_id=1, source_target_pairs={{0,12},{4,8},{8,4},{12,0},{1,13},{5,9},{9,5},{13,1},{2,14},{6,10},... | collective-permute-start | bytes 589832 | tf_op jit(solution)/shard_map/ppermute | solution.py:33
  134.1 3.8 collective-permute-start.6
  140.8 20.1 %collective-permute-start.7 = (bf16[192,2048]{1,0:T(8,128)(2,1)}, bf16[192,2048]{1,0:T(8,128)(2,1)}, u32[]{:S(2)}, u32[]{:S(2)}) collective-permute-start(bf16[192,2048]{1,0:T(8,128)(2,1)} %sums.8), channel_id=1, source_target_pairs={{0,2},{1,3},{2,0},{3,1},{4,6},{5,7},{6,4},{7,5},{8,10},{9,11},{10,... | collective-permute-start | bytes 2359304 | tf_op jit(solution)/shard_map/ppermute | solution.py:33
  164.8 208.1 %all-gather.12.cloned.1.call-start = ((), (), s32[]{:S(2)}) async-start(), calls=%async_computation.9 | async-start | bytes 3932160 | tf_op jit(solution)/shard_map/all_gather | solution.py:1095
  164.8 31.2 %collective-permute-start.9 = (bf16[192,2048]{1,0:T(8,128)(2,1)}, bf16[192,2048]{1,0:T(8,128)(2,1)}, u32[]{:S(2)}, u32[]{:S(2)}) collective-permute-start(bf16[192,2048]{1,0:T(8,128)(2,1)} %get-tuple-element.88.refs_2_.refs_0_), channel_id=1, source_target_pairs={{0,2},{1,3},{2,0},{3,1},{4,6},{5,7},{6,4},{7,5},{8,10},{9,11},{10,... | collective-permute-start | bytes 2359304 | tf_op jit(solution)/shard_map/ppermute | solution.py:33
  166.6 30.2 %collective-permute-start.8 = (bf16[192,2048]{1,0:T(8,128)(2,1)}, bf16[192,2048]{1,0:T(8,128)(2,1)}, u32[]{:S(2)}, u32[]{:S(2)}) collective-permute-start(bf16[192,2048]{1,0:T(8,128)(2,1)} %get-tuple-element.88.refs_2_.refs_0_), channel_id=1, source_target_pairs={{0,1},{1,0},{2,3},{3,2},{4,5},{5,4},{6,7},{7,6},{8,9},{9,8},{10,11... | collective-permute-start | bytes 2359304 | tf_op jit(solution)/shard_map/ppermute | solution.py:33
  196.7 2.9 collective-permute-start.10
  223.2 182.3 %reduce-scatter.4.cloned.1.call-start = ((), (), s32[]{:S(2)}) async-start(), calls=%async_computation.5 | async-start | bytes 5242880 | tf_op jit(solution)/shard_map/reduce_scatter | solution.py:1102
  246.4 3.8 collective-permute-start.12
  253.1 20.5 %collective-permute-start.13 = (bf16[192,2048]{1,0:T(8,128)(2,1)}, bf16[192,2048]{1,0:T(8,128)(2,1)}, u32[]{:S(2)}, u32[]{:S(2)}) collective-permute-start(bf16[192,2048]{1,0:T(8,128)(2,1)} %sums.9.refs_2_), channel_id=1, source_target_pairs={{0,2},{1,3},{2,0},{3,1},{4,6},{5,7},{6,4},{7,5},{8,10},{9,11},{10,... | collective-permute-start | bytes 2359304 | tf_op jit(solution)/shard_map/ppermute | solution.py:33
  276.8 23.5 %collective-permute-start.16 = (bf16[192,2048]{1,0:T(8,128)(2,1)}, bf16[192,2048]{1,0:T(8,128)(2,1)}, u32[]{:S(2)}, u32[]{:S(2)}) collective-permute-start(bf16[192,2048]{1,0:T(8,128)(2,1)} %sums.10.refs_2_), channel_id=1, source_target_pairs={{0,4},{4,0},{8,12},{12,8},{1,5},{5,1},{9,13},{13,9},{2,6},{6,2},{1... | collective-permute-start | bytes 2359304 | tf_op jit(solution)/shard_map/ppermute | solution.py:33
  301.0 1.4 copy-start.7
  301.1 238.2 %reduce-scatter.6.cloned.1.call-start = ((), (), s32[]{:S(2)}) async-start(), calls=%async_computation.6 | async-start | bytes 5242880 | tf_op jit(solution)/shard_map/reduce_scatter | solution.py:1102
  302.5 5.8 collective-permute-start.11
  302.5 18.9 %collective-permute-start.17 = (bf16[2,192,2048]{2,1,0:T(8,128)(2,1)}, bf16[2,192,2048]{2,1,0:T(8,128)(2,1)}, u32[]{:S(2)}, u32[]{:S(2)}) collective-permute-start(bf16[2,192,2048]{2,1,0:T(8,128)(2,1)} %get-tuple-element.99), channel_id=1, source_target_pairs={{0,1},{1,0},{2,3},{3,2},{4,5},{5,4},{6,7},{7,6},{8,9},{9,8},{10,11... | collective-permute-start | bytes 4718600 | tf_op jit(solution)/shard_map/ppermute | solution.py:33
  311.1 19.9 %collective-permute-start.15 = (bf16[192,2048]{1,0:T(8,128)(2,1)}, bf16[192,2048]{1,0:T(8,128)(2,1)}, u32[]{:S(2)}, u32[]{:S(2)}) collective-permute-start(bf16[192,2048]{1,0:T(8,128)(2,1)} %sums.11.refs_2_), channel_id=1, source_target_pairs={{0,2},{1,3},{2,0},{3,1},{4,6},{5,7},{6,4},{7,5},{8,10},{9,11},{10,... | collective-permute-start | bytes 2359304 | tf_op jit(solution)/shard_map/ppermute | solution.py:33
  321.3 34.1 %collective-permute-start.14 = (bf16[2,192,2048]{2,1,0:T(8,128)(2,1)}, bf16[2,192,2048]{2,1,0:T(8,128)(2,1)}, u32[]{:S(2)}, u32[]{:S(2)}) collective-permute-start(bf16[2,192,2048]{2,1,0:T(8,128)(2,1)} %get-tuple-element.97), channel_id=1, source_target_pairs={{0,1},{1,0},{2,3},{3,2},{4,5},{5,4},{6,7},{7,6},{8,9},{9,8},{10,11... | collective-permute-start | bytes 4718600 | tf_op jit(solution)/shard_map/ppermute | solution.py:33
  336.3 19.1 %collective-permute-start.21 = (bf16[192,2048]{1,0:T(8,128)(2,1)}, bf16[192,2048]{1,0:T(8,128)(2,1)}, u32[]{:S(2)}, u32[]{:S(2)}) collective-permute-start(bf16[192,2048]{1,0:T(8,128)(2,1)} %get-tuple-element.100.refs_2_.refs_0_), channel_id=1, source_target_pairs={{0,2},{1,3},{2,0},{3,1},{4,6},{5,7},{6,4},{7,5},{8,10},{9,11},{10,... | collective-permute-start | bytes 2359304 | tf_op jit(solution)/shard_map/ppermute | solution.py:33
  337.8 22.0 %collective-permute-start.20 = (bf16[192,2048]{1,0:T(8,128)(2,1)}, bf16[192,2048]{1,0:T(8,128)(2,1)}, u32[]{:S(2)}, u32[]{:S(2)}) collective-permute-start(bf16[192,2048]{1,0:T(8,128)(2,1)} %get-tuple-element.100.refs_2_.refs_0_), channel_id=1, source_target_pairs={{0,1},{1,0},{2,3},{3,2},{4,5},{5,4},{6,7},{7,6},{8,9},{9,8},{10,11... | collective-permute-start | bytes 2359304 | tf_op jit(solution)/shard_map/ppermute | solution.py:33
  355.4 4.4 collective-permute-start.22
  358.2 26.9 %collective-permute-start.18 = (bf16[192,2048]{1,0:T(8,128)(2,1)}, bf16[192,2048]{1,0:T(8,128)(2,1)}, u32[]{:S(2)}, u32[]{:S(2)}) collective-permute-start(bf16[192,2048]{1,0:T(8,128)(2,1)} %sums.13.refs_8_), channel_id=1, source_target_pairs={{0,2},{1,3},{2,0},{3,1},{4,6},{5,7},{6,4},{7,5},{8,10},{9,11},{10,... | collective-permute-start | bytes 2359304 | tf_op jit(solution)/shard_map/ppermute | solution.py:33
  368.4 29.6 %collective-permute-start.25 = (bf16[768,128]{1,0:T(8,128)(2,1)}, bf16[768,128]{1,0:T(8,128)(2,1)}, u32[]{:S(2)}, u32[]{:S(2)}) collective-permute-start(bf16[768,128]{1,0:T(8,128)(2,1)} %get-tuple-element.103), channel_id=1, source_target_pairs={{0,4},{4,0},{8,12},{12,8},{1,5},{5,1},{9,13},{13,9},{2,6},{6,2},{1... | collective-permute-start | bytes 589832 | tf_op jit(solution)/shard_map/ppermute | solution.py:33
  369.6 28.4 %collective-permute-start.26 = (bf16[768,128]{1,0:T(8,128)(2,1)}, bf16[768,128]{1,0:T(8,128)(2,1)}, u32[]{:S(2)}, u32[]{:S(2)}) collective-permute-start(bf16[768,128]{1,0:T(8,128)(2,1)} %get-tuple-element.104), channel_id=1, source_target_pairs={{0,8},{4,12},{8,0},{12,4},{1,9},{5,13},{9,1},{13,5},{2,10},{6,14},... | collective-permute-start | bytes 589832 | tf_op jit(solution)/shard_map/ppermute | solution.py:33
  371.9 26.1 %collective-permute-start.27 = (bf16[768,128]{1,0:T(8,128)(2,1)}, bf16[768,128]{1,0:T(8,128)(2,1)}, u32[]{:S(2)}, u32[]{:S(2)}) collective-permute-start(bf16[768,128]{1,0:T(8,128)(2,1)} %get-tuple-element.105), channel_id=1, source_target_pairs={{0,12},{4,8},{8,4},{12,0},{1,13},{5,9},{9,5},{13,1},{2,14},{6,10},... | collective-permute-start | bytes 589832 | tf_op jit(solution)/shard_map/ppermute | solution.py:33
  398.7 244.9 %reduce-scatter.8.cloned.1.call-start = ((), (), s32[]{:S(2)}) async-start(), calls=%async_computation.8 | async-start | bytes 5242880 | tf_op jit(solution)/shard_map/reduce_scatter | solution.py:1102
  399.2 53.2 %collective-permute-start.24 = (bf16[3,192,2048]{2,1,0:T(8,128)(2,1)}, bf16[3,192,2048]{2,1,0:T(8,128)(2,1)}, u32[]{:S(2)}, u32[]{:S(2)}) collective-permute-start(bf16[3,192,2048]{2,1,0:T(8,128)(2,1)} %others.1.refs_5_.refs_1_), channel_id=1, source_target_pairs={{0,2},{1,3},{2,0},{3,1},{4,6},{5,7},{6,4},{7,5},{8,10},{9,11},{10,... | collective-permute-start | bytes 7077896 | tf_op jit(solution)/shard_map/ppermute | solution.py:33
  399.8 48.1 %collective-permute-start.28 = (bf16[4,512,256]{2,1,0:T(8,128)(2,1)}, bf16[4,512,256]{2,1,0:T(8,128)(2,1)}, u32[]{:S(2)}, u32[]{:S(2)}) collective-permute-start(bf16[4,512,256]{2,1,0:T(8,128)(2,1)} %get-tuple-element.111), channel_id=1, source_target_pairs={{0,16},{16,0},{1,17},{17,1},{2,18},{18,2},{3,19},{19,3},{4,20},{20... | collective-permute-start | bytes 3145736 | tf_op jit(solution)/shard_map/ppermute | solution.py:33
  401.1 59.0 %collective-permute-start.23 = (bf16[3,192,2048]{2,1,0:T(8,128)(2,1)}, bf16[3,192,2048]{2,1,0:T(8,128)(2,1)}, u32[]{:S(2)}, u32[]{:S(2)}) collective-permute-start(bf16[3,192,2048]{2,1,0:T(8,128)(2,1)} %others.1.refs_5_.refs_1_), channel_id=1, source_target_pairs={{0,1},{1,0},{2,3},{3,2},{4,5},{5,4},{6,7},{7,6},{8,9},{9,8},{10,11... | collective-permute-start | bytes 7077896 | tf_op jit(solution)/shard_map/ppermute | solution.py:33
  408.1 44.3 %collective-permute-start.29 = (bf16[1,256,1024]{2,1,0:T(8,128)(2,1)}, bf16[1,256,1024]{2,1,0:T(8,128)(2,1)}, u32[]{:S(2)}, u32[]{:S(2)}) collective-permute-start(bf16[1,256,1024]{2,1,0:T(8,128)(2,1)} %one_block.3.refs_12_), channel_id=1, source_target_pairs={{0,4},{4,0},{8,12},{12,8},{1,5},{5,1},{9,13},{13,9},{2,6},{6,2},{1... | collective-permute-start | bytes 1572872 | tf_op jit(solution)/shard_map/ppermute | solution.py:33
  453.1 9.4 %collective-permute-start.30 = (bf16[3,192,2048]{2,1,0:T(8,128)(2,1)}, bf16[3,192,2048]{2,1,0:T(8,128)(2,1)}, u32[]{:S(2)}, u32[]{:S(2)}) collective-permute-start(bf16[3,192,2048]{2,1,0:T(8,128)(2,1)} %tie.14.refs_3_), channel_id=1, source_target_pairs={{0,1},{1,0},{2,3},{3,2},{4,5},{5,4},{6,7},{7,6},{8,9},{9,8},{10,11... | collective-permute-start | bytes 7077896 | tf_op jit(solution)/shard_map/ppermute | solution.py:33
  453.1 24.0 %collective-permute-start.19 = (bf16[192,2048]{1,0:T(8,128)(2,1)}, bf16[192,2048]{1,0:T(8,128)(2,1)}, u32[]{:S(2)}, u32[]{:S(2)}) collective-permute-start(bf16[192,2048]{1,0:T(8,128)(2,1)} %sums.12.refs_7_), channel_id=1, source_target_pairs={{0,2},{1,3},{2,0},{3,1},{4,6},{5,7},{6,4},{7,5},{8,10},{9,11},{10,... | collective-permute-start | bytes 2359304 | tf_op jit(solution)/shard_map/ppermute | solution.py:33
  453.7 46.3 %collective-permute-start.31 = (bf16[768,384]{1,0:T(8,128)(2,1)}, bf16[768,384]{1,0:T(8,128)(2,1)}, u32[]{:S(2)}, u32[]{:S(2)}) collective-permute-start(bf16[768,384]{1,0:T(8,128)(2,1)} %get-tuple-element.112.refs_6_), channel_id=1, source_target_pairs={{0,4},{4,0},{8,12},{12,8},{1,5},{5,1},{9,13},{13,9},{2,6},{6,2},{1... | collective-permute-start | bytes 1769480 | tf_op jit(solution)/shard_map/ppermute | solution.py:33
  460.1 60.3 %collective-permute-start.32 = (bf16[768,384]{1,0:T(8,128)(2,1)}, bf16[768,384]{1,0:T(8,128)(2,1)}, u32[]{:S(2)}, u32[]{:S(2)}) collective-permute-start(bf16[768,384]{1,0:T(8,128)(2,1)} %get-tuple-element.113.refs_7_), channel_id=1, source_target_pairs={{0,8},{4,12},{8,0},{12,4},{1,9},{5,13},{9,1},{13,5},{2,10},{6,14},... | collective-permute-start | bytes 1769480 | tf_op jit(solution)/shard_map/ppermute | solution.py:33
  460.1 60.3 %collective-permute-start.33 = (bf16[768,384]{1,0:T(8,128)(2,1)}, bf16[768,384]{1,0:T(8,128)(2,1)}, u32[]{:S(2)}, u32[]{:S(2)}) collective-permute-start(bf16[768,384]{1,0:T(8,128)(2,1)} %get-tuple-element.114.refs_8_), channel_id=1, source_target_pairs={{0,12},{4,8},{8,4},{12,0},{1,13},{5,9},{9,5},{13,1},{2,14},{6,10},... | collective-permute-start | bytes 1769480 | tf_op jit(solution)/shard_map/ppermute | solution.py:33
  521.1 150.6 %all-gather.10.cloned.1.call-start = ((), (), s32[]{:S(2)}) async-start(), calls=%async_computation.7 | async-start | bytes 3932160 | tf_op jit(solution)/shard_map/all_gather | solution.py:1182
  532.6 3.8 collective-permute-start.34
  539.3 19.9 %collective-permute-start.36 = (bf16[192,2048]{1,0:T(8,128)(2,1)}, bf16[192,2048]{1,0:T(8,128)(2,1)}, u32[]{:S(2)}, u32[]{:S(2)}) collective-permute-start(bf16[192,2048]{1,0:T(8,128)(2,1)} %sums.15.refs_2_.refs_1_), channel_id=1, source_target_pairs={{0,2},{1,3},{2,0},{3,1},{4,6},{5,7},{6,4},{7,5},{8,10},{9,11},{10,... | collective-permute-start | bytes 2359304 | tf_op jit(solution)/shard_map/ppermute | solution.py:33
  564.0 59.1 %collective-permute-start.38 = (bf16[208,2048]{1,0:T(8,128)(2,1)}, bf16[208,2048]{1,0:T(8,128)(2,1)S(1)}, u32[]{:S(2)}, u32[]{:S(2)}) collective-permute-start(bf16[208,2048]{1,0:T(8,128)(2,1)} %input_back.1.refs_0_.refs_4_), channel_id=1, source_target_pairs={{0,2},{1,3},{2,0},{3,1},{4,6},{5,7},{6,4},{7,5},{8,10},{9,11},{10,... | collective-permute-start | bytes 2555912 | tf_op jit(solution)/shard_map/ppermute | solution.py:33
  564.4 20.2 %copy-start = (bf16[208,2048]{1,0:T(8,128)(2,1)S(1)}, bf16[208,2048]{1,0:T(8,128)(2,1)}, u32[]{:S(2)}) copy-start(bf16[208,2048]{1,0:T(8,128)(2,1)} %input_back.1.refs_0_.refs_4_) | copy-start | bytes 2555908
  564.4 57.9 %collective-permute-start.39 = (bf16[4,256,384]{2,1,0:T(8,128)(2,1)}, bf16[4,256,384]{2,1,0:T(8,128)(2,1)S(1)}, u32[]{:S(2)}, u32[]{:S(2)}) collective-permute-start(bf16[4,256,384]{2,1,0:T(8,128)(2,1)} %get-tuple-element.127), channel_id=1, source_target_pairs={{0,16},{16,0},{1,17},{17,1},{2,18},{18,2},{3,19},{19,3},{4,20},{20... | collective-permute-start | bytes 2359304 | tf_op jit(solution)/shard_map/ppermute | solution.py:33
  566.5 55.8 %collective-permute-start.35 = (bf16[192,2048]{1,0:T(8,128)(2,1)}, bf16[192,2048]{1,0:T(8,128)(2,1)S(1)}, u32[]{:S(2)}, u32[]{:S(2)}) collective-permute-start(bf16[192,2048]{1,0:T(8,128)(2,1)} %tie.16), channel_id=1, source_target_pairs={{0,4},{4,0},{8,12},{12,8},{1,5},{5,1},{9,13},{13,9},{2,6},{6,2},{1... | collective-permute-start | bytes 2359304 | tf_op jit(solution)/shard_map/ppermute | solution.py:33
  584.5 37.8 %collective-permute-start.40 = (bf16[2,512,256]{2,1,0:T(8,128)(2,1)}, bf16[2,512,256]{2,1,0:T(8,128)(2,1)S(1)}, u32[]{:S(2)}, u32[]{:S(2)}) collective-permute-start(bf16[2,512,256]{2,1,0:T(8,128)(2,1)} %tie.18), channel_id=1, source_target_pairs={{0,8},{4,12},{8,0},{12,4},{1,9},{5,13},{9,1},{13,5},{2,10},{6,14},... | collective-permute-start | bytes 1572872 | tf_op jit(solution)/shard_map/ppermute | solution.py:33
  584.6 41.0 %collective-permute-start.37 = (bf16[208,2048]{1,0:T(8,128)(2,1)S(1)}, bf16[208,2048]{1,0:T(8,128)(2,1)}, u32[]{:S(2)}, u32[]{:S(2)}) collective-permute-start(bf16[208,2048]{1,0:T(8,128)(2,1)S(1)} %copy-done), channel_id=1, source_target_pairs={{0,1},{1,0},{2,3},{3,2},{4,5},{5,4},{6,7},{7,6},{8,9},{9,8},{10,11... | collective-permute-start | bytes 2555912 | tf_op jit(solution)/shard_map/ppermute | solution.py:33
  622.3 0.8 copy-start.4
  622.3 1.1 copy-start.3
  623.1 0.9 copy-start.2
  624.0 0.9 copy-start.1
  625.5 2.8 collective-permute-start.41
  637.1 23.7 %collective-permute-start.43 = (bf16[1,256,1024]{2,1,0:T(8,128)(2,1)}, bf16[1,256,1024]{2,1,0:T(8,128)(2,1)}, u32[]{:S(2)}, u32[]{:S(2)}) collective-permute-start(bf16[1,256,1024]{2,1,0:T(8,128)(2,1)} %one_block.4.refs_7_), channel_id=1, source_target_pairs={{0,4},{4,0},{8,12},{12,8},{1,5},{5,1},{9,13},{13,9},{2,6},{6,2},{1... | collective-permute-start | bytes 1572872 | tf_op jit(solution)/shard_map/ppermute | solution.py:33
  641.0 0.6 copy-start.5
  642.2 6.6 collective-permute-start.44
  646.1 22.2 %collective-permute-start.42 = (bf16[1,256,1024]{2,1,0:T(8,128)(2,1)}, bf16[1,256,1024]{2,1,0:T(8,128)(2,1)}, u32[]{:S(2)}, u32[]{:S(2)}) collective-permute-start(bf16[1,256,1024]{2,1,0:T(8,128)(2,1)} %one_block.5.refs_2_), channel_id=1, source_target_pairs={{0,4},{4,0},{8,12},{12,8},{1,5},{5,1},{9,13},{13,9},{2,6},{6,2},{1... | collective-permute-start | bytes 1572872 | tf_op jit(solution)/shard_map/ppermute | solution.py:33
  656.5 19.0 %collective-permute-start.45 = (bf16[272,384]{1,0:T(8,128)(2,1)}, bf16[272,384]{1,0:T(8,128)(2,1)}, u32[]{:S(2)}, u32[]{:S(2)}) collective-permute-start(bf16[272,384]{1,0:T(8,128)(2,1)} %get-tuple-element.133), channel_id=1, source_target_pairs={{0,4},{4,0},{8,12},{12,8},{1,5},{5,1},{9,13},{13,9},{2,6},{6,2},{1... | collective-permute-start | bytes 626696 | tf_op jit(solution)/shard_map/ppermute | solution.py:33
  656.5 19.0 %collective-permute-start.46 = (bf16[272,384]{1,0:T(8,128)(2,1)}, bf16[272,384]{1,0:T(8,128)(2,1)}, u32[]{:S(2)}, u32[]{:S(2)}) collective-permute-start(bf16[272,384]{1,0:T(8,128)(2,1)} %get-tuple-element.134), channel_id=1, source_target_pairs={{0,8},{4,12},{8,0},{12,4},{1,9},{5,13},{9,1},{13,5},{2,10},{6,14},... | collective-permute-start | bytes 626696 | tf_op jit(solution)/shard_map/ppermute | solution.py:33
  656.6 22.9 %collective-permute-start.47 = (bf16[272,384]{1,0:T(8,128)(2,1)}, bf16[272,384]{1,0:T(8,128)(2,1)}, u32[]{:S(2)}, u32[]{:S(2)}) collective-permute-start(bf16[272,384]{1,0:T(8,128)(2,1)} %get-tuple-element.135), channel_id=1, source_target_pairs={{0,12},{4,8},{8,4},{12,0},{1,13},{5,9},{9,5},{13,1},{2,14},{6,10},... | collective-permute-start | bytes 626696 | tf_op jit(solution)/shard_map/ppermute | solution.py:33
  660.8 23.3 %collective-permute-start.48 = (bf16[1,512,256]{2,1,0:T(8,128)(2,1)}, bf16[1,512,256]{2,1,0:T(8,128)(2,1)}, u32[]{:S(2)}, u32[]{:S(2)}) collective-permute-start(bf16[1,512,256]{2,1,0:T(8,128)(2,1)} %get-tuple-element.140), channel_id=1, source_target_pairs={{0,4},{4,0},{8,12},{12,8},{1,5},{5,1},{9,13},{13,9},{2,6},{6,2},{1... | collective-permute-start | bytes 786440 | tf_op jit(solution)/shard_map/ppermute | solution.py:33
Sparse Core Ops, SparseCore 0:
  66.8 56.5 all-gather.5
  164.9 46.0 all-gather.7
  223.4 62.7 all-gather.11
  301.2 104.3 reduce-scatter.3
  408.6 122.8 reduce-scatter.5
  534.3 101.4 reduce-scatter.7
  637.4 28.3 all-gather.9
